TPU v7x, 32 devices: a whole 2x2x4 slice. The times are simulated.
32 devices in a mesh: section: 4 (over y, x), dom: 8 (over z, core).
Axes of the slice: x: 2, y: 2, z: 4, core: 2. Of those that a mesh axis runs over, the one named last changes fastest.
Arguments:
- features: bfloat16 [4, 16384, 128], P(None, 'dom'), may hold values from -6 to 6
- sources: int32 [4, 16384, 8], P(None, 'dom'), may hold values from 0 to 2111, as said below
- send_index: int32 [4, 512], P(None, 'dom'), may hold values from 0 to 2047, as said below
- labels: int32 [4, 16384], P(None, 'dom'), may hold values from 0 to 39
- label_mask: int32 [4, 16384], P(None, 'dom'), may hold values from 0 to 1, as said below
- w_in: float32 [128, 256], P('dom'), may hold values from -0.5 to 0.5
- w_gat: float32 [2, 2, 256, 256], P(None, None, 'dom'), may hold values from -0.375 to 0.375
- w_out: float32 [64, 40], P('dom'), may hold values from -0.75 to 0.75
- small_params: float32 [1128], replicated, may hold values from -1 to 1
- stat_l_in: float32 [128, 128], P('dom')
- stat_r_in: float32 [256, 256], replicated
- stat_l_gat: float32 [2, 2, 256, 256], P(None, None, 'dom')
- stat_r_gat: float32 [2, 2, 256, 256], replicated, as said below
- stat_l_out: float32 [64, 64], P('dom')
- stat_r_out: float32 [40, 40], replicated
- root_l_in: float32 [128, 128], P('dom')
- root_r_in: float32 [256, 256], replicated
- root_l_gat: float32 [2, 2, 256, 256], P(None, None, 'dom')
- root_r_gat: float32 [2, 2, 256, 256], replicated, as said below
- root_l_out: float32 [64, 64], P('dom')
- root_r_out: float32 [40, 40], replicated
- adam_first: float32 [1128], replicated
- adam_second: float32 [1128], replicated
- ema_in: float32 [128, 256], P('dom'), may hold values from -0.5 to 0.5
- ema_gat: float32 [2, 2, 256, 256], P(None, None, 'dom'), may hold values from -0.375 to 0.375
- ema_out: float32 [64, 40], P('dom'), may hold values from -0.75 to 0.75
- ema_small: float32 [1128], replicated, may hold values from -1 to 1
Outputs:
- new_w_in: float32 [128, 256], P('dom')
- new_w_gat: float32 [2, 2, 256, 256], P(None, None, 'dom')
- new_w_out: float32 [64, 40], P('dom')
- new_small: float32 [1128], replicated
- new_l_in: float32 [128, 128], P('dom')
- new_r_in: float32 [256, 256], replicated
- new_l_gat: float32 [2, 2, 256, 256], P(None, None, 'dom')
- new_r_gat: float32 [2, 2, 256, 256], replicated
- new_l_out: float32 [64, 64], P('dom')
- new_r_out: float32 [40, 40], replicated
- new_first: float32 [1128], replicated
- new_second: float32 [1128], replicated
- new_ema_in: float32 [128, 256], P('dom')
- new_ema_gat: float32 [2, 2, 256, 256], P(None, None, 'dom')
- new_ema_out: float32 [64, 40], P('dom')
- new_ema_small: float32 [1128], replicated
- mean_loss: float32 [], replicated
- grad_norm: float32 [], replicated
Inputs may be any that keep to these rules, and one draw needn't show every extreme that they name: `sources`: every source is a node of the same graph: graphs of 64 nodes, 32 of them on either side of each partition boundary; entries below 2048 are the partition's own nodes, 2048 + j the j-th extended row from the previous partition, 2080 + j the j-th from the next. `send_index`: per partition the first 32 entries are its nodes 0 to 31 in some order, the last 32 its nodes 2016 to 2047 in some order. `label_mask`: node 0 of every micro-batch counts. `stat_r_gat`: symmetric. `root_r_gat`: symmetric.
All inputs are finite; a program needn't handle non-finite values.
Results may differ from a plain program's by a relative error of at most 0.014.
Values may be sent and summed in bfloat16 or wider, within the bound.
No kernel may reach another device: no remote copies, remote signals or barrier semaphores. Data moves between devices by JAX's collectives and lax.ppermute only.
A program may use at most 384 MiB of HBM per device.

v0:
```python
from functools import partial

import jax
import jax.numpy as jnp
from jax import lax
from jax.sharding import PartitionSpec as P

FEAT = 128
HEADS = 4
HSIZE = 64
CLASSES = 40
STEPS = 5
HID = 256
SMALL = 1128


highest = lax.Precision.HIGHEST
leak_slope = 0.2
smooth = 0.1
clip_norm = 0.001
shampoo_rate = 0.3
shampoo_decay = 0.5
weight_decay = 0.0001
adam_rate = 0.1
beta_one = 0.9
beta_two = 0.999
adam_eps = 1e-08
adam_decay = 0.01
ema_keep = 0.9


def with_halo(value, sides, width):
    for axis, dim in sides:
        size, length = (lax.axis_size(axis), value.shape[dim])
        up = [(i, (i + 1) % size) for i in range(size)]
        down = [(j, i) for i, j in up]
        last = lax.slice_in_dim(value, length - width, length, axis=dim)
        initial = lax.slice_in_dim(value, 0, width, axis=dim)
        before = lax.ppermute(last, axis, up)
        after = lax.ppermute(initial, axis, down)
        value = jnp.concatenate([before, value, after], axis=dim)
    return value


def leaky_relu(values):
    return jnp.where(values > 0, values, leak_slope * values)


def elu_slope(values):
    return jnp.where(values > 0, 1.0, jnp.exp(jnp.minimum(values, 0.0)))


def attend(left_rows, right_rows, attention, sources_all):
    count_nodes = right_rows.shape[0]
    picked = left_rows[sources_all]
    mixed_rows = leaky_relu(picked + right_rows[:, None, :])
    heads_view = mixed_rows.reshape(count_nodes, -1, HEADS, HSIZE)
    scores = jnp.einsum("nkhd,hd->nkh", heads_view, attention, precision=highest)
    weights = jnp.exp(scores)
    weights = weights / jnp.sum(weights, axis=1, keepdims=True)
    values = picked.reshape(count_nodes, -1, HEADS, HSIZE)
    result = jnp.einsum("nkh,nkhd->nhd", weights, values, precision=highest)
    return result.reshape(count_nodes, HEADS * HSIZE)


def split_small(small_params):
    bias_in = small_params[0:HID]
    attention = small_params[HID : 3 * HID].reshape(2, HEADS, HSIZE)
    bias_one = small_params[3 * HID : 4 * HID]
    bias_two = small_params[4 * HID : 4 * HID + HSIZE]
    bias_out = small_params[4 * HID + HSIZE :]
    return (bias_in, attention, bias_one, bias_two, bias_out)


def assemble(bias_in_g, att_g, bias_one_g, bias_two_g, bias_out_g):
    return jnp.concatenate([bias_in_g, att_g, bias_one_g, bias_two_g, bias_out_g])


def zero_grads():
    return (
        jnp.zeros((FEAT, HID), jnp.float32),
        jnp.zeros((2, 2, HID, HID), jnp.float32),
        jnp.zeros((HSIZE, CLASSES), jnp.float32),
        jnp.zeros((SMALL,), jnp.float32),
        jnp.zeros((), jnp.float32),
    )


def scaled_sum(totals, terms, factor):
    return tuple((total_one + term_one * factor for total_one, term_one in zip(totals, terms)))


def precondition(gradient, weight_rows, stat_rows, stat_right, root_rows, root_right, start):
    count_rows = weight_rows.shape[-2]
    grad_rows = lax.dynamic_slice_in_dim(gradient, start, count_rows, gradient.ndim - 2)
    flipped = jnp.swapaxes(gradient, -1, -2)
    new_left = shampoo_decay * stat_rows + (1.0 - shampoo_decay) * jnp.matmul(
        grad_rows, flipped, precision=highest
    )
    new_right = shampoo_decay * stat_right + (1.0 - shampoo_decay) * jnp.matmul(
        flipped, gradient, precision=highest
    )
    update = jnp.matmul(
        root_rows, jnp.matmul(gradient, root_right, precision=highest), precision=highest
    )
    new_weight = weight_rows - shampoo_rate * (update + weight_decay * weight_rows)
    return (new_weight, new_left, new_right)


def adamw_step(parameter, gradient, moment_one, moment_two):
    moment_one = beta_one * moment_one + (1.0 - beta_one) * gradient
    moment_two = beta_two * moment_two + (1.0 - beta_two) * gradient * gradient
    corr_one = 1.0 - beta_one**STEPS
    corr_two = 1.0 - beta_two**STEPS
    update = moment_one / corr_one / (jnp.sqrt(moment_two / corr_two) + adam_eps)
    return (parameter - adam_rate * (update + adam_decay * parameter), moment_one, moment_two)


def average(old_value, new_value):
    return ema_keep * old_value + (1.0 - ema_keep) * new_value


def per_device(
    features,
    sources,
    send_index,
    labels,
    label_mask,
    w_in,
    w_gat,
    w_out,
    small_params,
    stat_l_in,
    stat_r_in,
    stat_l_gat,
    stat_r_gat,
    stat_l_out,
    stat_r_out,
    root_l_in,
    root_r_in,
    root_l_gat,
    root_r_gat,
    root_l_out,
    root_r_out,
    adam_first,
    adam_second,
    ema_in,
    ema_gat,
    ema_out,
    ema_small,
):
    full_in, full_gat, full_out = (
        lax.all_gather(w_in.astype(jnp.bfloat16), "dom", axis=0, tiled=True),
        lax.all_gather(w_gat.astype(jnp.bfloat16), "dom", axis=2, tiled=True),
        lax.all_gather(w_out.astype(jnp.bfloat16), "dom", axis=0, tiled=True),
    )
    label_count = lax.psum(jnp.sum(label_mask.astype(jnp.float32)), "dom")
    node_count = features.shape[1]
    halo_width = send_index.shape[1] // 2
    section_id = lax.axis_index("section")
    bias_in, attention, bias_one, bias_two, bias_out = split_small(small_params)
    self_index = jnp.arange(node_count, dtype=jnp.int32)[:, None]
    zero_halo = jnp.zeros((2 * halo_width, HID), jnp.bfloat16)

    def sources_of(micro_idx):
        return jnp.concatenate([self_index, sources[micro_idx]], axis=1)

    def project(layer_no, inputs, halo_rows):
        extended = jnp.concatenate([inputs, halo_rows], axis=0)
        left_proj = jnp.dot(
            extended, full_gat[layer_no, 0], preferred_element_type=jnp.float32
        ).astype(jnp.bfloat16)
        right_proj = jnp.dot(
            inputs, full_gat[layer_no, 1], preferred_element_type=jnp.float32
        ).astype(jnp.bfloat16)
        return (extended, left_proj, right_proj)

    def input_pre(micro_idx):
        return jnp.dot(features[micro_idx], full_in, preferred_element_type=jnp.float32) + bias_in

    micro_idx = section_id
    kept_inputs = []
    kept_halos = []
    current = jax.nn.elu(input_pre(micro_idx)).astype(jnp.bfloat16)
    for layer_no in range(2):
        outgoing = current[send_index[micro_idx]]
        received = with_halo(outgoing, (("dom", 0),), halo_width)
        halo_rows = jnp.concatenate([received[:halo_width], received[3 * halo_width :]], axis=0)
        kept_inputs.append(current)
        kept_halos.append(halo_rows)
        forward_extended, forward_left_proj, forward_right_proj = project(
            layer_no, current, halo_rows
        )
        forward_layer_out = attend(
            forward_left_proj.astype(jnp.float32),
            forward_right_proj.astype(jnp.float32),
            attention[layer_no],
            sources_of(micro_idx),
        )
        if layer_no == 0:
            forward_layer_out = jax.nn.elu(forward_layer_out + bias_one)
        current = forward_layer_out.astype(jnp.bfloat16)
    head_view = current.astype(jnp.float32).reshape(node_count, HEADS, HSIZE)
    pooled = (jnp.mean(head_view, axis=1) + bias_two).astype(jnp.bfloat16)
    logits = jnp.dot(pooled, full_out, preferred_element_type=jnp.float32) + bias_out
    log_prob = jax.nn.log_softmax(logits, axis=-1)
    onehot = (labels[micro_idx][:, None] == jnp.arange(CLASSES, dtype=jnp.int32)[None, :]).astype(
        jnp.float32
    )
    mask_now = label_mask[micro_idx].astype(jnp.float32)
    per_node = -(
        (1.0 - smooth) * jnp.sum(onehot * log_prob, axis=1)
        + smooth / CLASSES * jnp.sum(log_prob, axis=1)
    )
    tick_loss = jnp.sum(per_node * mask_now)
    d_logits = (jnp.exp(log_prob) - (1.0 - smooth) * onehot - smooth / CLASSES) * (
        mask_now / label_count
    )[:, None]
    d_logits = d_logits.astype(jnp.bfloat16)
    g_out = jnp.einsum("nh,nc->hc", pooled, d_logits, preferred_element_type=jnp.float32)
    d_pooled = jnp.einsum("nc,hc->nh", d_logits, full_out, preferred_element_type=jnp.float32)
    g_small = assemble(
        jnp.zeros((HID,), jnp.float32),
        jnp.zeros((2 * HID,), jnp.float32),
        jnp.zeros((HID,), jnp.float32),
        jnp.sum(d_pooled, axis=0),
        jnp.sum(d_logits.astype(jnp.float32), axis=0),
    )
    d_inputs = jnp.broadcast_to(d_pooled[:, None, :] / HEADS, (node_count, HEADS, HSIZE)).reshape(
        node_count, HID
    )
    empty = zero_grads()
    d_inputs, d_halo, totals = (
        d_inputs,
        zero_halo,
        (empty[0], empty[1], g_out, g_small, tick_loss),
    )
    coming = d_inputs.astype(jnp.bfloat16)
    for layer_no in (1, 0):
        backward_inputs = kept_inputs[layer_no]
        backward_halo_rows = kept_halos[layer_no]
        backward_extended, backward_left_proj, backward_right_proj = project(
            layer_no, backward_inputs, backward_halo_rows
        )
        layer_out, pullback = jax.vjp(
            partial(attend, sources_all=sources_of(micro_idx)),
            backward_left_proj.astype(jnp.float32),
            backward_right_proj.astype(jnp.float32),
            attention[layer_no],
        )
        d_out = coming.astype(jnp.float32)
        bias_grad = jnp.zeros((HID,), jnp.float32)
        if layer_no == 0:
            d_out = d_out * elu_slope(layer_out + bias_one)
            bias_grad = jnp.sum(d_out, axis=0)
        d_left, d_right, d_att = pullback(d_out)
        d_left = d_left.astype(jnp.bfloat16)
        d_right = d_right.astype(jnp.bfloat16)
        g_left = jnp.einsum(
            "nf,ng->fg", backward_extended, d_left, preferred_element_type=jnp.float32
        )
        g_right = jnp.einsum(
            "nf,ng->fg", backward_inputs, d_right, preferred_element_type=jnp.float32
        )
        d_ext = jnp.einsum(
            "ng,fg->nf", d_left, full_gat[layer_no, 0], preferred_element_type=jnp.float32
        )
        backward_d_inputs = d_ext[:node_count] + jnp.einsum(
            "ng,fg->nf", d_right, full_gat[layer_no, 1], preferred_element_type=jnp.float32
        )
        backward_d_halo = d_ext[node_count:].astype(jnp.bfloat16)
        g_gat = (
            jnp.zeros((2, 2, HID, HID), jnp.float32).at[layer_no].set(jnp.stack([g_left, g_right]))
        )
        att_grad = jnp.zeros((2, HEADS, HSIZE), jnp.float32).at[layer_no].set(d_att)
        backward_g_small = assemble(
            jnp.zeros((HID,), jnp.float32),
            att_grad.reshape(-1),
            bias_grad,
            jnp.zeros((HSIZE,), jnp.float32),
            jnp.zeros((CLASSES,), jnp.float32),
        )
        backward_empty = zero_grads()
        d_inputs = backward_d_inputs
        d_halo = backward_d_halo
        layer_grads = (
            backward_empty[0],
            g_gat,
            backward_empty[2],
            backward_g_small,
            backward_empty[4],
        )
        returned = with_halo(d_halo, (("dom", 0),), halo_width)
        back_rows = jnp.concatenate(
            [returned[:halo_width], returned[3 * halo_width :]], axis=0
        ).astype(jnp.float32)
        d_inputs = d_inputs.at[send_index[micro_idx]].add(back_rows)
        coming = d_inputs.astype(jnp.bfloat16)
        totals = scaled_sum(totals, layer_grads, 1.0)
    pre_act = input_pre(micro_idx)
    d_pre = (coming.astype(jnp.float32) * elu_slope(pre_act)).astype(jnp.bfloat16)
    g_in = jnp.einsum("nf,ng->fg", features[micro_idx], d_pre, preferred_element_type=jnp.float32)
    g_small = assemble(
        jnp.sum(d_pre.astype(jnp.float32), axis=0),
        jnp.zeros((2 * HID,), jnp.float32),
        jnp.zeros((HID,), jnp.float32),
        jnp.zeros((HSIZE,), jnp.float32),
        jnp.zeros((CLASSES,), jnp.float32),
    )
    empty = zero_grads()
    input_grads = (g_in, empty[1], empty[2], g_small, empty[4])
    totals = scaled_sum(totals, input_grads, 1.0)
    sum_a, sum_b, sum_c, sum_d, sum_e = totals
    summed = lax.psum((sum_a, sum_b, sum_c, sum_d, sum_e), ("section", "dom"))
    grad_in, grad_gat, grad_out, grad_small, loss_total = summed
    grad_norm = jnp.sqrt(
        jnp.sum(grad_in * grad_in)
        + jnp.sum(grad_gat * grad_gat)
        + jnp.sum(grad_out * grad_out)
        + jnp.sum(grad_small * grad_small)
    )
    clip_scale = jnp.minimum(1.0, clip_norm / grad_norm)
    dom_id = lax.axis_index("dom")
    new_w_in, new_l_in, new_r_in = precondition(
        grad_in * clip_scale,
        w_in,
        stat_l_in,
        stat_r_in,
        root_l_in,
        root_r_in,
        dom_id * w_in.shape[0],
    )
    new_w_gat, new_l_gat, new_r_gat = precondition(
        grad_gat * clip_scale,
        w_gat,
        stat_l_gat,
        stat_r_gat,
        root_l_gat,
        root_r_gat,
        dom_id * w_gat.shape[2],
    )
    new_w_out, new_l_out, new_r_out = precondition(
        grad_out * clip_scale,
        w_out,
        stat_l_out,
        stat_r_out,
        root_l_out,
        root_r_out,
        dom_id * w_out.shape[0],
    )
    new_small, new_first, new_second = adamw_step(
        small_params, grad_small * clip_scale, adam_first, adam_second
    )
    mean_loss = loss_total / label_count
    return (
        new_w_in,
        new_w_gat,
        new_w_out,
        new_small,
        new_l_in,
        new_r_in,
        new_l_gat,
        new_r_gat,
        new_l_out,
        new_r_out,
        new_first,
        new_second,
        average(ema_in, new_w_in),
        average(ema_gat, new_w_gat),
        average(ema_out, new_w_out),
        average(ema_small, new_small),
        mean_loss,
        grad_norm,
    )


def solution(mesh):
    placed = (
        P(None, "dom", None),
        P(None, "dom", None),
        P(None, "dom"),
        P(None, "dom"),
        P(None, "dom"),
        P("dom", None),
        P(None, None, "dom", None),
        P("dom", None),
        P(),
        P("dom", None),
        P(),
        P(None, None, "dom", None),
        P(),
        P("dom", None),
        P(),
        P("dom", None),
        P(),
        P(None, None, "dom", None),
        P(),
        P("dom", None),
        P(),
        P(),
        P(),
        P("dom", None),
        P(None, None, "dom", None),
        P("dom", None),
        P(),
    )
    return jax.shard_map(
        per_device,
        mesh=mesh,
        in_specs=placed,
        out_specs=(
            P("dom", None),
            P(None, None, "dom", None),
            P("dom", None),
            P(),
            P("dom", None),
            P(),
            P(None, None, "dom", None),
            P(),
            P("dom", None),
            P(),
            P(),
            P(),
            P("dom", None),
            P(None, None, "dom", None),
            P("dom", None),
            P(),
            P(),
            P(),
        ),
        check_vma=False,
    )
```

profile of v0, /device:TPU:0, one launch (start us, length us, event | category | flops | bytes accessed | tf_op | source)
XLA Modules:
  0.0 1771.4 jit_solution(18063301848573971866)
XLA Ops:
  9.7 15.6 all_gather.9
  34.1 14.5 psum.42
  50.4 15.8 all_gather.10
  78.8 4.8 copy.116
  83.5 13.6 all_gather.11
  100.1 71.1 %gather_fusion.1 = f32[18432,256]{1,0:T(8,128)} fusion(f32[2112,256]{1,0:T(8,128)} %get-tuple-element.106, s32[18432]{0:T(1024)S(1)} %broadcast_clamp_fusion), kind=kCustom, calls=%fused_computation.1 | custom fusion | bytes 37822464 | tf_op jit(solution)/shard_map/gather | solution.py:55
  171.3 32.1 %gather.24 = f32[2048,9,4,64]{3,2,1,0:T(4,128)} reshape(f32[18432,256]{1,0:T(8,128)} %gather_fusion.1) | data formatting | bytes 37748736 | tf_op jit(solution)/shard_map/gather | solution.py:55
  203.4 30.3 %multiply_reduce_fusion.6 = f32[4,2048,9]{0,2,1:T(8,128)S(1)} fusion(f32[2048,9,4,64]{3,2,1,0:T(4,128)} %gather.24, f32[4,64]{1,0:T(4,128)S(1)} %squeeze.20, f32[2048,4,64]{2,1,0:T(4,128)} %copy.116), kind=kLoop, calls=%fused_computation.18 | loop fusion | flops 28237824 | bytes 21267456 | tf_op jit(solution)/shard_map/nkhd,hd->nkh/dot_general | solution.py:58
  233.7 10.9 bitcast_reduce_fusion.1
  245.8 6.9 fusion.13
  252.7 72.8 %gather_fusion.2 = bf16[18432,256]{1,0:T(8,128)(2,1)} fusion(bf16[2112,256]{1,0:T(8,128)(2,1)S(1)} %get-tuple-element.107, s32[18432]{0:T(1024)S(1)} %broadcast_clamp_fusion), kind=kCustom, calls=%fused_computation.2 | custom fusion | bytes 18948096 | tf_op jit(solution)/shard_map/gather | solution.py:55
  325.5 27.5 %reshape.405 = bf16[2048,9,4,64]{3,2,1,0:T(4,128)(2,1)} reshape(bf16[18432,256]{1,0:T(8,128)(2,1)} %gather_fusion.2) | data formatting | bytes 18874368 | tf_op jit(solution)/shard_map/reshape | solution.py:61
  353.0 30.4 %multiply_reduce_fusion.5 = f32[2048,4,64]{2,1,0:T(4,128)} fusion(f32[2048,4,9]{1,2,0:T(8,128)} %fusion.13, bf16[2048,9,4,64]{3,2,1,0:T(4,128)(2,1)} %reshape.405), kind=kLoop, calls=%fused_computation.17 | loop fusion | flops 13631488 | bytes 11829248
  383.5 5.2 copy.145
  388.7 3.6 fusion.24
  405.1 24.1 %reshape.427 = f32[2048,9,256]{2,1,0:T(8,128)} reshape(f32[18432,256]{1,0:T(8,128)} %gather_fusion.1) | data formatting | bytes 37748736 | tf_op jit(solution)/shard_map/gather | solution.py:55
  429.2 10.4 copy.143
  439.6 30.6 %copy.127 = f32[2048,9,256]{0,2,1:T(8,128)} copy(f32[2048,9,256]{2,1,0:T(8,128)} %reshape.427) | data formatting | bytes 37748736 | tf_op jit(solution)/shard_map/gather | solution.py:55
  470.2 4.8 copy.118
  478.0 71.0 %gather_fusion.4 = f32[18432,256]{1,0:T(8,128)} fusion(f32[2112,256]{1,0:T(8,128)} %get-tuple-element.108, s32[18432]{0:T(1024)S(1)} %broadcast_clamp_fusion), kind=kCustom, calls=%fused_computation.4 | custom fusion | bytes 37822464 | tf_op jit(solution)/shard_map/gather | solution.py:55
  549.0 24.1 %reshape.451 = f32[2048,9,256]{2,1,0:T(8,128)} reshape(f32[18432,256]{1,0:T(8,128)} %gather_fusion.4) | data formatting | bytes 37748736 | tf_op jit(solution)/shard_map/gather | solution.py:55
  573.1 32.1 %gather.28 = f32[2048,9,4,64]{3,2,1,0:T(4,128)} reshape(f32[18432,256]{1,0:T(8,128)} %gather_fusion.4) | data formatting | bytes 37748736 | tf_op jit(solution)/shard_map/gather | solution.py:55
  605.2 30.3 %multiply_reduce_fusion.4 = f32[4,2048,9]{0,2,1:T(8,128)S(1)} fusion(f32[2048,9,4,64]{3,2,1,0:T(4,128)} %gather.28, f32[4,64]{1,0:T(4,128)S(1)} %copy-done.46, f32[2048,4,64]{2,1,0:T(4,128)} %copy.118), kind=kLoop, calls=%fused_computation.16 | loop fusion | flops 28237824 | bytes 21267456 | tf_op jit(solution)/shard_map/nkhd,hd->nkh/dot_general | solution.py:58
  635.5 10.9 bitcast_reduce_fusion
  647.7 7.1 fusion.12
  654.8 72.8 %gather_fusion.5 = bf16[18432,256]{1,0:T(8,128)(2,1)} fusion(bf16[2112,256]{1,0:T(8,128)(2,1)S(1)} %get-tuple-element.109, s32[18432]{0:T(1024)S(1)} %broadcast_clamp_fusion), kind=kCustom, calls=%fused_computation.5 | custom fusion | bytes 18948096 | tf_op jit(solution)/shard_map/gather | solution.py:55
  727.5 27.5 %reshape.407 = bf16[2048,9,4,64]{3,2,1,0:T(4,128)(2,1)} reshape(bf16[18432,256]{1,0:T(8,128)(2,1)} %gather_fusion.5) | data formatting | bytes 18874368 | tf_op jit(solution)/shard_map/reshape | solution.py:61
  755.1 9.9 copy.157
  765.1 29.8 %multiply_reduce_fusion.3 = bf16[2048,4,64]{2,1,0:T(4,128)(2,1)} fusion(f32[2048,4,9]{1,2,0:T(8,128)} %fusion.12, bf16[2048,9,4,64]{3,2,1,0:T(4,128)(2,1)} %reshape.407), kind=kLoop, calls=%fused_computation.15 | loop fusion | flops 13631488 | bytes 10780672
  802.6 21.0 %fusion = f32[2048,4,1,9]{3,2,1,0:T(1,128)} fusion(bf16[2048,9,4,64]{3,2,1,0:T(4,128)(2,1)} %reshape.407, bf16[2048,64]{1,0:T(8,128)(2,1)S(1)} %copy.186), kind=kOutput, calls=%fused_computation.23 | convolution fusion | flops 9437184 | bytes 9994240 | tf_op jit(solution)/shard_map/transpose(jvp(nkh,nkhd->nhd))/dot_general | solution.py:62
  823.6 18.1 %copy.162 = f32[2048,4,1,9]{1,3,0,2:T(8,128)} copy(f32[2048,4,1,9]{3,2,1,0:T(1,128)} %fusion) | data formatting | bytes 589824 | tf_op jit(solution)/shard_map/transpose(jvp(nkh,nkhd->nhd))/dot_general | solution.py:62
  841.8 16.2 fusion.11
  858.1 12.9 fusion.7
  871.1 35.0 %add_reduce_fusion.1 = bf16[2048,4,64]{2,1,0:T(4,128)(2,1)} fusion(f32[2048,9,4,64]{3,2,1,0:T(4,128)} %gather.28, f32[2048,4,64]{2,1,0:T(4,128)} %copy.118, f32[4,64]{1,0:T(4,128)S(1)} %copy-done.46, f32[4,2048,9]{0,2,1:T(8,128)} %fusion.7), kind=kLoop, calls=%fused_computation.21 | loop fusion | flops 37224448 | bytes 22316032 | tf_op jit(solution)/shard_map/transpose(jvp())/reduce_sum | solution.py:56
  906.1 32.2 %multiply_reduce_fusion.1 = (f32[4,64]{1,0:T(4,128)}, f32[2048,9,4,64]{3,2,1,0:T(4,128)}) fusion(f32[2048,9,4,64]{3,2,1,0:T(4,128)} %gather.28, f32[4,2048,9]{0,2,1:T(8,128)} %fusion.7, f32[2048,4,64]{2,1,0:T(4,128)} %copy.118, f32[4,64]{1,0:T(4,128)S(1)} %copy-done.46), kind=kLoop, calls=%fused_computation.13 | loop fusion | flops 33029888 | bytes 40142848 | tf_op jit(solution)/shard_map/transpose(jvp(nkhd,hd->nkh))/dot_general | solution.py:58
  938.3 30.6 %copy.120 = f32[2048,9,256]{0,2,1:T(8,128)} copy(f32[2048,9,256]{2,1,0:T(8,128)} %reshape.451) | data formatting | bytes 37748736 | tf_op jit(solution)/shard_map/gather | solution.py:55
  968.9 4.1 copy.124
  972.9 34.1 %copy.122 = f32[2048,9,4,64]{0,3,2,1:T(8,128)} copy(f32[2048,9,4,64]{3,2,1,0:T(4,128)} %get-tuple-element.86) | data formatting | bytes 37748736 | tf_op jit(solution)/shard_map/transpose(jvp(nkhd,hd->nkh))/transpose | solution.py:58
  1007.1 8.8 broadcast_multiply_fusion.1
  1015.8 25.3 %bitcast_add_fusion.1 = f32[2048,9,256]{0,2,1:T(8,128)} fusion(f32[2048,4,64,9]{0,2,1,3:T(8,128)} %broadcast_multiply_fusion.1, f32[2048,9,4,64]{0,3,2,1:T(8,128)} %copy.122, f32[2048,9,256]{0,2,1:T(8,128)} %copy.120, f32[2048,256]{0,1:T(8,128)S(1)} %copy-done.9), kind=kLoop, calls=%fused_computation.26 | loop fusion | flops 33030144 | bytes 77594624 | tf_op jit(solution)/shard_map/transpose(jvp())/add_any | solution.py:56
  1041.2 26.4 %copy.123 = f32[2048,9,256]{2,1,0:T(8,128)} copy(f32[2048,9,256]{0,2,1:T(8,128)} %bitcast_add_fusion.1) | data formatting | bytes 37748736 | tf_op jit(solution)/shard_map/transpose(jvp())/add_any | solution.py:56
  1067.6 26.5 %reshape.470 = f32[18432,256]{1,0:T(8,128)} reshape(f32[2048,9,256]{2,1,0:T(8,128)} %copy.123) | data formatting | bytes 37748736 | tf_op jit(solution)/shard_map/transpose(jvp())/add_any | solution.py:56
  1094.1 100.5 %scatter_custom_fusion = f32[2112,256]{1,0:T(8,128)} fusion(s32[18432]{0:T(1024)} %copy-done.31, f32[18432,256]{1,0:T(8,128)} %reshape.470, f32[]{:T(128)} %constant.191.clone.1), kind=kCustom, calls=%fused_computation.118 | custom fusion | flops 4718592 | bytes 2163200 | tf_op jit(solution)/shard_map/transpose(jvp())/scatter-add | solution.py:55
  1196.9 3.5 collective-permute-start.5
  1206.2 4.2 scatter_custom_fusion.1
  1210.4 4.7 fusion.84
  1218.0 4.8 copy.187
  1222.8 29.9 %multiply_reduce_fusion.2 = f32[2048,4,9]{1,2,0:T(8,128)} fusion(f32[2048,4,64]{2,1,0:T(4,128)} %copy.187, bf16[2048,9,4,64]{3,2,1,0:T(4,128)(2,1)} %reshape.405), kind=kLoop, calls=%fused_computation.14 | loop fusion | flops 14082048 | bytes 11829248 | tf_op jit(solution)/shard_map/transpose(jvp(nkh,nkhd->nhd))/dot_general | solution.py:62
  1252.7 16.2 fusion.8
  1269.0 12.6 fusion.10
  1281.7 35.2 %add_reduce_fusion = bf16[2048,4,64]{2,1,0:T(4,128)(2,1)} fusion(f32[2048,9,4,64]{3,2,1,0:T(4,128)} %gather.24, f32[2048,4,64]{2,1,0:T(4,128)} %copy.116, f32[4,64]{1,0:T(4,128)S(1)} %copy-done.45, f32[4,2048,9]{0,2,1:T(8,128)} %fusion.10), kind=kLoop, calls=%fused_computation.19 | loop fusion | flops 37224448 | bytes 22316032 | tf_op jit(solution)/shard_map/transpose(jvp())/reduce_sum | solution.py:56
  1316.8 32.5 %multiply_reduce_fusion = (f32[4,64]{1,0:T(4,128)}, f32[2048,9,4,64]{3,2,1,0:T(4,128)}) fusion(f32[2048,9,4,64]{3,2,1,0:T(4,128)} %gather.24, f32[4,2048,9]{0,2,1:T(8,128)} %fusion.10, f32[2048,4,64]{2,1,0:T(4,128)} %copy.116, f32[4,64]{1,0:T(4,128)S(1)} %copy-done.45), kind=kLoop, calls=%fused_computation.12 | loop fusion | flops 33029888 | bytes 40142848 | tf_op jit(solution)/shard_map/transpose(jvp(nkhd,hd->nkh))/dot_general | solution.py:58
  1349.4 4.1 copy.130
  1355.9 10.6 broadcast_multiply_fusion
  1366.5 34.3 %copy.128 = f32[2048,9,4,64]{0,3,2,1:T(8,128)} copy(f32[2048,9,4,64]{3,2,1,0:T(4,128)} %get-tuple-element.88) | data formatting | bytes 37748736 | tf_op jit(solution)/shard_map/transpose(jvp(nkhd,hd->nkh))/transpose | solution.py:58
  1400.8 27.8 %bitcast_add_fusion = f32[2048,9,256]{0,2,1:T(8,128)} fusion(f32[2048,4,64,9]{0,2,1,3:T(8,128)} %broadcast_multiply_fusion, f32[2048,9,4,64]{0,3,2,1:T(8,128)} %copy.128, f32[2048,9,256]{0,2,1:T(8,128)} %copy.127, f32[2048,256]{0,1:T(8,128)} %fusion.14), kind=kLoop, calls=%fused_computation.25 | loop fusion | flops 33030144 | bytes 77594624 | tf_op jit(solution)/shard_map/transpose(jvp())/add_any | solution.py:56
  1428.6 26.3 %copy.129 = f32[2048,9,256]{2,1,0:T(8,128)} copy(f32[2048,9,256]{0,2,1:T(8,128)} %bitcast_add_fusion) | data formatting | bytes 37748736 | tf_op jit(solution)/shard_map/transpose(jvp())/add_any | solution.py:56
  1454.9 26.4 %reshape.486 = f32[18432,256]{1,0:T(8,128)} reshape(f32[2048,9,256]{2,1,0:T(8,128)} %copy.129) | data formatting | bytes 37748736 | tf_op jit(solution)/shard_map/transpose(jvp())/add_any | solution.py:56
  1481.4 100.5 %scatter_custom_fusion.2 = f32[2112,256]{1,0:T(8,128)} fusion(s32[18432]{0:T(1024)} %copy-done.31, f32[18432,256]{1,0:T(8,128)} %reshape.486, f32[]{:T(128)} %constant.191.clone.1), kind=kCustom, calls=%fused_computation.116 | custom fusion | flops 4718592 | bytes 2163200 | tf_op jit(solution)/shard_map/transpose(jvp())/scatter-add | solution.py:55
  1584.2 3.5 collective-permute-start.7
  1592.5 3.9 scatter_custom_fusion.3
  1605.0 39.3 %all-reduce.2 = (f32[64,40]{0,1:T(8,128)S(1)}, f32[1128]{0:T(1024)S(1)}, f32[]{:T(128)}) all-reduce(f32[64,40]{0,1:T(8,128)S(1)} %fusion.82, f32[1128]{0:T(1024)S(1)} %add_add_fusion, f32[]{:T(128)} %multiply_reduce_fusion.10), channel_id=1, replica_groups=mesh['section'=4,'dom'=8] {'section','dom'}, use_global_device_ids=true, to_apply=%region_19.20 | all-reduce | flops 3689 | bytes 29512 | tf_op jit(solution)/shard_map/psum | solution.py:314
  1646.8 83.8 %all-reduce.6.cloned.1.call-done = (f32[128,256]{1,0:T(8,128)}, f32[2,2,256,256]{3,2,1,0:T(8,128)}) async-done(((f32[128,256]{1,0:T(8,128)}, f32[2,2,256,256]{3,2,1,0:T(8,128)}), (f32[128,256]{1,0:T(8,128)}, f32[2,2,256,256]{3,2,1,0:T(8,128)})) %all-reduce.6.cloned.1.call-update) | async-done | bytes 1179664 | tf_op jit(solution)/shard_map/psum | solution.py:314
  1744.2 4.1 fusion.26
  (241 shorter events, 109.5 us)
Async XLA Ops:
  7.2 18.1 %copy-start = (bf16[4,2048,128]{2,1,0:T(8,128)(2,1)S(1)}, bf16[4,2048,128]{2,1,0:T(8,128)(2,1)}, u32[]{:S(2)}) copy-start(bf16[4,2048,128]{2,1,0:T(8,128)(2,1)} %param.35) | copy-start | bytes 6291460
  7.2 70.1 %copy-start.57 = (f32[8,40]{1,0:T(8,128)S(1)}, f32[8,40]{1,0:T(8,128)}, u32[]{:S(2)}) copy-start(f32[8,40]{1,0:T(8,128)} %param.42) | copy-start | bytes 3844
  7.2 1723.4 %all-reduce.6.cloned.1.call-start = ((), (), s32[]{:S(2)}) async-start(), calls=%async_computation | async-start | bytes 2359296 | tf_op jit(solution)/shard_map/psum | solution.py:314
  8.1 58.1 %copy-start.64 = (s32[64]{0:T(128)}, s32[64]{0:T(128)S(1)}, u32[]{:S(2)}) copy-start(s32[64]{0:T(128)S(1)} %fusion.77) | copy-start | bytes 772
  8.1 58.1 %copy-start.61 = (s32[1024]{0:T(1024)}, s32[1024]{0:T(1024)S(1)}, u32[]{:S(2)}) copy-start(s32[1024]{0:T(1024)S(1)} %pad_clamp_fusion) | copy-start | bytes 12292
  9.0 91.2 %copy-start.53 = (f32[256]{0:T(256)}, f32[256]{0:T(256)S(1)}, u32[]{:S(2)}) copy-start(f32[256]{0:T(256)S(1)} %get-tuple-element.101) | copy-start | bytes 3076
  27.6 69.4 %copy-start.7 = (bf16[2048,256]{1,0:T(8,128)(2,1)}, bf16[2048,256]{1,0:T(8,128)(2,1)S(1)}, u32[]{:S(2)}) copy-start(bf16[2048,256]{1,0:T(8,128)(2,1)S(1)} %get-tuple-element.104) | copy-start | bytes 3145732
  28.4 68.7 %collective-permute-start = (bf16[32,256]{1,0:T(8,128)(2,1)S(1)}, bf16[32,256]{1,0:T(8,128)(2,1)S(1)}, u32[]{:S(2)}, u32[]{:S(2)}) collective-permute-start(bf16[32,256]{1,0:T(8,128)(2,1)S(1)} %get-tuple-element.98), channel_id=1, source_target_pairs={{0,1},{1,2},{2,3},{3,4},{4,5},{5,6},{6,7},{7,0},{8,9},{9,10},{10,1... | collective-permute-start | bytes 49160 | tf_op jit(solution)/shard_map/ppermute | solution.py:39
  28.7 68.4 %collective-permute-start.1 = (bf16[32,256]{1,0:T(8,128)(2,1)S(1)}, bf16[32,256]{1,0:T(8,128)(2,1)S(1)}, u32[]{:S(2)}, u32[]{:S(2)}) collective-permute-start(bf16[32,256]{1,0:T(8,128)(2,1)S(1)} %get-tuple-element.99), channel_id=1, source_target_pairs={{1,0},{2,1},{3,2},{4,3},{5,4},{6,5},{7,6},{0,7},{9,8},{10,9},{11,1... | collective-permute-start | bytes 49160 | tf_op jit(solution)/shard_map/ppermute | solution.py:40
  34.1 137.1 %copy-start.33 = (f32[1,2048]{1,0:T(1,128)}, f32[1,2048]{1,0:T(1,128)S(1)}, u32[]{:S(2)}) copy-start(f32[1,2048]{1,0:T(1,128)S(1)} %dynamic-slice_convert_fusion) | copy-start | bytes 24580
  69.5 101.7 %copy-start.31 = (s32[18432]{0:T(1024)}, s32[18432]{0:T(1024)S(1)}, u32[]{:S(2)}) copy-start(s32[18432]{0:T(1024)S(1)} %reshape.484) | copy-start | bytes 221188
  78.1 125.3 %copy-start.44 = (f32[4,64]{1,0:T(4,128)}, f32[4,64]{1,0:T(4,128)S(1)}, u32[]{:S(2)}) copy-start(f32[4,64]{1,0:T(4,128)S(1)} %squeeze.20) | copy-start | bytes 3076
  97.1 74.2 %copy-start.35 = (bf16[32,256]{1,0:T(8,128)(2,1)}, bf16[32,256]{1,0:T(8,128)(2,1)S(1)}, u32[]{:S(2)}) copy-start(bf16[32,256]{1,0:T(8,128)(2,1)S(1)} %collective-permute-done) | copy-start | bytes 49156
  97.1 74.2 %copy-start.37 = (bf16[32,256]{1,0:T(8,128)(2,1)}, bf16[32,256]{1,0:T(8,128)(2,1)S(1)}, u32[]{:S(2)}) copy-start(bf16[32,256]{1,0:T(8,128)(2,1)S(1)} %collective-permute-done.1) | copy-start | bytes 49156
  233.7 12.1 copy-start.1
  353.0 35.7 %copy-start.60 = (f32[4,64]{1,0:T(4,128)S(1)}, f32[4,64]{1,0:T(4,128)}, u32[]{:S(2)}) copy-start(f32[4,64]{1,0:T(4,128)} %add.272) | copy-start | bytes 3076
  383.5 11.7 copy-start.54
  397.7 31.5 %copy-start.14 = (bf16[2048,256]{1,0:T(8,128)(2,1)}, bf16[2048,256]{1,0:T(8,128)(2,1)S(1)}, u32[]{:S(2)}) copy-start(bf16[2048,256]{1,0:T(8,128)(2,1)S(1)} %fusion.21) | copy-start | bytes 3145732
  398.5 76.5 %collective-permute-start.2 = (bf16[32,256]{1,0:T(8,128)(2,1)S(1)}, bf16[32,256]{1,0:T(8,128)(2,1)S(1)}, u32[]{:S(2)}, u32[]{:S(2)}) collective-permute-start(bf16[32,256]{1,0:T(8,128)(2,1)S(1)} %get-tuple-element.96), channel_id=1, source_target_pairs={{0,1},{1,2},{2,3},{3,4},{4,5},{5,6},{6,7},{7,0},{8,9},{9,10},{10,1... | collective-permute-start | bytes 49160 | tf_op jit(solution)/shard_map/ppermute | solution.py:39
  398.9 76.1 %collective-permute-start.3 = (bf16[32,256]{1,0:T(8,128)(2,1)S(1)}, bf16[32,256]{1,0:T(8,128)(2,1)S(1)}, u32[]{:S(2)}, u32[]{:S(2)}) collective-permute-start(bf16[32,256]{1,0:T(8,128)(2,1)S(1)} %get-tuple-element.97), channel_id=1, source_target_pairs={{1,0},{2,1},{3,2},{4,3},{5,4},{6,5},{7,6},{0,7},{9,8},{10,9},{11,1... | collective-permute-start | bytes 49160 | tf_op jit(solution)/shard_map/ppermute | solution.py:40
  475.0 74.0 %copy-start.39 = (bf16[32,256]{1,0:T(8,128)(2,1)}, bf16[32,256]{1,0:T(8,128)(2,1)S(1)}, u32[]{:S(2)}) copy-start(bf16[32,256]{1,0:T(8,128)(2,1)S(1)} %collective-permute-done.2) | copy-start | bytes 49156
  475.0 74.0 %copy-start.41 = (bf16[32,256]{1,0:T(8,128)(2,1)}, bf16[32,256]{1,0:T(8,128)(2,1)S(1)}, u32[]{:S(2)}) copy-start(bf16[32,256]{1,0:T(8,128)(2,1)S(1)} %collective-permute-done.3) | copy-start | bytes 49156
  573.1 32.1 %copy-start.46 = (f32[4,64]{1,0:T(4,128)S(1)}, f32[4,64]{1,0:T(4,128)}, u32[]{:S(2)}) copy-start(f32[4,64]{1,0:T(4,128)} %squeeze.23) | copy-start | bytes 3076
  635.5 12.2 copy-start.2
  765.0 33.7 %copy-start.32 = (bf16[64,40]{1,0:T(8,128)(2,1)S(1)}, bf16[64,40]{1,0:T(8,128)(2,1)}, u32[]{:S(2)}) copy-start(bf16[64,40]{1,0:T(8,128)(2,1)} %all_gather.11) | copy-start | bytes 15364
  765.0 33.7 %copy-start.62 = (f32[64]{0:T(128)S(1)}, f32[64]{0:T(128)}, u32[]{:S(2)}) copy-start(f32[64]{0:T(128)} %slice.182) | copy-start | bytes 772
  765.0 33.7 %copy-start.65 = (f32[40]{0:T(128)S(1)}, f32[40]{0:T(128)}, u32[]{:S(2)}) copy-start(f32[40]{0:T(128)} %slice.183) | copy-start | bytes 484
  765.0 34.1 %copy-start.49 = (f32[2048]{0:T(1024)S(1)}, f32[2048]{0:T(1024)}, u32[]{:S(2)}) copy-start(f32[2048]{0:T(1024)} %broadcast_divide_fusion) | copy-start | bytes 24580
  765.0 34.1 %copy-start.50 = (s32[1,2048]{1,0:T(1,128)S(1)}, s32[1,2048]{1,0:T(1,128)}, u32[]{:S(2)}) copy-start(s32[1,2048]{1,0:T(1,128)} %constant_dynamic-slice_fusion) | copy-start | bytes 24580
  823.6 18.1 %copy-start.21 = (f32[2048,4]{1,0:T(8,128)S(1)}, f32[2048,4]{1,0:T(8,128)}, u32[]{:S(2)}) copy-start(f32[2048,4]{1,0:T(8,128)} %multiply_divide_fusion.1) | copy-start | bytes 98308
  841.8 16.3 copy-start.4
  841.8 16.3 copy-start.13
  972.9 34.1 %copy-start.22 = (f32[2048,64]{0,1:T(8,128)S(1)}, f32[2048,64]{0,1:T(8,128)}, u32[]{:S(2)}) copy-start(f32[2048,64]{0,1:T(8,128)} %get-tuple-element.83) | copy-start | bytes 1572868
  1094.1 109.6 %copy-start.15 = (bf16[2048,256]{1,0:T(8,128)(2,1)S(1)}, bf16[2048,256]{1,0:T(8,128)(2,1)}, u32[]{:S(2)}) copy-start(bf16[2048,256]{1,0:T(8,128)(2,1)} %copy-done.14) | copy-start | bytes 3145732
  1094.1 109.6 %copy-start.40 = (bf16[32,256]{1,0:T(8,128)(2,1)S(1)}, bf16[32,256]{1,0:T(8,128)(2,1)}, u32[]{:S(2)}) copy-start(bf16[32,256]{1,0:T(8,128)(2,1)} %copy-done.39) | copy-start | bytes 49156
  1094.1 109.6 %copy-start.42 = (bf16[32,256]{1,0:T(8,128)(2,1)S(1)}, bf16[32,256]{1,0:T(8,128)(2,1)}, u32[]{:S(2)}) copy-start(bf16[32,256]{1,0:T(8,128)(2,1)} %copy-done.41) | copy-start | bytes 49156
  1194.6 10.4 copy-start.16
  1194.6 10.4 copy-start.17
  1194.6 15.8 copy-start.55
  1196.9 9.3 collective-permute-start.4
  1196.9 9.3 collective-permute-start.5
  1222.8 29.9 %copy-start.20 = (f32[2048,4]{1,0:T(8,128)S(1)}, f32[2048,4]{1,0:T(8,128)}, u32[]{:S(2)}) copy-start(f32[2048,4]{1,0:T(8,128)} %multiply_divide_fusion) | copy-start | bytes 98308
  1252.7 16.3 copy-start.3
  1252.7 16.3 copy-start.11
  1269.0 12.6 copy-start.45
  1316.8 36.6 %copy-start.8 = (bf16[2048,256]{1,0:T(8,128)(2,1)S(1)}, bf16[2048,256]{1,0:T(8,128)(2,1)}, u32[]{:S(2)}) copy-start(bf16[2048,256]{1,0:T(8,128)(2,1)} %copy-done.7) | copy-start | bytes 3145732
  1316.8 39.0 %copy-start.25 = (f32[2048,4,9]{0,1,2:T(4,128)S(1)}, f32[2048,4,9]{0,1,2:T(4,128)}, u32[]{:S(2)}) copy-start(f32[2048,4,9]{0,1,2:T(4,128)} %copy.143) | copy-start | bytes 884740
  1481.4 109.4 %copy-start.36 = (bf16[32,256]{1,0:T(8,128)(2,1)S(1)}, bf16[32,256]{1,0:T(8,128)(2,1)}, u32[]{:S(2)}) copy-start(bf16[32,256]{1,0:T(8,128)(2,1)} %copy-done.35) | copy-start | bytes 49156
  1481.4 109.4 %copy-start.38 = (bf16[32,256]{1,0:T(8,128)(2,1)S(1)}, bf16[32,256]{1,0:T(8,128)(2,1)}, u32[]{:S(2)}) copy-start(bf16[32,256]{1,0:T(8,128)(2,1)} %copy-done.37) | copy-start | bytes 49156
  1581.8 9.5 copy-start.29
  1584.1 8.4 collective-permute-start.6
  1584.2 8.4 collective-permute-start.7
  1590.7 10.1 copy-start.24
  1590.8 10.4 copy-start.59
  1590.8 11.4 copy-start.34
  1590.8 11.4 copy-start.47
  1590.8 11.3 copy-start.48
  1591.4 147.8 %copy-start.51 = (f32[40,40]{1,0:T(8,128)S(1)}, f32[40,40]{1,0:T(8,128)}, u32[]{:S(2)}) copy-start(f32[40,40]{1,0:T(8,128)} %param.49) | copy-start | bytes 19204
  1599.7 155.5 %copy-start.58 = (f32[8,40]{1,0:T(8,128)S(1)}, f32[8,40]{1,0:T(8,128)}, u32[]{:S(2)}) copy-start(f32[8,40]{1,0:T(8,128)} %param.42) | copy-start | bytes 3844
  1599.7 157.0 %copy-start.52 = (f32[1128]{0:T(1024)S(1)}, f32[1128]{0:T(1024)}, u32[]{:S(2)}) copy-start(f32[1128]{0:T(1024)} %param.43) | copy-start | bytes 13540
  1599.7 158.3 %copy-start.43 = (f32[16,256]{1,0:T(8,128)S(1)}, f32[16,256]{1,0:T(8,128)}, u32[]{:S(2)}) copy-start(f32[16,256]{1,0:T(8,128)} %param.40) | copy-start | bytes 49156
  1599.7 158.3 %copy-start.56 = (f32[16,256]{1,0:T(8,128)S(1)}, f32[16,256]{1,0:T(8,128)}, u32[]{:S(2)}) copy-start(f32[16,256]{1,0:T(8,128)} %param.58) | copy-start | bytes 49156
  1599.7 159.8 %copy-start.30 = (f32[2,2,32,256]{3,2,1,0:T(8,128)S(1)}, f32[2,2,32,256]{3,2,1,0:T(8,128)}, u32[]{:S(2)}) copy-start(f32[2,2,32,256]{3,2,1,0:T(8,128)} %param.41) | copy-start | bytes 393220
  1601.1 147.3 %copy-start.26 = (f32[2,2,256,256]{3,2,1,0:T(8,128)S(1)}, f32[2,2,256,256]{3,2,1,0:T(8,128)}, u32[]{:S(2)}) copy-start(f32[2,2,256,256]{3,2,1,0:T(8,128)} %param.53) | copy-start | bytes 3145732
  (11 other events, 82.7 us)
Sparse Core Ops, SparseCore 0:
  1600.9 129.6 all-reduce.5
where the time goes:
time: 1790 us; the launch traced here: 1770 us
  local copies, waits for them, and re-layouts  782 us (44%)
  other arithmetic  695 us (39%)
  blocking collectives  98.7 us (6%)
  waiting for transfers between devices  83.8 us (5%)
  matrix products  75.9 us (4%)
  between operations  21.4 us (1%)
    gather x10, local copies, waits for them, and re-layouts, attend(): picked = left_rows[sources_all]  461 us
    scatter-add x2, other arithmetic, attend(): picked = left_rows[sources_all]  201 us
    dot_general x4, other arithmetic, attend(): jnp.einsum('nkhd,hd->nkh', heads_view, attention, precision=highest)  125 us
    add_any x4, local copies, waits for them, and re-layouts, attend(): mixed_rows = leaky_relu(picked + right_rows[:, None, :])  106 us
    psum x1, waiting for transfers between devices, per_device(): summed = lax.psum((sum_a, sum_b, sum_c, sum_d, sum_e), ('section', 'dom'))  83.8 us
    unnamed x4, other arithmetic  74.2 us
    reduce_sum x2, other arithmetic, attend(): mixed_rows = leaky_relu(picked + right_rows[:, None, :])  70.2 us
    transpose x2, local copies, waits for them, and re-layouts, attend(): jnp.einsum('nkhd,hd->nkh', heads_view, attention, precision=highest)  68.5 us
  transfers between devices with their start and end apart: 9, of which 1 were waited for; matrix products, arithmetic and copies ran while one was open for 6% of the time, Pallas kernels for 0%

commit v1 on v0

v1 whole, which is shorter than its diff:
```python
import jax
import jax.numpy as jnp
from jax import lax
from jax.experimental import pallas as pl
from jax.experimental.pallas import tpu as pltpu
from jax.sharding import PartitionSpec as P

FEAT = 128
HEADS = 4
HSIZE = 64
CLASSES = 40
STEPS = 5
HID = 256
SMALL = 1128


highest = lax.Precision.HIGHEST
leak_slope = 0.2
smooth = 0.1
clip_norm = 0.001
shampoo_rate = 0.3
shampoo_decay = 0.5
weight_decay = 0.0001
adam_rate = 0.1
beta_one = 0.9
beta_two = 0.999
adam_eps = 1e-08
adam_decay = 0.01
ema_keep = 0.9


def split_small(small_params):
    bias_in = small_params[0:HID]
    attention = small_params[HID : 3 * HID].reshape(2, HEADS, HSIZE)
    bias_one = small_params[3 * HID : 4 * HID]
    bias_two = small_params[4 * HID : 4 * HID + HSIZE]
    bias_out = small_params[4 * HID + HSIZE :]
    return (bias_in, attention, bias_one, bias_two, bias_out)


GRAPH = 64
LANES = 128
DEG = 8
SLOTS = DEG + 1
ROWS = 1280
ROW_IN = 4 * HID
ROW_OUT = ROW_IN + FEAT
ROW_MISC = ROW_OUT + HSIZE

bf16 = jnp.bfloat16
f32 = jnp.float32


def dot_nn(a, b):
    return lax.dot_general(a, b, (((1,), (0,)), ((), ())), preferred_element_type=f32)


def dot_nt(a, b):
    return lax.dot_general(a, b, (((1,), (1,)), ((), ())), preferred_element_type=f32)


def tile_of(k):
    return slice(k * LANES, (k + 1) * LANES)


def head_of(h):
    return slice(h * HSIZE, (h + 1) * HSIZE)


def model_kernel(
    src_ref,
    lab_ref,
    msk_ref,
    feat_ref,
    wi_ref,
    wgt_ref,
    wg_ref,
    wot_ref,
    wo_ref,
    col_ref,
    am_ref,
    out_ref,
    e_ref,
    t_ref,
    al_ref,
    h_ref,
    slope_ref,
    xlr_ref,
    dx_ref,
    do_ref,
    pool_ref,
    dlog_ref,
    dt_ref,
    q_ref,
    ab_ref,
    da_ref,
    gb_ref,
    loss_ref,
):
    nodes = feat_ref.shape[0]
    blocks = nodes // LANES
    chunk = 4 * LANES
    chunks = nodes // chunk
    mixed = DEG * LANES

    row_id = lax.broadcasted_iota(jnp.int32, (LANES, LANES), 0)
    lane_id = lax.broadcasted_iota(jnp.int32, (LANES, LANES), 1)
    eye = jnp.where(row_id == lane_id, 1.0, 0.0).astype(bf16)
    head_row = lax.broadcasted_iota(jnp.int32, (16, HID), 0)
    head_col = lax.broadcasted_iota(jnp.int32, (16, HID), 1)
    head_mask = jnp.where(head_col // HSIZE == head_row, 1.0, 0.0).astype(bf16)

    bias_in = col_ref[:, 0:1]
    bias_one = col_ref[:, 1:2]
    bias_two = col_ref[0:HSIZE, 4:5]
    bias_out = col_ref[HSIZE : HSIZE + CLASSES, 4:5]
    for layer in range(2):
        wide = jnp.broadcast_to(col_ref[:, 2 + layer : 3 + layer], (HID, LANES))
        ab_ref[layer, 0] = wide.astype(bf16)
        ab_ref[layer, 1] = (leak_slope * wide).astype(bf16)
    da_ref[...] = jnp.zeros_like(da_ref)
    gb_ref[...] = jnp.zeros_like(gb_ref)
    loss_ref[...] = jnp.zeros_like(loss_ref)

    def lanes_of(i, width):
        return pl.ds(pl.multiple_of(i * width, width), width)

    @pl.loop(0, chunks)
    def _(c):
        at = lanes_of(c, chunk)
        pre = dot_nt(wi_ref[...], feat_ref[at, :]) + bias_in
        grown = jnp.exp(jnp.minimum(pre, 0.0))
        h_ref[0, :, at] = jnp.where(pre > 0, pre, grown - 1.0).astype(bf16)
        slope_ref[0, :, at] = jnp.where(pre > 0, 1.0, grown)

    for layer in range(2):

        @pl.loop(0, chunks)
        def _(c):
            at = lanes_of(c, chunk)
            xlr_ref[:, at] = dot_nn(wgt_ref[layer], h_ref[layer, :, at]).astype(bf16)

        @pl.loop(0, blocks)
        def _(i):
            at = lanes_of(i, LANES)
            if layer == 0:
                for k in range(DEG):
                    hit = row_id == src_ref[k : k + 1, at]
                    e_ref[i, 0:LANES, tile_of(k)] = jnp.where(hit, 1.0, 0.0).astype(bf16)
                    e_ref[i, LANES : 2 * LANES, tile_of(k)] = eye
            left = xlr_ref[0:HID, at]
            right = xlr_ref[HID : 2 * HID, at]
            both = jnp.concatenate([left, right], axis=1)
            t_ref[layer, i, :, 0:mixed] = dot_nn(both, e_ref[i]).astype(bf16)
            t_ref[layer, i, :, tile_of(DEG)] = left + right
            t = t_ref[layer, i]
            z = jnp.maximum(t, t * leak_slope)
            scores = dot_nn(am_ref[layer], z)
            grown = jnp.exp(scores[0:8] + scores[8:16])
            total = grown[:, tile_of(0)]
            for k in range(1, SLOTS):
                total = total + grown[:, tile_of(k)]
            inverse = 1.0 / total
            for k in range(SLOTS):
                al_ref[layer, i, :, tile_of(k)] = grown[:, tile_of(k)] * inverse
            pooled = None
            for h in range(HEADS):
                total = -right[head_of(h)].astype(f32).reshape(8, 8, LANES)
                for k in range(SLOTS):
                    part = jnp.broadcast_to(al_ref[layer, i, h : h + 1, tile_of(k)], (8, LANES))
                    value = t_ref[layer, i, head_of(h), tile_of(k)].astype(f32)
                    total = total + value.reshape(8, 8, LANES) * part[None]
                total = total.reshape(HSIZE, LANES)
                if layer == 0:
                    pre = total + bias_one[head_of(h)]
                    grown_one = jnp.exp(jnp.minimum(pre, 0.0))
                    h_ref[1, head_of(h), at] = jnp.where(pre > 0, pre, grown_one - 1.0).astype(bf16)
                    slope_ref[1, head_of(h), at] = jnp.where(pre > 0, 1.0, grown_one)
                else:
                    rounded = total.astype(bf16).astype(f32)
                    pooled = rounded if pooled is None else pooled + rounded
            if layer == 1:
                pool_ref[:, at] = (pooled * (1.0 / HEADS) + bias_two).astype(bf16)

    inv_count = col_ref[0:1, 5:6]

    @pl.loop(0, chunks)
    def _(c):
        at = lanes_of(c, chunk)
        logits = dot_nn(wot_ref[...], pool_ref[:, at]) + bias_out
        shifted = logits - jnp.max(logits, axis=0, keepdims=True)
        log_prob = shifted - jnp.log(jnp.sum(jnp.exp(shifted), axis=0, keepdims=True))
        class_id = lax.broadcasted_iota(jnp.int32, (CLASSES, chunk), 0)
        onehot = jnp.where(class_id == lab_ref[0:1, at], 1.0, 0.0)
        share = msk_ref[0:1, at].astype(f32) * inv_count
        term = jnp.sum(((smooth - 1.0) * onehot - smooth / CLASSES) * log_prob, axis=0, keepdims=True)
        loss_ref[...] += term * share
        d_logits = (jnp.exp(log_prob) - (1.0 - smooth) * onehot - smooth / CLASSES) * share
        d_logits = d_logits.astype(bf16)
        dlog_ref[:, at] = d_logits
        d_pooled = (dot_nn(wo_ref[...], d_logits) * (1.0 / HEADS)).astype(bf16)
        for h in range(HEADS):
            do_ref[head_of(h), at] = d_pooled

    for layer in (1, 0):

        @pl.loop(0, blocks)
        def _(i):
            at = lanes_of(i, LANES)
            d_out = do_ref[:, at]
            for k in range(SLOTS):
                q_ref[:, tile_of(k)] = t_ref[layer, i, :, tile_of(k)] * d_out
            d_alpha = dot_nn(head_mask, q_ref[...])[0:8]
            alpha = al_ref[layer, i]
            weighted = alpha * d_alpha
            total = weighted[:, tile_of(0)]
            for k in range(1, SLOTS):
                total = total + weighted[:, tile_of(k)]
            d_score = [
                weighted[:, tile_of(k)] - alpha[:, tile_of(k)] * total for k in range(SLOTS)
            ]
            for h in range(HEADS):
                d_head = d_out[head_of(h)].reshape(4, 16, LANES)
                slope_one = ab_ref[layer, 0, head_of(h)]
                slope_two = ab_ref[layer, 1, head_of(h)]
                for k in range(SLOTS):
                    ds = jnp.broadcast_to(d_score[k][h : h + 1], (16, LANES)).astype(bf16)
                    part = jnp.broadcast_to(alpha[h : h + 1, tile_of(k)], (16, LANES)).astype(bf16)
                    t = t_ref[layer, i, head_of(h), tile_of(k)]
                    slope = jnp.where(t > 0, slope_one, slope_two).reshape(4, 16, LANES)
                    dt_ref[head_of(h), tile_of(k)] = (slope * ds[None]).reshape(HSIZE, LANES)
                    q_ref[head_of(h), tile_of(k)] = (d_head * part[None]).reshape(HSIZE, LANES)
            t = t_ref[layer, i]
            z = jnp.maximum(t, t * leak_slope)
            ds_all = jnp.concatenate(d_score, axis=1)
            ds_all = jnp.concatenate([ds_all, jnp.zeros_like(ds_all)], axis=0).astype(bf16)
            da_ref[layer] += dot_nt(z, ds_all)
            spread = dot_nt(dt_ref[:, 0:mixed], e_ref[i])
            d_left = spread[:, 0:LANES] + dot_nt(q_ref[:, 0:mixed], e_ref[i, 0:LANES, :])
            self_dt = dt_ref[:, tile_of(DEG)].astype(f32)
            self_q = q_ref[:, tile_of(DEG)].astype(f32)
            dx_ref[layer, 0:HID, at] = (d_left + self_dt + self_q).astype(bf16)
            dx_ref[layer, HID : 2 * HID, at] = (spread[:, LANES : 2 * LANES] + self_dt).astype(bf16)

        @pl.loop(0, chunks)
        def _(c):
            at = lanes_of(c, chunk)
            d_in = dot_nn(wg_ref[layer], dx_ref[layer, :, at]).astype(bf16).astype(f32)
            d_in = d_in * slope_ref[layer, :, at]
            do_ref[:, at] = d_in.astype(bf16)
            if layer == 1:
                for k in range(4):
                    gb_ref[...] += d_in[:, tile_of(k)]

    for layer in range(2):
        for side in range(2):
            start = (2 * layer + side) * HID
            out_ref[start : start + HID, :] = dot_nt(
                h_ref[layer], dx_ref[layer, side * HID : (side + 1) * HID, :]
            ).astype(bf16)
    out_ref[ROW_IN : ROW_IN + FEAT, :] = dot_nn(do_ref[...], feat_ref[...]).T.astype(bf16)
    out_ref[ROW_OUT : ROW_OUT + HSIZE, :] = jnp.zeros((HSIZE, HID), bf16)
    out_ref[ROW_OUT : ROW_OUT + HSIZE, 0:CLASSES] = dot_nt(pool_ref[...], dlog_ref[...]).astype(bf16)
    ones = jnp.ones((nodes, LANES), bf16)
    lane_wide = lax.broadcasted_iota(jnp.int32, (HID, LANES), 1)
    columns = jnp.where(lane_wide == 0, dot_nn(do_ref[...], ones), 0.0)
    for layer in range(2):
        da = da_ref[layer]
        row_head = lax.broadcasted_iota(jnp.int32, (HID, 16), 0) // HSIZE
        lane_head = lax.broadcasted_iota(jnp.int32, (HID, 16), 1)
        da = jnp.sum(jnp.where(row_head == lane_head, da, 0.0), axis=1, keepdims=True)
        columns = columns + jnp.where(lane_wide == 1 + layer, da, 0.0)
    columns = columns + jnp.where(lane_wide == 3, jnp.sum(gb_ref[...], axis=1, keepdims=True), 0.0)
    g_bias_out = dot_nn(dlog_ref[...], ones)
    g_bias_two = lax.dot_general(
        wo_ref[...].astype(f32), g_bias_out, (((1,), (0,)), ((), ())),
        precision=highest, preferred_element_type=f32,
    )
    loss = jnp.broadcast_to(jnp.sum(loss_ref[...], axis=1, keepdims=True), (8, LANES))
    loss_high = loss.astype(bf16).astype(f32)
    rest = HID - HSIZE - CLASSES - 16
    last = jnp.concatenate(
        [g_bias_two, g_bias_out, loss_high, loss - loss_high, jnp.zeros((rest, LANES), f32)], axis=0
    )
    columns = columns + jnp.where(lane_wide == 4, last, 0.0)
    out_ref[ROW_MISC : ROW_MISC + 16, :] = columns.T[0:16].astype(bf16)
    out_ref[ROW_MISC + 16 :, :] = jnp.zeros((ROWS - ROW_MISC - 16, HID), bf16)


def run_model(src, lab, msk, feat, w_in, w_gat, w_out, small_params, inv_count):
    nodes = feat.shape[0]
    blocks = nodes // LANES
    bias_in, attention, bias_one, bias_two, bias_out = split_small(small_params)
    flat = attention.reshape(2, HID)
    last = jnp.concatenate([bias_two, bias_out, jnp.zeros((HID - HSIZE - CLASSES,), f32)])
    count_col = jnp.full((HID,), inv_count, f32)
    col = jnp.stack([bias_in, bias_one, flat[0], flat[1], last, count_col, last, last], axis=1)
    head_row = jnp.arange(8, dtype=jnp.int32)[:, None]
    head_mask = (jnp.arange(HID, dtype=jnp.int32)[None, :] // HSIZE == head_row).astype(f32)
    high = flat.astype(bf16).astype(f32)
    both = jnp.concatenate([head_mask * high[:, None, :], head_mask * (flat - high)[:, None, :]], axis=1)
    am = both.astype(bf16)
    wgt = jnp.swapaxes(w_gat, -1, -2).reshape(2, 2 * HID, HID)
    wg = jnp.swapaxes(w_gat, 1, 2).reshape(2, HID, 2 * HID)
    scratch = [
        pltpu.VMEM((blocks, 2 * LANES, DEG * LANES), bf16),
        pltpu.VMEM((2, blocks, HID, SLOTS * LANES), bf16),
        pltpu.VMEM((2, blocks, 8, SLOTS * LANES), f32),
        pltpu.VMEM((2, HID, nodes), bf16),
        pltpu.VMEM((2, HID, nodes), f32),
        pltpu.VMEM((2 * HID, nodes), bf16),
        pltpu.VMEM((2, 2 * HID, nodes), bf16),
        pltpu.VMEM((HID, nodes), bf16),
        pltpu.VMEM((HSIZE, nodes), bf16),
        pltpu.VMEM((CLASSES, nodes), bf16),
        pltpu.VMEM((HID, SLOTS * LANES), bf16),
        pltpu.VMEM((HID, SLOTS * LANES), bf16),
        pltpu.VMEM((2, 2, HID, LANES), bf16),
        pltpu.VMEM((2, HID, 16), f32),
        pltpu.VMEM((HID, LANES), f32),
        pltpu.VMEM((1, 4 * LANES), f32),
    ]
    return pl.pallas_call(
        model_kernel,
        out_shape=jax.ShapeDtypeStruct((ROWS, HID), bf16),
        in_specs=[pl.BlockSpec(memory_space=pltpu.VMEM)] * 11,
        out_specs=pl.BlockSpec(memory_space=pltpu.VMEM),
        scratch_shapes=scratch,
        compiler_params=pltpu.CompilerParams(vmem_limit_bytes=56 * 1024 * 1024),
        name="model",
    )(src, lab, msk, feat, w_in.T, wgt, wg, w_out.T, w_out, col, am)


def precondition(gradient, weight_rows, stat_rows, stat_right, root_rows, root_right, start):
    count_rows = weight_rows.shape[-2]
    grad_rows = lax.dynamic_slice_in_dim(gradient, start, count_rows, gradient.ndim - 2)
    flipped = jnp.swapaxes(gradient, -1, -2)
    new_left = shampoo_decay * stat_rows + (1.0 - shampoo_decay) * jnp.matmul(
        grad_rows, flipped, precision=highest
    )
    new_right = shampoo_decay * stat_right + (1.0 - shampoo_decay) * jnp.matmul(
        flipped, gradient, precision=highest
    )
    update = jnp.matmul(
        root_rows, jnp.matmul(gradient, root_right, precision=highest), precision=highest
    )
    new_weight = weight_rows - shampoo_rate * (update + weight_decay * weight_rows)
    return (new_weight, new_left, new_right)


def adamw_step(parameter, gradient, moment_one, moment_two):
    moment_one = beta_one * moment_one + (1.0 - beta_one) * gradient
    moment_two = beta_two * moment_two + (1.0 - beta_two) * gradient * gradient
    corr_one = 1.0 - beta_one**STEPS
    corr_two = 1.0 - beta_two**STEPS
    update = moment_one / corr_one / (jnp.sqrt(moment_two / corr_two) + adam_eps)
    return (parameter - adam_rate * (update + adam_decay * parameter), moment_one, moment_two)


def average(old_value, new_value):
    return ema_keep * old_value + (1.0 - ema_keep) * new_value


def per_device(
    features,
    sources,
    send_index,
    labels,
    label_mask,
    w_in,
    w_gat,
    w_out,
    small_params,
    stat_l_in,
    stat_r_in,
    stat_l_gat,
    stat_r_gat,
    stat_l_out,
    stat_r_out,
    root_l_in,
    root_r_in,
    root_l_gat,
    root_r_gat,
    root_l_out,
    root_r_out,
    adam_first,
    adam_second,
    ema_in,
    ema_gat,
    ema_out,
    ema_small,
):
    dom_size = lax.axis_size("dom")
    all_size = dom_size * lax.axis_size("section")
    dom_id = lax.axis_index("dom")
    section_id = lax.axis_index("section")
    nodes = features.shape[1]
    half = send_index.shape[1] // 2
    rows_in, rows_gat, rows_out = (w_in.shape[0], w_gat.shape[2], w_out.shape[0])

    def of_micro(value):
        return lax.dynamic_index_in_dim(value, section_id, 0, keepdims=False)

    feat, src, send = (of_micro(features), of_micro(sources).T, of_micro(send_index))
    marks = jnp.stack([of_micro(labels), of_micro(label_mask)])
    down = [((i + 1) % dom_size, i) for i in range(dom_size)]
    feat_next = lax.ppermute(feat[:half], "dom", down)
    ints = jnp.concatenate([src[:, :half], marks[:, :half], send[None, :half]], axis=0)
    ints_next = lax.ppermute(ints, "dom", down)

    count = jnp.sum(label_mask)
    digits = jnp.stack([lax.div(count, 256), lax.rem(count, 256)]).astype(bf16)
    packed = jnp.concatenate(
        [
            w_in.astype(bf16),
            w_gat.astype(bf16).reshape(4 * rows_gat, HID),
            jnp.pad(w_out.astype(bf16), ((0, 0), (0, HID - CLASSES))),
            jnp.pad(digits[None, :], ((0, 0), (0, HID - 2))),
        ],
        axis=0,
    )
    whole = lax.all_gather(packed, "dom", axis=0, tiled=False)
    full_in = whole[:, :rows_in].reshape(FEAT, HID)
    cut = rows_in + 4 * rows_gat
    full_gat = whole[:, rows_in:cut].reshape(dom_size, 2, 2, rows_gat, HID)
    full_gat = full_gat.transpose(1, 2, 0, 3, 4).reshape(2, 2, HID, HID)
    full_out = whole[:, cut : cut + rows_out, :CLASSES].reshape(HSIZE, CLASSES)
    digits = jnp.sum(whole[:, cut + rows_out, :2].astype(f32), axis=0)
    label_count = digits[0] * 256.0 + digits[1]

    feat = jnp.concatenate([feat[half:], feat_next], axis=0)
    src = jnp.concatenate([src[:, half:], ints_next[:DEG]], axis=1)
    marks = jnp.concatenate([marks[:, half:], ints_next[DEG : DEG + 2]], axis=1)
    table = jnp.concatenate([send[half:] - (nodes - half), half + ints_next[DEG + 2]])
    edge = src[:, nodes - GRAPH :]
    spots = jnp.arange(2 * half, dtype=jnp.int32)[None, :, None] + nodes
    looked = jnp.sum(jnp.where(edge[:, None, :] == spots, table[None, :, None], 0), axis=1)
    edge = jnp.where(edge >= nodes, looked, (edge - half) % GRAPH)
    src = jnp.concatenate([(src[:, : nodes - GRAPH] - half) % GRAPH, edge], axis=1)
    lane = jnp.arange(nodes, dtype=jnp.int32)[None, :]
    src = src + (lane // GRAPH) % 2 * GRAPH

    partial = run_model(
        src, marks[0:1], marks[1:2], feat, full_in, full_gat, full_out, small_params, 1.0 / label_count
    )
    parts = lax.all_to_all(partial.reshape(all_size, -1, HID), ("section", "dom"), 0, 0)
    mine = jnp.sum(parts.astype(f32), axis=0)
    shared = jnp.broadcast_to(mine.astype(bf16)[None], (all_size,) + mine.shape)
    summed = lax.all_to_all(shared, ("section", "dom"), 0, 0).reshape(ROWS, HID).astype(f32)

    grad_gat = summed[:ROW_IN].reshape(2, 2, HID, HID)
    grad_in = summed[ROW_IN:ROW_OUT]
    grad_out = summed[ROW_OUT:ROW_MISC, :CLASSES]
    misc = summed[ROW_MISC : ROW_MISC + 8]
    grad_small = jnp.concatenate([misc[:4].reshape(-1), misc[4, : HSIZE + CLASSES]])
    spot = HSIZE + CLASSES
    mean_loss = misc[4, spot] + misc[4, spot + 8]
    grad_norm = jnp.sqrt(
        jnp.sum(grad_in * grad_in)
        + jnp.sum(grad_gat * grad_gat)
        + jnp.sum(grad_out * grad_out)
        + jnp.sum(grad_small * grad_small)
    )
    clip_scale = jnp.minimum(1.0, clip_norm / grad_norm)
    new_w_in, new_l_in, new_r_in = precondition(
        grad_in * clip_scale,
        w_in,
        stat_l_in,
        stat_r_in,
        root_l_in,
        root_r_in,
        dom_id * w_in.shape[0],
    )
    new_w_gat, new_l_gat, new_r_gat = precondition(
        grad_gat * clip_scale,
        w_gat,
        stat_l_gat,
        stat_r_gat,
        root_l_gat,
        root_r_gat,
        dom_id * w_gat.shape[2],
    )
    new_w_out, new_l_out, new_r_out = precondition(
        grad_out * clip_scale,
        w_out,
        stat_l_out,
        stat_r_out,
        root_l_out,
        root_r_out,
        dom_id * w_out.shape[0],
    )
    new_small, new_first, new_second = adamw_step(
        small_params, grad_small * clip_scale, adam_first, adam_second
    )
    return (
        new_w_in,
        new_w_gat,
        new_w_out,
        new_small,
        new_l_in,
        new_r_in,
        new_l_gat,
        new_r_gat,
        new_l_out,
        new_r_out,
        new_first,
        new_second,
        average(ema_in, new_w_in),
        average(ema_gat, new_w_gat),
        average(ema_out, new_w_out),
        average(ema_small, new_small),
        mean_loss,
        grad_norm,
    )


def solution(mesh):
    placed = (
        P(None, "dom", None),
        P(None, "dom", None),
        P(None, "dom"),
        P(None, "dom"),
        P(None, "dom"),
        P("dom", None),
        P(None, None, "dom", None),
        P("dom", None),
        P(),
        P("dom", None),
        P(),
        P(None, None, "dom", None),
        P(),
        P("dom", None),
        P(),
        P("dom", None),
        P(),
        P(None, None, "dom", None),
        P(),
        P("dom", None),
        P(),
        P(),
        P(),
        P("dom", None),
        P(None, None, "dom", None),
        P("dom", None),
        P(),
    )
    return jax.shard_map(
        per_device,
        mesh=mesh,
        in_specs=placed,
        out_specs=(
            P("dom", None),
            P(None, None, "dom", None),
            P("dom", None),
            P(),
            P("dom", None),
            P(),
            P(None, None, "dom", None),
            P(),
            P("dom", None),
            P(),
            P(),
            P(),
            P("dom", None),
            P(None, None, "dom", None),
            P("dom", None),
            P(),
            P(),
            P(),
        ),
        check_vma=False,
    )
```

time: 1790 us -> 181 us (0.10)
  local copies, waits for them, and re-layouts: 782 us -> 14.2 us
  other arithmetic: 695 us -> 12 us
  Pallas kernels: 0 us -> 65.2 us
  waiting for transfers between devices: 83.8 us -> 19 us
  matrix products: 75.9 us -> 12.9 us
  blocking collectives: 98.7 us -> 37.4 us
    gather x12 -> x0, local copies, waits for them, and re-layouts: 463 us -> none  [the longest x10 461 us: attend(): picked = left_rows[sources_all]]
    scatter-add x4 -> x0, other arithmetic: 209 us -> none  [the longest x2 201 us: attend(): picked = left_rows[sources_all]]
    dot_general x7 -> x0, other arithmetic: 175 us -> none  [the longest x4 125 us: attend(): jnp.einsum('nkhd,hd->nkh', heads_view, attention, precision=highest)]
    reduce_sum x13 -> x4, other arithmetic: 135 us -> 1.65 us  [the longest x1 1.41 us: per_device(): count = jnp.sum(label_mask)]
    add_any x4 -> x0, local copies, waits for them, and re-layouts: 106 us -> none  [attend(): mixed_rows = leaky_relu(picked + right_rows[:, None, :])]
    psum x1 -> x0, waiting for transfers between devices: 83.8 us -> none  [per_device(): summed = lax.psum((sum_a, sum_b, sum_c, sum_d, sum_e), ('section', 'dom'))]
    unnamed x4 -> x1, other arithmetic: 74.2 us -> 0.01 us
    transpose x2 -> x4, local copies, waits for them, and re-layouts: 68.5 us -> 3.15 us  [the longest x1 1.08 us: run_model(): wgt = jnp.swapaxes(w_gat, -1, -2).reshape(2, 2 * HID, HID)]
  transfers between devices with their start and end apart: 9 -> 3, of which waited for: 1 -> 1; matrix products, arithmetic and copies ran while one was open for 6% -> 10% of each run, Pallas kernels for 0% -> 0%
where the time goes in v1:
time: 181 us; the launch traced here: 180 us
  Pallas kernels  65.2 us (36%)
  blocking collectives  37.4 us (21%)
  waiting for transfers between devices  19 us (10%)
  local copies, waits for them, and re-layouts  14.2 us (8%)
  matrix products  12.9 us (7%)
  other arithmetic  12 us (7%)
  between operations  10.7 us (6%)
  starting transfers between devices  8.74 us (5%)
    pallas_call x1, Pallas kernels, run_model(): pl.pallas_call(model_kernel, out_shape=jax.ShapeDtypeStruct((ROWS, HID),...  65.2 us
    all_to_all x1, blocking collectives, per_device(): lax.all_to_all(partial.reshape(all_size, -1, HID), ('section', 'dom'), 0, 0)  22.1 us
    all_to_all x1, waiting for transfers between devices, per_device(): lax.all_to_all(shared, ('section', 'dom'), 0, 0).reshape(ROWS, HID)  19 us
    all_gather x1, blocking collectives, per_device(): whole = lax.all_gather(packed, 'dom', axis=0, tiled=False)  15.3 us
    dot_general x3, matrix products, precondition(): jnp.matmul(flipped, gradient, precision=highest)  4.88 us
    ppermute x1, starting transfers between devices, per_device(): feat_next = lax.ppermute(feat[:half], 'dom', down)  4.49 us
  transfers between devices with their start and end apart: 3, of which 1 were waited for; matrix products, arithmetic and copies ran while one was open for 10% of the time, Pallas kernels for 0%

profile of v1, /device:TPU:0, one launch (start us, length us, event | category | flops | bytes accessed | tf_op | source)
XLA Modules:
  0.0 180.1 jit_solution(12274943761967494996)
XLA Ops:
  0.7 0.0 copy-start
  0.7 1.6 copy-done
  2.3 4.5 %collective-permute-start.1 = (bf16[32,128]{1,0:T(8,128)(2,1)S(1)}, bf16[32,128]{1,0:T(8,128)(2,1)S(1)}, u32[]{:S(2)}, u32[]{:S(2)}) collective-permute-start(bf16[32,128]{1,0:T(8,128)(2,1)S(1)} %dynamic-slice_bitcast_fusion.2), channel_id=1, source_target_pairs={{1,0},{2,1},{3,2},{4,3},{5,4},{6,5},{7,6},{0,7},{9,8},{10,9},{11,1... | collective-permute-start | bytes 24584 | tf_op jit(solution)/shard_map/ppermute | solution.py:407
  6.7 0.7 constant_dynamic-slice_fusion
  7.4 0.1 add_bitcast_fusion
  7.5 0.8 dynamic-slice_bitcast_fusion.1
  8.4 0.8 constant_dynamic-slice_fusion.1
  9.2 0.7 collective-permute-start
  9.9 1.4 reduce_sum.76
  12.6 0.7 slice.150
  13.3 0.8 fusion.46
  14.2 0.1 pad_add_fusion
  14.3 0.1 slice.159
  14.4 0.1 add_select_fusion
  15.1 0.7 convert_element_type.65
  15.8 0.7 convert_element_type.63
  16.6 0.9 convert_element_type.64
  17.5 0.1 fusion.41
  17.6 15.3 %all-gather.1 = bf16[8,153,256]{2,1,0:T(8,128)(2,1)S(1)} all-gather(bf16[1,153,256]{2,1,0:T(8,128)(2,1)S(1)} %fusion.20), channel_id=2, replica_groups=mesh['section'=4,'dom'=8] {'dom'}, dimensions={0}, use_global_device_ids=true | all-gather | bytes 705024 | tf_op jit(solution)/shard_map/all_gather | solution.py:422
  32.9 0.6 slice_bitcast_fusion.1
  33.5 0.0 slice-start
  33.6 0.8 dynamic-slice_bitcast_fusion
  34.4 0.6 fusion.47
  35.0 0.7 copy.71.wot_ref
  35.7 0.5 copy.69
  36.2 0.6 pad_maximum_fusion.1.am_ref
  36.8 0.7 copy.68
  39.0 0.8 copy.72.col_ref
  39.8 1.1 reshape.262.wg_ref
  40.9 1.1 copy.70
  42.0 0.1 pad_add_fusion.5
  42.1 0.1 pad_add_fusion.3
  42.2 0.1 select_reduce_fusion
  42.3 0.7 add_add_fusion.src_ref
  43.0 0.7 pad_add_fusion.1
  43.7 0.8 pad_maximum_fusion.feat_ref
  44.6 65.2 %model.1 = bf16[1280,256]{1,0:T(8,128)(2,1)} custom-call(s32[8,2048]{1,0:T(8,128)} %add_add_fusion.src_ref, s32[1,2048]{1,0:T(1,128)} %get-tuple-element.27.lab_ref, s32[1,2048]{1,0:T(1,128)} %get-tuple-element.26.msk_ref, bf16[2048,128]{1,0:T(8,128)(2,1)} %pad_maximum_fusion.feat_ref, bf16[256,128]{1,0:T(8,128)(2,1)} %bitcast.103, ...), custom_call_target="tpu_custom_call" | custom-call | tf_op jit(solution)/shard_map/model/pallas_call | solution.py:323
  109.8 22.1 %all_to_all.10 = bf16[32,40,256]{2,1,0:T(8,128)(2,1)S(1)} all-to-all(bf16[32,40,256]{2,1,0:T(8,128)(2,1)} %bitcast.100), channel_id=1, replica_groups=mesh['section'=4,'dom'=8] {'section','dom'}, dimensions={0} | all-to-all | bytes 1310720 | tf_op jit(solution)/shard_map/all_to_all | solution.py:446
  131.9 0.1 reduce_sum.78
  132.0 0.9 broadcast_in_dim.16
  132.9 3.5 %all-to-all-start.1 = ((bf16[32,40,256]{2,1,0:T(8,128)(2,1)}), bf16[32,40,256]{2,1,0:T(8,128)(2,1)}, u32[]{:S(2)}, u32[]{:S(2)}) async-start(bf16[32,40,256]{2,1,0:T(8,128)(2,1)} %broadcast_in_dim.16), calls=%async_computation.1 | async-start | bytes 1310720 | tf_op jit(solution)/shard_map/all_to_all | solution.py:449
  136.4 19.0 %all-to-all-done.1 = bf16[32,40,256]{2,1,0:T(8,128)(2,1)} async-done(((bf16[32,40,256]{2,1,0:T(8,128)(2,1)}), bf16[32,40,256]{2,1,0:T(8,128)(2,1)}, u32[]{:S(2)}, u32[]{:S(2)}) %all-to-all-start.1) | async-done | bytes 655392 | tf_op jit(solution)/shard_map/all_to_all | solution.py:449
  155.4 1.2 bitcast_convert_fusion
  156.5 0.6 multiply_reduce_fusion.2
  157.2 0.9 multiply_reduce_fusion
  158.0 0.6 multiply_reduce_fusion.1
  158.7 0.6 fusion.45
  161.2 0.6 fusion.31
  162.5 0.0 copy-start.6
  162.6 0.0 copy-start.3
  162.6 0.1 slice_multiply_fusion
  162.7 0.8 fusion.6
  163.5 0.2 fusion.50
  163.8 0.3 fusion.48
  164.1 1.1 fusion.1
  165.2 2.9 %fusion = f32[2,2,256,256]{3,2,1,0:T(8,128)} fusion(f32[2,2,256,256]{3,2,1,0:T(8,128)S(1)} %copy-done.3, f32[2,2,256,256]{3,2,1,0:T(8,128)S(1)} %bitcast.95), kind=kOutput, calls=%fused_computation.1 | convolution fusion | flops 805830656 | bytes 3145728 | tf_op jit(solution)/shard_map/dot_general | solution.py:341
  168.2 1.1 fusion.49
  170.8 0.8 fusion.11
  171.6 0.8 fusion.10
  172.5 1.7 fusion.5
  174.2 0.6 multiply_add_fusion.2
  174.8 0.8 multiply_add_fusion.4
  175.6 0.8 multiply_add_fusion.1
  176.4 1.5 multiply_add_fusion
  (74 shorter events, 0.4 us)
Async XLA Ops:
  0.7 1.6 copy-start
  2.3 41.5 %collective-permute-start.1 = (bf16[32,128]{1,0:T(8,128)(2,1)S(1)}, bf16[32,128]{1,0:T(8,128)(2,1)S(1)}, u32[]{:S(2)}, u32[]{:S(2)}) collective-permute-start(bf16[32,128]{1,0:T(8,128)(2,1)S(1)} %dynamic-slice_bitcast_fusion.2), channel_id=1, source_target_pairs={{1,0},{2,1},{3,2},{4,3},{5,4},{6,5},{7,6},{0,7},{9,8},{10,9},{11,1... | collective-permute-start | bytes 24584 | tf_op jit(solution)/shard_map/ppermute | solution.py:407
  9.2 32.8 %collective-permute-start = (s32[11,32]{1,0:T(8,128)S(1)}, s32[11,32]{1,0:T(8,128)S(1)}, u32[]{:S(2)}, u32[]{:S(2)}) collective-permute-start(s32[11,32]{1,0:T(8,128)S(1)} %pad_add_fusion.2), channel_id=1, source_target_pairs={{1,0},{2,1},{3,2},{4,3},{5,4},{6,5},{7,6},{0,7},{9,8},{10,9},{11,1... | collective-permute-start | bytes 4232 | tf_op jit(solution)/shard_map/ppermute | solution.py:409
  33.5 4.1 %slice-start = ((f32[1128]{0:T(1024)}), f32[104]{0:T(128)S(1)}, s32[]{:S(2)}) async-start(f32[1128]{0:T(1024)} %param.35), calls=%async_computation.2 | async-start | bytes 1024 | tf_op jit(solution)/shard_map/slice | solution.py:36
  37.6 6.2 %copy-start.1 = (bf16[2016,128]{1,0:T(8,128)(2,1)S(1)}, bf16[2016,128]{1,0:T(8,128)(2,1)}, u32[]{:S(2)}) copy-start(bf16[2016,128]{1,0:T(8,128)(2,1)} %dynamic-slice_bitcast_fusion) | copy-start | bytes 1548292
  132.9 22.5 %all-to-all-start.1 = ((bf16[32,40,256]{2,1,0:T(8,128)(2,1)}), bf16[32,40,256]{2,1,0:T(8,128)(2,1)}, u32[]{:S(2)}, u32[]{:S(2)}) async-start(bf16[32,40,256]{2,1,0:T(8,128)(2,1)} %broadcast_in_dim.16), calls=%async_computation.1 | async-start | bytes 1310720 | tf_op jit(solution)/shard_map/all_to_all | solution.py:449
  158.0 4.7 %copy-start.13 = (f32[40,40]{1,0:T(8,128)S(1)}, f32[40,40]{1,0:T(8,128)}, u32[]{:S(2)}) copy-start(f32[40,40]{1,0:T(8,128)} %param.41) | copy-start | bytes 19204
  158.7 4.9 %copy-start.12 = (f32[40,40]{1,0:T(8,128)S(1)}, f32[40,40]{1,0:T(8,128)}, u32[]{:S(2)}) copy-start(f32[40,40]{1,0:T(8,128)} %param.47) | copy-start | bytes 19204
  162.5 1.2 copy-start.6
  162.6 1.5 copy-start.5
  162.6 2.6 %copy-start.3 = (f32[2,2,256,256]{3,2,1,0:T(8,128)S(1)}, f32[2,2,256,256]{3,2,1,0:T(8,128)}, u32[]{:S(2)}) copy-start(f32[2,2,256,256]{3,2,1,0:T(8,128)} %param.39) | copy-start | bytes 3145732
  165.2 2.9 %copy-start.2 = (f32[2,2,256,256]{3,2,1,0:T(8,128)S(1)}, f32[2,2,256,256]{3,2,1,0:T(8,128)}, u32[]{:S(2)}) copy-start(f32[2,2,256,256]{3,2,1,0:T(8,128)} %param.45) | copy-start | bytes 3145732
  168.1 2.7 %copy-start.23 = (f32[8,64]{1,0:T(8,128)S(1)}, f32[8,64]{1,0:T(8,128)}, u32[]{:S(2)}) copy-start(f32[8,64]{1,0:T(8,128)} %param.40) | copy-start | bytes 6148
  168.1 3.5 %copy-start.16 = (f32[16,128]{1,0:T(8,128)S(1)}, f32[16,128]{1,0:T(8,128)}, u32[]{:S(2)}) copy-start(f32[16,128]{1,0:T(8,128)} %param.36) | copy-start | bytes 24580
  168.2 4.3 %copy-start.7 = (f32[2,2,32,256]{3,2,1,0:T(8,128)S(1)}, f32[2,2,32,256]{3,2,1,0:T(8,128)}, u32[]{:S(2)}) copy-start(f32[2,2,32,256]{3,2,1,0:T(8,128)} %param.38) | copy-start | bytes 393220
  169.3 4.9 %copy-start.11 = (f32[1128]{0:T(1024)S(1)}, f32[1128]{0:T(1024)}, u32[]{:S(2)}) copy-start(f32[1128]{0:T(1024)} %param.35) | copy-start | bytes 13540
  169.3 4.8 %copy-start.17 = (f32[1128]{0:T(1024)S(1)}, f32[1128]{0:T(1024)}, u32[]{:S(2)}) copy-start(f32[1128]{0:T(1024)} %param.53) | copy-start | bytes 13540
  169.3 4.8 %copy-start.18 = (f32[1128]{0:T(1024)S(1)}, f32[1128]{0:T(1024)}, u32[]{:S(2)}) copy-start(f32[1128]{0:T(1024)} %param.48) | copy-start | bytes 13540
  169.3 4.8 %copy-start.19 = (f32[1128]{0:T(1024)S(1)}, f32[1128]{0:T(1024)}, u32[]{:S(2)}) copy-start(f32[1128]{0:T(1024)} %param.49) | copy-start | bytes 13540
  169.4 5.5 %copy-start.15 = (f32[8,40]{1,0:T(8,128)S(1)}, f32[8,40]{1,0:T(8,128)}, u32[]{:S(2)}) copy-start(f32[8,40]{1,0:T(8,128)} %param.34) | copy-start | bytes 3844
  169.4 5.4 %copy-start.21 = (f32[8,40]{1,0:T(8,128)S(1)}, f32[8,40]{1,0:T(8,128)}, u32[]{:S(2)}) copy-start(f32[8,40]{1,0:T(8,128)} %param.52) | copy-start | bytes 3844
  169.4 5.4 %copy-start.22 = (f32[8,64]{1,0:T(8,128)S(1)}, f32[8,64]{1,0:T(8,128)}, u32[]{:S(2)}) copy-start(f32[8,64]{1,0:T(8,128)} %param.46) | copy-start | bytes 6148
  169.4 6.2 %copy-start.10 = (f32[16,256]{1,0:T(8,128)S(1)}, f32[16,256]{1,0:T(8,128)}, u32[]{:S(2)}) copy-start(f32[16,256]{1,0:T(8,128)} %param.32) | copy-start | bytes 49156
  169.4 6.2 %copy-start.14 = (f32[16,256]{1,0:T(8,128)S(1)}, f32[16,256]{1,0:T(8,128)}, u32[]{:S(2)}) copy-start(f32[16,256]{1,0:T(8,128)} %param.50) | copy-start | bytes 49156
  169.4 6.2 %copy-start.20 = (f32[16,128]{1,0:T(8,128)S(1)}, f32[16,128]{1,0:T(8,128)}, u32[]{:S(2)}) copy-start(f32[16,128]{1,0:T(8,128)} %param.42) | copy-start | bytes 24580
  169.4 7.0 %copy-start.4 = (f32[2,2,32,256]{3,2,1,0:T(8,128)S(1)}, f32[2,2,32,256]{3,2,1,0:T(8,128)}, u32[]{:S(2)}) copy-start(f32[2,2,32,256]{3,2,1,0:T(8,128)} %param.33) | copy-start | bytes 393220
  169.4 6.9 %copy-start.8 = (f32[2,2,32,256]{3,2,1,0:T(8,128)S(1)}, f32[2,2,32,256]{3,2,1,0:T(8,128)}, u32[]{:S(2)}) copy-start(f32[2,2,32,256]{3,2,1,0:T(8,128)} %param.51) | copy-start | bytes 393220
  169.5 6.9 %copy-start.9 = (f32[2,2,32,256]{3,2,1,0:T(8,128)S(1)}, f32[2,2,32,256]{3,2,1,0:T(8,128)}, u32[]{:S(2)}) copy-start(f32[2,2,32,256]{3,2,1,0:T(8,128)} %param.44) | copy-start | bytes 393220

commit v2 on v1

v2 whole, which is shorter than its diff:
```python
import jax
import jax.numpy as jnp
from jax import lax
from jax.experimental import pallas as pl
from jax.experimental.pallas import tpu as pltpu
from jax.sharding import PartitionSpec as P

FEAT = 128
HEADS = 4
HSIZE = 64
CLASSES = 40
STEPS = 5
HID = 256
SMALL = 1128


highest = lax.Precision.HIGHEST
leak_slope = 0.2
smooth = 0.1
clip_norm = 0.001
shampoo_rate = 0.3
shampoo_decay = 0.5
weight_decay = 0.0001
adam_rate = 0.1
beta_one = 0.9
beta_two = 0.999
adam_eps = 1e-08
adam_decay = 0.01
ema_keep = 0.9


def split_small(small_params):
    bias_in = small_params[0:HID]
    attention = small_params[HID : 3 * HID].reshape(2, HEADS, HSIZE)
    bias_one = small_params[3 * HID : 4 * HID]
    bias_two = small_params[4 * HID : 4 * HID + HSIZE]
    bias_out = small_params[4 * HID + HSIZE :]
    return (bias_in, attention, bias_one, bias_two, bias_out)


GRAPH = 64
LANES = 128
DEG = 8
SLOTS = DEG + 1
ROWS = 1280
GROUPS = 8
IN_G = FEAT // GROUPS
GAT_G = HID // GROUPS
OUT_G = HSIZE // GROUPS
TAIL_G = IN_G + 4 * GAT_G
PACK_G = TAIL_G + 2 * OUT_G
HALF = GRAPH // 2
ROW_IN = 4 * HID
ROW_OUT = ROW_IN + FEAT
ROW_MISC = ROW_OUT + HSIZE

bf16 = jnp.bfloat16
f32 = jnp.float32


def dot_nn(a, b):
    return lax.dot_general(a, b, (((1,), (0,)), ((), ())), preferred_element_type=f32)


def dot_nt(a, b):
    return lax.dot_general(a, b, (((1,), (1,)), ((), ())), preferred_element_type=f32)


def tile_of(k):
    return slice(k * LANES, (k + 1) * LANES)


def head_of(h):
    return slice(h * HSIZE, (h + 1) * HSIZE)


def row_of(ref, micro, width):
    picked = ref[0:1, 0:width]
    for other in range(1, ref.shape[0]):
        picked = jnp.where(micro == other, ref[other : other + 1, 0:width], picked)
    return picked


def pack_kernel(
    micro_ref,
    feat_ref,
    src_ref,
    lab_ref,
    msk_ref,
    send_ref,
    win_ref,
    wgat_ref,
    wout_ref,
    pack_ref,
    ints_ref,
    first_ref,
    tail_ref,
):
    micro = micro_ref[0]
    first_ref[...] = feat_ref[0]
    ints_ref[...] = jnp.zeros_like(ints_ref)
    shift = LANES - HALF
    ints_ref[0:DEG, :] = pltpu.roll(src_ref[0], shift, 1)
    ints_ref[DEG : DEG + 1, :] = pltpu.roll(row_of(lab_ref, micro, LANES), shift, 1)
    ints_ref[DEG + 1 : DEG + 2, :] = pltpu.roll(row_of(msk_ref, micro, LANES), shift, 1)
    send = row_of(send_ref, micro, 2 * HALF)
    ints_ref[DEG + 2 : DEG + 3, :] = jnp.concatenate([send, send], axis=1)
    if win_ref.shape[0] != IN_G:
        pack_ref[...] = jnp.zeros_like(pack_ref)
        return
    pack_ref[0:IN_G, :] = win_ref[...].astype(bf16)
    for layer in range(2):
        for side in range(2):
            start = IN_G + (2 * layer + side) * GAT_G
            pack_ref[start : start + GAT_G, :] = wgat_ref[layer, side].astype(bf16)
    tail_ref[...] = jnp.zeros_like(tail_ref)
    tail_ref[0:OUT_G, 0:CLASSES] = wout_ref[...]
    count = jnp.sum(jnp.sum(msk_ref[...].astype(f32), axis=1, keepdims=True), axis=0, keepdims=True)
    high = jnp.floor(count * (1.0 / 256.0))
    lane = lax.broadcasted_iota(jnp.int32, (1, HID), 1)
    low = jnp.where(lane == 1, count - 256.0 * high, 0.0)
    tail_ref[OUT_G : OUT_G + 1, :] = jnp.where(lane == 0, high, low)
    pack_ref[TAIL_G:PACK_G, :] = tail_ref[...].astype(bf16)


def vmem(count):
    return [pl.BlockSpec(memory_space=pltpu.VMEM)] * count


def pack_inputs(micro, features, src_all, labels, label_mask, send_index, w_in, w_gat, w_out):
    grid_spec = pltpu.PrefetchScalarGridSpec(
        num_scalar_prefetch=1,
        grid=(1,),
        in_specs=[
            pl.BlockSpec((1, HALF, FEAT), lambda i, m: (m[0], 0, 0)),
            pl.BlockSpec((1, DEG, LANES), lambda i, m: (m[0], 0, 0)),
        ]
        + vmem(6),
        out_specs=vmem(3),
        scratch_shapes=[pltpu.VMEM((2 * OUT_G, HID), f32)],
    )
    return pl.pallas_call(
        pack_kernel,
        grid_spec=grid_spec,
        out_shape=(
            jax.ShapeDtypeStruct((PACK_G, HID), bf16),
            jax.ShapeDtypeStruct((16, LANES), jnp.int32),
            jax.ShapeDtypeStruct((HALF, FEAT), bf16),
        ),
        compiler_params=pltpu.CompilerParams(vmem_limit_bytes=60 * 1024 * 1024),
        name="pack",
    )(micro, features, src_all, labels, label_mask, send_index, w_in, w_gat, w_out)


def gather_weights(packed, w_in, w_gat, w_out, label_mask):
    size = lax.axis_size("dom")
    if size == GROUPS:
        return lax.all_gather(packed, "dom", axis=0, tiled=False)
    rows_in, rows_gat, rows_out = (w_in.shape[0], w_gat.shape[2], w_out.shape[0])
    count = jnp.sum(label_mask)
    digits = jnp.stack([lax.div(count, 256), lax.rem(count, 256)]).astype(bf16)
    packed = jnp.concatenate(
        [
            w_in.astype(bf16),
            w_gat.astype(bf16).reshape(4 * rows_gat, HID),
            jnp.pad(w_out.astype(bf16), ((0, 0), (0, HID - CLASSES))),
            jnp.pad(digits[None, :], ((0, 0), (0, HID - 2))),
        ],
        axis=0,
    )
    whole = lax.all_gather(packed, "dom", axis=0, tiled=False)
    cut = rows_in + 4 * rows_gat
    part_in = whole[:, :rows_in].reshape(GROUPS, IN_G, HID)
    part_gat = whole[:, rows_in:cut].reshape(GROUPS, size // GROUPS, 4, rows_gat, HID)
    part_gat = part_gat.transpose(0, 2, 1, 3, 4).reshape(GROUPS, 4 * GAT_G, HID)
    part_out = whole[:, cut : cut + rows_out].reshape(GROUPS, OUT_G, HID)
    counts = whole[:, cut + rows_out].reshape(GROUPS, size // GROUPS, HID)
    counts = jnp.pad(counts, ((0, 0), (0, OUT_G - size // GROUPS), (0, 0)))
    return jnp.concatenate([part_in, part_gat, part_out, counts], axis=1)


def column_of(row):
    return jnp.broadcast_to(row.reshape(1, -1), (LANES, row.shape[0])).T


def model_kernel(
    micro_ref,
    feat_ref,
    src_ref,
    lab_ref,
    msk_ref,
    send_ref,
    whole_ref,
    ints_ref,
    next_ref,
    small_ref,
    out_ref,
    e_ref,
    t_ref,
    al_ref,
    att_ref,
    h_ref,
    slope_ref,
    xlr_ref,
    dx_ref,
    do_ref,
    pool_ref,
    dlog_ref,
    w_ref,
    sum_ref,
    a_ref,
    da_ref,
    gb_ref,
    loss_ref,
    node_ref,
    edge_ref,
    mark_ref,
    wi_ref,
    wgt_ref,
    wg_ref,
    wo_ref,
    wof_ref,
    am_ref,
):
    nodes = feat_ref.shape[1]
    blocks = nodes // LANES
    chunk = 4 * LANES
    chunks = nodes // chunk
    mixed = DEG * LANES
    micro = micro_ref[0]
    final = nodes - LANES

    node_ref[0 : nodes - HALF, :] = feat_ref[0, HALF:nodes, :]
    node_ref[nodes - HALF : nodes, :] = next_ref[...]
    lane_row = lax.broadcasted_iota(jnp.int32, (1, LANES), 1)
    kept = lane_row < LANES - HALF
    edge_ref[...] = pltpu.roll(src_ref[0], nodes - HALF, 1)
    edge_ref[:, final:nodes] = jnp.where(kept, edge_ref[:, final:nodes], ints_ref[0:DEG, :])
    for place, ref in enumerate((lab_ref, msk_ref)):
        mark_ref[place : place + 1, :] = pltpu.roll(row_of(ref, micro, nodes), nodes - HALF, 1)
        came = ints_ref[DEG + place : DEG + place + 1, :]
        mark_ref[place : place + 1, final:nodes] = jnp.where(kept, mark_ref[place : place + 1, final:nodes], came)
    send = row_of(send_ref, micro, 2 * HALF)
    send = jnp.concatenate([send, send], axis=1)
    arrived = pltpu.roll(ints_ref[DEG + 2 : DEG + 3, :], HALF, 1)
    table = jnp.where(
        lane_row < HALF, pltpu.roll(send, HALF, 1) - (nodes - HALF), arrived + HALF
    )
    spot_row = lax.broadcasted_iota(jnp.int32, (GRAPH, LANES), 0)
    spot_lane = lax.broadcasted_iota(jnp.int32, (GRAPH, LANES), 1)
    table = jnp.sum(jnp.where(spot_row == spot_lane, table.astype(f32), 0.0), axis=1, keepdims=True)
    looked = []
    for k in range(DEG):
        far = edge_ref[k : k + 1, final:nodes] - nodes == spot_row
        looked.append(jnp.sum(jnp.where(far, table, 0.0), axis=0, keepdims=True))
    looked = jnp.concatenate(looked, axis=0).astype(jnp.int32)
    raw = edge_ref[:, final:nodes]
    looked = jnp.where(raw >= nodes, looked, jnp.bitwise_and(raw - HALF, GRAPH - 1))
    local = jnp.bitwise_and(edge_ref[...] - HALF, GRAPH - 1)
    lane_all = lax.broadcasted_iota(jnp.int32, (DEG, nodes), 1)
    second = jnp.bitwise_and(lane_all, GRAPH)
    edge_ref[...] = local + second
    edge_ref[:, final:nodes] = looked + jnp.bitwise_and(
        lax.broadcasted_iota(jnp.int32, (DEG, LANES), 1), GRAPH
    )

    digits = jnp.zeros((OUT_G, HID), f32)
    for g in range(GROUPS):
        wi_ref[g * IN_G : (g + 1) * IN_G, :] = whole_ref[g, 0:IN_G, :]
        for layer in range(2):
            for side in range(2):
                start = IN_G + (2 * layer + side) * GAT_G
                wg_ref[layer, g * GAT_G : (g + 1) * GAT_G, side * HID : (side + 1) * HID] = whole_ref[
                    g, start : start + GAT_G, :
                ]
        tail = whole_ref[g, TAIL_G:PACK_G, :].astype(f32)
        wof_ref[g * OUT_G : (g + 1) * OUT_G, :] = tail[0:OUT_G]
        digits = digits + tail[OUT_G : 2 * OUT_G]
    for layer in range(2):
        for side in range(2):
            wgt_ref[layer, side * HID : (side + 1) * HID, :] = wg_ref[
                layer, :, side * HID : (side + 1) * HID
            ].T
    wi_t = wi_ref[...].T
    wo_ref[...] = wof_ref[:, 0:CLASSES].astype(bf16)
    wo_t = wof_ref[...].T[0:CLASSES].astype(bf16)
    digits = jnp.sum(digits, axis=0, keepdims=True)
    inv_count = 1.0 / (digits[:, 0:1] * 256.0 + digits[:, 1:2])

    row_id = lax.broadcasted_iota(jnp.int32, (LANES, LANES), 0)
    lane_id = lax.broadcasted_iota(jnp.int32, (LANES, LANES), 1)
    eye = jnp.where(row_id == lane_id, 1.0, 0.0).astype(bf16)
    head_row = lax.broadcasted_iota(jnp.int32, (16, HID), 0)
    head_col = lax.broadcasted_iota(jnp.int32, (16, HID), 1)
    head_mask = jnp.where(head_col // HSIZE == head_row, 1.0, 0.0)

    bias_in = column_of(small_ref[0:HID])[:, 0:1]
    bias_one = column_of(small_ref[3 * HID : 4 * HID])[:, 0:1]
    bias_two = column_of(small_ref[4 * HID : 4 * HID + HSIZE])[:, 0:1]
    bias_out = column_of(small_ref[4 * HID + HSIZE : SMALL])[:, 0:1]
    for layer in range(2):
        row = small_ref[(1 + layer) * HID : (2 + layer) * HID]
        a_ref[layer] = column_of(row)
        row = row.reshape(1, HID)
        high = row.astype(bf16).astype(f32)
        am_ref[layer] = jnp.concatenate([head_mask[0:8] * high, head_mask[0:8] * (row - high)], axis=0).astype(bf16)
    fold_row = lax.broadcasted_iota(jnp.int32, (16, HEADS * 16), 0)
    fold_col = lax.broadcasted_iota(jnp.int32, (16, HEADS * 16), 1)
    fold = jnp.where(fold_col // 16 == fold_row, 1.0, 0.0).astype(bf16)
    spots = lax.broadcasted_iota(jnp.int32, (GRAPH, LANES), 0).astype(f32).astype(bf16)
    spots = spots.reshape(4, 16, LANES)
    half_lane = lax.broadcasted_iota(jnp.int32, (16, LANES), 1)
    first_half = (half_lane < GRAPH).astype(f32).astype(bf16)[None] > 0
    own_spot = jnp.bitwise_and(half_lane, GRAPH - 1).astype(f32).astype(bf16)
    zero = jnp.zeros((4, 16, LANES), bf16)
    da_ref[...] = jnp.zeros_like(da_ref)
    gb_ref[...] = jnp.zeros_like(gb_ref)
    loss_ref[...] = jnp.zeros_like(loss_ref)

    def lanes_of(i, width):
        return pl.ds(pl.multiple_of(i * width, width), width)

    @pl.loop(0, chunks)
    def _(c):
        at = lanes_of(c, chunk)
        pre = dot_nt(wi_t, node_ref[at, :]) + bias_in
        grown = jnp.exp(jnp.minimum(pre, 0.0))
        h_ref[0, :, at] = jnp.where(pre > 0, pre, grown - 1.0).astype(bf16)
        slope_ref[0, :, at] = jnp.where(pre > 0, 1.0, grown)

    for layer in range(2):

        @pl.loop(0, chunks)
        def _(c):
            at = lanes_of(c, chunk)
            xlr_ref[layer, :, at] = dot_nn(wgt_ref[layer], h_ref[layer, :, at]).astype(bf16)

        @pl.loop(0, blocks, unroll=4)
        def _(i):
            at = lanes_of(i, LANES)
            if layer == 0:
                for k in range(DEG):
                    hit = row_id == edge_ref[k : k + 1, at]
                    e_ref[i, 0:LANES, tile_of(k)] = jnp.where(hit, 1.0, 0.0).astype(bf16)
                    e_ref[i, LANES : 2 * LANES, tile_of(k)] = eye
            left = xlr_ref[layer, 0:HID, at]
            right = xlr_ref[layer, HID : 2 * HID, at]
            both = jnp.concatenate([left, right], axis=1)
            t_ref[layer, i, :, 0:mixed] = dot_nn(both, e_ref[i]).astype(bf16)
            t_ref[layer, i, :, tile_of(DEG)] = left + right
            t = t_ref[layer, i]
            z = jnp.maximum(t, t * leak_slope)
            scores = dot_nn(am_ref[layer], z)
            grown = jnp.exp(scores[0:8] + scores[8:16])
            total = grown[:, tile_of(0)]
            for k in range(1, SLOTS):
                total = total + grown[:, tile_of(k)]
            inverse = 1.0 / total
            grids = [zero] * HEADS
            for k in range(SLOTS):
                alpha = grown[:, tile_of(k)] * inverse
                al_ref[layer, i, :, tile_of(k)] = alpha
                if k == DEG:
                    spot = own_spot
                else:
                    spot = jnp.bitwise_and(edge_ref[k : k + 1, at], GRAPH - 1).astype(f32)
                    spot = jnp.broadcast_to(spot, (16, LANES)).astype(bf16)
                hit = spots == spot[None]
                for h in range(HEADS):
                    part = jnp.broadcast_to(alpha[h : h + 1], (16, LANES)).astype(bf16)
                    grids[h] = grids[h] + jnp.where(hit, part[None], zero)
            pooled = None
            for h in range(HEADS):
                upper = jnp.where(first_half, grids[h], zero).reshape(GRAPH, LANES)
                lower = jnp.where(first_half, zero, grids[h]).reshape(GRAPH, LANES)
                grid = jnp.concatenate([upper, lower], axis=0)
                att_ref[layer, i, h] = grid
                total = dot_nn(left[head_of(h)], grid)
                if layer == 0:
                    pre = total + bias_one[head_of(h)]
                    grown_one = jnp.exp(jnp.minimum(pre, 0.0))
                    h_ref[1, head_of(h), at] = jnp.where(pre > 0, pre, grown_one - 1.0).astype(bf16)
                    slope_ref[1, head_of(h), at] = jnp.where(pre > 0, 1.0, grown_one)
                else:
                    rounded = total.astype(bf16).astype(f32)
                    pooled = rounded if pooled is None else pooled + rounded
            if layer == 1:
                pool_ref[:, at] = (pooled * (1.0 / HEADS) + bias_two).astype(bf16)

    @pl.loop(0, chunks)
    def _(c):
        at = lanes_of(c, chunk)
        logits = dot_nn(wo_t, pool_ref[:, at]) + bias_out
        shifted = logits - jnp.max(logits, axis=0, keepdims=True)
        log_prob = shifted - jnp.log(jnp.sum(jnp.exp(shifted), axis=0, keepdims=True))
        class_id = lax.broadcasted_iota(jnp.int32, (CLASSES, chunk), 0)
        onehot = jnp.where(class_id == mark_ref[0:1, at], 1.0, 0.0)
        share = mark_ref[1:2, at].astype(f32) * inv_count
        term = jnp.sum(((smooth - 1.0) * onehot - smooth / CLASSES) * log_prob, axis=0, keepdims=True)
        loss_ref[...] += term * share
        d_logits = (jnp.exp(log_prob) - (1.0 - smooth) * onehot - smooth / CLASSES) * share
        d_logits = d_logits.astype(bf16)
        dlog_ref[:, at] = d_logits
        d_pooled = (dot_nn(wo_ref[...], d_logits) * (1.0 / HEADS)).astype(bf16)
        for h in range(HEADS):
            do_ref[head_of(h), at] = d_pooled

    for layer in (1, 0):

        @pl.loop(0, blocks, unroll=4)
        def _(i):
            at = lanes_of(i, LANES)
            d_out = do_ref[:, at]
            for h in range(HEADS):
                d_head = d_out[head_of(h)].reshape(4, 16, LANES)
                for k in range(SLOTS):
                    product = t_ref[layer, i, head_of(h), tile_of(k)].reshape(4, 16, LANES) * d_head
                    sum_ref[h * 16 : (h + 1) * 16, tile_of(k)] = (product[0] + product[1]) + (product[2] + product[3])
            d_alpha = dot_nn(fold, sum_ref[...])[0:8]
            alpha = al_ref[layer, i]
            weighted = alpha * d_alpha
            total = weighted[:, tile_of(0)]
            for k in range(1, SLOTS):
                total = total + weighted[:, tile_of(k)]
            for k in range(SLOTS):
                d_score = weighted[:, tile_of(k)] - alpha[:, tile_of(k)] * total
                for h in range(HEADS):
                    one = jnp.broadcast_to(d_score[h : h + 1], (16, LANES))
                    two = (one * leak_slope).astype(bf16)[None]
                    one = one.astype(bf16)[None]
                    t = t_ref[layer, i, head_of(h), tile_of(k)].reshape(4, 16, LANES)
                    w_ref[head_of(h), tile_of(k)] = jnp.where(t > 0, one, two).reshape(HSIZE, LANES)
            spread = dot_nt(w_ref[:, 0:mixed], e_ref[i])
            own = w_ref[:, tile_of(DEG)].astype(f32)
            left_w = spread[:, 0:LANES] + own
            right_w = spread[:, LANES : 2 * LANES] + own
            left = xlr_ref[layer, 0:HID, at].astype(f32)
            right = xlr_ref[layer, HID : 2 * HID, at].astype(f32)
            da_ref[layer] += left * left_w + right * right_w
            wide = a_ref[layer]
            for h in range(HEADS):
                passed = dot_nt(d_out[head_of(h)], att_ref[layer, i, h])
                d_left = wide[head_of(h)] * left_w[head_of(h)] + passed
                dx_ref[layer, head_of(h), at] = d_left.astype(bf16)
            dx_ref[layer, HID : 2 * HID, at] = (wide * right_w).astype(bf16)

        @pl.loop(0, chunks)
        def _(c):
            at = lanes_of(c, chunk)
            d_in = dot_nn(wg_ref[layer], dx_ref[layer, :, at]).astype(bf16).astype(f32)
            d_in = d_in * slope_ref[layer, :, at]
            do_ref[:, at] = d_in.astype(bf16)
            if layer == 1:
                for k in range(4):
                    gb_ref[...] += d_in[:, tile_of(k)]

    for layer in range(2):
        for side in range(2):
            start = (2 * layer + side) * HID
            out_ref[start : start + HID, :] = dot_nt(
                h_ref[layer], dx_ref[layer, side * HID : (side + 1) * HID, :]
            ).astype(bf16)
    out_ref[ROW_IN : ROW_IN + FEAT, :] = dot_nn(do_ref[...], node_ref[...]).T.astype(bf16)
    out_ref[ROW_OUT : ROW_OUT + HSIZE, :] = jnp.zeros((HSIZE, HID), bf16)
    out_ref[ROW_OUT : ROW_OUT + HSIZE, 0:CLASSES] = dot_nt(pool_ref[...], dlog_ref[...]).astype(bf16)
    ones = jnp.ones((nodes, LANES), bf16)
    lane_wide = lax.broadcasted_iota(jnp.int32, (HID, LANES), 1)
    columns = jnp.where(lane_wide == 0, dot_nn(do_ref[...], ones), 0.0)
    for layer in range(2):
        da = jnp.sum(da_ref[layer], axis=1, keepdims=True)
        columns = columns + jnp.where(lane_wide == 1 + layer, da, 0.0)
    columns = columns + jnp.where(lane_wide == 3, jnp.sum(gb_ref[...], axis=1, keepdims=True), 0.0)
    g_bias_out = dot_nn(dlog_ref[...], ones)
    g_bias_two = lax.dot_general(
        wo_ref[...].astype(f32), g_bias_out, (((1,), (0,)), ((), ())),
        precision=highest, preferred_element_type=f32,
    )
    loss = jnp.broadcast_to(jnp.sum(loss_ref[...], axis=1, keepdims=True), (8, LANES))
    loss_high = loss.astype(bf16).astype(f32)
    rest = HID - HSIZE - CLASSES - 16
    last = jnp.concatenate(
        [g_bias_two, g_bias_out, loss_high, loss - loss_high, jnp.zeros((rest, LANES), f32)], axis=0
    )
    columns = columns + jnp.where(lane_wide == 4, last, 0.0)
    out_ref[ROW_MISC : ROW_MISC + 16, :] = columns.T[0:16].astype(bf16)
    out_ref[ROW_MISC + 16 :, :] = jnp.zeros((ROWS - ROW_MISC - 16, HID), bf16)


def run_model(micro, features, src_all, labels, label_mask, send_index, whole, ints, first, small_params):
    nodes = features.shape[1]
    blocks = nodes // LANES
    scratch = [
        pltpu.VMEM((blocks, 2 * LANES, DEG * LANES), bf16),
        pltpu.VMEM((2, blocks, HID, SLOTS * LANES), bf16),
        pltpu.VMEM((2, blocks, 8, SLOTS * LANES), f32),
        pltpu.VMEM((2, blocks, HEADS, LANES, LANES), bf16),
        pltpu.VMEM((2, HID, nodes), bf16),
        pltpu.VMEM((2, HID, nodes), f32),
        pltpu.VMEM((2, 2 * HID, nodes), bf16),
        pltpu.VMEM((2, 2 * HID, nodes), bf16),
        pltpu.VMEM((HID, nodes), bf16),
        pltpu.VMEM((HSIZE, nodes), bf16),
        pltpu.VMEM((CLASSES, nodes), bf16),
        pltpu.VMEM((HID, SLOTS * LANES), bf16),
        pltpu.VMEM((HEADS * 16, SLOTS * LANES), bf16),
        pltpu.VMEM((2, HID, LANES), f32),
        pltpu.VMEM((2, HID, LANES), f32),
        pltpu.VMEM((HID, LANES), f32),
        pltpu.VMEM((1, 4 * LANES), f32),
        pltpu.VMEM((nodes, FEAT), bf16),
        pltpu.VMEM((DEG, nodes), jnp.int32),
        pltpu.VMEM((8, nodes), jnp.int32),
        pltpu.VMEM((FEAT, HID), bf16),
        pltpu.VMEM((2, 2 * HID, HID), bf16),
        pltpu.VMEM((2, HID, 2 * HID), bf16),
        pltpu.VMEM((HSIZE, CLASSES), bf16),
        pltpu.VMEM((HSIZE, HID), f32),
        pltpu.VMEM((2, 16, HID), bf16),
    ]
    grid_spec = pltpu.PrefetchScalarGridSpec(
        num_scalar_prefetch=1,
        grid=(1,),
        in_specs=[
            pl.BlockSpec((1, nodes, FEAT), lambda i, m: (m[0], 0, 0)),
            pl.BlockSpec((1, DEG, nodes), lambda i, m: (m[0], 0, 0)),
        ]
        + vmem(7),
        out_specs=vmem(1)[0],
        scratch_shapes=scratch,
    )
    return pl.pallas_call(
        model_kernel,
        grid_spec=grid_spec,
        out_shape=jax.ShapeDtypeStruct((ROWS, HID), bf16),
        compiler_params=pltpu.CompilerParams(vmem_limit_bytes=60 * 1024 * 1024),
        name="model",
    )(micro, features, src_all, labels, label_mask, send_index, whole, ints, first, small_params)


def adamw_step(parameter, gradient, moment_one, moment_two):
    moment_one = beta_one * moment_one + (1.0 - beta_one) * gradient
    moment_two = beta_two * moment_two + (1.0 - beta_two) * gradient * gradient
    corr_one = 1.0 - beta_one**STEPS
    corr_two = 1.0 - beta_two**STEPS
    update = moment_one / corr_one / (jnp.sqrt(moment_two / corr_two) + adam_eps)
    return (parameter - adam_rate * (update + adam_decay * parameter), moment_one, moment_two)


def average(old_value, new_value):
    return ema_keep * old_value + (1.0 - ema_keep) * new_value


def dot_tn(a, b):
    return lax.dot_general(a, b, (((0,), (0,)), ((), ())), preferred_element_type=f32)


def halves(value):
    high = value.astype(bf16)
    return high, (value - high.astype(f32)).astype(bf16)


def wide_rows(total):
    return max(total, 16)


def own_rows(gradient, start, count):
    total = gradient.shape[0]
    row = lax.broadcasted_iota(jnp.int32, (wide_rows(count), total), 0) + start
    lane = lax.broadcasted_iota(jnp.int32, (wide_rows(count), total), 1)
    pick = jnp.where(row == lane, 1.0, 0.0).astype(bf16)
    return dot_nn(pick, gradient).astype(bf16)


def precondition(gradient, weight, stat_l, stat_r, root_l, root_r, ema, outs, scale, start):
    (new_w, new_l, new_r, new_ema) = outs
    count = weight.shape[0]
    square = (1.0 - shampoo_decay) * scale * scale
    mine = own_rows(gradient, start, count)
    new_l[...] = shampoo_decay * stat_l + square * dot_nt(mine, gradient)[0:count]
    new_r[...] = shampoo_decay * stat_r + square * dot_tn(gradient, gradient)
    high, low = halves(root_l)
    middle = dot_nn(high, gradient) + dot_nn(low, gradient)
    m_high, m_low = halves(middle * scale)
    r_high, r_low = halves(root_r)
    update = dot_nn(m_high, r_high) + dot_nn(m_low, r_high) + dot_nn(m_high, r_low)
    weight = weight - shampoo_rate * (update + weight_decay * weight)
    new_w[...] = weight
    new_ema[...] = average(ema, weight)


def update_kernel(
    dom_ref,
    sum_ref,
    w_in,
    w_gat,
    w_out,
    small,
    l_in,
    r_in,
    l_gat,
    r_gat,
    l_out,
    r_out,
    rl_in,
    rr_in,
    rl_gat,
    rr_gat,
    rl_out,
    rr_out,
    first,
    second,
    e_in,
    e_gat,
    e_out,
    e_small,
    n_w_in,
    n_w_gat,
    n_w_out,
    n_small,
    n_l_in,
    n_r_in,
    n_l_gat,
    n_r_gat,
    n_l_out,
    n_r_out,
    n_first,
    n_second,
    n_e_in,
    n_e_gat,
    n_e_out,
    n_e_small,
    loss_ref,
    norm_ref,
):
    dom = dom_ref[0]
    grads = sum_ref[0:ROW_MISC, :].astype(f32)
    squares = jnp.sum(grads * grads)
    misc = sum_ref[ROW_MISC : ROW_MISC + 8, :].astype(f32)
    row = lax.broadcasted_iota(jnp.int32, (8, HID), 0)
    lane = lax.broadcasted_iota(jnp.int32, (8, HID), 1)
    spot = HSIZE + CLASSES
    loss_ref[0] = jnp.sum(jnp.where((row == 4) & ((lane == spot) | (lane == spot + 8)), misc, 0.0))
    small_part = jnp.where((row < 4) | ((row == 4) & (lane < spot)), misc, 0.0)
    squares = squares + jnp.sum(small_part * small_part)
    norm = jnp.sqrt(jnp.broadcast_to(squares, (1, 1)))
    scale = jnp.minimum(1.0, clip_norm / norm)
    norm_ref[0] = jnp.sum(norm)
    for layer in range(2):
        for side in range(2):
            at = (layer, side)
            begin = (2 * layer + side) * HID
            precondition(
                sum_ref[begin : begin + HID, :],
                w_gat[at],
                l_gat[at],
                r_gat[at],
                rl_gat[at],
                rr_gat[at],
                e_gat[at],
                (n_w_gat.at[at], n_l_gat.at[at], n_r_gat.at[at], n_e_gat.at[at]),
                scale,
                dom * w_gat.shape[2],
            )
    precondition(
        sum_ref[ROW_IN:ROW_OUT, :],
        w_in[...],
        l_in[...],
        r_in[...],
        rl_in[...],
        rr_in[...],
        e_in[...],
        (n_w_in, n_l_in, n_r_in, n_e_in),
        scale,
        dom * w_in.shape[0],
    )
    precondition(
        sum_ref[ROW_OUT:ROW_MISC, 0:CLASSES],
        w_out[...],
        l_out[...],
        r_out[...],
        rl_out[...],
        rr_out[...],
        e_out[...],
        (n_w_out, n_l_out, n_r_out, n_e_out),
        scale,
        dom * w_out.shape[0],
    )
    for place in range(5):
        width = HID if place < 4 else spot
        at = pl.ds(place * HID, width)
        gradient = misc[place : place + 1, 0:width] * scale

        def line(ref):
            return ref[at].reshape(1, width)

        new_value, moment_one, moment_two = adamw_step(line(small), gradient, line(first), line(second))
        n_small[at] = new_value.reshape(width)
        n_first[at] = moment_one.reshape(width)
        n_second[at] = moment_two.reshape(width)
        n_e_small[at] = average(line(e_small), new_value).reshape(width)


def per_device(
    features,
    sources,
    send_index,
    labels,
    label_mask,
    w_in,
    w_gat,
    w_out,
    small_params,
    stat_l_in,
    stat_r_in,
    stat_l_gat,
    stat_r_gat,
    stat_l_out,
    stat_r_out,
    root_l_in,
    root_r_in,
    root_l_gat,
    root_r_gat,
    root_l_out,
    root_r_out,
    adam_first,
    adam_second,
    ema_in,
    ema_gat,
    ema_out,
    ema_small,
):
    all_size = lax.axis_size("dom") * lax.axis_size("section")
    dom_id = lax.axis_index("dom").astype(jnp.int32).reshape(1)
    micro = lax.axis_index("section").astype(jnp.int32).reshape(1)
    size = lax.axis_size("dom")
    src_all = jnp.swapaxes(sources, 1, 2)
    packed, ints, first_rows = pack_inputs(
        micro, features, src_all, labels, label_mask, send_index, w_in, w_gat, w_out
    )
    down = [((i + 1) % size, i) for i in range(size)]
    first_rows = lax.ppermute(first_rows, "dom", down)
    ints = lax.ppermute(ints, "dom", down)
    whole = gather_weights(packed, w_in, w_gat, w_out, label_mask)
    partial = run_model(
        micro, features, src_all, labels, label_mask, send_index, whole, ints, first_rows, small_params
    )
    parts = lax.all_to_all(partial.reshape(all_size, -1, HID), ("section", "dom"), 0, 0)
    mine = jnp.sum(parts.astype(f32), axis=0)
    shared = jnp.broadcast_to(mine.astype(bf16)[None], (all_size,) + mine.shape)
    summed = lax.all_to_all(shared, ("section", "dom"), 0, 0).reshape(ROWS, HID)
    state = (
        w_in,
        w_gat,
        w_out,
        small_params,
        stat_l_in,
        stat_r_in,
        stat_l_gat,
        stat_r_gat,
        stat_l_out,
        stat_r_out,
        root_l_in,
        root_r_in,
        root_l_gat,
        root_r_gat,
        root_l_out,
        root_r_out,
        adam_first,
        adam_second,
        ema_in,
        ema_gat,
        ema_out,
        ema_small,
    )
    like = state[:10] + (adam_first, adam_second, ema_in, ema_gat, ema_out, ema_small)
    results = pl.pallas_call(
        update_kernel,
        out_shape=[jax.ShapeDtypeStruct(v.shape, f32) for v in like] + [jax.ShapeDtypeStruct((1,), f32)] * 2,
        in_specs=[pl.BlockSpec(memory_space=pltpu.SMEM)] + vmem(23),
        out_specs=vmem(16) + [pl.BlockSpec(memory_space=pltpu.SMEM)] * 2,
        compiler_params=pltpu.CompilerParams(vmem_limit_bytes=60 * 1024 * 1024),
        name="update",
    )(dom_id, summed, *state)
    return tuple(results[:16]) + (results[16].reshape(()), results[17].reshape(()))


def solution(mesh):
    placed = (
        P(None, "dom", None),
        P(None, "dom", None),
        P(None, "dom"),
        P(None, "dom"),
        P(None, "dom"),
        P("dom", None),
        P(None, None, "dom", None),
        P("dom", None),
        P(),
        P("dom", None),
        P(),
        P(None, None, "dom", None),
        P(),
        P("dom", None),
        P(),
        P("dom", None),
        P(),
        P(None, None, "dom", None),
        P(),
        P("dom", None),
        P(),
        P(),
        P(),
        P("dom", None),
        P(None, None, "dom", None),
        P("dom", None),
        P(),
    )
    return jax.shard_map(
        per_device,
        mesh=mesh,
        in_specs=placed,
        out_specs=(
            P("dom", None),
            P(None, None, "dom", None),
            P("dom", None),
            P(),
            P("dom", None),
            P(),
            P(None, None, "dom", None),
            P(),
            P("dom", None),
            P(),
            P(),
            P(),
            P("dom", None),
            P(None, None, "dom", None),
            P("dom", None),
            P(),
            P(),
            P(),
        ),
        check_vma=False,
    )
```

time: 181 us -> 123 us (0.68)
  matrix products: 12.9 us -> 0 us
  other arithmetic: 12 us -> 0.1 us
  local copies, waits for them, and re-layouts: 14.2 us -> 2.31 us
  Pallas kernels: 65.2 us -> 54.6 us
  between operations: 10.7 us -> 0.69 us
    dot_general x12 -> x0, matrix products: 12.9 us -> none  [the longest x3 4.88 us: precondition(): jnp.matmul(flipped, gradient, precision=highest)]
    pallas_call x1 -> x3, Pallas kernels: 65.2 us -> 54.6 us  [the longest x1 48.2 us: run_model(): pl.pallas_call(model_kernel, grid_spec=grid_spec, out_shape=jax.ShapeDtyp...]
    reduce_sum x7 -> x0, other arithmetic: 4.26 us -> none  [the longest x1 1.41 us: per_device(): count = jnp.sum(label_mask)]
    slice x14 -> x0, local copies, waits for them, and re-layouts: 3.66 us -> none  [the longest x1 0.84 us: run_model(): flat[1]]
    convert_element_type x6 -> x0, other arithmetic: 3.51 us -> none  [the longest x1 1.18 us: per_device(): lax.all_to_all(shared, ('section', 'dom'), 0, 0).reshape(ROWS, HID)]
    transpose x4 -> x0, local copies, waits for them, and re-layouts: 3.15 us -> none  [the longest x1 1.08 us: run_model(): wgt = jnp.swapaxes(w_gat, -1, -2).reshape(2, 2 * HID, HID)]
    reshape x3 -> x0, local copies, waits for them, and re-layouts: 2.49 us -> none  [the longest x1 1.15 us: run_model(): wg = jnp.swapaxes(w_gat, 1, 2).reshape(2, HID, 2 * HID)]
    concatenate x6 -> x0, other arithmetic: 2.29 us -> none  [the longest x1 0.83 us: per_device(): feat = jnp.concatenate([feat[half:], feat_next], axis=0)]
  transfers between devices with their start and end apart: 3 -> 3, of which waited for: 1 -> 1; matrix products, arithmetic and copies ran while one was open for 10% -> 0% of each run, Pallas kernels for 0% -> 0%
where the time goes in v2:
time: 123 us
  Pallas kernels  54.6 us (44%)
  blocking collectives  38.5 us (31%)
  waiting for transfers between devices  19.2 us (16%)
  starting transfers between devices  7.78 us (6%)
  local copies, waits for them, and re-layouts  2.31 us (2%)
    pallas_call x1, Pallas kernels, run_model(): pl.pallas_call(model_kernel, grid_spec=grid_spec, out_shape=jax.ShapeDtyp...  48.2 us
    all_to_all x1, blocking collectives, per_device(): lax.all_to_all(partial.reshape(all_size, -1, HID), ('section', 'dom'), 0, 0)  22.1 us
    all_to_all x1, waiting for transfers between devices, per_device(): summed = lax.all_to_all(shared, ('section', 'dom'), 0, 0).reshape(ROWS, HID)  19.2 us
    all_gather x1, blocking collectives, gather_weights(): return lax.all_gather(packed, 'dom', axis=0, tiled=False)  16.4 us
    pallas_call x1, Pallas kernels, per_device(): pl.pallas_call(update_kernel, out_shape=[jax.ShapeDtypeStruct(v.shape, f3...  4.6 us
    ppermute x1, starting transfers between devices, per_device(): ints = lax.ppermute(ints, 'dom', down)  4.49 us
    all_to_all x1, starting transfers between devices, per_device(): summed = lax.all_to_all(shared, ('section', 'dom'), 0, 0).reshape(ROWS, HID)  2.62 us
  transfers between devices with their start and end apart: 3, of which 1 were waited for; matrix products, arithmetic and copies ran while one was open for 0% of the time, Pallas kernels for 0%

profile of v2, /device:TPU:0, one launch (start us, length us, event | category | flops | bytes accessed | tf_op | source)
XLA Modules:
  0.0 123.1 jit_solution(11392607545443961520)
XLA Ops:
  0.7 1.8 %pack.1 = (bf16[160,256]{1,0:T(8,128)(2,1)}, s32[16,128]{1,0:T(8,128)}, bf16[32,128]{1,0:T(8,128)(2,1)}) custom-call(s32[1]{0:T(128)} %bitcast.1.micro_ref, bf16[4,2048,128]{2,1,0:T(8,128)(2,1)} %feat_ref.3, s32[4,8,2048]{2,1,0:T(8,128)} %bitcast.11, s32[4,2048]{1,0:T(4,128)} %lab_ref.3, s32[4,2048]{1,0:T(4,128)} %msk_ref.3, s32[4,64]{1,0:T(4,128)} %send_ref.3, ...), custom_call_target="tpu_custom_call" | custom-call | tf_op jit(solution)/shard_map/pack/pallas_call | solution.py:142
  2.4 4.5 %collective-permute-start = (s32[16,128]{1,0:T(8,128)}, s32[16,128]{1,0:T(8,128)S(1)}, u32[]{:S(2)}, u32[]{:S(2)}) collective-permute-start(s32[16,128]{1,0:T(8,128)} %get-tuple-element.40), channel_id=1, source_target_pairs={{1,0},{2,1},{3,2},{4,3},{5,4},{6,5},{7,6},{0,7},{9,8},{10,9},{11,1... | collective-permute-start | bytes 24584 | tf_op jit(solution)/shard_map/ppermute | solution.py:742
  6.9 0.7 collective-permute-start.1
  7.6 16.4 %all-gather = bf16[1280,256]{1,0:T(8,128)(2,1)} all-gather(bf16[160,256]{1,0:T(8,128)(2,1)} %get-tuple-element.39), channel_id=2, replica_groups=mesh['section'=4,'dom'=8] {'dom'}, dimensions={0}, use_global_device_ids=true | all-gather | bytes 737280 | tf_op jit(solution)/shard_map/all_gather | solution.py:158
  24.0 0.0 collective-permute-done.ints_ref
  24.0 0.0 copy-start.1
  24.0 0.0 collective-permute-done.1.next_ref
  24.0 0.0 copy-start.2
  24.0 0.6 copy-done.1
  24.6 0.0 copy-done.2
  24.6 48.2 %model.1 = bf16[1280,256]{1,0:T(8,128)(2,1)} custom-call(s32[1]{0:T(128)} %bitcast.1.micro_ref, bf16[4,2048,128]{2,1,0:T(8,128)(2,1)} %feat_ref.3, s32[4,8,2048]{2,1,0:T(8,128)} %bitcast.12, s32[4,2048]{1,0:T(4,128)} %lab_ref.3, s32[4,2048]{1,0:T(4,128)} %msk_ref.3, s32[4,64]{1,0:T(4,128)} %send_ref.3, bf16[8,160,256]{2,1,0:T(8,128)(2,1)} %bitcast.8, ...), custom_call_target="tpu_custom_call" | custom-call | tf_op jit(solution)/shard_map/model/pallas_call | solution.py:531
  72.8 22.1 %all_to_all.10 = bf16[32,40,256]{2,1,0:T(8,128)(2,1)S(1)} all-to-all(bf16[32,40,256]{2,1,0:T(8,128)(2,1)} %bitcast.9), channel_id=1, replica_groups=mesh['section'=4,'dom'=8] {'section','dom'}, dimensions={0} | all-to-all | bytes 1310720 | tf_op jit(solution)/shard_map/all_to_all | solution.py:747
  94.9 0.1 reduce_sum.12
  95.0 0.9 broadcast_in_dim.2
  95.9 2.6 %all-to-all-start.1 = ((bf16[32,40,256]{2,1,0:T(8,128)(2,1)}), bf16[32,40,256]{2,1,0:T(8,128)(2,1)S(1)}, u32[]{:S(2)}, u32[]{:S(2)}) async-start(bf16[32,40,256]{2,1,0:T(8,128)(2,1)} %broadcast_in_dim.2), calls=%async_computation.1 | async-start | bytes 1310720 | tf_op jit(solution)/shard_map/all_to_all | solution.py:750
  98.5 19.2 %all-to-all-done.1 = bf16[32,40,256]{2,1,0:T(8,128)(2,1)S(1)} async-done(((bf16[32,40,256]{2,1,0:T(8,128)(2,1)}), bf16[32,40,256]{2,1,0:T(8,128)(2,1)S(1)}, u32[]{:S(2)}, u32[]{:S(2)}) %all-to-all-start.1) | async-done | bytes 655392 | tf_op jit(solution)/shard_map/all_to_all | solution.py:750
  117.7 0.0 copy-start
  117.7 0.8 copy-done
  118.5 4.6 %update.1 = (f32[16,256]{1,0:T(8,128)}, f32[2,2,32,256]{3,2,1,0:T(8,128)}, f32[8,40]{1,0:T(8,128)}, f32[1128]{0:T(1024)}, f32[16,128]{1,0:T(8,128)}, /*index=5*/...) custom-call(s32[1]{0:T(128)} %bitcast.dom_ref, ...), custom_call_target="tpu_custom_call" | custom-call | tf_op jit(solution)/shard_map/update/pallas_call | solution.py:776
Async XLA Ops:
  2.4 21.5 %collective-permute-start = (s32[16,128]{1,0:T(8,128)}, s32[16,128]{1,0:T(8,128)S(1)}, u32[]{:S(2)}, u32[]{:S(2)}) collective-permute-start(s32[16,128]{1,0:T(8,128)} %get-tuple-element.40), channel_id=1, source_target_pairs={{1,0},{2,1},{3,2},{4,3},{5,4},{6,5},{7,6},{0,7},{9,8},{10,9},{11,1... | collective-permute-start | bytes 24584 | tf_op jit(solution)/shard_map/ppermute | solution.py:742
  6.9 17.0 %collective-permute-start.1 = (bf16[32,128]{1,0:T(8,128)(2,1)}, bf16[32,128]{1,0:T(8,128)(2,1)S(1)}, u32[]{:S(2)}, u32[]{:S(2)}) collective-permute-start(bf16[32,128]{1,0:T(8,128)(2,1)} %get-tuple-element.41), channel_id=1, source_target_pairs={{1,0},{2,1},{3,2},{4,3},{5,4},{6,5},{7,6},{0,7},{9,8},{10,9},{11,1... | collective-permute-start | bytes 24584 | tf_op jit(solution)/shard_map/ppermute | solution.py:741
  24.0 0.6 copy-start.1
  24.0 0.6 copy-start.2
  95.9 21.8 %all-to-all-start.1 = ((bf16[32,40,256]{2,1,0:T(8,128)(2,1)}), bf16[32,40,256]{2,1,0:T(8,128)(2,1)S(1)}, u32[]{:S(2)}, u32[]{:S(2)}) async-start(bf16[32,40,256]{2,1,0:T(8,128)(2,1)} %broadcast_in_dim.2), calls=%async_computation.1 | async-start | bytes 1310720 | tf_op jit(solution)/shard_map/all_to_all | solution.py:750
  117.7 0.8 copy-start

commit v3 on v2

--- a/solution.py
+++ b/solution.py
@@ -42,6 +42,7 @@
 LANES = 128
 DEG = 8
 SLOTS = DEG + 1
+WAYS = 4
 ROWS = 1280
 GROUPS = 8
 IN_G = FEAT // GROUPS
@@ -49,6 +50,8 @@
 OUT_G = HSIZE // GROUPS
 TAIL_G = IN_G + 4 * GAT_G
 PACK_G = TAIL_G + 2 * OUT_G
+HALO_G = PACK_G + 32
+PIECE = ROWS // 8
 HALF = GRAPH // 2
 ROW_IN = 4 * HID
 ROW_OUT = ROW_IN + FEAT
@@ -82,7 +85,7 @@
 
 
 def pack_kernel(
-    micro_ref,
+    place_ref,
     feat_ref,
     src_ref,
     lab_ref,
@@ -92,21 +95,25 @@
     wgat_ref,
     wout_ref,
     pack_ref,
+    tail_ref,
     ints_ref,
-    first_ref,
-    tail_ref,
 ):
-    micro = micro_ref[0]
-    first_ref[...] = feat_ref[0]
+    micro = place_ref[0]
+    nodes = lab_ref.shape[1]
+    pack_ref[PACK_G : PACK_G + 16, 0:FEAT] = feat_ref[0, 0:16]
+    pack_ref[PACK_G : PACK_G + 16, FEAT : 2 * FEAT] = feat_ref[0, 16:32]
+    shift = LANES - HALF
     ints_ref[...] = jnp.zeros_like(ints_ref)
-    shift = LANES - HALF
-    ints_ref[0:DEG, :] = pltpu.roll(src_ref[0], shift, 1)
-    ints_ref[DEG : DEG + 1, :] = pltpu.roll(row_of(lab_ref, micro, LANES), shift, 1)
-    ints_ref[DEG + 1 : DEG + 2, :] = pltpu.roll(row_of(msk_ref, micro, LANES), shift, 1)
+    far = src_ref[0]
+    far = jnp.where(far >= nodes, far - nodes + GRAPH, far)
+    ints_ref[0:DEG, 0:LANES] = pltpu.roll(far, shift, 1).astype(f32)
+    ints_ref[DEG : DEG + 1, 0:LANES] = pltpu.roll(row_of(lab_ref, micro, LANES), shift, 1).astype(f32)
+    ints_ref[DEG + 1 : DEG + 2, 0:LANES] = pltpu.roll(row_of(msk_ref, micro, LANES), shift, 1).astype(f32)
     send = row_of(send_ref, micro, 2 * HALF)
-    ints_ref[DEG + 2 : DEG + 3, :] = jnp.concatenate([send, send], axis=1)
+    ints_ref[DEG + 2 : DEG + 3, 0:LANES] = jnp.concatenate([send, send], axis=1).astype(f32)
+    pack_ref[PACK_G + 16 : HALO_G, :] = ints_ref[...].astype(bf16)
     if win_ref.shape[0] != IN_G:
-        pack_ref[...] = jnp.zeros_like(pack_ref)
+        pack_ref[0:PACK_G, :] = jnp.zeros((PACK_G, HID), bf16)
         return
     pack_ref[0:IN_G, :] = win_ref[...].astype(bf16)
     for layer in range(2):
@@ -127,7 +134,7 @@
     return [pl.BlockSpec(memory_space=pltpu.VMEM)] * count
 
 
-def pack_inputs(micro, features, src_all, labels, label_mask, send_index, w_in, w_gat, w_out):
+def pack_inputs(place, features, src_all, labels, label_mask, send_index, w_in, w_gat, w_out):
     grid_spec = pltpu.PrefetchScalarGridSpec(
         num_scalar_prefetch=1,
         grid=(1,),
@@ -136,26 +143,29 @@
             pl.BlockSpec((1, DEG, LANES), lambda i, m: (m[0], 0, 0)),
         ]
         + vmem(6),
-        out_specs=vmem(3),
-        scratch_shapes=[pltpu.VMEM((2 * OUT_G, HID), f32)],
+        out_specs=vmem(1)[0],
+        scratch_shapes=[pltpu.VMEM((2 * OUT_G, HID), f32), pltpu.VMEM((16, HID), f32)],
     )
     return pl.pallas_call(
         pack_kernel,
         grid_spec=grid_spec,
-        out_shape=(
-            jax.ShapeDtypeStruct((PACK_G, HID), bf16),
-            jax.ShapeDtypeStruct((16, LANES), jnp.int32),
-            jax.ShapeDtypeStruct((HALF, FEAT), bf16),
-        ),
+        out_shape=jax.ShapeDtypeStruct((HALO_G, HID), bf16),
         compiler_params=pltpu.CompilerParams(vmem_limit_bytes=60 * 1024 * 1024),
         name="pack",
-    )(micro, features, src_all, labels, label_mask, send_index, w_in, w_gat, w_out)
+    )(place, features, src_all, labels, label_mask, send_index, w_in, w_gat, w_out)
+
+
+def crossed(value, axis, mask):
+    return lax.ppermute(value, axis, [(i, i ^ mask) for i in range(lax.axis_size(axis))])
 
 
 def gather_weights(packed, w_in, w_gat, w_out, label_mask):
     size = lax.axis_size("dom")
     if size == GROUPS:
-        return lax.all_gather(packed, "dom", axis=0, tiled=False)
+        near = [packed] + [crossed(packed, "dom", 2 * j) for j in range(1, 4)]
+        return near + [crossed(piece, "dom", 1) for piece in near], lax.axis_index("dom")
+    halo = lax.ppermute(packed[PACK_G:], "dom", [((i + 1) % size, i) for i in range(size)])
+    halo = jnp.broadcast_to(halo[None], (GROUPS,) + halo.shape)
     rows_in, rows_gat, rows_out = (w_in.shape[0], w_gat.shape[2], w_out.shape[0])
     count = jnp.sum(label_mask)
     digits = jnp.stack([lax.div(count, 256), lax.rem(count, 256)]).astype(bf16)
@@ -176,7 +186,8 @@
     part_out = whole[:, cut : cut + rows_out].reshape(GROUPS, OUT_G, HID)
     counts = whole[:, cut + rows_out].reshape(GROUPS, size // GROUPS, HID)
     counts = jnp.pad(counts, ((0, 0), (0, OUT_G - size // GROUPS), (0, 0)))
-    return jnp.concatenate([part_in, part_gat, part_out, counts], axis=1)
+    whole = jnp.concatenate([part_in, part_gat, part_out, counts, halo], axis=1)
+    return [whole[g] for g in (0, 2, 4, 6, 1, 3, 5, 7)], 0
 
 
 def column_of(row):
@@ -184,17 +195,23 @@
 
 
 def model_kernel(
-    micro_ref,
+    place_ref,
     feat_ref,
     src_ref,
     lab_ref,
     msk_ref,
     send_ref,
-    whole_ref,
-    ints_ref,
-    next_ref,
+    piece_0,
+    piece_1,
+    piece_2,
+    piece_3,
+    piece_4,
+    piece_5,
+    piece_6,
+    piece_7,
     small_ref,
-    out_ref,
+    keep_ref,
+    send_out_ref,
     e_ref,
     t_ref,
     al_ref,
@@ -221,28 +238,56 @@
     wo_ref,
     wof_ref,
     am_ref,
+    out_ref,
+    eye_ref,
+    halo_ref,
 ):
     nodes = feat_ref.shape[1]
     blocks = nodes // LANES
     chunk = 4 * LANES
     chunks = nodes // chunk
     mixed = DEG * LANES
-    micro = micro_ref[0]
+    micro = place_ref[0]
+    after = jnp.bitwise_and(place_ref[2] + 1, GROUPS - 1)
     final = nodes - LANES
 
+    digits = jnp.zeros((OUT_G, HID), f32)
+    pieces = (piece_0, piece_1, piece_2, piece_3, piece_4, piece_5, piece_6, piece_7)
+    for j, piece in enumerate(pieces):
+        group = jnp.bitwise_xor(place_ref[2], 2 * (j & 3) + (j >> 2))
+
+        def rows_of(width):
+            return pl.ds(pl.multiple_of(group * width, width), width)
+
+        wi_ref[rows_of(IN_G), :] = piece[0:IN_G, :]
+        for layer in range(2):
+            for side in range(2):
+                start = IN_G + (2 * layer + side) * GAT_G
+                wg_ref[layer, rows_of(GAT_G), side * HID : (side + 1) * HID] = piece[start : start + GAT_G, :]
+        tail = piece[TAIL_G:PACK_G, :].astype(f32)
+        wof_ref[rows_of(OUT_G), :] = tail[0:OUT_G]
+        digits = digits + tail[OUT_G : 2 * OUT_G]
+        halo_ref[group] = piece[PACK_G:HALO_G, :]
+
     node_ref[0 : nodes - HALF, :] = feat_ref[0, HALF:nodes, :]
-    node_ref[nodes - HALF : nodes, :] = next_ref[...]
+    node_ref[nodes - HALF : nodes - 16, :] = halo_ref[after, 0:16, 0:FEAT]
+    node_ref[nodes - 16 : nodes, :] = halo_ref[after, 0:16, FEAT : 2 * FEAT]
+    ints = halo_ref[after, 16:32, 0:LANES].astype(f32).astype(jnp.int32)
     lane_row = lax.broadcasted_iota(jnp.int32, (1, LANES), 1)
     kept = lane_row < LANES - HALF
     edge_ref[...] = pltpu.roll(src_ref[0], nodes - HALF, 1)
-    edge_ref[:, final:nodes] = jnp.where(kept, edge_ref[:, final:nodes], ints_ref[0:DEG, :])
+    edge_ref[:, final:nodes] = jnp.where(
+        kept,
+        edge_ref[:, final:nodes],
+        jnp.where(ints[0:DEG] >= GRAPH, ints[0:DEG] + (nodes - GRAPH), ints[0:DEG]),
+    )
     for place, ref in enumerate((lab_ref, msk_ref)):
         mark_ref[place : place + 1, :] = pltpu.roll(row_of(ref, micro, nodes), nodes - HALF, 1)
-        came = ints_ref[DEG + place : DEG + place + 1, :]
+        came = ints[DEG + place : DEG + place + 1]
         mark_ref[place : place + 1, final:nodes] = jnp.where(kept, mark_ref[place : place + 1, final:nodes], came)
     send = row_of(send_ref, micro, 2 * HALF)
     send = jnp.concatenate([send, send], axis=1)
-    arrived = pltpu.roll(ints_ref[DEG + 2 : DEG + 3, :], HALF, 1)
+    arrived = pltpu.roll(ints[DEG + 2 : DEG + 3], HALF, 1)
     table = jnp.where(
         lane_row < HALF, pltpu.roll(send, HALF, 1) - (nodes - HALF), arrived + HALF
     )
@@ -264,18 +309,6 @@
         lax.broadcasted_iota(jnp.int32, (DEG, LANES), 1), GRAPH
     )
 
-    digits = jnp.zeros((OUT_G, HID), f32)
-    for g in range(GROUPS):
-        wi_ref[g * IN_G : (g + 1) * IN_G, :] = whole_ref[g, 0:IN_G, :]
-        for layer in range(2):
-            for side in range(2):
-                start = IN_G + (2 * layer + side) * GAT_G
-                wg_ref[layer, g * GAT_G : (g + 1) * GAT_G, side * HID : (side + 1) * HID] = whole_ref[
-                    g, start : start + GAT_G, :
-                ]
-        tail = whole_ref[g, TAIL_G:PACK_G, :].astype(f32)
-        wof_ref[g * OUT_G : (g + 1) * OUT_G, :] = tail[0:OUT_G]
-        digits = digits + tail[OUT_G : 2 * OUT_G]
     for layer in range(2):
         for side in range(2):
             wgt_ref[layer, side * HID : (side + 1) * HID, :] = wg_ref[
@@ -320,7 +353,7 @@
     def lanes_of(i, width):
         return pl.ds(pl.multiple_of(i * width, width), width)
 
-    @pl.loop(0, chunks)
+    @pl.loop(0, chunks, unroll=4)
     def _(c):
         at = lanes_of(c, chunk)
         pre = dot_nt(wi_t, node_ref[at, :]) + bias_in
@@ -328,66 +361,85 @@
         h_ref[0, :, at] = jnp.where(pre > 0, pre, grown - 1.0).astype(bf16)
         slope_ref[0, :, at] = jnp.where(pre > 0, 1.0, grown)
 
+    wide_spots = lax.broadcasted_iota(jnp.int32, (LANES, LANES), 0).astype(f32).astype(bf16)
+    wide_spots = wide_spots.reshape(8, 16, LANES)
+    for k in range(DEG):
+        eye_ref[:, tile_of(k)] = eye
+
+    @pl.loop(0, blocks)
+    def _(i):
+        at = lanes_of(i, LANES)
+        for k in range(DEG):
+            spot = jnp.broadcast_to(edge_ref[k : k + 1, at].astype(f32), (16, LANES)).astype(bf16)
+            hit = wide_spots == spot[None]
+            hit = jnp.where(hit, jnp.ones((8, 16, LANES), bf16), jnp.zeros((8, 16, LANES), bf16))
+            e_ref[i, :, tile_of(k)] = hit.reshape(LANES, LANES)
+
     for layer in range(2):
 
-        @pl.loop(0, chunks)
+        @pl.loop(0, chunks, unroll=4)
         def _(c):
             at = lanes_of(c, chunk)
             xlr_ref[layer, :, at] = dot_nn(wgt_ref[layer], h_ref[layer, :, at]).astype(bf16)
 
-        @pl.loop(0, blocks, unroll=4)
-        def _(i):
-            at = lanes_of(i, LANES)
-            if layer == 0:
-                for k in range(DEG):
-                    hit = row_id == edge_ref[k : k + 1, at]
-                    e_ref[i, 0:LANES, tile_of(k)] = jnp.where(hit, 1.0, 0.0).astype(bf16)
-                    e_ref[i, LANES : 2 * LANES, tile_of(k)] = eye
-            left = xlr_ref[layer, 0:HID, at]
-            right = xlr_ref[layer, HID : 2 * HID, at]
-            both = jnp.concatenate([left, right], axis=1)
-            t_ref[layer, i, :, 0:mixed] = dot_nn(both, e_ref[i]).astype(bf16)
-            t_ref[layer, i, :, tile_of(DEG)] = left + right
-            t = t_ref[layer, i]
-            z = jnp.maximum(t, t * leak_slope)
-            scores = dot_nn(am_ref[layer], z)
-            grown = jnp.exp(scores[0:8] + scores[8:16])
-            total = grown[:, tile_of(0)]
-            for k in range(1, SLOTS):
-                total = total + grown[:, tile_of(k)]
-            inverse = 1.0 / total
-            grids = [zero] * HEADS
-            for k in range(SLOTS):
-                alpha = grown[:, tile_of(k)] * inverse
-                al_ref[layer, i, :, tile_of(k)] = alpha
-                if k == DEG:
-                    spot = own_spot
-                else:
-                    spot = jnp.bitwise_and(edge_ref[k : k + 1, at], GRAPH - 1).astype(f32)
-                    spot = jnp.broadcast_to(spot, (16, LANES)).astype(bf16)
-                hit = spots == spot[None]
+        @pl.loop(0, blocks // WAYS)
+        def _(step):
+            ids = [step * WAYS + u for u in range(WAYS)]
+            ats = [lanes_of(i, LANES) for i in ids]
+            ways = range(WAYS)
+            left = [xlr_ref[layer, 0:HID, ats[u]] for u in ways]
+            grown = []
+            for u in ways:
+                right = xlr_ref[layer, HID : 2 * HID, ats[u]]
+                mixed_rows = dot_nn(left[u], e_ref[ids[u]]).astype(bf16)
+                mixed_rows = mixed_rows + jnp.concatenate([right] * DEG, axis=1)
+                own = left[u] + right
+                t_ref[layer, ids[u], :, 0:mixed] = mixed_rows
+                t_ref[layer, ids[u], :, tile_of(DEG)] = own
+                t = jnp.concatenate([mixed_rows, own], axis=1)
+                z = jnp.maximum(t, t * leak_slope)
+                scores = dot_nn(am_ref[layer], z)
+                grown.append(jnp.exp(scores[0:8] + scores[8:16]))
+            grids_all = []
+            for u in ways:
+                total = grown[u][:, tile_of(0)]
+                for k in range(1, SLOTS):
+                    total = total + grown[u][:, tile_of(k)]
+                inverse = 1.0 / total
+                grids = [zero] * HEADS
+                for k in range(SLOTS):
+                    alpha = grown[u][:, tile_of(k)] * inverse
+                    al_ref[layer, ids[u], :, tile_of(k)] = alpha
+                    if k == DEG:
+                        spot = own_spot
+                    else:
+                        spot = jnp.bitwise_and(edge_ref[k : k + 1, ats[u]], GRAPH - 1).astype(f32)
+                        spot = jnp.broadcast_to(spot, (16, LANES)).astype(bf16)
+                    hit = spots == spot[None]
+                    for h in range(HEADS):
+                        part = jnp.broadcast_to(alpha[h : h + 1], (16, LANES)).astype(bf16)
+                        grids[h] = grids[h] + jnp.where(hit, part[None], zero)
+                grids_all.append(grids)
+            for u in ways:
+                pooled = None
                 for h in range(HEADS):
-                    part = jnp.broadcast_to(alpha[h : h + 1], (16, LANES)).astype(bf16)
-                    grids[h] = grids[h] + jnp.where(hit, part[None], zero)
-            pooled = None
-            for h in range(HEADS):
-                upper = jnp.where(first_half, grids[h], zero).reshape(GRAPH, LANES)
-                lower = jnp.where(first_half, zero, grids[h]).reshape(GRAPH, LANES)
-                grid = jnp.concatenate([upper, lower], axis=0)
-                att_ref[layer, i, h] = grid
-                total = dot_nn(left[head_of(h)], grid)
-                if layer == 0:
-                    pre = total + bias_one[head_of(h)]
-                    grown_one = jnp.exp(jnp.minimum(pre, 0.0))
-                    h_ref[1, head_of(h), at] = jnp.where(pre > 0, pre, grown_one - 1.0).astype(bf16)
-                    slope_ref[1, head_of(h), at] = jnp.where(pre > 0, 1.0, grown_one)
-                else:
-                    rounded = total.astype(bf16).astype(f32)
-                    pooled = rounded if pooled is None else pooled + rounded
-            if layer == 1:
-                pool_ref[:, at] = (pooled * (1.0 / HEADS) + bias_two).astype(bf16)
-
-    @pl.loop(0, chunks)
+                    upper = jnp.where(first_half, grids_all[u][h], zero).reshape(GRAPH, LANES)
+                    lower = jnp.where(first_half, zero, grids_all[u][h]).reshape(GRAPH, LANES)
+                    grid = jnp.concatenate([upper, lower], axis=0)
+                    att_ref[layer, ids[u], h] = grid
+                    total = dot_nn(left[u][head_of(h)], grid)
+                    if layer == 0:
+                        pre = total + bias_one[head_of(h)]
+                        grown_one = jnp.exp(jnp.minimum(pre, 0.0))
+                        h_ref[1, head_of(h), ats[u]] = jnp.where(pre > 0, pre, grown_one - 1.0).astype(bf16)
+                        slope_ref[1, head_of(h), ats[u]] = jnp.where(pre > 0, 1.0, grown_one)
+                    else:
+                        rounded = total.astype(bf16).astype(f32)
+                        pooled = rounded if pooled is None else pooled + rounded
+                if layer == 1:
+                    pool_ref[:, ats[u]] = (pooled * (1.0 / HEADS) + bias_two).astype(bf16)
+
+    @pl.loop(0, chunks, unroll=4)
     def _(c):
         at = lanes_of(c, chunk)
         logits = dot_nn(wo_t, pool_ref[:, at]) + bias_out
@@ -407,44 +459,54 @@
 
     for layer in (1, 0):
 
-        @pl.loop(0, blocks, unroll=4)
-        def _(i):
-            at = lanes_of(i, LANES)
-            d_out = do_ref[:, at]
-            for h in range(HEADS):
-                d_head = d_out[head_of(h)].reshape(4, 16, LANES)
+        @pl.loop(0, blocks // WAYS)
+        def _(step):
+            ids = [step * WAYS + u for u in range(WAYS)]
+            ats = [lanes_of(i, LANES) for i in ids]
+            ways = range(WAYS)
+            d_out = [do_ref[:, ats[u]] for u in ways]
+            d_alpha = []
+            for u in ways:
+                for h in range(HEADS):
+                    d_head = d_out[u][head_of(h)].reshape(4, 16, LANES)
+                    for k in range(SLOTS):
+                        t = t_ref[layer, ids[u], head_of(h), tile_of(k)].reshape(4, 16, LANES)
+                        product = t * d_head
+                        sum_ref[u, h * 16 : (h + 1) * 16, tile_of(k)] = (product[0] + product[1]) + (
+                            product[2] + product[3]
+                        )
+                d_alpha.append(dot_nn(fold, sum_ref[u])[0:8])
+            for u in ways:
+                alpha = al_ref[layer, ids[u]]
+                weighted = alpha * d_alpha[u]
+                total = weighted[:, tile_of(0)]
+                for k in range(1, SLOTS):
+                    total = total + weighted[:, tile_of(k)]
                 for k in range(SLOTS):
-                    product = t_ref[layer, i, head_of(h), tile_of(k)].reshape(4, 16, LANES) * d_head
-                    sum_ref[h * 16 : (h + 1) * 16, tile_of(k)] = (product[0] + product[1]) + (product[2] + product[3])
-            d_alpha = dot_nn(fold, sum_ref[...])[0:8]
-            alpha = al_ref[layer, i]
-            weighted = alpha * d_alpha
-            total = weighted[:, tile_of(0)]
-            for k in range(1, SLOTS):
-                total = total + weighted[:, tile_of(k)]
-            for k in range(SLOTS):
-                d_score = weighted[:, tile_of(k)] - alpha[:, tile_of(k)] * total
+                    d_score = weighted[:, tile_of(k)] - alpha[:, tile_of(k)] * total
+                    for h in range(HEADS):
+                        one = jnp.broadcast_to(d_score[h : h + 1], (16, LANES))
+                        two = (one * leak_slope).astype(bf16)[None]
+                        one = one.astype(bf16)[None]
+                        t = t_ref[layer, ids[u], head_of(h), tile_of(k)].reshape(4, 16, LANES)
+                        w_ref[u, head_of(h), tile_of(k)] = jnp.where(t > 0, one, two).reshape(HSIZE, LANES)
+            for u in ways:
+                together = jnp.concatenate([e_ref[ids[u]], eye_ref[...]], axis=0)
+                spread = dot_nt(w_ref[u, :, 0:mixed], together)
+                own = w_ref[u, :, tile_of(DEG)].astype(f32)
+                left_w = spread[:, 0:LANES] + own
+                right_w = spread[:, LANES : 2 * LANES] + own
+                left = xlr_ref[layer, 0:HID, ats[u]].astype(f32)
+                right = xlr_ref[layer, HID : 2 * HID, ats[u]].astype(f32)
+                da_ref[layer] += left * left_w + right * right_w
+                wide = a_ref[layer]
                 for h in range(HEADS):
-                    one = jnp.broadcast_to(d_score[h : h + 1], (16, LANES))
-                    two = (one * leak_slope).astype(bf16)[None]
-                    one = one.astype(bf16)[None]
-                    t = t_ref[layer, i, head_of(h), tile_of(k)].reshape(4, 16, LANES)
-                    w_ref[head_of(h), tile_of(k)] = jnp.where(t > 0, one, two).reshape(HSIZE, LANES)
-            spread = dot_nt(w_ref[:, 0:mixed], e_ref[i])
-            own = w_ref[:, tile_of(DEG)].astype(f32)
-            left_w = spread[:, 0:LANES] + own
-            right_w = spread[:, LANES : 2 * LANES] + own
-            left = xlr_ref[layer, 0:HID, at].astype(f32)
-            right = xlr_ref[layer, HID : 2 * HID, at].astype(f32)
-            da_ref[layer] += left * left_w + right * right_w
-            wide = a_ref[layer]
-            for h in range(HEADS):
-                passed = dot_nt(d_out[head_of(h)], att_ref[layer, i, h])
-                d_left = wide[head_of(h)] * left_w[head_of(h)] + passed
-                dx_ref[layer, head_of(h), at] = d_left.astype(bf16)
-            dx_ref[layer, HID : 2 * HID, at] = (wide * right_w).astype(bf16)
-
-        @pl.loop(0, chunks)
+                    passed = dot_nt(d_out[u][head_of(h)], att_ref[layer, ids[u], h])
+                    d_left = wide[head_of(h)] * left_w[head_of(h)] + passed
+                    dx_ref[layer, head_of(h), ats[u]] = d_left.astype(bf16)
+                dx_ref[layer, HID : 2 * HID, ats[u]] = (wide * right_w).astype(bf16)
+
+        @pl.loop(0, chunks, unroll=4)
         def _(c):
             at = lanes_of(c, chunk)
             d_in = dot_nn(wg_ref[layer], dx_ref[layer, :, at]).astype(bf16).astype(f32)
@@ -484,13 +546,17 @@
     columns = columns + jnp.where(lane_wide == 4, last, 0.0)
     out_ref[ROW_MISC : ROW_MISC + 16, :] = columns.T[0:16].astype(bf16)
     out_ref[ROW_MISC + 16 :, :] = jnp.zeros((ROWS - ROW_MISC - 16, HID), bf16)
-
-
-def run_model(micro, features, src_all, labels, label_mask, send_index, whole, ints, first, small_params):
+    core = jnp.bitwise_and(place_ref[1], 1)
+    width = ROWS // 2
+    keep_ref[...] = out_ref[pl.ds(pl.multiple_of(core * width, width), width), :]
+    send_out_ref[...] = out_ref[pl.ds(pl.multiple_of((1 - core) * width, width), width), :]
+
+
+def run_model(place, features, src_all, labels, label_mask, send_index, pieces, small_params):
     nodes = features.shape[1]
     blocks = nodes // LANES
     scratch = [
-        pltpu.VMEM((blocks, 2 * LANES, DEG * LANES), bf16),
+        pltpu.VMEM((blocks, LANES, DEG * LANES), bf16),
         pltpu.VMEM((2, blocks, HID, SLOTS * LANES), bf16),
         pltpu.VMEM((2, blocks, 8, SLOTS * LANES), f32),
         pltpu.VMEM((2, blocks, HEADS, LANES, LANES), bf16),
@@ -501,8 +567,8 @@
         pltpu.VMEM((HID, nodes), bf16),
         pltpu.VMEM((HSIZE, nodes), bf16),
         pltpu.VMEM((CLASSES, nodes), bf16),
-        pltpu.VMEM((HID, SLOTS * LANES), bf16),
-        pltpu.VMEM((HEADS * 16, SLOTS * LANES), bf16),
+        pltpu.VMEM((WAYS, HID, SLOTS * LANES), bf16),
+        pltpu.VMEM((WAYS, HEADS * 16, SLOTS * LANES), bf16),
         pltpu.VMEM((2, HID, LANES), f32),
         pltpu.VMEM((2, HID, LANES), f32),
         pltpu.VMEM((HID, LANES), f32),
@@ -516,6 +582,9 @@
         pltpu.VMEM((HSIZE, CLASSES), bf16),
         pltpu.VMEM((HSIZE, HID), f32),
         pltpu.VMEM((2, 16, HID), bf16),
+        pltpu.VMEM((ROWS, HID), bf16),
+        pltpu.VMEM((LANES, DEG * LANES), bf16),
+        pltpu.VMEM((GROUPS, HALO_G - PACK_G, HID), bf16),
     ]
     grid_spec = pltpu.PrefetchScalarGridSpec(
         num_scalar_prefetch=1,
@@ -524,17 +593,84 @@
             pl.BlockSpec((1, nodes, FEAT), lambda i, m: (m[0], 0, 0)),
             pl.BlockSpec((1, DEG, nodes), lambda i, m: (m[0], 0, 0)),
         ]
-        + vmem(7),
-        out_specs=vmem(1)[0],
+        + vmem(12),
+        out_specs=vmem(2),
         scratch_shapes=scratch,
     )
     return pl.pallas_call(
         model_kernel,
         grid_spec=grid_spec,
-        out_shape=jax.ShapeDtypeStruct((ROWS, HID), bf16),
-        compiler_params=pltpu.CompilerParams(vmem_limit_bytes=60 * 1024 * 1024),
+        out_shape=[jax.ShapeDtypeStruct((ROWS // 2, HID), bf16)] * 2,
+        compiler_params=pltpu.CompilerParams(vmem_limit_bytes=54 * 1024 * 1024),
         name="model",
-    )(micro, features, src_all, labels, label_mask, send_index, whole, ints, first, small_params)
+    )(place, features, src_all, labels, label_mask, send_index, *pieces, small_params)
+
+
+def settled(total, is_last):
+    base = ROW_MISC % PIECE
+    block = total[base : base + 8]
+    row = lax.broadcasted_iota(jnp.int32, (8, HID), 0)
+    lane = lax.broadcasted_iota(jnp.int32, (8, HID), 1)
+    spot = HSIZE + CLASSES
+    joined = block + pltpu.roll(block, HID - 8, 1)
+    high = joined.astype(bf16).astype(f32)
+    low = pltpu.roll(joined - high, 8, 1)
+    here = (row == 4) & (lane >= spot) & (lane < spot + 16) & (is_last == 1)
+    block = jnp.where(here, jnp.where(lane < spot + 8, high, low), block)
+    return jnp.concatenate([total[:base], block, total[base + 8 :]], axis=0).astype(bf16)
+
+
+def last_piece(core, section):
+    return jnp.where((core == 1) & (section == 3), 1, 0)
+
+
+def split_kernel(place_ref, keep_ref, got_ref, *out_refs):
+    section = place_ref[0]
+    core = jnp.bitwise_and(place_ref[1], 1)
+    for j, out_ref in enumerate(out_refs):
+        part = jnp.bitwise_xor(section, j)
+        at = pl.ds(pl.multiple_of(part * PIECE, PIECE), PIECE)
+        total = keep_ref[at, :].astype(f32) + got_ref[at, :].astype(f32)
+        out_ref[...] = settled(total, last_piece(core, part))
+
+
+def join_kernel(place_ref, own_ref, one_ref, two_ref, three_ref, out_ref):
+    pair = own_ref[...].astype(f32) + one_ref[...].astype(f32)
+    other = two_ref[...].astype(f32) + three_ref[...].astype(f32)
+    core = jnp.bitwise_and(place_ref[1], 1)
+    out_ref[...] = settled(pair + other, last_piece(core, place_ref[0]))
+
+
+def small_call(kernel, name, place, count, operands):
+    shape = jax.ShapeDtypeStruct((PIECE, HID), bf16)
+    return pl.pallas_call(
+        kernel,
+        out_shape=[shape] * count if count > 1 else shape,
+        in_specs=[pl.BlockSpec(memory_space=pltpu.SMEM)] + vmem(len(operands)),
+        out_specs=vmem(count) if count > 1 else vmem(1)[0],
+        compiler_params=pltpu.CompilerParams(vmem_limit_bytes=8 * 1024 * 1024),
+        name=name,
+    )(place, *operands)
+
+
+def sum_gradients(place, keep, send):
+    if lax.axis_size("dom") == 8 and lax.axis_size("section") == 4:
+        got = crossed(send, "dom", 1)
+        parts = small_call(split_kernel, "split", place, 4, (keep, got))
+        came = [crossed(parts[j], "section", j) for j in range(1, 4)]
+        mine = small_call(join_kernel, "join", place, 1, (parts[0], *came))
+        came = [crossed(mine, "dom", 2 * j) for j in range(1, 4)]
+        mine = small_call(join_kernel, "join", place, 1, (mine, *came))
+        near = [mine] + [crossed(mine, "section", j) for j in range(1, 4)]
+        return near + [crossed(piece, "dom", 1) for piece in near], place
+    all_size = lax.axis_size("dom") * lax.axis_size("section")
+    swap = jnp.bitwise_and(place[1], 1) == 1
+    partial = jnp.concatenate([jnp.where(swap, send, keep), jnp.where(swap, keep, send)], axis=0)
+    parts = lax.all_to_all(partial.reshape(all_size, -1, HID), ("section", "dom"), 0, 0)
+    mine = jnp.sum(parts.astype(f32), axis=0)
+    shared = jnp.broadcast_to(mine.astype(bf16)[None], (all_size,) + mine.shape)
+    summed = lax.all_to_all(shared, ("section", "dom"), 0, 0).reshape(8, PIECE, HID)
+    return [summed[j] for j in range(8)], place * jnp.array([0, 2, 0], jnp.int32)
 
 
 def adamw_step(parameter, gradient, moment_one, moment_two):
@@ -590,7 +726,15 @@
 
 def update_kernel(
     dom_ref,
-    sum_ref,
+    place_ref,
+    piece_0,
+    piece_1,
+    piece_2,
+    piece_3,
+    piece_4,
+    piece_5,
+    piece_6,
+    piece_7,
     w_in,
     w_gat,
     w_out,
@@ -631,8 +775,14 @@
     n_e_small,
     loss_ref,
     norm_ref,
+    sum_ref,
 ):
     dom = dom_ref[0]
+    core = jnp.bitwise_and(place_ref[1], 1)
+    pieces = (piece_0, piece_1, piece_2, piece_3, piece_4, piece_5, piece_6, piece_7)
+    for j, piece in enumerate(pieces):
+        spot = jnp.bitwise_xor(core, j >> 2) * 4 + jnp.bitwise_xor(place_ref[0], j & 3)
+        sum_ref[pl.ds(pl.multiple_of(spot * PIECE, PIECE), PIECE), :] = piece[...]
     grads = sum_ref[0:ROW_MISC, :].astype(f32)
     squares = jnp.sum(grads * grads)
     misc = sum_ref[ROW_MISC : ROW_MISC + 8, :].astype(f32)
@@ -729,25 +879,17 @@
     ema_out,
     ema_small,
 ):
-    all_size = lax.axis_size("dom") * lax.axis_size("section")
     dom_id = lax.axis_index("dom").astype(jnp.int32).reshape(1)
-    micro = lax.axis_index("section").astype(jnp.int32).reshape(1)
-    size = lax.axis_size("dom")
+    section_id = lax.axis_index("section")
+    place = jnp.stack([section_id, lax.axis_index("dom"), lax.axis_index("dom")]).astype(jnp.int32)
     src_all = jnp.swapaxes(sources, 1, 2)
-    packed, ints, first_rows = pack_inputs(
-        micro, features, src_all, labels, label_mask, send_index, w_in, w_gat, w_out
-    )
-    down = [((i + 1) % size, i) for i in range(size)]
-    first_rows = lax.ppermute(first_rows, "dom", down)
-    ints = lax.ppermute(ints, "dom", down)
-    whole = gather_weights(packed, w_in, w_gat, w_out, label_mask)
-    partial = run_model(
-        micro, features, src_all, labels, label_mask, send_index, whole, ints, first_rows, small_params
-    )
-    parts = lax.all_to_all(partial.reshape(all_size, -1, HID), ("section", "dom"), 0, 0)
-    mine = jnp.sum(parts.astype(f32), axis=0)
-    shared = jnp.broadcast_to(mine.astype(bf16)[None], (all_size,) + mine.shape)
-    summed = lax.all_to_all(shared, ("section", "dom"), 0, 0).reshape(ROWS, HID)
+    packed = pack_inputs(place, features, src_all, labels, label_mask, send_index, w_in, w_gat, w_out)
+    pieces, spot = gather_weights(packed, w_in, w_gat, w_out, label_mask)
+    place = jnp.stack([section_id, lax.axis_index("dom"), spot]).astype(jnp.int32)
+    keep, send = run_model(
+        place, features, src_all, labels, label_mask, send_index, pieces, small_params
+    )
+    pieces, spot = sum_gradients(place, keep, send)
     state = (
         w_in,
         w_gat,
@@ -776,11 +918,12 @@
     results = pl.pallas_call(
         update_kernel,
         out_shape=[jax.ShapeDtypeStruct(v.shape, f32) for v in like] + [jax.ShapeDtypeStruct((1,), f32)] * 2,
-        in_specs=[pl.BlockSpec(memory_space=pltpu.SMEM)] + vmem(23),
+        in_specs=[pl.BlockSpec(memory_space=pltpu.SMEM)] * 2 + vmem(30),
         out_specs=vmem(16) + [pl.BlockSpec(memory_space=pltpu.SMEM)] * 2,
-        compiler_params=pltpu.CompilerParams(vmem_limit_bytes=60 * 1024 * 1024),
+        scratch_shapes=[pltpu.VMEM((ROWS, HID), bf16)],
+        compiler_params=pltpu.CompilerParams(vmem_limit_bytes=16 * 1024 * 1024),
         name="update",
-    )(dom_id, summed, *state)
+    )(dom_id, spot, *pieces, *state)
     return tuple(results[:16]) + (results[16].reshape(()), results[17].reshape(()))
 
 

time: 123 us -> 92.6 us (0.75)
  blocking collectives: 38.5 us -> 0 us
  starting transfers between devices: 7.78 us -> 18.1 us
  Pallas kernels: 54.6 us -> 46.3 us
  waiting for transfers between devices: 19.2 us -> 24.1 us
    ppermute x2 -> x21, waiting for transfers between devices: 0.01 us -> 24.1 us  [crossed(): lax.ppermute(value, axis, [(i, i ^ mask) for i in range(lax.axis_size(axi...]
    all_to_all x1 -> x0, blocking collectives: 22.1 us -> none  [per_device(): lax.all_to_all(partial.reshape(all_size, -1, HID), ('section', 'dom'), 0, 0)]
    all_to_all x1 -> x0, waiting for transfers between devices: 19.2 us -> none  [per_device(): summed = lax.all_to_all(shared, ('section', 'dom'), 0, 0).reshape(ROWS, HID)]
    all_gather x1 -> x0, blocking collectives: 16.4 us -> none  [gather_weights(): return lax.all_gather(packed, 'dom', axis=0, tiled=False)]
    ppermute x2 -> x21, starting transfers between devices: 5.16 us -> 18.1 us  [crossed(): lax.ppermute(value, axis, [(i, i ^ mask) for i in range(lax.axis_size(axi...]
    pallas_call x2 -> x5, Pallas kernels: 50 us -> 43.1 us  [the longest x1 38.4 us: run_model(): pl.pallas_call(model_kernel, grid_spec=grid_spec, out_shape=[jax.ShapeDty...]
    all_to_all x1 -> x0, starting transfers between devices: 2.62 us -> none  [per_device(): summed = lax.all_to_all(shared, ('section', 'dom'), 0, 0).reshape(ROWS, HID)]
    pallas_call x1, Pallas kernels: 4.6 us -> 3.17 us  [per_device(): pl.pallas_call(update_kernel, out_shape=[jax.ShapeDtypeStruct(v.shape, f3...]
  transfers between devices with their start and end apart: 3 -> 21, of which waited for: 1 -> 16; matrix products, arithmetic and copies ran while one was open for 0% -> 0% of each run, Pallas kernels for 0% -> 0%
where the time goes in v3:
time: 92.6 us; the launch traced here: 92.4 us
  Pallas kernels  46.3 us (50%)
  waiting for transfers between devices  24.1 us (26%)
  starting transfers between devices  18.1 us (20%)
  local copies, waits for them, and re-layouts  2.22 us (2%)
  between operations  1.17 us (1%)
    pallas_call x1, Pallas kernels, run_model(): pl.pallas_call(model_kernel, grid_spec=grid_spec, out_shape=[jax.ShapeDty...  38.4 us
    ppermute x21, waiting for transfers between devices, crossed(): lax.ppermute(value, axis, [(i, i ^ mask) for i in range(lax.axis_size(axi...  24.1 us
    ppermute x21, starting transfers between devices, crossed(): lax.ppermute(value, axis, [(i, i ^ mask) for i in range(lax.axis_size(axi...  18.1 us
    pallas_call x1, Pallas kernels, per_device(): pl.pallas_call(update_kernel, out_shape=[jax.ShapeDtypeStruct(v.shape, f3...  3.17 us
    pallas_call x1, Pallas kernels, pack_inputs(): pl.pallas_call(pack_kernel, grid_spec=grid_spec, out_shape=jax.ShapeDtype...  2.57 us
    unnamed x62, local copies, waits for them, and re-layouts  2.22 us
    pallas_call x3, Pallas kernels, small_call(): pl.pallas_call(kernel, out_shape=[shape] * count if count > 1 else shape,...  2.13 us
  transfers between devices with their start and end apart: 21, of which 16 were waited for; matrix products, arithmetic and copies ran while one was open for 0% of the time, Pallas kernels for 0%

profile of v3, /device:TPU:0, one launch (start us, length us, event | category | flops | bytes accessed | tf_op | source)
XLA Modules:
  0.0 92.4 jit_solution(1073473029742740454)
XLA Ops:
  0.7 0.6 pad_add_fusion.place_ref
  1.3 0.0 copy-start.20
  1.3 0.0 copy-start.21
  1.3 0.0 copy-start.22
  1.3 0.0 copy-start.23
  1.3 2.6 %pack.1.piece_0 = bf16[192,256]{1,0:T(8,128)(2,1)} custom-call(s32[3]{0:T(128)} %pad_add_fusion.place_ref, bf16[4,2048,128]{2,1,0:T(8,128)(2,1)} %feat_ref.3, s32[4,8,2048]{2,1,0:T(8,128)} %bitcast.5, s32[4,2048]{1,0:T(4,128)} %lab_ref.3, s32[4,2048]{1,0:T(4,128)} %msk_ref.3, s32[4,64]{1,0:T(4,128)} %send_ref.3, f32[16,256]{1,0:T(8,128)} %w_in.1, ...), custom_call_target="tpu_custom_call" | custom-call | tf_op jit(solution)/shard_map/pack/pallas_call | solution.py:149
  3.9 0.0 copy-start.2
  3.9 0.0 copy-start.4
  3.9 0.0 copy-start.5
  3.9 0.0 copy-start.6
  3.9 0.0 copy-start.7
  3.9 0.0 copy-start.8
  4.0 0.0 copy-start.9
  4.0 0.0 copy-start.10
  4.0 0.0 copy-start.11
  4.0 0.0 copy-start.12
  4.0 0.0 copy-start.15
  4.0 0.0 copy-start.16
  4.0 5.1 %collective-permute-start.2 = (bf16[192,256]{1,0:T(8,128)(2,1)}, bf16[192,256]{1,0:T(8,128)(2,1)S(1)}, u32[]{:S(2)}, u32[]{:S(2)}) collective-permute-start(bf16[192,256]{1,0:T(8,128)(2,1)} %pack.1.piece_0), channel_id=1, source_target_pairs={{0,6},{1,7},{2,4},{3,5},{4,2},{5,3},{6,0},{7,1},{8,14},{9,15},{10,... | collective-permute-start | bytes 294920 | tf_op jit(solution)/shard_map/ppermute | solution.py:159
  9.1 0.0 collective-permute-start.1
  9.2 0.6 collective-permute-start
  9.8 3.3 %collective-permute-done.2.piece_3 = bf16[192,256]{1,0:T(8,128)(2,1)S(1)} collective-permute-done((bf16[192,256]{1,0:T(8,128)(2,1)}, bf16[192,256]{1,0:T(8,128)(2,1)S(1)}, u32[]{:S(2)}, u32[]{:S(2)}) %collective-permute-start.2) | collective-permute-done | bytes 98336 | tf_op jit(solution)/shard_map/ppermute | solution.py:159
  13.1 0.0 collective-permute-start.6
  13.1 4.6 %collective-permute-done.1.piece_2 = bf16[192,256]{1,0:T(8,128)(2,1)S(1)} collective-permute-done((bf16[192,256]{1,0:T(8,128)(2,1)}, bf16[192,256]{1,0:T(8,128)(2,1)S(1)}, u32[]{:S(2)}, u32[]{:S(2)}) %collective-permute-start.1) | collective-permute-done | bytes 98336 | tf_op jit(solution)/shard_map/ppermute | solution.py:159
  17.6 0.0 collective-permute-start.5
  17.6 0.0 collective-permute-done.piece_1
  17.6 0.0 copy-start.26
  17.6 0.5 collective-permute-start.4
  18.1 0.0 collective-permute-done.3.piece_4
  18.2 0.8 collective-permute-done.5.piece_6
  18.9 0.2 collective-permute-done.4.piece_5
  19.1 0.5 copy-done.29
  19.6 0.6 copy-done.30
  20.2 38.4 %model.1 = (bf16[640,256]{1,0:T(8,128)(2,1)}, bf16[640,256]{1,0:T(8,128)(2,1)}) custom-call(s32[3]{0:T(128)} %pad_add_fusion.place_ref, bf16[4,2048,128]{2,1,0:T(8,128)(2,1)} %feat_ref.3, s32[4,8,2048]{2,1,0:T(8,128)} %bitcast.6, s32[4,2048]{1,0:T(4,128)} %lab_ref.3, s32[4,2048]{1,0:T(4,128)} %msk_ref.3, s32[4,64]{1,0:T(4,128)} %send_ref.3, ...), custom_call_target="tpu_custom_call" | custom-call | tf_op jit(solution)/shard_map/model/pallas_call | solution.py:600
  58.6 0.2 collective-permute-start.7
  58.8 1.7 %collective-permute-done.7.got_ref = bf16[640,256]{1,0:T(8,128)(2,1)S(1)} collective-permute-done((bf16[640,256]{1,0:T(8,128)(2,1)}, bf16[640,256]{1,0:T(8,128)(2,1)S(1)}, u32[]{:S(2)}, u32[]{:S(2)}) %collective-permute-start.7) | collective-permute-done | bytes 327712 | tf_op jit(solution)/shard_map/ppermute | solution.py:159
  60.4 1.0 %copy-done.3 = bf16[640,256]{1,0:T(8,128)(2,1)S(1)} copy-done((bf16[640,256]{1,0:T(8,128)(2,1)S(1)}, bf16[640,256]{1,0:T(8,128)(2,1)}, u32[]{:S(2)}) %copy-start.3) | copy-done | bytes 327704
  61.4 0.7 split.1
  62.2 1.6 %collective-permute-start.8 = (bf16[160,256]{1,0:T(8,128)(2,1)S(1)}, bf16[160,256]{1,0:T(8,128)(2,1)S(1)}, u32[]{:S(2)}, u32[]{:S(2)}) collective-permute-start(bf16[160,256]{1,0:T(8,128)(2,1)S(1)} %get-tuple-element.45), channel_id=1, source_target_pairs={{0,8},{8,0},{16,24},{24,16},{1,9},{9,1},{17,25},{25,17},{2,10},{10... | collective-permute-start | bytes 245768 | tf_op jit(solution)/shard_map/ppermute | solution.py:159
  63.7 1.5 %collective-permute-start.9 = (bf16[160,256]{1,0:T(8,128)(2,1)S(1)}, bf16[160,256]{1,0:T(8,128)(2,1)S(1)}, u32[]{:S(2)}, u32[]{:S(2)}) collective-permute-start(bf16[160,256]{1,0:T(8,128)(2,1)S(1)} %get-tuple-element.46), channel_id=1, source_target_pairs={{0,16},{8,24},{16,0},{24,8},{1,17},{9,25},{17,1},{25,9},{2,18},{10... | collective-permute-start | bytes 245768 | tf_op jit(solution)/shard_map/ppermute | solution.py:159
  65.2 0.5 collective-permute-start.10
  65.7 1.0 %collective-permute-done.8.one_ref = bf16[160,256]{1,0:T(8,128)(2,1)S(1)} collective-permute-done((bf16[160,256]{1,0:T(8,128)(2,1)S(1)}, bf16[160,256]{1,0:T(8,128)(2,1)S(1)}, u32[]{:S(2)}, u32[]{:S(2)}) %collective-permute-start.8) | collective-permute-done | bytes 81952 | tf_op jit(solution)/shard_map/ppermute | solution.py:159
  66.7 2.3 %collective-permute-done.9.two_ref = bf16[160,256]{1,0:T(8,128)(2,1)S(1)} collective-permute-done((bf16[160,256]{1,0:T(8,128)(2,1)S(1)}, bf16[160,256]{1,0:T(8,128)(2,1)S(1)}, u32[]{:S(2)}, u32[]{:S(2)}) %collective-permute-start.9) | collective-permute-done | bytes 81952 | tf_op jit(solution)/shard_map/ppermute | solution.py:159
  69.0 1.6 %collective-permute-done.10.three_ref = bf16[160,256]{1,0:T(8,128)(2,1)S(1)} collective-permute-done((bf16[160,256]{1,0:T(8,128)(2,1)S(1)}, bf16[160,256]{1,0:T(8,128)(2,1)S(1)}, u32[]{:S(2)}, u32[]{:S(2)}) %collective-permute-start.10) | collective-permute-done | bytes 81952 | tf_op jit(solution)/shard_map/ppermute | solution.py:159
  70.6 0.7 join.2.own_ref
  71.3 2.6 %collective-permute-start.13 = (bf16[160,256]{1,0:T(8,128)(2,1)S(1)}, bf16[160,256]{1,0:T(8,128)(2,1)S(1)}, u32[]{:S(2)}, u32[]{:S(2)}) collective-permute-start(bf16[160,256]{1,0:T(8,128)(2,1)S(1)} %join.2.own_ref), channel_id=1, source_target_pairs={{0,6},{1,7},{2,4},{3,5},{4,2},{5,3},{6,0},{7,1},{8,14},{9,15},{10,... | collective-permute-start | bytes 245768 | tf_op jit(solution)/shard_map/ppermute | solution.py:159
  73.8 0.0 collective-permute-start.12
  73.8 1.9 %collective-permute-start.11 = (bf16[160,256]{1,0:T(8,128)(2,1)S(1)}, bf16[160,256]{1,0:T(8,128)(2,1)S(1)}, u32[]{:S(2)}, u32[]{:S(2)}) collective-permute-start(bf16[160,256]{1,0:T(8,128)(2,1)S(1)} %join.2.own_ref), channel_id=1, source_target_pairs={{0,2},{1,3},{2,0},{3,1},{4,6},{5,7},{6,4},{7,5},{8,10},{9,11},{10,... | collective-permute-start | bytes 245768 | tf_op jit(solution)/shard_map/ppermute | solution.py:159
  75.7 2.7 %collective-permute-done.13.three_ref = bf16[160,256]{1,0:T(8,128)(2,1)S(1)} collective-permute-done((bf16[160,256]{1,0:T(8,128)(2,1)S(1)}, bf16[160,256]{1,0:T(8,128)(2,1)S(1)}, u32[]{:S(2)}, u32[]{:S(2)}) %collective-permute-start.13) | collective-permute-done | bytes 81952 | tf_op jit(solution)/shard_map/ppermute | solution.py:159
  78.4 1.9 %collective-permute-done.12.two_ref = bf16[160,256]{1,0:T(8,128)(2,1)S(1)} collective-permute-done((bf16[160,256]{1,0:T(8,128)(2,1)S(1)}, bf16[160,256]{1,0:T(8,128)(2,1)S(1)}, u32[]{:S(2)}, u32[]{:S(2)}) %collective-permute-start.12) | collective-permute-done | bytes 81952 | tf_op jit(solution)/shard_map/ppermute | solution.py:159
  80.3 0.0 collective-permute-done.11.one_ref
  80.3 0.7 join.3.piece_0
  81.0 0.9 collective-permute-start.16
  81.9 1.2 %collective-permute-start.15 = (bf16[160,256]{1,0:T(8,128)(2,1)S(1)}, bf16[160,256]{1,0:T(8,128)(2,1)S(1)}, u32[]{:S(2)}, u32[]{:S(2)}) collective-permute-start(bf16[160,256]{1,0:T(8,128)(2,1)S(1)} %join.3.piece_0), channel_id=1, source_target_pairs={{0,16},{8,24},{16,0},{24,8},{1,17},{9,25},{17,1},{25,9},{2,18},{10... | collective-permute-start | bytes 245768 | tf_op jit(solution)/shard_map/ppermute | solution.py:159
  83.1 1.4 %collective-permute-start.14 = (bf16[160,256]{1,0:T(8,128)(2,1)S(1)}, bf16[160,256]{1,0:T(8,128)(2,1)S(1)}, u32[]{:S(2)}, u32[]{:S(2)}) collective-permute-start(bf16[160,256]{1,0:T(8,128)(2,1)S(1)} %join.3.piece_0), channel_id=1, source_target_pairs={{0,8},{8,0},{16,24},{24,16},{1,9},{9,1},{17,25},{25,17},{2,10},{10... | collective-permute-start | bytes 245768 | tf_op jit(solution)/shard_map/ppermute | solution.py:159
  84.5 2.1 %collective-permute-done.16.piece_3 = bf16[160,256]{1,0:T(8,128)(2,1)S(1)} collective-permute-done((bf16[160,256]{1,0:T(8,128)(2,1)S(1)}, bf16[160,256]{1,0:T(8,128)(2,1)S(1)}, u32[]{:S(2)}, u32[]{:S(2)}) %collective-permute-start.16) | collective-permute-done | bytes 81952 | tf_op jit(solution)/shard_map/ppermute | solution.py:159
  86.6 0.0 collective-permute-start.20
  86.6 0.6 collective-permute-done.15.piece_2
  87.2 0.4 collective-permute-done.14.piece_1
  87.6 0.1 collective-permute-start.18
  87.7 0.2 collective-permute-done.20.piece_7
  87.9 0.6 collective-permute-done.19.piece_6
  88.5 0.4 collective-permute-done.18.piece_5
  89.0 3.2 %update.1 = (f32[16,256]{1,0:T(8,128)}, f32[2,2,32,256]{3,2,1,0:T(8,128)}, f32[8,40]{1,0:T(8,128)}, f32[1128]{0:T(1024)}, f32[16,128]{1,0:T(8,128)}, /*index=5*/...) custom-call(s32[1]{0:T(128)} %bitcast.dom_ref, ...), custom_call_target="tpu_custom_call" | custom-call | tf_op jit(solution)/shard_map/update/pallas_call | solution.py:918
  (47 shorter events, 0.1 us)
Async XLA Ops:
  1.2 87.6 %copy-start.14 = (f32[16,256]{1,0:T(8,128)S(1)}, f32[16,256]{1,0:T(8,128)}, u32[]{:S(2)}) copy-start(f32[16,256]{1,0:T(8,128)} %e_in.1) | copy-start | bytes 49156
  1.2 87.6 %copy-start.17 = (f32[16,128]{1,0:T(8,128)S(1)}, f32[16,128]{1,0:T(8,128)}, u32[]{:S(2)}) copy-start(f32[16,128]{1,0:T(8,128)} %rl_in.1) | copy-start | bytes 24580
  1.3 87.6 %copy-start.18 = (f32[1128]{0:T(1024)S(1)}, f32[1128]{0:T(1024)}, u32[]{:S(2)}) copy-start(f32[1128]{0:T(1024)} %first.1) | copy-start | bytes 13540
  1.3 87.6 %copy-start.19 = (f32[1128]{0:T(1024)S(1)}, f32[1128]{0:T(1024)}, u32[]{:S(2)}) copy-start(f32[1128]{0:T(1024)} %second.1) | copy-start | bytes 13540
  1.3 87.6 %copy-start.20 = (f32[1128]{0:T(1024)S(1)}, f32[1128]{0:T(1024)}, u32[]{:S(2)}) copy-start(f32[1128]{0:T(1024)} %e_small.1) | copy-start | bytes 13540
  1.3 87.6 %copy-start.21 = (f32[8,64]{1,0:T(8,128)S(1)}, f32[8,64]{1,0:T(8,128)}, u32[]{:S(2)}) copy-start(f32[8,64]{1,0:T(8,128)} %l_out.1) | copy-start | bytes 6148
  1.3 87.6 %copy-start.22 = (f32[8,64]{1,0:T(8,128)S(1)}, f32[8,64]{1,0:T(8,128)}, u32[]{:S(2)}) copy-start(f32[8,64]{1,0:T(8,128)} %rl_out.1) | copy-start | bytes 6148
  1.3 87.6 %copy-start.23 = (f32[8,40]{1,0:T(8,128)S(1)}, f32[8,40]{1,0:T(8,128)}, u32[]{:S(2)}) copy-start(f32[8,40]{1,0:T(8,128)} %e_out.1) | copy-start | bytes 3844
  3.9 56.6 %copy-start.13 = (s32[3]{0:T(128)S(1)}, s32[3]{0:T(128)}, u32[]{:S(2)}) copy-start(s32[3]{0:T(128)} %pad_add_fusion.place_ref) | copy-start | bytes 40
  3.9 85.0 %copy-start = (f32[2,2,256,256]{3,2,1,0:T(8,128)S(1)}, f32[2,2,256,256]{3,2,1,0:T(8,128)}, u32[]{:S(2)}) copy-start(f32[2,2,256,256]{3,2,1,0:T(8,128)} %r_gat.1) | copy-start | bytes 3145732
  3.9 85.0 %copy-start.1 = (f32[2,2,256,256]{3,2,1,0:T(8,128)S(1)}, f32[2,2,256,256]{3,2,1,0:T(8,128)}, u32[]{:S(2)}) copy-start(f32[2,2,256,256]{3,2,1,0:T(8,128)} %rr_gat.1) | copy-start | bytes 3145732
  3.9 85.0 %copy-start.2 = (f32[2,2,32,256]{3,2,1,0:T(8,128)S(1)}, f32[2,2,32,256]{3,2,1,0:T(8,128)}, u32[]{:S(2)}) copy-start(f32[2,2,32,256]{3,2,1,0:T(8,128)} %w_gat.1) | copy-start | bytes 393220
  3.9 85.0 %copy-start.4 = (f32[256,256]{1,0:T(8,128)S(1)}, f32[256,256]{1,0:T(8,128)}, u32[]{:S(2)}) copy-start(f32[256,256]{1,0:T(8,128)} %r_in.1) | copy-start | bytes 786436
  3.9 85.0 %copy-start.5 = (f32[256,256]{1,0:T(8,128)S(1)}, f32[256,256]{1,0:T(8,128)}, u32[]{:S(2)}) copy-start(f32[256,256]{1,0:T(8,128)} %rr_in.1) | copy-start | bytes 786436
  3.9 85.0 %copy-start.6 = (f32[2,2,32,256]{3,2,1,0:T(8,128)S(1)}, f32[2,2,32,256]{3,2,1,0:T(8,128)}, u32[]{:S(2)}) copy-start(f32[2,2,32,256]{3,2,1,0:T(8,128)} %l_gat.1) | copy-start | bytes 393220
  3.9 85.0 %copy-start.7 = (f32[2,2,32,256]{3,2,1,0:T(8,128)S(1)}, f32[2,2,32,256]{3,2,1,0:T(8,128)}, u32[]{:S(2)}) copy-start(f32[2,2,32,256]{3,2,1,0:T(8,128)} %rl_gat.1) | copy-start | bytes 393220
  3.9 85.0 %copy-start.8 = (f32[2,2,32,256]{3,2,1,0:T(8,128)S(1)}, f32[2,2,32,256]{3,2,1,0:T(8,128)}, u32[]{:S(2)}) copy-start(f32[2,2,32,256]{3,2,1,0:T(8,128)} %e_gat.1) | copy-start | bytes 393220
  4.0 85.0 %copy-start.9 = (f32[16,256]{1,0:T(8,128)S(1)}, f32[16,256]{1,0:T(8,128)}, u32[]{:S(2)}) copy-start(f32[16,256]{1,0:T(8,128)} %w_in.1) | copy-start | bytes 49156
  4.0 85.0 %copy-start.10 = (f32[1128]{0:T(1024)S(1)}, f32[1128]{0:T(1024)}, u32[]{:S(2)}) copy-start(f32[1128]{0:T(1024)} %small.1) | copy-start | bytes 13540
  4.0 85.0 %copy-start.11 = (f32[40,40]{1,0:T(8,128)S(1)}, f32[40,40]{1,0:T(8,128)}, u32[]{:S(2)}) copy-start(f32[40,40]{1,0:T(8,128)} %r_out.1) | copy-start | bytes 19204
  4.0 85.0 %copy-start.12 = (f32[40,40]{1,0:T(8,128)S(1)}, f32[40,40]{1,0:T(8,128)}, u32[]{:S(2)}) copy-start(f32[40,40]{1,0:T(8,128)} %rr_out.1) | copy-start | bytes 19204
  4.0 85.0 %copy-start.15 = (f32[8,40]{1,0:T(8,128)S(1)}, f32[8,40]{1,0:T(8,128)}, u32[]{:S(2)}) copy-start(f32[8,40]{1,0:T(8,128)} %w_out.1) | copy-start | bytes 3844
  4.0 85.0 %copy-start.16 = (f32[16,128]{1,0:T(8,128)S(1)}, f32[16,128]{1,0:T(8,128)}, u32[]{:S(2)}) copy-start(f32[16,128]{1,0:T(8,128)} %l_in.1) | copy-start | bytes 24580
  4.0 9.0 %collective-permute-start.2 = (bf16[192,256]{1,0:T(8,128)(2,1)}, bf16[192,256]{1,0:T(8,128)(2,1)S(1)}, u32[]{:S(2)}, u32[]{:S(2)}) collective-permute-start(bf16[192,256]{1,0:T(8,128)(2,1)} %pack.1.piece_0), channel_id=1, source_target_pairs={{0,6},{1,7},{2,4},{3,5},{4,2},{5,3},{6,0},{7,1},{8,14},{9,15},{10,... | collective-permute-start | bytes 294920 | tf_op jit(solution)/shard_map/ppermute | solution.py:159
  9.1 8.5 %collective-permute-start.1 = (bf16[192,256]{1,0:T(8,128)(2,1)}, bf16[192,256]{1,0:T(8,128)(2,1)S(1)}, u32[]{:S(2)}, u32[]{:S(2)}) collective-permute-start(bf16[192,256]{1,0:T(8,128)(2,1)} %pack.1.piece_0), channel_id=1, source_target_pairs={{0,4},{1,5},{2,6},{3,7},{4,0},{5,1},{6,2},{7,3},{8,12},{9,13},{10,... | collective-permute-start | bytes 294920 | tf_op jit(solution)/shard_map/ppermute | solution.py:159
  9.2 8.5 %collective-permute-start = (bf16[192,256]{1,0:T(8,128)(2,1)}, bf16[192,256]{1,0:T(8,128)(2,1)S(1)}, u32[]{:S(2)}, u32[]{:S(2)}) collective-permute-start(bf16[192,256]{1,0:T(8,128)(2,1)} %pack.1.piece_0), channel_id=1, source_target_pairs={{0,2},{1,3},{2,0},{3,1},{4,6},{5,7},{6,4},{7,5},{8,10},{9,11},{10,... | collective-permute-start | bytes 294920 | tf_op jit(solution)/shard_map/ppermute | solution.py:159
  9.8 8.4 %collective-permute-start.3 = (bf16[192,256]{1,0:T(8,128)(2,1)}, bf16[192,256]{1,0:T(8,128)(2,1)S(1)}, u32[]{:S(2)}, u32[]{:S(2)}) collective-permute-start(bf16[192,256]{1,0:T(8,128)(2,1)} %pack.1.piece_0), channel_id=1, source_target_pairs={{0,1},{1,0},{2,3},{3,2},{4,5},{5,4},{6,7},{7,6},{8,9},{9,8},{10,11... | collective-permute-start | bytes 294920 | tf_op jit(solution)/shard_map/ppermute | solution.py:159
  13.1 6.0 %copy-start.24 = (bf16[192,256]{1,0:T(8,128)(2,1)}, bf16[192,256]{1,0:T(8,128)(2,1)S(1)}, u32[]{:S(2)}) copy-start(bf16[192,256]{1,0:T(8,128)(2,1)S(1)} %collective-permute-done.2.piece_3) | copy-start | bytes 294916
  13.1 5.1 %collective-permute-start.6 = (bf16[192,256]{1,0:T(8,128)(2,1)S(1)}, bf16[192,256]{1,0:T(8,128)(2,1)S(1)}, u32[]{:S(2)}, u32[]{:S(2)}) collective-permute-start(bf16[192,256]{1,0:T(8,128)(2,1)S(1)} %collective-permute-done.2.piece_3), channel_id=1, source_target_pairs={{0,1},{1,0},{2,3},{3,2},{4,5},{5,4},{6,7},{7,6},{8,9},{9,8},{10,11... | collective-permute-start | bytes 294920 | tf_op jit(solution)/shard_map/ppermute | solution.py:159
  17.6 1.5 %copy-start.25 = (bf16[192,256]{1,0:T(8,128)(2,1)}, bf16[192,256]{1,0:T(8,128)(2,1)S(1)}, u32[]{:S(2)}) copy-start(bf16[192,256]{1,0:T(8,128)(2,1)S(1)} %collective-permute-done.1.piece_2) | copy-start | bytes 294916
  17.6 1.3 %collective-permute-start.5 = (bf16[192,256]{1,0:T(8,128)(2,1)S(1)}, bf16[192,256]{1,0:T(8,128)(2,1)S(1)}, u32[]{:S(2)}, u32[]{:S(2)}) collective-permute-start(bf16[192,256]{1,0:T(8,128)(2,1)S(1)} %collective-permute-done.1.piece_2), channel_id=1, source_target_pairs={{0,1},{1,0},{2,3},{3,2},{4,5},{5,4},{6,7},{7,6},{8,9},{9,8},{10,11... | collective-permute-start | bytes 294920 | tf_op jit(solution)/shard_map/ppermute | solution.py:159
  17.6 1.5 %copy-start.26 = (bf16[192,256]{1,0:T(8,128)(2,1)}, bf16[192,256]{1,0:T(8,128)(2,1)S(1)}, u32[]{:S(2)}) copy-start(bf16[192,256]{1,0:T(8,128)(2,1)S(1)} %collective-permute-done.piece_1) | copy-start | bytes 294916
  17.6 1.4 %collective-permute-start.4 = (bf16[192,256]{1,0:T(8,128)(2,1)S(1)}, bf16[192,256]{1,0:T(8,128)(2,1)S(1)}, u32[]{:S(2)}, u32[]{:S(2)}) collective-permute-start(bf16[192,256]{1,0:T(8,128)(2,1)S(1)} %collective-permute-done.piece_1), channel_id=1, source_target_pairs={{0,1},{1,0},{2,3},{3,2},{4,5},{5,4},{6,7},{7,6},{8,9},{9,8},{10,11... | collective-permute-start | bytes 294920 | tf_op jit(solution)/shard_map/ppermute | solution.py:159
  18.1 1.0 %copy-start.27 = (bf16[192,256]{1,0:T(8,128)(2,1)}, bf16[192,256]{1,0:T(8,128)(2,1)S(1)}, u32[]{:S(2)}) copy-start(bf16[192,256]{1,0:T(8,128)(2,1)S(1)} %collective-permute-done.3.piece_4) | copy-start | bytes 294916
  18.2 0.9 %copy-start.28 = (bf16[192,256]{1,0:T(8,128)(2,1)}, bf16[192,256]{1,0:T(8,128)(2,1)S(1)}, u32[]{:S(2)}) copy-start(bf16[192,256]{1,0:T(8,128)(2,1)S(1)} %collective-permute-done.6.piece_7) | copy-start | bytes 294916
  18.9 0.6 copy-start.29
  19.6 0.6 copy-start.30
  58.6 1.8 %collective-permute-start.7 = (bf16[640,256]{1,0:T(8,128)(2,1)}, bf16[640,256]{1,0:T(8,128)(2,1)S(1)}, u32[]{:S(2)}, u32[]{:S(2)}) collective-permute-start(bf16[640,256]{1,0:T(8,128)(2,1)} %get-tuple-element.43), channel_id=1, source_target_pairs={{0,1},{1,0},{2,3},{3,2},{4,5},{5,4},{6,7},{7,6},{8,9},{9,8},{10,11... | collective-permute-start | bytes 983048 | tf_op jit(solution)/shard_map/ppermute | solution.py:159
  60.4 1.0 %copy-start.3 = (bf16[640,256]{1,0:T(8,128)(2,1)S(1)}, bf16[640,256]{1,0:T(8,128)(2,1)}, u32[]{:S(2)}) copy-start(bf16[640,256]{1,0:T(8,128)(2,1)} %get-tuple-element.42.keep_ref) | copy-start | bytes 983044
  62.2 4.6 %collective-permute-start.8 = (bf16[160,256]{1,0:T(8,128)(2,1)S(1)}, bf16[160,256]{1,0:T(8,128)(2,1)S(1)}, u32[]{:S(2)}, u32[]{:S(2)}) collective-permute-start(bf16[160,256]{1,0:T(8,128)(2,1)S(1)} %get-tuple-element.45), channel_id=1, source_target_pairs={{0,8},{8,0},{16,24},{24,16},{1,9},{9,1},{17,25},{25,17},{2,10},{10... | collective-permute-start | bytes 245768 | tf_op jit(solution)/shard_map/ppermute | solution.py:159
  63.7 5.3 %collective-permute-start.9 = (bf16[160,256]{1,0:T(8,128)(2,1)S(1)}, bf16[160,256]{1,0:T(8,128)(2,1)S(1)}, u32[]{:S(2)}, u32[]{:S(2)}) collective-permute-start(bf16[160,256]{1,0:T(8,128)(2,1)S(1)} %get-tuple-element.46), channel_id=1, source_target_pairs={{0,16},{8,24},{16,0},{24,8},{1,17},{9,25},{17,1},{25,9},{2,18},{10... | collective-permute-start | bytes 245768 | tf_op jit(solution)/shard_map/ppermute | solution.py:159
  65.2 5.3 %collective-permute-start.10 = (bf16[160,256]{1,0:T(8,128)(2,1)S(1)}, bf16[160,256]{1,0:T(8,128)(2,1)S(1)}, u32[]{:S(2)}, u32[]{:S(2)}) collective-permute-start(bf16[160,256]{1,0:T(8,128)(2,1)S(1)} %get-tuple-element.47), channel_id=1, source_target_pairs={{0,24},{8,16},{16,8},{24,0},{1,25},{9,17},{17,9},{25,1},{2,26},{10... | collective-permute-start | bytes 245768 | tf_op jit(solution)/shard_map/ppermute | solution.py:159
  71.3 7.1 %collective-permute-start.13 = (bf16[160,256]{1,0:T(8,128)(2,1)S(1)}, bf16[160,256]{1,0:T(8,128)(2,1)S(1)}, u32[]{:S(2)}, u32[]{:S(2)}) collective-permute-start(bf16[160,256]{1,0:T(8,128)(2,1)S(1)} %join.2.own_ref), channel_id=1, source_target_pairs={{0,6},{1,7},{2,4},{3,5},{4,2},{5,3},{6,0},{7,1},{8,14},{9,15},{10,... | collective-permute-start | bytes 245768 | tf_op jit(solution)/shard_map/ppermute | solution.py:159
  73.8 6.5 %collective-permute-start.12 = (bf16[160,256]{1,0:T(8,128)(2,1)S(1)}, bf16[160,256]{1,0:T(8,128)(2,1)S(1)}, u32[]{:S(2)}, u32[]{:S(2)}) collective-permute-start(bf16[160,256]{1,0:T(8,128)(2,1)S(1)} %join.2.own_ref), channel_id=1, source_target_pairs={{0,4},{1,5},{2,6},{3,7},{4,0},{5,1},{6,2},{7,3},{8,12},{9,13},{10,... | collective-permute-start | bytes 245768 | tf_op jit(solution)/shard_map/ppermute | solution.py:159
  73.8 6.5 %collective-permute-start.11 = (bf16[160,256]{1,0:T(8,128)(2,1)S(1)}, bf16[160,256]{1,0:T(8,128)(2,1)S(1)}, u32[]{:S(2)}, u32[]{:S(2)}) collective-permute-start(bf16[160,256]{1,0:T(8,128)(2,1)S(1)} %join.2.own_ref), channel_id=1, source_target_pairs={{0,2},{1,3},{2,0},{3,1},{4,6},{5,7},{6,4},{7,5},{8,10},{9,11},{10,... | collective-permute-start | bytes 245768 | tf_op jit(solution)/shard_map/ppermute | solution.py:159
  81.0 5.6 %collective-permute-start.16 = (bf16[160,256]{1,0:T(8,128)(2,1)S(1)}, bf16[160,256]{1,0:T(8,128)(2,1)S(1)}, u32[]{:S(2)}, u32[]{:S(2)}) collective-permute-start(bf16[160,256]{1,0:T(8,128)(2,1)S(1)} %join.3.piece_0), channel_id=1, source_target_pairs={{0,24},{8,16},{16,8},{24,0},{1,25},{9,17},{17,9},{25,1},{2,26},{10... | collective-permute-start | bytes 245768 | tf_op jit(solution)/shard_map/ppermute | solution.py:159
  81.9 5.3 %collective-permute-start.15 = (bf16[160,256]{1,0:T(8,128)(2,1)S(1)}, bf16[160,256]{1,0:T(8,128)(2,1)S(1)}, u32[]{:S(2)}, u32[]{:S(2)}) collective-permute-start(bf16[160,256]{1,0:T(8,128)(2,1)S(1)} %join.3.piece_0), channel_id=1, source_target_pairs={{0,16},{8,24},{16,0},{24,8},{1,17},{9,25},{17,1},{25,9},{2,18},{10... | collective-permute-start | bytes 245768 | tf_op jit(solution)/shard_map/ppermute | solution.py:159
  83.1 4.4 %collective-permute-start.14 = (bf16[160,256]{1,0:T(8,128)(2,1)S(1)}, bf16[160,256]{1,0:T(8,128)(2,1)S(1)}, u32[]{:S(2)}, u32[]{:S(2)}) collective-permute-start(bf16[160,256]{1,0:T(8,128)(2,1)S(1)} %join.3.piece_0), channel_id=1, source_target_pairs={{0,8},{8,0},{16,24},{24,16},{1,9},{9,1},{17,25},{25,17},{2,10},{10... | collective-permute-start | bytes 245768 | tf_op jit(solution)/shard_map/ppermute | solution.py:159
  84.5 3.2 %collective-permute-start.17 = (bf16[160,256]{1,0:T(8,128)(2,1)S(1)}, bf16[160,256]{1,0:T(8,128)(2,1)S(1)}, u32[]{:S(2)}, u32[]{:S(2)}) collective-permute-start(bf16[160,256]{1,0:T(8,128)(2,1)S(1)} %join.3.piece_0), channel_id=1, source_target_pairs={{0,1},{1,0},{2,3},{3,2},{4,5},{5,4},{6,7},{7,6},{8,9},{9,8},{10,11... | collective-permute-start | bytes 245768 | tf_op jit(solution)/shard_map/ppermute | solution.py:159
  86.6 1.3 %collective-permute-start.20 = (bf16[160,256]{1,0:T(8,128)(2,1)S(1)}, bf16[160,256]{1,0:T(8,128)(2,1)S(1)}, u32[]{:S(2)}, u32[]{:S(2)}) collective-permute-start(bf16[160,256]{1,0:T(8,128)(2,1)S(1)} %collective-permute-done.16.piece_3), channel_id=1, source_target_pairs={{0,1},{1,0},{2,3},{3,2},{4,5},{5,4},{6,7},{7,6},{8,9},{9,8},{10,11... | collective-permute-start | bytes 245768 | tf_op jit(solution)/shard_map/ppermute | solution.py:159
  87.2 1.3 %collective-permute-start.19 = (bf16[160,256]{1,0:T(8,128)(2,1)S(1)}, bf16[160,256]{1,0:T(8,128)(2,1)S(1)}, u32[]{:S(2)}, u32[]{:S(2)}) collective-permute-start(bf16[160,256]{1,0:T(8,128)(2,1)S(1)} %collective-permute-done.15.piece_2), channel_id=1, source_target_pairs={{0,1},{1,0},{2,3},{3,2},{4,5},{5,4},{6,7},{7,6},{8,9},{9,8},{10,11... | collective-permute-start | bytes 245768 | tf_op jit(solution)/shard_map/ppermute | solution.py:159
  87.6 1.3 %collective-permute-start.18 = (bf16[160,256]{1,0:T(8,128)(2,1)S(1)}, bf16[160,256]{1,0:T(8,128)(2,1)S(1)}, u32[]{:S(2)}, u32[]{:S(2)}) collective-permute-start(bf16[160,256]{1,0:T(8,128)(2,1)S(1)} %collective-permute-done.14.piece_1), channel_id=1, source_target_pairs={{0,1},{1,0},{2,3},{3,2},{4,5},{5,4},{6,7},{7,6},{8,9},{9,8},{10,11... | collective-permute-start | bytes 245768 | tf_op jit(solution)/shard_map/ppermute | solution.py:159

commit v4 on v3

--- a/solution.py
+++ b/solution.py
@@ -50,7 +50,8 @@
 OUT_G = HSIZE // GROUPS
 TAIL_G = IN_G + 4 * GAT_G
 PACK_G = TAIL_G + 2 * OUT_G
-HALO_G = PACK_G + 32
+HALO_G = PACK_G + 16
+CODES = slice(HID - LANES, HID)
 PIECE = ROWS // 8
 HALF = GRAPH // 2
 ROW_IN = 4 * HID
@@ -85,7 +86,7 @@
 
 
 def pack_kernel(
-    place_ref,
+    section_ref,
     feat_ref,
     src_ref,
     lab_ref,
@@ -96,37 +97,35 @@
     wout_ref,
     pack_ref,
     tail_ref,
-    ints_ref,
 ):
-    micro = place_ref[0]
+    micro = section_ref[0]
     nodes = lab_ref.shape[1]
-    pack_ref[PACK_G : PACK_G + 16, 0:FEAT] = feat_ref[0, 0:16]
-    pack_ref[PACK_G : PACK_G + 16, FEAT : 2 * FEAT] = feat_ref[0, 16:32]
+    pack_ref[PACK_G:HALO_G, 0:FEAT] = feat_ref[0, 0:16]
+    pack_ref[PACK_G:HALO_G, FEAT : 2 * FEAT] = feat_ref[0, 16:32]
     shift = LANES - HALF
-    ints_ref[...] = jnp.zeros_like(ints_ref)
+    tail_ref[...] = jnp.zeros_like(tail_ref)
     far = src_ref[0]
     far = jnp.where(far >= nodes, far - nodes + GRAPH, far)
-    ints_ref[0:DEG, 0:LANES] = pltpu.roll(far, shift, 1).astype(f32)
-    ints_ref[DEG : DEG + 1, 0:LANES] = pltpu.roll(row_of(lab_ref, micro, LANES), shift, 1).astype(f32)
-    ints_ref[DEG + 1 : DEG + 2, 0:LANES] = pltpu.roll(row_of(msk_ref, micro, LANES), shift, 1).astype(f32)
+    tail_ref[0:DEG, CODES] = pltpu.roll(far, shift, 1).astype(f32)
+    tail_ref[DEG : DEG + 1, CODES] = pltpu.roll(row_of(lab_ref, micro, LANES), shift, 1).astype(f32)
+    tail_ref[DEG + 1 : DEG + 2, CODES] = pltpu.roll(row_of(msk_ref, micro, LANES), shift, 1).astype(f32)
     send = row_of(send_ref, micro, 2 * HALF)
-    ints_ref[DEG + 2 : DEG + 3, 0:LANES] = jnp.concatenate([send, send], axis=1).astype(f32)
-    pack_ref[PACK_G + 16 : HALO_G, :] = ints_ref[...].astype(bf16)
+    tail_ref[DEG + 2 : DEG + 3, CODES] = jnp.concatenate([send, send], axis=1).astype(f32)
     if win_ref.shape[0] != IN_G:
-        pack_ref[0:PACK_G, :] = jnp.zeros((PACK_G, HID), bf16)
+        pack_ref[0:TAIL_G, :] = jnp.zeros((TAIL_G, HID), bf16)
+        pack_ref[TAIL_G:PACK_G, :] = tail_ref[...].astype(bf16)
         return
     pack_ref[0:IN_G, :] = win_ref[...].astype(bf16)
     for layer in range(2):
         for side in range(2):
             start = IN_G + (2 * layer + side) * GAT_G
             pack_ref[start : start + GAT_G, :] = wgat_ref[layer, side].astype(bf16)
-    tail_ref[...] = jnp.zeros_like(tail_ref)
     tail_ref[0:OUT_G, 0:CLASSES] = wout_ref[...]
     count = jnp.sum(jnp.sum(msk_ref[...].astype(f32), axis=1, keepdims=True), axis=0, keepdims=True)
     high = jnp.floor(count * (1.0 / 256.0))
-    lane = lax.broadcasted_iota(jnp.int32, (1, HID), 1)
+    lane = lax.broadcasted_iota(jnp.int32, (1, LANES), 1)
     low = jnp.where(lane == 1, count - 256.0 * high, 0.0)
-    tail_ref[OUT_G : OUT_G + 1, :] = jnp.where(lane == 0, high, low)
+    tail_ref[OUT_G : OUT_G + 1, 0:LANES] = jnp.where(lane == 0, high, low)
     pack_ref[TAIL_G:PACK_G, :] = tail_ref[...].astype(bf16)
 
 
@@ -134,7 +133,7 @@
     return [pl.BlockSpec(memory_space=pltpu.VMEM)] * count
 
 
-def pack_inputs(place, features, src_all, labels, label_mask, send_index, w_in, w_gat, w_out):
+def pack_inputs(section_id, features, src_all, labels, label_mask, send_index, w_in, w_gat, w_out):
     grid_spec = pltpu.PrefetchScalarGridSpec(
         num_scalar_prefetch=1,
         grid=(1,),
@@ -144,7 +143,7 @@
         ]
         + vmem(6),
         out_specs=vmem(1)[0],
-        scratch_shapes=[pltpu.VMEM((2 * OUT_G, HID), f32), pltpu.VMEM((16, HID), f32)],
+        scratch_shapes=[pltpu.VMEM((2 * OUT_G, HID), f32)],
     )
     return pl.pallas_call(
         pack_kernel,
@@ -152,19 +151,19 @@
         out_shape=jax.ShapeDtypeStruct((HALO_G, HID), bf16),
         compiler_params=pltpu.CompilerParams(vmem_limit_bytes=60 * 1024 * 1024),
         name="pack",
-    )(place, features, src_all, labels, label_mask, send_index, w_in, w_gat, w_out)
+    )(section_id, features, src_all, labels, label_mask, send_index, w_in, w_gat, w_out)
 
 
 def crossed(value, axis, mask):
     return lax.ppermute(value, axis, [(i, i ^ mask) for i in range(lax.axis_size(axis))])
 
 
-def gather_weights(packed, w_in, w_gat, w_out, label_mask):
+def gather_weights(dom_id, packed, w_in, w_gat, w_out, label_mask):
     size = lax.axis_size("dom")
     if size == GROUPS:
         near = [packed] + [crossed(packed, "dom", 2 * j) for j in range(1, 4)]
-        return near + [crossed(piece, "dom", 1) for piece in near], lax.axis_index("dom")
-    halo = lax.ppermute(packed[PACK_G:], "dom", [((i + 1) % size, i) for i in range(size)])
+        return near + [crossed(piece, "dom", 1) for piece in near], dom_id
+    halo = lax.ppermute(packed[TAIL_G:], "dom", [((i + 1) % size, i) for i in range(size)])
     halo = jnp.broadcast_to(halo[None], (GROUPS,) + halo.shape)
     rows_in, rows_gat, rows_out = (w_in.shape[0], w_gat.shape[2], w_out.shape[0])
     count = jnp.sum(label_mask)
@@ -186,8 +185,10 @@
     part_out = whole[:, cut : cut + rows_out].reshape(GROUPS, OUT_G, HID)
     counts = whole[:, cut + rows_out].reshape(GROUPS, size // GROUPS, HID)
     counts = jnp.pad(counts, ((0, 0), (0, OUT_G - size // GROUPS), (0, 0)))
-    whole = jnp.concatenate([part_in, part_gat, part_out, counts, halo], axis=1)
-    return [whole[g] for g in (0, 2, 4, 6, 1, 3, 5, 7)], 0
+    tail = jnp.concatenate([part_out, counts], axis=1)
+    tail = jnp.concatenate([tail[:, :, :LANES], halo[:, : 2 * OUT_G, LANES:]], axis=2)
+    whole = jnp.concatenate([part_in, part_gat, tail, halo[:, 2 * OUT_G :]], axis=1)
+    return [whole[g] for g in (0, 2, 4, 6, 1, 3, 5, 7)], dom_id * 0
 
 
 def column_of(row):
@@ -195,7 +196,9 @@
 
 
 def model_kernel(
-    place_ref,
+    section_ref,
+    dom_ref,
+    spot_ref,
     feat_ref,
     src_ref,
     lab_ref,
@@ -218,8 +221,7 @@
     att_ref,
     h_ref,
     slope_ref,
-    xlr_ref,
-    dx_ref,
+    both_ref,
     do_ref,
     pool_ref,
     dlog_ref,
@@ -247,14 +249,14 @@
     chunk = 4 * LANES
     chunks = nodes // chunk
     mixed = DEG * LANES
-    micro = place_ref[0]
-    after = jnp.bitwise_and(place_ref[2] + 1, GROUPS - 1)
+    micro = section_ref[0]
+    after = jnp.bitwise_and(spot_ref[0] + 1, GROUPS - 1)
     final = nodes - LANES
 
-    digits = jnp.zeros((OUT_G, HID), f32)
+    digits = jnp.zeros((OUT_G, LANES), f32)
     pieces = (piece_0, piece_1, piece_2, piece_3, piece_4, piece_5, piece_6, piece_7)
     for j, piece in enumerate(pieces):
-        group = jnp.bitwise_xor(place_ref[2], 2 * (j & 3) + (j >> 2))
+        group = jnp.bitwise_xor(spot_ref[0], 2 * (j & 3) + (j >> 2))
 
         def rows_of(width):
             return pl.ds(pl.multiple_of(group * width, width), width)
@@ -265,14 +267,14 @@
                 start = IN_G + (2 * layer + side) * GAT_G
                 wg_ref[layer, rows_of(GAT_G), side * HID : (side + 1) * HID] = piece[start : start + GAT_G, :]
         tail = piece[TAIL_G:PACK_G, :].astype(f32)
-        wof_ref[rows_of(OUT_G), :] = tail[0:OUT_G]
-        digits = digits + tail[OUT_G : 2 * OUT_G]
-        halo_ref[group] = piece[PACK_G:HALO_G, :]
+        wof_ref[rows_of(OUT_G), :] = tail[0:OUT_G, 0:LANES]
+        digits = digits + tail[OUT_G : 2 * OUT_G, 0:LANES]
+        halo_ref[group] = piece[TAIL_G:HALO_G, :]
 
     node_ref[0 : nodes - HALF, :] = feat_ref[0, HALF:nodes, :]
-    node_ref[nodes - HALF : nodes - 16, :] = halo_ref[after, 0:16, 0:FEAT]
-    node_ref[nodes - 16 : nodes, :] = halo_ref[after, 0:16, FEAT : 2 * FEAT]
-    ints = halo_ref[after, 16:32, 0:LANES].astype(f32).astype(jnp.int32)
+    node_ref[nodes - HALF : nodes - 16, :] = halo_ref[after, 16:32, 0:FEAT]
+    node_ref[nodes - 16 : nodes, :] = halo_ref[after, 16:32, FEAT : 2 * FEAT]
+    ints = halo_ref[after, 0:16, CODES].astype(f32).astype(jnp.int32)
     lane_row = lax.broadcasted_iota(jnp.int32, (1, LANES), 1)
     kept = lane_row < LANES - HALF
     edge_ref[...] = pltpu.roll(src_ref[0], nodes - HALF, 1)
@@ -380,18 +382,19 @@
         @pl.loop(0, chunks, unroll=4)
         def _(c):
             at = lanes_of(c, chunk)
-            xlr_ref[layer, :, at] = dot_nn(wgt_ref[layer], h_ref[layer, :, at]).astype(bf16)
+            both_ref[layer, :, at] = dot_nn(wgt_ref[layer], h_ref[layer, :, at]).astype(bf16)
 
         @pl.loop(0, blocks // WAYS)
         def _(step):
             ids = [step * WAYS + u for u in range(WAYS)]
             ats = [lanes_of(i, LANES) for i in ids]
             ways = range(WAYS)
-            left = [xlr_ref[layer, 0:HID, ats[u]] for u in ways]
+            left = [both_ref[layer, 0:HID, ats[u]] for u in ways]
             grown = []
             for u in ways:
-                right = xlr_ref[layer, HID : 2 * HID, ats[u]]
-                mixed_rows = dot_nn(left[u], e_ref[ids[u]]).astype(bf16)
+                right = both_ref[layer, HID : 2 * HID, ats[u]]
+                left_f = left[u].astype(f32)
+                mixed_rows = jnp.concatenate([jnp.take_along_axis(left_f, jnp.broadcast_to(edge_ref[k : k + 1, ats[u]], (HID, LANES)), axis=1, mode='promise_in_bounds').astype(bf16) for k in range(DEG)],axis=1)
                 mixed_rows = mixed_rows + jnp.concatenate([right] * DEG, axis=1)
                 own = left[u] + right
                 t_ref[layer, ids[u], :, 0:mixed] = mixed_rows
@@ -496,20 +499,20 @@
                 own = w_ref[u, :, tile_of(DEG)].astype(f32)
                 left_w = spread[:, 0:LANES] + own
                 right_w = spread[:, LANES : 2 * LANES] + own
-                left = xlr_ref[layer, 0:HID, ats[u]].astype(f32)
-                right = xlr_ref[layer, HID : 2 * HID, ats[u]].astype(f32)
+                left = both_ref[layer, 0:HID, ats[u]].astype(f32)
+                right = both_ref[layer, HID : 2 * HID, ats[u]].astype(f32)
                 da_ref[layer] += left * left_w + right * right_w
                 wide = a_ref[layer]
                 for h in range(HEADS):
                     passed = dot_nt(d_out[u][head_of(h)], att_ref[layer, ids[u], h])
                     d_left = wide[head_of(h)] * left_w[head_of(h)] + passed
-                    dx_ref[layer, head_of(h), ats[u]] = d_left.astype(bf16)
-                dx_ref[layer, HID : 2 * HID, ats[u]] = (wide * right_w).astype(bf16)
+                    both_ref[1 + layer, head_of(h), ats[u]] = d_left.astype(bf16)
+                both_ref[1 + layer, HID : 2 * HID, ats[u]] = (wide * right_w).astype(bf16)
 
         @pl.loop(0, chunks, unroll=4)
         def _(c):
             at = lanes_of(c, chunk)
-            d_in = dot_nn(wg_ref[layer], dx_ref[layer, :, at]).astype(bf16).astype(f32)
+            d_in = dot_nn(wg_ref[layer], both_ref[1 + layer, :, at]).astype(bf16).astype(f32)
             d_in = d_in * slope_ref[layer, :, at]
             do_ref[:, at] = d_in.astype(bf16)
             if layer == 1:
@@ -520,7 +523,7 @@
         for side in range(2):
             start = (2 * layer + side) * HID
             out_ref[start : start + HID, :] = dot_nt(
-                h_ref[layer], dx_ref[layer, side * HID : (side + 1) * HID, :]
+                h_ref[layer], both_ref[1 + layer, side * HID : (side + 1) * HID, :]
             ).astype(bf16)
     out_ref[ROW_IN : ROW_IN + FEAT, :] = dot_nn(do_ref[...], node_ref[...]).T.astype(bf16)
     out_ref[ROW_OUT : ROW_OUT + HSIZE, :] = jnp.zeros((HSIZE, HID), bf16)
@@ -546,13 +549,13 @@
     columns = columns + jnp.where(lane_wide == 4, last, 0.0)
     out_ref[ROW_MISC : ROW_MISC + 16, :] = columns.T[0:16].astype(bf16)
     out_ref[ROW_MISC + 16 :, :] = jnp.zeros((ROWS - ROW_MISC - 16, HID), bf16)
-    core = jnp.bitwise_and(place_ref[1], 1)
+    core = jnp.bitwise_and(dom_ref[0], 1)
     width = ROWS // 2
     keep_ref[...] = out_ref[pl.ds(pl.multiple_of(core * width, width), width), :]
     send_out_ref[...] = out_ref[pl.ds(pl.multiple_of((1 - core) * width, width), width), :]
 
 
-def run_model(place, features, src_all, labels, label_mask, send_index, pieces, small_params):
+def run_model(section_id, dom_id, spot, features, src_all, labels, label_mask, send_index, pieces, small_params):
     nodes = features.shape[1]
     blocks = nodes // LANES
     scratch = [
@@ -562,8 +565,7 @@
         pltpu.VMEM((2, blocks, HEADS, LANES, LANES), bf16),
         pltpu.VMEM((2, HID, nodes), bf16),
         pltpu.VMEM((2, HID, nodes), f32),
-        pltpu.VMEM((2, 2 * HID, nodes), bf16),
-        pltpu.VMEM((2, 2 * HID, nodes), bf16),
+        pltpu.VMEM((3, 2 * HID, nodes), bf16),
         pltpu.VMEM((HID, nodes), bf16),
         pltpu.VMEM((HSIZE, nodes), bf16),
         pltpu.VMEM((CLASSES, nodes), bf16),
@@ -580,18 +582,18 @@
         pltpu.VMEM((2, 2 * HID, HID), bf16),
         pltpu.VMEM((2, HID, 2 * HID), bf16),
         pltpu.VMEM((HSIZE, CLASSES), bf16),
-        pltpu.VMEM((HSIZE, HID), f32),
+        pltpu.VMEM((HSIZE, LANES), f32),
         pltpu.VMEM((2, 16, HID), bf16),
         pltpu.VMEM((ROWS, HID), bf16),
         pltpu.VMEM((LANES, DEG * LANES), bf16),
-        pltpu.VMEM((GROUPS, HALO_G - PACK_G, HID), bf16),
+        pltpu.VMEM((GROUPS, 32, HID), bf16),
     ]
     grid_spec = pltpu.PrefetchScalarGridSpec(
-        num_scalar_prefetch=1,
+        num_scalar_prefetch=3,
         grid=(1,),
         in_specs=[
-            pl.BlockSpec((1, nodes, FEAT), lambda i, m: (m[0], 0, 0)),
-            pl.BlockSpec((1, DEG, nodes), lambda i, m: (m[0], 0, 0)),
+            pl.BlockSpec((1, nodes, FEAT), lambda i, m, d, p: (m[0], 0, 0)),
+            pl.BlockSpec((1, DEG, nodes), lambda i, m, d, p: (m[0], 0, 0)),
         ]
         + vmem(12),
         out_specs=vmem(2),
@@ -601,9 +603,9 @@
         model_kernel,
         grid_spec=grid_spec,
         out_shape=[jax.ShapeDtypeStruct((ROWS // 2, HID), bf16)] * 2,
-        compiler_params=pltpu.CompilerParams(vmem_limit_bytes=54 * 1024 * 1024),
+        compiler_params=pltpu.CompilerParams(vmem_limit_bytes=50 * 1024 * 1024),
         name="model",
-    )(place, features, src_all, labels, label_mask, send_index, *pieces, small_params)
+    )(section_id, dom_id, spot, features, src_all, labels, label_mask, send_index, *pieces, small_params)
 
 
 def settled(total, is_last):
@@ -624,9 +626,9 @@
     return jnp.where((core == 1) & (section == 3), 1, 0)
 
 
-def split_kernel(place_ref, keep_ref, got_ref, *out_refs):
-    section = place_ref[0]
-    core = jnp.bitwise_and(place_ref[1], 1)
+def split_kernel(section_ref, dom_ref, keep_ref, got_ref, *out_refs):
+    section = section_ref[0]
+    core = jnp.bitwise_and(dom_ref[0], 1)
     for j, out_ref in enumerate(out_refs):
         part = jnp.bitwise_xor(section, j)
         at = pl.ds(pl.multiple_of(part * PIECE, PIECE), PIECE)
@@ -634,43 +636,43 @@
         out_ref[...] = settled(total, last_piece(core, part))
 
 
-def join_kernel(place_ref, own_ref, one_ref, two_ref, three_ref, out_ref):
+def join_kernel(section_ref, dom_ref, own_ref, one_ref, two_ref, three_ref, out_ref):
     pair = own_ref[...].astype(f32) + one_ref[...].astype(f32)
     other = two_ref[...].astype(f32) + three_ref[...].astype(f32)
-    core = jnp.bitwise_and(place_ref[1], 1)
-    out_ref[...] = settled(pair + other, last_piece(core, place_ref[0]))
-
-
-def small_call(kernel, name, place, count, operands):
+    core = jnp.bitwise_and(dom_ref[0], 1)
+    out_ref[...] = settled(pair + other, last_piece(core, section_ref[0]))
+
+
+def small_call(kernel, name, ids, count, operands):
     shape = jax.ShapeDtypeStruct((PIECE, HID), bf16)
     return pl.pallas_call(
         kernel,
         out_shape=[shape] * count if count > 1 else shape,
-        in_specs=[pl.BlockSpec(memory_space=pltpu.SMEM)] + vmem(len(operands)),
+        in_specs=[pl.BlockSpec(memory_space=pltpu.SMEM)] * 2 + vmem(len(operands)),
         out_specs=vmem(count) if count > 1 else vmem(1)[0],
         compiler_params=pltpu.CompilerParams(vmem_limit_bytes=8 * 1024 * 1024),
         name=name,
-    )(place, *operands)
-
-
-def sum_gradients(place, keep, send):
+    )(*ids, *operands)
+
+
+def sum_gradients(ids, keep, send):
     if lax.axis_size("dom") == 8 and lax.axis_size("section") == 4:
         got = crossed(send, "dom", 1)
-        parts = small_call(split_kernel, "split", place, 4, (keep, got))
+        parts = small_call(split_kernel, "split", ids, 4, (keep, got))
         came = [crossed(parts[j], "section", j) for j in range(1, 4)]
-        mine = small_call(join_kernel, "join", place, 1, (parts[0], *came))
+        mine = small_call(join_kernel, "join", ids, 1, (parts[0], *came))
         came = [crossed(mine, "dom", 2 * j) for j in range(1, 4)]
-        mine = small_call(join_kernel, "join", place, 1, (mine, *came))
+        mine = small_call(join_kernel, "join", ids, 1, (mine, *came))
         near = [mine] + [crossed(mine, "section", j) for j in range(1, 4)]
-        return near + [crossed(piece, "dom", 1) for piece in near], place
+        return near + [crossed(piece, "dom", 1) for piece in near], ids
     all_size = lax.axis_size("dom") * lax.axis_size("section")
-    swap = jnp.bitwise_and(place[1], 1) == 1
+    swap = jnp.bitwise_and(ids[1][0], 1) == 1
     partial = jnp.concatenate([jnp.where(swap, send, keep), jnp.where(swap, keep, send)], axis=0)
     parts = lax.all_to_all(partial.reshape(all_size, -1, HID), ("section", "dom"), 0, 0)
     mine = jnp.sum(parts.astype(f32), axis=0)
     shared = jnp.broadcast_to(mine.astype(bf16)[None], (all_size,) + mine.shape)
     summed = lax.all_to_all(shared, ("section", "dom"), 0, 0).reshape(8, PIECE, HID)
-    return [summed[j] for j in range(8)], place * jnp.array([0, 2, 0], jnp.int32)
+    return [summed[j] for j in range(8)], (ids[0] * 0, ids[1] * 0)
 
 
 def adamw_step(parameter, gradient, moment_one, moment_two):
@@ -726,7 +728,8 @@
 
 def update_kernel(
     dom_ref,
-    place_ref,
+    section_ref,
+    spot_ref,
     piece_0,
     piece_1,
     piece_2,
@@ -778,10 +781,10 @@
     sum_ref,
 ):
     dom = dom_ref[0]
-    core = jnp.bitwise_and(place_ref[1], 1)
+    core = jnp.bitwise_and(spot_ref[0], 1)
     pieces = (piece_0, piece_1, piece_2, piece_3, piece_4, piece_5, piece_6, piece_7)
     for j, piece in enumerate(pieces):
-        spot = jnp.bitwise_xor(core, j >> 2) * 4 + jnp.bitwise_xor(place_ref[0], j & 3)
+        spot = jnp.bitwise_xor(core, j >> 2) * 4 + jnp.bitwise_xor(section_ref[0], j & 3)
         sum_ref[pl.ds(pl.multiple_of(spot * PIECE, PIECE), PIECE), :] = piece[...]
     grads = sum_ref[0:ROW_MISC, :].astype(f32)
     squares = jnp.sum(grads * grads)
@@ -880,16 +883,14 @@
     ema_small,
 ):
     dom_id = lax.axis_index("dom").astype(jnp.int32).reshape(1)
-    section_id = lax.axis_index("section")
-    place = jnp.stack([section_id, lax.axis_index("dom"), lax.axis_index("dom")]).astype(jnp.int32)
+    section_id = lax.axis_index("section").astype(jnp.int32).reshape(1)
     src_all = jnp.swapaxes(sources, 1, 2)
-    packed = pack_inputs(place, features, src_all, labels, label_mask, send_index, w_in, w_gat, w_out)
-    pieces, spot = gather_weights(packed, w_in, w_gat, w_out, label_mask)
-    place = jnp.stack([section_id, lax.axis_index("dom"), spot]).astype(jnp.int32)
+    packed = pack_inputs(section_id, features, src_all, labels, label_mask, send_index, w_in, w_gat, w_out)
+    pieces, spot = gather_weights(dom_id, packed, w_in, w_gat, w_out, label_mask)
     keep, send = run_model(
-        place, features, src_all, labels, label_mask, send_index, pieces, small_params
-    )
-    pieces, spot = sum_gradients(place, keep, send)
+        section_id, dom_id, spot, features, src_all, labels, label_mask, send_index, pieces, small_params
+    )
+    pieces, spots = sum_gradients((section_id, dom_id), keep, send)
     state = (
         w_in,
         w_gat,
@@ -918,12 +919,12 @@
     results = pl.pallas_call(
         update_kernel,
         out_shape=[jax.ShapeDtypeStruct(v.shape, f32) for v in like] + [jax.ShapeDtypeStruct((1,), f32)] * 2,
-        in_specs=[pl.BlockSpec(memory_space=pltpu.SMEM)] * 2 + vmem(30),
+        in_specs=[pl.BlockSpec(memory_space=pltpu.SMEM)] * 3 + vmem(30),
         out_specs=vmem(16) + [pl.BlockSpec(memory_space=pltpu.SMEM)] * 2,
         scratch_shapes=[pltpu.VMEM((ROWS, HID), bf16)],
         compiler_params=pltpu.CompilerParams(vmem_limit_bytes=16 * 1024 * 1024),
         name="update",
-    )(dom_id, spot, *pieces, *state)
+    )(dom_id, *spots, *pieces, *state)
     return tuple(results[:16]) + (results[16].reshape(()), results[17].reshape(()))
 
 

time: 92.6 us -> 81 us (0.87)
  Pallas kernels: 46.3 us -> 37 us
  local copies, waits for them, and re-layouts: 2.22 us -> 1.03 us
    pallas_call x1, Pallas kernels: 38.4 us -> 31.9 us  [run_model(): pl.pallas_call(model_kernel, grid_spec=grid_spec, out_shape=[jax.ShapeDty...]
    pallas_call x3, Pallas kernels: 2.13 us -> 0.52 us  [small_call(): pl.pallas_call(kernel, out_shape=[shape] * count if count > 1 else shape,...]
    unnamed x62 -> x56, local copies, waits for them, and re-layouts: 2.22 us -> 1.03 us
where the time goes in v4:
time: 81 us; the launch traced here: 80.9 us
  Pallas kernels  37 us (46%)
  waiting for transfers between devices  23.6 us (29%)
  starting transfers between devices  18.1 us (22%)
  between operations  1.21 us (1%)
  local copies, waits for them, and re-layouts  1.03 us (1%)
    pallas_call x1, Pallas kernels, run_model(): pl.pallas_call(model_kernel, grid_spec=grid_spec, out_shape=[jax.ShapeDty...  31.9 us
    ppermute x21, waiting for transfers between devices, crossed(): lax.ppermute(value, axis, [(i, i ^ mask) for i in range(lax.axis_size(axi...  23.6 us
    ppermute x21, starting transfers between devices, crossed(): lax.ppermute(value, axis, [(i, i ^ mask) for i in range(lax.axis_size(axi...  18.1 us
    pallas_call x1, Pallas kernels, per_device(): pl.pallas_call(update_kernel, out_shape=[jax.ShapeDtypeStruct(v.shape, f3...  2.63 us
    pallas_call x1, Pallas kernels, pack_inputs(): pl.pallas_call(pack_kernel, grid_spec=grid_spec, out_shape=jax.ShapeDtype...  1.9 us
  transfers between devices with their start and end apart: 21, of which 16 were waited for; matrix products, arithmetic and copies ran while one was open for 0% of the time, Pallas kernels for 0%

profile of v4, /device:TPU:0, one launch (start us, length us, event | category | flops | bytes accessed | tf_op | source)
XLA Modules:
  0.0 80.9 jit_solution(16773182785678815390)
XLA Ops:
  0.7 1.9 %pack.1.piece_0 = bf16[176,256]{1,0:T(8,128)(2,1)} custom-call(s32[1]{0:T(128)} %bitcast.1.section_ref, bf16[4,2048,128]{2,1,0:T(8,128)(2,1)} %feat_ref.3, s32[4,8,2048]{2,1,0:T(8,128)} %bitcast.5, s32[4,2048]{1,0:T(4,128)} %lab_ref.3, s32[4,2048]{1,0:T(4,128)} %msk_ref.3, s32[4,64]{1,0:T(4,128)} %send_ref.3, f32[16,256]{1,0:T(8,128)} %w_in.1, ...), custom_call_target="tpu_custom_call" | custom-call | tf_op jit(solution)/shard_map/pack/pallas_call | solution.py:148
  2.6 5.0 %collective-permute-start.2 = (bf16[176,256]{1,0:T(8,128)(2,1)}, bf16[176,256]{1,0:T(8,128)(2,1)S(1)}, u32[]{:S(2)}, u32[]{:S(2)}) collective-permute-start(bf16[176,256]{1,0:T(8,128)(2,1)} %pack.1.piece_0), channel_id=1, source_target_pairs={{0,6},{1,7},{2,4},{3,5},{4,2},{5,3},{6,0},{7,1},{8,14},{9,15},{10,... | collective-permute-start | bytes 270344 | tf_op jit(solution)/shard_map/ppermute | solution.py:158
  7.7 0.0 collective-permute-start.1
  7.7 0.6 collective-permute-start
  8.2 0.0 collective-permute-start.3
  8.2 3.0 %collective-permute-done.2.piece_3 = bf16[176,256]{1,0:T(8,128)(2,1)S(1)} collective-permute-done((bf16[176,256]{1,0:T(8,128)(2,1)}, bf16[176,256]{1,0:T(8,128)(2,1)S(1)}, u32[]{:S(2)}, u32[]{:S(2)}) %collective-permute-start.2) | collective-permute-done | bytes 90144 | tf_op jit(solution)/shard_map/ppermute | solution.py:158
  11.2 0.0 collective-permute-start.6
  11.2 4.2 %collective-permute-done.1.piece_2 = bf16[176,256]{1,0:T(8,128)(2,1)S(1)} collective-permute-done((bf16[176,256]{1,0:T(8,128)(2,1)}, bf16[176,256]{1,0:T(8,128)(2,1)S(1)}, u32[]{:S(2)}, u32[]{:S(2)}) %collective-permute-start.1) | collective-permute-done | bytes 90144 | tf_op jit(solution)/shard_map/ppermute | solution.py:158
  15.4 0.0 collective-permute-start.5
  15.4 0.0 collective-permute-done.piece_1
  15.4 0.5 collective-permute-start.4
  16.0 0.0 collective-permute-done.3.piece_4
  16.0 0.0 collective-permute-done.6.piece_7
  16.0 0.8 collective-permute-done.5.piece_6
  16.7 0.2 collective-permute-done.4.piece_5
  16.9 0.0 copy-start.5
  16.9 0.9 %copy-done.5 = bf16[176,256]{1,0:T(8,128)(2,1)S(1)} copy-done((bf16[176,256]{1,0:T(8,128)(2,1)S(1)}, bf16[176,256]{1,0:T(8,128)(2,1)}, u32[]{:S(2)}) %copy-start.5) | copy-done | bytes 90136
  17.8 0.0 copy-start.7
  17.8 0.0 copy-start.10
  17.9 0.0 copy-start.11
  17.9 0.0 copy-start.12
  17.9 0.0 copy-start.13
  17.9 0.0 copy-start.15
  17.9 0.0 copy-start.16
  17.9 0.0 copy-start.17
  17.9 0.0 copy-start.18
  17.9 0.0 copy-start.19
  17.9 0.0 copy-start.20
  18.0 0.0 copy-start.21
  18.0 0.0 copy-start.22
  18.0 0.0 copy-start.23
  18.0 0.0 copy-start.25
  18.0 0.0 copy-start.26
  18.0 0.0 copy-start.27
  18.0 31.9 %model.1 = (bf16[640,256]{1,0:T(8,128)(2,1)S(1)}, bf16[640,256]{1,0:T(8,128)(2,1)S(1)}) custom-call(s32[1]{0:T(128)} %bitcast.1.section_ref, s32[1]{0:T(128)} %bitcast.dom_ref.spot_ref, s32[1]{0:T(128)} %bitcast.dom_ref.spot_ref, bf16[4,2048,128]{2,1,0:T(8,128)(2,1)S(1)} %copy-done, s32[4,8,2048]{2,1,0:T(8,128)S(1)} %bitcast.6, s32[4,2048]{1,0:T(4,128)S(1)} %copy-done.8, ...), custom_call_target="tpu_custom_call" | custom-call | tf_op jit(solution)/shard_map/model/pallas_call | solution.py:602
  50.0 0.4 collective-permute-start.7
  50.4 1.3 %collective-permute-done.7.got_ref = bf16[640,256]{1,0:T(8,128)(2,1)S(1)} collective-permute-done((bf16[640,256]{1,0:T(8,128)(2,1)S(1)}, bf16[640,256]{1,0:T(8,128)(2,1)S(1)}, u32[]{:S(2)}, u32[]{:S(2)}) %collective-permute-start.7) | collective-permute-done | bytes 327712 | tf_op jit(solution)/shard_map/ppermute | solution.py:158
  51.6 0.2 split.1
  51.9 1.6 %collective-permute-start.8 = (bf16[160,256]{1,0:T(8,128)(2,1)S(1)}, bf16[160,256]{1,0:T(8,128)(2,1)S(1)}, u32[]{:S(2)}, u32[]{:S(2)}) collective-permute-start(bf16[160,256]{1,0:T(8,128)(2,1)S(1)} %get-tuple-element.45), channel_id=1, source_target_pairs={{0,8},{8,0},{16,24},{24,16},{1,9},{9,1},{17,25},{25,17},{2,10},{10... | collective-permute-start | bytes 245768 | tf_op jit(solution)/shard_map/ppermute | solution.py:158
  53.4 1.5 %collective-permute-start.9 = (bf16[160,256]{1,0:T(8,128)(2,1)S(1)}, bf16[160,256]{1,0:T(8,128)(2,1)S(1)}, u32[]{:S(2)}, u32[]{:S(2)}) collective-permute-start(bf16[160,256]{1,0:T(8,128)(2,1)S(1)} %get-tuple-element.46), channel_id=1, source_target_pairs={{0,16},{8,24},{16,0},{24,8},{1,17},{9,25},{17,1},{25,9},{2,18},{10... | collective-permute-start | bytes 245768 | tf_op jit(solution)/shard_map/ppermute | solution.py:158
  54.9 0.5 collective-permute-start.10
  55.4 1.2 %collective-permute-done.8.one_ref = bf16[160,256]{1,0:T(8,128)(2,1)S(1)} collective-permute-done((bf16[160,256]{1,0:T(8,128)(2,1)S(1)}, bf16[160,256]{1,0:T(8,128)(2,1)S(1)}, u32[]{:S(2)}, u32[]{:S(2)}) %collective-permute-start.8) | collective-permute-done | bytes 81952 | tf_op jit(solution)/shard_map/ppermute | solution.py:158
  56.6 2.0 %collective-permute-done.9.two_ref = bf16[160,256]{1,0:T(8,128)(2,1)S(1)} collective-permute-done((bf16[160,256]{1,0:T(8,128)(2,1)S(1)}, bf16[160,256]{1,0:T(8,128)(2,1)S(1)}, u32[]{:S(2)}, u32[]{:S(2)}) %collective-permute-start.9) | collective-permute-done | bytes 81952 | tf_op jit(solution)/shard_map/ppermute | solution.py:158
  58.7 1.6 %collective-permute-done.10.three_ref = bf16[160,256]{1,0:T(8,128)(2,1)S(1)} collective-permute-done((bf16[160,256]{1,0:T(8,128)(2,1)S(1)}, bf16[160,256]{1,0:T(8,128)(2,1)S(1)}, u32[]{:S(2)}, u32[]{:S(2)}) %collective-permute-start.10) | collective-permute-done | bytes 81952 | tf_op jit(solution)/shard_map/ppermute | solution.py:158
  60.3 0.2 join.2.own_ref
  60.4 2.6 %collective-permute-start.13 = (bf16[160,256]{1,0:T(8,128)(2,1)S(1)}, bf16[160,256]{1,0:T(8,128)(2,1)S(1)}, u32[]{:S(2)}, u32[]{:S(2)}) collective-permute-start(bf16[160,256]{1,0:T(8,128)(2,1)S(1)} %join.2.own_ref), channel_id=1, source_target_pairs={{0,6},{1,7},{2,4},{3,5},{4,2},{5,3},{6,0},{7,1},{8,14},{9,15},{10,... | collective-permute-start | bytes 245768 | tf_op jit(solution)/shard_map/ppermute | solution.py:158
  63.0 0.0 collective-permute-start.12
  63.0 1.8 %collective-permute-start.11 = (bf16[160,256]{1,0:T(8,128)(2,1)S(1)}, bf16[160,256]{1,0:T(8,128)(2,1)S(1)}, u32[]{:S(2)}, u32[]{:S(2)}) collective-permute-start(bf16[160,256]{1,0:T(8,128)(2,1)S(1)} %join.2.own_ref), channel_id=1, source_target_pairs={{0,2},{1,3},{2,0},{3,1},{4,6},{5,7},{6,4},{7,5},{8,10},{9,11},{10,... | collective-permute-start | bytes 245768 | tf_op jit(solution)/shard_map/ppermute | solution.py:158
  64.9 2.5 %collective-permute-done.13.three_ref = bf16[160,256]{1,0:T(8,128)(2,1)S(1)} collective-permute-done((bf16[160,256]{1,0:T(8,128)(2,1)S(1)}, bf16[160,256]{1,0:T(8,128)(2,1)S(1)}, u32[]{:S(2)}, u32[]{:S(2)}) %collective-permute-start.13) | collective-permute-done | bytes 81952 | tf_op jit(solution)/shard_map/ppermute | solution.py:158
  67.4 2.3 %collective-permute-done.12.two_ref = bf16[160,256]{1,0:T(8,128)(2,1)S(1)} collective-permute-done((bf16[160,256]{1,0:T(8,128)(2,1)S(1)}, bf16[160,256]{1,0:T(8,128)(2,1)S(1)}, u32[]{:S(2)}, u32[]{:S(2)}) %collective-permute-start.12) | collective-permute-done | bytes 81952 | tf_op jit(solution)/shard_map/ppermute | solution.py:158
  69.6 0.0 collective-permute-done.11.one_ref
  69.7 0.2 join.3.piece_0
  69.8 0.9 %collective-permute-start.16 = (bf16[160,256]{1,0:T(8,128)(2,1)S(1)}, bf16[160,256]{1,0:T(8,128)(2,1)S(1)}, u32[]{:S(2)}, u32[]{:S(2)}) collective-permute-start(bf16[160,256]{1,0:T(8,128)(2,1)S(1)} %join.3.piece_0), channel_id=1, source_target_pairs={{0,24},{8,16},{16,8},{24,0},{1,25},{9,17},{17,9},{25,1},{2,26},{10... | collective-permute-start | bytes 245768 | tf_op jit(solution)/shard_map/ppermute | solution.py:158
  70.7 1.5 %collective-permute-start.15 = (bf16[160,256]{1,0:T(8,128)(2,1)S(1)}, bf16[160,256]{1,0:T(8,128)(2,1)S(1)}, u32[]{:S(2)}, u32[]{:S(2)}) collective-permute-start(bf16[160,256]{1,0:T(8,128)(2,1)S(1)} %join.3.piece_0), channel_id=1, source_target_pairs={{0,16},{8,24},{16,0},{24,8},{1,17},{9,25},{17,1},{25,9},{2,18},{10... | collective-permute-start | bytes 245768 | tf_op jit(solution)/shard_map/ppermute | solution.py:158
  72.2 1.2 %collective-permute-start.14 = (bf16[160,256]{1,0:T(8,128)(2,1)S(1)}, bf16[160,256]{1,0:T(8,128)(2,1)S(1)}, u32[]{:S(2)}, u32[]{:S(2)}) collective-permute-start(bf16[160,256]{1,0:T(8,128)(2,1)S(1)} %join.3.piece_0), channel_id=1, source_target_pairs={{0,8},{8,0},{16,24},{24,16},{1,9},{9,1},{17,25},{25,17},{2,10},{10... | collective-permute-start | bytes 245768 | tf_op jit(solution)/shard_map/ppermute | solution.py:158
  73.3 0.0 collective-permute-start.17
  73.3 2.1 %collective-permute-done.16.piece_3 = bf16[160,256]{1,0:T(8,128)(2,1)S(1)} collective-permute-done((bf16[160,256]{1,0:T(8,128)(2,1)S(1)}, bf16[160,256]{1,0:T(8,128)(2,1)S(1)}, u32[]{:S(2)}, u32[]{:S(2)}) %collective-permute-start.16) | collective-permute-done | bytes 81952 | tf_op jit(solution)/shard_map/ppermute | solution.py:158
  75.4 0.0 collective-permute-start.20
  75.4 0.6 collective-permute-done.15.piece_2
  76.0 0.6 collective-permute-done.14.piece_1
  76.6 0.1 collective-permute-done.20.piece_7
  76.7 0.6 collective-permute-done.19.piece_6
  77.3 0.6 collective-permute-done.18.piece_5
  78.1 2.6 %update.1 = (f32[16,256]{1,0:T(8,128)}, f32[2,2,32,256]{3,2,1,0:T(8,128)}, f32[8,40]{1,0:T(8,128)}, f32[1128]{0:T(1024)}, f32[16,128]{1,0:T(8,128)}, /*index=5*/...) custom-call(s32[1]{0:T(128)} %bitcast.dom_ref.spot_ref, ...), custom_call_target="tpu_custom_call" | custom-call | tf_op jit(solution)/shard_map/update/pallas_call | solution.py:919
  (40 shorter events, 0.1 us)
Async XLA Ops:
  0.7 16.2 %copy-start.9 = (s32[4,2048]{1,0:T(4,128)S(1)}, s32[4,2048]{1,0:T(4,128)}, u32[]{:S(2)}) copy-start(s32[4,2048]{1,0:T(4,128)} %msk_ref.3) | copy-start | bytes 98308
  0.7 16.2 %copy-start.8 = (s32[4,2048]{1,0:T(4,128)S(1)}, s32[4,2048]{1,0:T(4,128)}, u32[]{:S(2)}) copy-start(s32[4,2048]{1,0:T(4,128)} %lab_ref.3) | copy-start | bytes 98308
  0.7 16.2 %copy-start.24 = (s32[4,64]{1,0:T(4,128)S(1)}, s32[4,64]{1,0:T(4,128)}, u32[]{:S(2)}) copy-start(s32[4,64]{1,0:T(4,128)} %send_ref.3) | copy-start | bytes 3076
  0.7 16.2 %copy-start = (bf16[4,2048,128]{2,1,0:T(8,128)(2,1)S(1)}, bf16[4,2048,128]{2,1,0:T(8,128)(2,1)}, u32[]{:S(2)}) copy-start(bf16[4,2048,128]{2,1,0:T(8,128)(2,1)} %feat_ref.3) | copy-start | bytes 6291460
  0.7 16.2 %copy-start.3 = (s32[4,2048,8]{1,2,0:T(8,128)S(1)}, s32[4,2048,8]{1,2,0:T(8,128)}, u32[]{:S(2)}) copy-start(s32[4,2048,8]{1,2,0:T(8,128)} %param.28) | copy-start | bytes 786436
  0.7 16.2 %copy-start.14 = (f32[1128]{0:T(1024)S(1)}, f32[1128]{0:T(1024)}, u32[]{:S(2)}) copy-start(f32[1128]{0:T(1024)} %small.1) | copy-start | bytes 13540
  2.6 8.6 %collective-permute-start.2 = (bf16[176,256]{1,0:T(8,128)(2,1)}, bf16[176,256]{1,0:T(8,128)(2,1)S(1)}, u32[]{:S(2)}, u32[]{:S(2)}) collective-permute-start(bf16[176,256]{1,0:T(8,128)(2,1)} %pack.1.piece_0), channel_id=1, source_target_pairs={{0,6},{1,7},{2,4},{3,5},{4,2},{5,3},{6,0},{7,1},{8,14},{9,15},{10,... | collective-permute-start | bytes 270344 | tf_op jit(solution)/shard_map/ppermute | solution.py:158
  7.7 7.8 %collective-permute-start.1 = (bf16[176,256]{1,0:T(8,128)(2,1)}, bf16[176,256]{1,0:T(8,128)(2,1)S(1)}, u32[]{:S(2)}, u32[]{:S(2)}) collective-permute-start(bf16[176,256]{1,0:T(8,128)(2,1)} %pack.1.piece_0), channel_id=1, source_target_pairs={{0,4},{1,5},{2,6},{3,7},{4,0},{5,1},{6,2},{7,3},{8,12},{9,13},{10,... | collective-permute-start | bytes 270344 | tf_op jit(solution)/shard_map/ppermute | solution.py:158
  7.7 7.8 %collective-permute-start = (bf16[176,256]{1,0:T(8,128)(2,1)}, bf16[176,256]{1,0:T(8,128)(2,1)S(1)}, u32[]{:S(2)}, u32[]{:S(2)}) collective-permute-start(bf16[176,256]{1,0:T(8,128)(2,1)} %pack.1.piece_0), channel_id=1, source_target_pairs={{0,2},{1,3},{2,0},{3,1},{4,6},{5,7},{6,4},{7,5},{8,10},{9,11},{10,... | collective-permute-start | bytes 270344 | tf_op jit(solution)/shard_map/ppermute | solution.py:158
  8.2 7.7 %collective-permute-start.3 = (bf16[176,256]{1,0:T(8,128)(2,1)}, bf16[176,256]{1,0:T(8,128)(2,1)S(1)}, u32[]{:S(2)}, u32[]{:S(2)}) collective-permute-start(bf16[176,256]{1,0:T(8,128)(2,1)} %pack.1.piece_0), channel_id=1, source_target_pairs={{0,1},{1,0},{2,3},{3,2},{4,5},{5,4},{6,7},{7,6},{8,9},{9,8},{10,11... | collective-permute-start | bytes 270344 | tf_op jit(solution)/shard_map/ppermute | solution.py:158
  11.2 4.7 %collective-permute-start.6 = (bf16[176,256]{1,0:T(8,128)(2,1)S(1)}, bf16[176,256]{1,0:T(8,128)(2,1)S(1)}, u32[]{:S(2)}, u32[]{:S(2)}) collective-permute-start(bf16[176,256]{1,0:T(8,128)(2,1)S(1)} %collective-permute-done.2.piece_3), channel_id=1, source_target_pairs={{0,1},{1,0},{2,3},{3,2},{4,5},{5,4},{6,7},{7,6},{8,9},{9,8},{10,11... | collective-permute-start | bytes 270344 | tf_op jit(solution)/shard_map/ppermute | solution.py:158
  15.4 1.3 %collective-permute-start.5 = (bf16[176,256]{1,0:T(8,128)(2,1)S(1)}, bf16[176,256]{1,0:T(8,128)(2,1)S(1)}, u32[]{:S(2)}, u32[]{:S(2)}) collective-permute-start(bf16[176,256]{1,0:T(8,128)(2,1)S(1)} %collective-permute-done.1.piece_2), channel_id=1, source_target_pairs={{0,1},{1,0},{2,3},{3,2},{4,5},{5,4},{6,7},{7,6},{8,9},{9,8},{10,11... | collective-permute-start | bytes 270344 | tf_op jit(solution)/shard_map/ppermute | solution.py:158
  15.4 1.4 %collective-permute-start.4 = (bf16[176,256]{1,0:T(8,128)(2,1)S(1)}, bf16[176,256]{1,0:T(8,128)(2,1)S(1)}, u32[]{:S(2)}, u32[]{:S(2)}) collective-permute-start(bf16[176,256]{1,0:T(8,128)(2,1)S(1)} %collective-permute-done.piece_1), channel_id=1, source_target_pairs={{0,1},{1,0},{2,3},{3,2},{4,5},{5,4},{6,7},{7,6},{8,9},{9,8},{10,11... | collective-permute-start | bytes 270344 | tf_op jit(solution)/shard_map/ppermute | solution.py:158
  16.9 0.9 %copy-start.5 = (bf16[176,256]{1,0:T(8,128)(2,1)S(1)}, bf16[176,256]{1,0:T(8,128)(2,1)}, u32[]{:S(2)}) copy-start(bf16[176,256]{1,0:T(8,128)(2,1)} %pack.1.piece_0) | copy-start | bytes 270340
  17.8 60.1 %copy-start.1 = (f32[2,2,256,256]{3,2,1,0:T(8,128)S(1)}, f32[2,2,256,256]{3,2,1,0:T(8,128)}, u32[]{:S(2)}) copy-start(f32[2,2,256,256]{3,2,1,0:T(8,128)} %r_gat.1) | copy-start | bytes 3145732
  17.8 60.1 %copy-start.2 = (f32[2,2,256,256]{3,2,1,0:T(8,128)S(1)}, f32[2,2,256,256]{3,2,1,0:T(8,128)}, u32[]{:S(2)}) copy-start(f32[2,2,256,256]{3,2,1,0:T(8,128)} %rr_gat.1) | copy-start | bytes 3145732
  17.8 60.1 %copy-start.4 = (f32[2,2,32,256]{3,2,1,0:T(8,128)S(1)}, f32[2,2,32,256]{3,2,1,0:T(8,128)}, u32[]{:S(2)}) copy-start(f32[2,2,32,256]{3,2,1,0:T(8,128)} %w_gat.1) | copy-start | bytes 393220
  17.8 60.1 %copy-start.6 = (f32[256,256]{1,0:T(8,128)S(1)}, f32[256,256]{1,0:T(8,128)}, u32[]{:S(2)}) copy-start(f32[256,256]{1,0:T(8,128)} %r_in.1) | copy-start | bytes 786436
  17.8 60.1 %copy-start.7 = (f32[256,256]{1,0:T(8,128)S(1)}, f32[256,256]{1,0:T(8,128)}, u32[]{:S(2)}) copy-start(f32[256,256]{1,0:T(8,128)} %rr_in.1) | copy-start | bytes 786436
  17.8 60.1 %copy-start.10 = (f32[2,2,32,256]{3,2,1,0:T(8,128)S(1)}, f32[2,2,32,256]{3,2,1,0:T(8,128)}, u32[]{:S(2)}) copy-start(f32[2,2,32,256]{3,2,1,0:T(8,128)} %l_gat.1) | copy-start | bytes 393220
  17.9 60.1 %copy-start.11 = (f32[2,2,32,256]{3,2,1,0:T(8,128)S(1)}, f32[2,2,32,256]{3,2,1,0:T(8,128)}, u32[]{:S(2)}) copy-start(f32[2,2,32,256]{3,2,1,0:T(8,128)} %rl_gat.1) | copy-start | bytes 393220
  17.9 60.1 %copy-start.12 = (f32[2,2,32,256]{3,2,1,0:T(8,128)S(1)}, f32[2,2,32,256]{3,2,1,0:T(8,128)}, u32[]{:S(2)}) copy-start(f32[2,2,32,256]{3,2,1,0:T(8,128)} %e_gat.1) | copy-start | bytes 393220
  17.9 60.1 %copy-start.13 = (f32[16,256]{1,0:T(8,128)S(1)}, f32[16,256]{1,0:T(8,128)}, u32[]{:S(2)}) copy-start(f32[16,256]{1,0:T(8,128)} %w_in.1) | copy-start | bytes 49156
  17.9 60.1 %copy-start.15 = (f32[40,40]{1,0:T(8,128)S(1)}, f32[40,40]{1,0:T(8,128)}, u32[]{:S(2)}) copy-start(f32[40,40]{1,0:T(8,128)} %r_out.1) | copy-start | bytes 19204
  17.9 60.1 %copy-start.16 = (f32[40,40]{1,0:T(8,128)S(1)}, f32[40,40]{1,0:T(8,128)}, u32[]{:S(2)}) copy-start(f32[40,40]{1,0:T(8,128)} %rr_out.1) | copy-start | bytes 19204
  17.9 60.1 %copy-start.17 = (f32[16,256]{1,0:T(8,128)S(1)}, f32[16,256]{1,0:T(8,128)}, u32[]{:S(2)}) copy-start(f32[16,256]{1,0:T(8,128)} %e_in.1) | copy-start | bytes 49156
  17.9 60.1 %copy-start.18 = (f32[8,40]{1,0:T(8,128)S(1)}, f32[8,40]{1,0:T(8,128)}, u32[]{:S(2)}) copy-start(f32[8,40]{1,0:T(8,128)} %w_out.1) | copy-start | bytes 3844
  17.9 60.1 %copy-start.19 = (f32[16,128]{1,0:T(8,128)S(1)}, f32[16,128]{1,0:T(8,128)}, u32[]{:S(2)}) copy-start(f32[16,128]{1,0:T(8,128)} %l_in.1) | copy-start | bytes 24580
  17.9 60.1 %copy-start.20 = (f32[16,128]{1,0:T(8,128)S(1)}, f32[16,128]{1,0:T(8,128)}, u32[]{:S(2)}) copy-start(f32[16,128]{1,0:T(8,128)} %rl_in.1) | copy-start | bytes 24580
  18.0 60.0 %copy-start.21 = (f32[1128]{0:T(1024)S(1)}, f32[1128]{0:T(1024)}, u32[]{:S(2)}) copy-start(f32[1128]{0:T(1024)} %first.1) | copy-start | bytes 13540
  18.0 60.0 %copy-start.22 = (f32[1128]{0:T(1024)S(1)}, f32[1128]{0:T(1024)}, u32[]{:S(2)}) copy-start(f32[1128]{0:T(1024)} %second.1) | copy-start | bytes 13540
  18.0 60.0 %copy-start.23 = (f32[1128]{0:T(1024)S(1)}, f32[1128]{0:T(1024)}, u32[]{:S(2)}) copy-start(f32[1128]{0:T(1024)} %e_small.1) | copy-start | bytes 13540
  18.0 60.0 %copy-start.25 = (f32[8,64]{1,0:T(8,128)S(1)}, f32[8,64]{1,0:T(8,128)}, u32[]{:S(2)}) copy-start(f32[8,64]{1,0:T(8,128)} %l_out.1) | copy-start | bytes 6148
  18.0 60.0 %copy-start.26 = (f32[8,64]{1,0:T(8,128)S(1)}, f32[8,64]{1,0:T(8,128)}, u32[]{:S(2)}) copy-start(f32[8,64]{1,0:T(8,128)} %rl_out.1) | copy-start | bytes 6148
  18.0 60.0 %copy-start.27 = (f32[8,40]{1,0:T(8,128)S(1)}, f32[8,40]{1,0:T(8,128)}, u32[]{:S(2)}) copy-start(f32[8,40]{1,0:T(8,128)} %e_out.1) | copy-start | bytes 3844
  50.0 1.7 %collective-permute-start.7 = (bf16[640,256]{1,0:T(8,128)(2,1)S(1)}, bf16[640,256]{1,0:T(8,128)(2,1)S(1)}, u32[]{:S(2)}, u32[]{:S(2)}) collective-permute-start(bf16[640,256]{1,0:T(8,128)(2,1)S(1)} %get-tuple-element.43), channel_id=1, source_target_pairs={{0,1},{1,0},{2,3},{3,2},{4,5},{5,4},{6,7},{7,6},{8,9},{9,8},{10,11... | collective-permute-start | bytes 983048 | tf_op jit(solution)/shard_map/ppermute | solution.py:158
  51.9 4.8 %collective-permute-start.8 = (bf16[160,256]{1,0:T(8,128)(2,1)S(1)}, bf16[160,256]{1,0:T(8,128)(2,1)S(1)}, u32[]{:S(2)}, u32[]{:S(2)}) collective-permute-start(bf16[160,256]{1,0:T(8,128)(2,1)S(1)} %get-tuple-element.45), channel_id=1, source_target_pairs={{0,8},{8,0},{16,24},{24,16},{1,9},{9,1},{17,25},{25,17},{2,10},{10... | collective-permute-start | bytes 245768 | tf_op jit(solution)/shard_map/ppermute | solution.py:158
  53.4 5.3 %collective-permute-start.9 = (bf16[160,256]{1,0:T(8,128)(2,1)S(1)}, bf16[160,256]{1,0:T(8,128)(2,1)S(1)}, u32[]{:S(2)}, u32[]{:S(2)}) collective-permute-start(bf16[160,256]{1,0:T(8,128)(2,1)S(1)} %get-tuple-element.46), channel_id=1, source_target_pairs={{0,16},{8,24},{16,0},{24,8},{1,17},{9,25},{17,1},{25,9},{2,18},{10... | collective-permute-start | bytes 245768 | tf_op jit(solution)/shard_map/ppermute | solution.py:158
  54.9 5.3 %collective-permute-start.10 = (bf16[160,256]{1,0:T(8,128)(2,1)S(1)}, bf16[160,256]{1,0:T(8,128)(2,1)S(1)}, u32[]{:S(2)}, u32[]{:S(2)}) collective-permute-start(bf16[160,256]{1,0:T(8,128)(2,1)S(1)} %get-tuple-element.47), channel_id=1, source_target_pairs={{0,24},{8,16},{16,8},{24,0},{1,25},{9,17},{17,9},{25,1},{2,26},{10... | collective-permute-start | bytes 245768 | tf_op jit(solution)/shard_map/ppermute | solution.py:158
  60.4 6.9 %collective-permute-start.13 = (bf16[160,256]{1,0:T(8,128)(2,1)S(1)}, bf16[160,256]{1,0:T(8,128)(2,1)S(1)}, u32[]{:S(2)}, u32[]{:S(2)}) collective-permute-start(bf16[160,256]{1,0:T(8,128)(2,1)S(1)} %join.2.own_ref), channel_id=1, source_target_pairs={{0,6},{1,7},{2,4},{3,5},{4,2},{5,3},{6,0},{7,1},{8,14},{9,15},{10,... | collective-permute-start | bytes 245768 | tf_op jit(solution)/shard_map/ppermute | solution.py:158
  63.0 6.6 %collective-permute-start.12 = (bf16[160,256]{1,0:T(8,128)(2,1)S(1)}, bf16[160,256]{1,0:T(8,128)(2,1)S(1)}, u32[]{:S(2)}, u32[]{:S(2)}) collective-permute-start(bf16[160,256]{1,0:T(8,128)(2,1)S(1)} %join.2.own_ref), channel_id=1, source_target_pairs={{0,4},{1,5},{2,6},{3,7},{4,0},{5,1},{6,2},{7,3},{8,12},{9,13},{10,... | collective-permute-start | bytes 245768 | tf_op jit(solution)/shard_map/ppermute | solution.py:158
  63.0 6.6 %collective-permute-start.11 = (bf16[160,256]{1,0:T(8,128)(2,1)S(1)}, bf16[160,256]{1,0:T(8,128)(2,1)S(1)}, u32[]{:S(2)}, u32[]{:S(2)}) collective-permute-start(bf16[160,256]{1,0:T(8,128)(2,1)S(1)} %join.2.own_ref), channel_id=1, source_target_pairs={{0,2},{1,3},{2,0},{3,1},{4,6},{5,7},{6,4},{7,5},{8,10},{9,11},{10,... | collective-permute-start | bytes 245768 | tf_op jit(solution)/shard_map/ppermute | solution.py:158
  69.8 5.6 %collective-permute-start.16 = (bf16[160,256]{1,0:T(8,128)(2,1)S(1)}, bf16[160,256]{1,0:T(8,128)(2,1)S(1)}, u32[]{:S(2)}, u32[]{:S(2)}) collective-permute-start(bf16[160,256]{1,0:T(8,128)(2,1)S(1)} %join.3.piece_0), channel_id=1, source_target_pairs={{0,24},{8,16},{16,8},{24,0},{1,25},{9,17},{17,9},{25,1},{2,26},{10... | collective-permute-start | bytes 245768 | tf_op jit(solution)/shard_map/ppermute | solution.py:158
  70.7 5.3 %collective-permute-start.15 = (bf16[160,256]{1,0:T(8,128)(2,1)S(1)}, bf16[160,256]{1,0:T(8,128)(2,1)S(1)}, u32[]{:S(2)}, u32[]{:S(2)}) collective-permute-start(bf16[160,256]{1,0:T(8,128)(2,1)S(1)} %join.3.piece_0), channel_id=1, source_target_pairs={{0,16},{8,24},{16,0},{24,8},{1,17},{9,25},{17,1},{25,9},{2,18},{10... | collective-permute-start | bytes 245768 | tf_op jit(solution)/shard_map/ppermute | solution.py:158
  72.2 4.4 %collective-permute-start.14 = (bf16[160,256]{1,0:T(8,128)(2,1)S(1)}, bf16[160,256]{1,0:T(8,128)(2,1)S(1)}, u32[]{:S(2)}, u32[]{:S(2)}) collective-permute-start(bf16[160,256]{1,0:T(8,128)(2,1)S(1)} %join.3.piece_0), channel_id=1, source_target_pairs={{0,8},{8,0},{16,24},{24,16},{1,9},{9,1},{17,25},{25,17},{2,10},{10... | collective-permute-start | bytes 245768 | tf_op jit(solution)/shard_map/ppermute | solution.py:158
  73.3 3.3 %collective-permute-start.17 = (bf16[160,256]{1,0:T(8,128)(2,1)S(1)}, bf16[160,256]{1,0:T(8,128)(2,1)S(1)}, u32[]{:S(2)}, u32[]{:S(2)}) collective-permute-start(bf16[160,256]{1,0:T(8,128)(2,1)S(1)} %join.3.piece_0), channel_id=1, source_target_pairs={{0,1},{1,0},{2,3},{3,2},{4,5},{5,4},{6,7},{7,6},{8,9},{9,8},{10,11... | collective-permute-start | bytes 245768 | tf_op jit(solution)/shard_map/ppermute | solution.py:158
  75.4 1.3 %collective-permute-start.20 = (bf16[160,256]{1,0:T(8,128)(2,1)S(1)}, bf16[160,256]{1,0:T(8,128)(2,1)S(1)}, u32[]{:S(2)}, u32[]{:S(2)}) collective-permute-start(bf16[160,256]{1,0:T(8,128)(2,1)S(1)} %collective-permute-done.16.piece_3), channel_id=1, source_target_pairs={{0,1},{1,0},{2,3},{3,2},{4,5},{5,4},{6,7},{7,6},{8,9},{9,8},{10,11... | collective-permute-start | bytes 245768 | tf_op jit(solution)/shard_map/ppermute | solution.py:158
  76.0 1.3 %collective-permute-start.19 = (bf16[160,256]{1,0:T(8,128)(2,1)S(1)}, bf16[160,256]{1,0:T(8,128)(2,1)S(1)}, u32[]{:S(2)}, u32[]{:S(2)}) collective-permute-start(bf16[160,256]{1,0:T(8,128)(2,1)S(1)} %collective-permute-done.15.piece_2), channel_id=1, source_target_pairs={{0,1},{1,0},{2,3},{3,2},{4,5},{5,4},{6,7},{7,6},{8,9},{9,8},{10,11... | collective-permute-start | bytes 245768 | tf_op jit(solution)/shard_map/ppermute | solution.py:158
  76.6 1.3 %collective-permute-start.18 = (bf16[160,256]{1,0:T(8,128)(2,1)S(1)}, bf16[160,256]{1,0:T(8,128)(2,1)S(1)}, u32[]{:S(2)}, u32[]{:S(2)}) collective-permute-start(bf16[160,256]{1,0:T(8,128)(2,1)S(1)} %collective-permute-done.14.piece_1), channel_id=1, source_target_pairs={{0,1},{1,0},{2,3},{3,2},{4,5},{5,4},{6,7},{7,6},{8,9},{9,8},{10,11... | collective-permute-start | bytes 245768 | tf_op jit(solution)/shard_map/ppermute | solution.py:158

commit v5 on v4

--- a/solution.py
+++ b/solution.py
@@ -149,7 +149,7 @@
         pack_kernel,
         grid_spec=grid_spec,
         out_shape=jax.ShapeDtypeStruct((HALO_G, HID), bf16),
-        compiler_params=pltpu.CompilerParams(vmem_limit_bytes=60 * 1024 * 1024),
+        compiler_params=pltpu.CompilerParams(vmem_limit_bytes=58 * 1024 * 1024),
         name="pack",
     )(section_id, features, src_all, labels, label_mask, send_index, w_in, w_gat, w_out)
 
@@ -360,8 +360,8 @@
         at = lanes_of(c, chunk)
         pre = dot_nt(wi_t, node_ref[at, :]) + bias_in
         grown = jnp.exp(jnp.minimum(pre, 0.0))
-        h_ref[0, :, at] = jnp.where(pre > 0, pre, grown - 1.0).astype(bf16)
-        slope_ref[0, :, at] = jnp.where(pre > 0, 1.0, grown)
+        h_ref[0, :, at] = (jnp.maximum(pre, 0.0) + (grown - 1.0)).astype(bf16)
+        slope_ref[0, :, at] = grown
 
     wide_spots = lax.broadcasted_iota(jnp.int32, (LANES, LANES), 0).astype(f32).astype(bf16)
     wide_spots = wide_spots.reshape(8, 16, LANES)
@@ -394,7 +394,12 @@
             for u in ways:
                 right = both_ref[layer, HID : 2 * HID, ats[u]]
                 left_f = left[u].astype(f32)
-                mixed_rows = jnp.concatenate([jnp.take_along_axis(left_f, jnp.broadcast_to(edge_ref[k : k + 1, ats[u]], (HID, LANES)), axis=1, mode='promise_in_bounds').astype(bf16) for k in range(DEG)],axis=1)
+                mixed_rows = [dot_nn(left[u], e_ref[ids[u], :, 0 : 2 * LANES]).astype(bf16)]
+                for k in range(2, DEG):
+                    index = jnp.broadcast_to(edge_ref[k : k + 1, ats[u]], (HID, LANES))
+                    picked = jnp.take_along_axis(left_f, index, axis=1, mode="promise_in_bounds")
+                    mixed_rows.append(picked.astype(bf16))
+                mixed_rows = jnp.concatenate(mixed_rows, axis=1)
                 mixed_rows = mixed_rows + jnp.concatenate([right] * DEG, axis=1)
                 own = left[u] + right
                 t_ref[layer, ids[u], :, 0:mixed] = mixed_rows
@@ -434,8 +439,8 @@
                     if layer == 0:
                         pre = total + bias_one[head_of(h)]
                         grown_one = jnp.exp(jnp.minimum(pre, 0.0))
-                        h_ref[1, head_of(h), ats[u]] = jnp.where(pre > 0, pre, grown_one - 1.0).astype(bf16)
-                        slope_ref[1, head_of(h), ats[u]] = jnp.where(pre > 0, 1.0, grown_one)
+                        h_ref[1, head_of(h), ats[u]] = (jnp.maximum(pre, 0.0) + (grown_one - 1.0)).astype(bf16)
+                        slope_ref[1, head_of(h), ats[u]] = grown_one
                     else:
                         rounded = total.astype(bf16).astype(f32)
                         pooled = rounded if pooled is None else pooled + rounded
@@ -525,12 +530,13 @@
             out_ref[start : start + HID, :] = dot_nt(
                 h_ref[layer], both_ref[1 + layer, side * HID : (side + 1) * HID, :]
             ).astype(bf16)
-    out_ref[ROW_IN : ROW_IN + FEAT, :] = dot_nn(do_ref[...], node_ref[...]).T.astype(bf16)
+    ones = jnp.ones((nodes, LANES), bf16)
+    with_sums = dot_nn(do_ref[...], jnp.concatenate([node_ref[...], ones], axis=1))
+    out_ref[ROW_IN : ROW_IN + FEAT, :] = with_sums[:, 0:FEAT].T.astype(bf16)
     out_ref[ROW_OUT : ROW_OUT + HSIZE, :] = jnp.zeros((HSIZE, HID), bf16)
     out_ref[ROW_OUT : ROW_OUT + HSIZE, 0:CLASSES] = dot_nt(pool_ref[...], dlog_ref[...]).astype(bf16)
-    ones = jnp.ones((nodes, LANES), bf16)
     lane_wide = lax.broadcasted_iota(jnp.int32, (HID, LANES), 1)
-    columns = jnp.where(lane_wide == 0, dot_nn(do_ref[...], ones), 0.0)
+    columns = jnp.where(lane_wide == 0, with_sums[:, FEAT:], 0.0)
     for layer in range(2):
         da = jnp.sum(da_ref[layer], axis=1, keepdims=True)
         columns = columns + jnp.where(lane_wide == 1 + layer, da, 0.0)
@@ -588,6 +594,9 @@
         pltpu.VMEM((LANES, DEG * LANES), bf16),
         pltpu.VMEM((GROUPS, 32, HID), bf16),
     ]
+    def body(*refs):
+        pl.run_scoped(lambda *buffers: model_kernel(*refs, *buffers), *scratch)
+
     grid_spec = pltpu.PrefetchScalarGridSpec(
         num_scalar_prefetch=3,
         grid=(1,),
@@ -597,10 +606,9 @@
         ]
         + vmem(12),
         out_specs=vmem(2),
-        scratch_shapes=scratch,
     )
     return pl.pallas_call(
-        model_kernel,
+        body,
         grid_spec=grid_spec,
         out_shape=[jax.ShapeDtypeStruct((ROWS // 2, HID), bf16)] * 2,
         compiler_params=pltpu.CompilerParams(vmem_limit_bytes=50 * 1024 * 1024),

time: 81 us -> 74.9 us (0.925)
  Pallas kernels: 37 us -> 30.8 us
    pallas_call x1, Pallas kernels: 31.9 us -> 25.8 us  [run_model(): pl.pallas_call(body, grid_spec=grid_spec, out_shape=[jax.ShapeDtypeStruct...]
where the time goes in v5:
time: 74.9 us; the launch traced here: 74.7 us
  Pallas kernels  30.8 us (41%)
  waiting for transfers between devices  23.7 us (32%)
  starting transfers between devices  18.1 us (24%)
  between operations  1.05 us (1%)
  local copies, waits for them, and re-layouts  1.03 us (1%)
    pallas_call x1, Pallas kernels, run_model(): pl.pallas_call(body, grid_spec=grid_spec, out_shape=[jax.ShapeDtypeStruct...  25.8 us
    ppermute x21, waiting for transfers between devices, crossed(): lax.ppermute(value, axis, [(i, i ^ mask) for i in range(lax.axis_size(axi...  23.7 us
    ppermute x21, starting transfers between devices, crossed(): lax.ppermute(value, axis, [(i, i ^ mask) for i in range(lax.axis_size(axi...  18.1 us
    pallas_call x1, Pallas kernels, per_device(): pl.pallas_call(update_kernel, out_shape=[jax.ShapeDtypeStruct(v.shape, f3...  2.63 us
    pallas_call x1, Pallas kernels, pack_inputs(): pl.pallas_call(pack_kernel, grid_spec=grid_spec, out_shape=jax.ShapeDtype...  1.9 us
  transfers between devices with their start and end apart: 21, of which 16 were waited for; matrix products, arithmetic and copies ran while one was open for 0% of the time, Pallas kernels for 0%

profile of v5, /device:TPU:0, one launch (start us, length us, event | category | flops | bytes accessed | tf_op | source)
XLA Modules:
  0.0 74.7 jit_solution(4909040932679696463)
XLA Ops:
  0.7 1.9 %pack.1.refs_8_ = bf16[176,256]{1,0:T(8,128)(2,1)} custom-call(s32[1]{0:T(128)} %bitcast.1.section_ref.refs_0_, bf16[4,2048,128]{2,1,0:T(8,128)(2,1)} %refs_3_.1, s32[4,8,2048]{2,1,0:T(8,128)} %bitcast.5, s32[4,2048]{1,0:T(4,128)} %refs_5_.1, s32[4,2048]{1,0:T(4,128)} %refs_6_.1, s32[4,64]{1,0:T(4,128)} %refs_7_.1, f32[16,256]{1,0:T(8,128)} %w_in.1, ...), custom_call_target="tpu_custom_call" | custom-call | tf_op jit(solution)/shard_map/pack/pallas_call | solution.py:148
  2.6 5.0 %collective-permute-start.2 = (bf16[176,256]{1,0:T(8,128)(2,1)}, bf16[176,256]{1,0:T(8,128)(2,1)S(1)}, u32[]{:S(2)}, u32[]{:S(2)}) collective-permute-start(bf16[176,256]{1,0:T(8,128)(2,1)} %pack.1.refs_8_), channel_id=1, source_target_pairs={{0,6},{1,7},{2,4},{3,5},{4,2},{5,3},{6,0},{7,1},{8,14},{9,15},{10,... | collective-permute-start | bytes 270344 | tf_op jit(solution)/shard_map/ppermute | solution.py:158
  7.7 0.0 collective-permute-start.1
  7.7 0.6 collective-permute-start
  8.2 0.0 collective-permute-start.3
  8.2 3.0 %collective-permute-done.2.refs_11_ = bf16[176,256]{1,0:T(8,128)(2,1)S(1)} collective-permute-done((bf16[176,256]{1,0:T(8,128)(2,1)}, bf16[176,256]{1,0:T(8,128)(2,1)S(1)}, u32[]{:S(2)}, u32[]{:S(2)}) %collective-permute-start.2) | collective-permute-done | bytes 90144 | tf_op jit(solution)/shard_map/ppermute | solution.py:158
  11.2 0.0 collective-permute-start.6
  11.2 4.2 %collective-permute-done.1.refs_10_ = bf16[176,256]{1,0:T(8,128)(2,1)S(1)} collective-permute-done((bf16[176,256]{1,0:T(8,128)(2,1)}, bf16[176,256]{1,0:T(8,128)(2,1)S(1)}, u32[]{:S(2)}, u32[]{:S(2)}) %collective-permute-start.1) | collective-permute-done | bytes 90144 | tf_op jit(solution)/shard_map/ppermute | solution.py:158
  15.4 0.0 collective-permute-start.5
  15.4 0.0 collective-permute-done.refs_9_
  15.4 0.5 collective-permute-start.4
  16.0 0.8 %collective-permute-done.5.refs_14_ = bf16[176,256]{1,0:T(8,128)(2,1)S(1)} collective-permute-done((bf16[176,256]{1,0:T(8,128)(2,1)S(1)}, bf16[176,256]{1,0:T(8,128)(2,1)S(1)}, u32[]{:S(2)}, u32[]{:S(2)}) %collective-permute-start.5) | collective-permute-done | bytes 90144 | tf_op jit(solution)/shard_map/ppermute | solution.py:158
  16.7 0.2 collective-permute-done.4.refs_13_
  16.9 0.0 copy-start.5
  16.9 0.9 %copy-done.5 = bf16[176,256]{1,0:T(8,128)(2,1)S(1)} copy-done((bf16[176,256]{1,0:T(8,128)(2,1)S(1)}, bf16[176,256]{1,0:T(8,128)(2,1)}, u32[]{:S(2)}) %copy-start.5) | copy-done | bytes 90136
  17.8 0.0 copy-start.7
  17.8 0.0 copy-start.10
  17.9 0.0 copy-start.11
  17.9 0.0 copy-start.12
  17.9 0.0 copy-start.13
  17.9 0.0 copy-start.15
  17.9 0.0 copy-start.16
  17.9 0.0 copy-start.17
  17.9 0.0 copy-start.18
  17.9 0.0 copy-start.19
  17.9 0.0 copy-start.20
  18.0 0.0 copy-start.21
  18.0 0.0 copy-start.22
  18.0 0.0 copy-start.23
  18.0 0.0 copy-start.25
  18.0 0.0 copy-start.26
  18.0 0.0 copy-start.27
  18.0 25.8 %model.1 = (bf16[640,256]{1,0:T(8,128)(2,1)S(1)}, bf16[640,256]{1,0:T(8,128)(2,1)S(1)}) custom-call(s32[1]{0:T(128)} %bitcast.1.section_ref.refs_0_, s32[1]{0:T(128)} %bitcast.refs_1_.refs_2_.dom_ref.spot_ref, s32[1]{0:T(128)} %bitcast.refs_1_.refs_2_.dom_ref.spot_ref, bf16[4,2048,128]{2,1,0:T(8,128)(2,1)S(1)} %copy-done, s32[4,8,2048]{2,1,0:T(8,128)S(1)} %bitcast.6, ...), custom_call_target="tpu_custom_call" | custom-call | tf_op jit(solution)/shard_map/model/pallas_call | solution.py:610
  43.8 0.4 collective-permute-start.7
  44.3 1.3 %collective-permute-done.7.got_ref = bf16[640,256]{1,0:T(8,128)(2,1)S(1)} collective-permute-done((bf16[640,256]{1,0:T(8,128)(2,1)S(1)}, bf16[640,256]{1,0:T(8,128)(2,1)S(1)}, u32[]{:S(2)}, u32[]{:S(2)}) %collective-permute-start.7) | collective-permute-done | bytes 327712 | tf_op jit(solution)/shard_map/ppermute | solution.py:158
  45.5 0.2 split.1
  45.7 1.6 %collective-permute-start.8 = (bf16[160,256]{1,0:T(8,128)(2,1)S(1)}, bf16[160,256]{1,0:T(8,128)(2,1)S(1)}, u32[]{:S(2)}, u32[]{:S(2)}) collective-permute-start(bf16[160,256]{1,0:T(8,128)(2,1)S(1)} %get-tuple-element.45), channel_id=1, source_target_pairs={{0,8},{8,0},{16,24},{24,16},{1,9},{9,1},{17,25},{25,17},{2,10},{10... | collective-permute-start | bytes 245768 | tf_op jit(solution)/shard_map/ppermute | solution.py:158
  47.3 1.5 %collective-permute-start.9 = (bf16[160,256]{1,0:T(8,128)(2,1)S(1)}, bf16[160,256]{1,0:T(8,128)(2,1)S(1)}, u32[]{:S(2)}, u32[]{:S(2)}) collective-permute-start(bf16[160,256]{1,0:T(8,128)(2,1)S(1)} %get-tuple-element.46), channel_id=1, source_target_pairs={{0,16},{8,24},{16,0},{24,8},{1,17},{9,25},{17,1},{25,9},{2,18},{10... | collective-permute-start | bytes 245768 | tf_op jit(solution)/shard_map/ppermute | solution.py:158
  48.8 0.5 collective-permute-start.10
  49.3 1.2 %collective-permute-done.8.one_ref = bf16[160,256]{1,0:T(8,128)(2,1)S(1)} collective-permute-done((bf16[160,256]{1,0:T(8,128)(2,1)S(1)}, bf16[160,256]{1,0:T(8,128)(2,1)S(1)}, u32[]{:S(2)}, u32[]{:S(2)}) %collective-permute-start.8) | collective-permute-done | bytes 81952 | tf_op jit(solution)/shard_map/ppermute | solution.py:158
  50.5 2.1 %collective-permute-done.9.two_ref = bf16[160,256]{1,0:T(8,128)(2,1)S(1)} collective-permute-done((bf16[160,256]{1,0:T(8,128)(2,1)S(1)}, bf16[160,256]{1,0:T(8,128)(2,1)S(1)}, u32[]{:S(2)}, u32[]{:S(2)}) %collective-permute-start.9) | collective-permute-done | bytes 81952 | tf_op jit(solution)/shard_map/ppermute | solution.py:158
  52.6 1.6 %collective-permute-done.10.three_ref = bf16[160,256]{1,0:T(8,128)(2,1)S(1)} collective-permute-done((bf16[160,256]{1,0:T(8,128)(2,1)S(1)}, bf16[160,256]{1,0:T(8,128)(2,1)S(1)}, u32[]{:S(2)}, u32[]{:S(2)}) %collective-permute-start.10) | collective-permute-done | bytes 81952 | tf_op jit(solution)/shard_map/ppermute | solution.py:158
  54.1 0.2 join.2.own_ref
  54.3 2.6 %collective-permute-start.13 = (bf16[160,256]{1,0:T(8,128)(2,1)S(1)}, bf16[160,256]{1,0:T(8,128)(2,1)S(1)}, u32[]{:S(2)}, u32[]{:S(2)}) collective-permute-start(bf16[160,256]{1,0:T(8,128)(2,1)S(1)} %join.2.own_ref), channel_id=1, source_target_pairs={{0,6},{1,7},{2,4},{3,5},{4,2},{5,3},{6,0},{7,1},{8,14},{9,15},{10,... | collective-permute-start | bytes 245768 | tf_op jit(solution)/shard_map/ppermute | solution.py:158
  56.9 0.0 collective-permute-start.12
  56.9 1.9 %collective-permute-start.11 = (bf16[160,256]{1,0:T(8,128)(2,1)S(1)}, bf16[160,256]{1,0:T(8,128)(2,1)S(1)}, u32[]{:S(2)}, u32[]{:S(2)}) collective-permute-start(bf16[160,256]{1,0:T(8,128)(2,1)S(1)} %join.2.own_ref), channel_id=1, source_target_pairs={{0,2},{1,3},{2,0},{3,1},{4,6},{5,7},{6,4},{7,5},{8,10},{9,11},{10,... | collective-permute-start | bytes 245768 | tf_op jit(solution)/shard_map/ppermute | solution.py:158
  58.7 2.5 %collective-permute-done.13.three_ref = bf16[160,256]{1,0:T(8,128)(2,1)S(1)} collective-permute-done((bf16[160,256]{1,0:T(8,128)(2,1)S(1)}, bf16[160,256]{1,0:T(8,128)(2,1)S(1)}, u32[]{:S(2)}, u32[]{:S(2)}) %collective-permute-start.13) | collective-permute-done | bytes 81952 | tf_op jit(solution)/shard_map/ppermute | solution.py:158
  61.2 2.3 %collective-permute-done.12.two_ref = bf16[160,256]{1,0:T(8,128)(2,1)S(1)} collective-permute-done((bf16[160,256]{1,0:T(8,128)(2,1)S(1)}, bf16[160,256]{1,0:T(8,128)(2,1)S(1)}, u32[]{:S(2)}, u32[]{:S(2)}) %collective-permute-start.12) | collective-permute-done | bytes 81952 | tf_op jit(solution)/shard_map/ppermute | solution.py:158
  63.5 0.0 collective-permute-done.11.one_ref
  63.5 0.2 join.3.piece_0
  63.7 1.1 %collective-permute-start.16 = (bf16[160,256]{1,0:T(8,128)(2,1)S(1)}, bf16[160,256]{1,0:T(8,128)(2,1)S(1)}, u32[]{:S(2)}, u32[]{:S(2)}) collective-permute-start(bf16[160,256]{1,0:T(8,128)(2,1)S(1)} %join.3.piece_0), channel_id=1, source_target_pairs={{0,24},{8,16},{16,8},{24,0},{1,25},{9,17},{17,9},{25,1},{2,26},{10... | collective-permute-start | bytes 245768 | tf_op jit(solution)/shard_map/ppermute | solution.py:158
  64.8 1.4 %collective-permute-start.15 = (bf16[160,256]{1,0:T(8,128)(2,1)S(1)}, bf16[160,256]{1,0:T(8,128)(2,1)S(1)}, u32[]{:S(2)}, u32[]{:S(2)}) collective-permute-start(bf16[160,256]{1,0:T(8,128)(2,1)S(1)} %join.3.piece_0), channel_id=1, source_target_pairs={{0,16},{8,24},{16,0},{24,8},{1,17},{9,25},{17,1},{25,9},{2,18},{10... | collective-permute-start | bytes 245768 | tf_op jit(solution)/shard_map/ppermute | solution.py:158
  66.2 1.0 %collective-permute-start.14 = (bf16[160,256]{1,0:T(8,128)(2,1)S(1)}, bf16[160,256]{1,0:T(8,128)(2,1)S(1)}, u32[]{:S(2)}, u32[]{:S(2)}) collective-permute-start(bf16[160,256]{1,0:T(8,128)(2,1)S(1)} %join.3.piece_0), channel_id=1, source_target_pairs={{0,8},{8,0},{16,24},{24,16},{1,9},{9,1},{17,25},{25,17},{2,10},{10... | collective-permute-start | bytes 245768 | tf_op jit(solution)/shard_map/ppermute | solution.py:158
  67.2 0.0 collective-permute-start.17
  67.2 2.2 %collective-permute-done.16.piece_3 = bf16[160,256]{1,0:T(8,128)(2,1)S(1)} collective-permute-done((bf16[160,256]{1,0:T(8,128)(2,1)S(1)}, bf16[160,256]{1,0:T(8,128)(2,1)S(1)}, u32[]{:S(2)}, u32[]{:S(2)}) %collective-permute-start.16) | collective-permute-done | bytes 81952 | tf_op jit(solution)/shard_map/ppermute | solution.py:158
  69.5 0.6 collective-permute-done.15.piece_2
  70.0 0.0 collective-permute-start.19
  70.0 0.6 collective-permute-done.14.piece_1
  70.6 0.0 collective-permute-start.18
  70.6 0.0 collective-permute-done.17.piece_4
  70.6 0.1 collective-permute-done.20.piece_7
  70.7 0.6 collective-permute-done.19.piece_6
  71.3 0.6 collective-permute-done.18.piece_5
  72.1 2.6 %update.1 = (f32[16,256]{1,0:T(8,128)}, f32[2,2,32,256]{3,2,1,0:T(8,128)}, f32[8,40]{1,0:T(8,128)}, f32[1128]{0:T(1024)}, f32[16,128]{1,0:T(8,128)}, /*index=5*/...) custom-call(s32[1]{0:T(128)} %bitcast.refs_1_.refs_2_.dom_ref.spot_r, ...), custom_call_target="tpu_custom_call" | custom-call | tf_op jit(solution)/shard_map/update/pallas_call | solution.py:927
  (40 shorter events, 0.1 us)
Async XLA Ops:
  0.7 16.2 %copy-start.9 = (s32[4,2048]{1,0:T(4,128)S(1)}, s32[4,2048]{1,0:T(4,128)}, u32[]{:S(2)}) copy-start(s32[4,2048]{1,0:T(4,128)} %refs_6_.1) | copy-start | bytes 98308
  0.7 16.2 %copy-start.8 = (s32[4,2048]{1,0:T(4,128)S(1)}, s32[4,2048]{1,0:T(4,128)}, u32[]{:S(2)}) copy-start(s32[4,2048]{1,0:T(4,128)} %refs_5_.1) | copy-start | bytes 98308
  0.7 16.2 %copy-start.24 = (s32[4,64]{1,0:T(4,128)S(1)}, s32[4,64]{1,0:T(4,128)}, u32[]{:S(2)}) copy-start(s32[4,64]{1,0:T(4,128)} %refs_7_.1) | copy-start | bytes 3076
  0.7 16.2 %copy-start = (bf16[4,2048,128]{2,1,0:T(8,128)(2,1)S(1)}, bf16[4,2048,128]{2,1,0:T(8,128)(2,1)}, u32[]{:S(2)}) copy-start(bf16[4,2048,128]{2,1,0:T(8,128)(2,1)} %refs_3_.1) | copy-start | bytes 6291460
  0.7 16.2 %copy-start.3 = (s32[4,2048,8]{1,2,0:T(8,128)S(1)}, s32[4,2048,8]{1,2,0:T(8,128)}, u32[]{:S(2)}) copy-start(s32[4,2048,8]{1,2,0:T(8,128)} %param.28) | copy-start | bytes 786436
  0.7 16.2 %copy-start.14 = (f32[1128]{0:T(1024)S(1)}, f32[1128]{0:T(1024)}, u32[]{:S(2)}) copy-start(f32[1128]{0:T(1024)} %small.1) | copy-start | bytes 13540
  2.6 8.6 %collective-permute-start.2 = (bf16[176,256]{1,0:T(8,128)(2,1)}, bf16[176,256]{1,0:T(8,128)(2,1)S(1)}, u32[]{:S(2)}, u32[]{:S(2)}) collective-permute-start(bf16[176,256]{1,0:T(8,128)(2,1)} %pack.1.refs_8_), channel_id=1, source_target_pairs={{0,6},{1,7},{2,4},{3,5},{4,2},{5,3},{6,0},{7,1},{8,14},{9,15},{10,... | collective-permute-start | bytes 270344 | tf_op jit(solution)/shard_map/ppermute | solution.py:158
  7.7 7.8 %collective-permute-start.1 = (bf16[176,256]{1,0:T(8,128)(2,1)}, bf16[176,256]{1,0:T(8,128)(2,1)S(1)}, u32[]{:S(2)}, u32[]{:S(2)}) collective-permute-start(bf16[176,256]{1,0:T(8,128)(2,1)} %pack.1.refs_8_), channel_id=1, source_target_pairs={{0,4},{1,5},{2,6},{3,7},{4,0},{5,1},{6,2},{7,3},{8,12},{9,13},{10,... | collective-permute-start | bytes 270344 | tf_op jit(solution)/shard_map/ppermute | solution.py:158
  7.7 7.8 %collective-permute-start = (bf16[176,256]{1,0:T(8,128)(2,1)}, bf16[176,256]{1,0:T(8,128)(2,1)S(1)}, u32[]{:S(2)}, u32[]{:S(2)}) collective-permute-start(bf16[176,256]{1,0:T(8,128)(2,1)} %pack.1.refs_8_), channel_id=1, source_target_pairs={{0,2},{1,3},{2,0},{3,1},{4,6},{5,7},{6,4},{7,5},{8,10},{9,11},{10,... | collective-permute-start | bytes 270344 | tf_op jit(solution)/shard_map/ppermute | solution.py:158
  8.2 7.7 %collective-permute-start.3 = (bf16[176,256]{1,0:T(8,128)(2,1)}, bf16[176,256]{1,0:T(8,128)(2,1)S(1)}, u32[]{:S(2)}, u32[]{:S(2)}) collective-permute-start(bf16[176,256]{1,0:T(8,128)(2,1)} %pack.1.refs_8_), channel_id=1, source_target_pairs={{0,1},{1,0},{2,3},{3,2},{4,5},{5,4},{6,7},{7,6},{8,9},{9,8},{10,11... | collective-permute-start | bytes 270344 | tf_op jit(solution)/shard_map/ppermute | solution.py:158
  11.2 4.7 %collective-permute-start.6 = (bf16[176,256]{1,0:T(8,128)(2,1)S(1)}, bf16[176,256]{1,0:T(8,128)(2,1)S(1)}, u32[]{:S(2)}, u32[]{:S(2)}) collective-permute-start(bf16[176,256]{1,0:T(8,128)(2,1)S(1)} %collective-permute-done.2.refs_11_), channel_id=1, source_target_pairs={{0,1},{1,0},{2,3},{3,2},{4,5},{5,4},{6,7},{7,6},{8,9},{9,8},{10,11... | collective-permute-start | bytes 270344 | tf_op jit(solution)/shard_map/ppermute | solution.py:158
  15.4 1.3 %collective-permute-start.5 = (bf16[176,256]{1,0:T(8,128)(2,1)S(1)}, bf16[176,256]{1,0:T(8,128)(2,1)S(1)}, u32[]{:S(2)}, u32[]{:S(2)}) collective-permute-start(bf16[176,256]{1,0:T(8,128)(2,1)S(1)} %collective-permute-done.1.refs_10_), channel_id=1, source_target_pairs={{0,1},{1,0},{2,3},{3,2},{4,5},{5,4},{6,7},{7,6},{8,9},{9,8},{10,11... | collective-permute-start | bytes 270344 | tf_op jit(solution)/shard_map/ppermute | solution.py:158
  15.4 1.4 %collective-permute-start.4 = (bf16[176,256]{1,0:T(8,128)(2,1)S(1)}, bf16[176,256]{1,0:T(8,128)(2,1)S(1)}, u32[]{:S(2)}, u32[]{:S(2)}) collective-permute-start(bf16[176,256]{1,0:T(8,128)(2,1)S(1)} %collective-permute-done.refs_9_), channel_id=1, source_target_pairs={{0,1},{1,0},{2,3},{3,2},{4,5},{5,4},{6,7},{7,6},{8,9},{9,8},{10,11... | collective-permute-start | bytes 270344 | tf_op jit(solution)/shard_map/ppermute | solution.py:158
  16.9 0.9 %copy-start.5 = (bf16[176,256]{1,0:T(8,128)(2,1)S(1)}, bf16[176,256]{1,0:T(8,128)(2,1)}, u32[]{:S(2)}) copy-start(bf16[176,256]{1,0:T(8,128)(2,1)} %pack.1.refs_8_) | copy-start | bytes 270340
  17.8 54.1 %copy-start.1 = (f32[2,2,256,256]{3,2,1,0:T(8,128)S(1)}, f32[2,2,256,256]{3,2,1,0:T(8,128)}, u32[]{:S(2)}) copy-start(f32[2,2,256,256]{3,2,1,0:T(8,128)} %r_gat.1) | copy-start | bytes 3145732
  17.8 54.1 %copy-start.2 = (f32[2,2,256,256]{3,2,1,0:T(8,128)S(1)}, f32[2,2,256,256]{3,2,1,0:T(8,128)}, u32[]{:S(2)}) copy-start(f32[2,2,256,256]{3,2,1,0:T(8,128)} %rr_gat.1) | copy-start | bytes 3145732
  17.8 54.1 %copy-start.4 = (f32[2,2,32,256]{3,2,1,0:T(8,128)S(1)}, f32[2,2,32,256]{3,2,1,0:T(8,128)}, u32[]{:S(2)}) copy-start(f32[2,2,32,256]{3,2,1,0:T(8,128)} %w_gat.1) | copy-start | bytes 393220
  17.8 54.1 %copy-start.6 = (f32[256,256]{1,0:T(8,128)S(1)}, f32[256,256]{1,0:T(8,128)}, u32[]{:S(2)}) copy-start(f32[256,256]{1,0:T(8,128)} %r_in.1) | copy-start | bytes 786436
  17.8 54.1 %copy-start.7 = (f32[256,256]{1,0:T(8,128)S(1)}, f32[256,256]{1,0:T(8,128)}, u32[]{:S(2)}) copy-start(f32[256,256]{1,0:T(8,128)} %rr_in.1) | copy-start | bytes 786436
  17.8 54.1 %copy-start.10 = (f32[2,2,32,256]{3,2,1,0:T(8,128)S(1)}, f32[2,2,32,256]{3,2,1,0:T(8,128)}, u32[]{:S(2)}) copy-start(f32[2,2,32,256]{3,2,1,0:T(8,128)} %l_gat.1) | copy-start | bytes 393220
  17.9 54.1 %copy-start.11 = (f32[2,2,32,256]{3,2,1,0:T(8,128)S(1)}, f32[2,2,32,256]{3,2,1,0:T(8,128)}, u32[]{:S(2)}) copy-start(f32[2,2,32,256]{3,2,1,0:T(8,128)} %rl_gat.1) | copy-start | bytes 393220
  17.9 54.1 %copy-start.12 = (f32[2,2,32,256]{3,2,1,0:T(8,128)S(1)}, f32[2,2,32,256]{3,2,1,0:T(8,128)}, u32[]{:S(2)}) copy-start(f32[2,2,32,256]{3,2,1,0:T(8,128)} %e_gat.1) | copy-start | bytes 393220
  17.9 54.1 %copy-start.13 = (f32[16,256]{1,0:T(8,128)S(1)}, f32[16,256]{1,0:T(8,128)}, u32[]{:S(2)}) copy-start(f32[16,256]{1,0:T(8,128)} %w_in.1) | copy-start | bytes 49156
  17.9 54.1 %copy-start.15 = (f32[40,40]{1,0:T(8,128)S(1)}, f32[40,40]{1,0:T(8,128)}, u32[]{:S(2)}) copy-start(f32[40,40]{1,0:T(8,128)} %r_out.1) | copy-start | bytes 19204
  17.9 54.1 %copy-start.16 = (f32[40,40]{1,0:T(8,128)S(1)}, f32[40,40]{1,0:T(8,128)}, u32[]{:S(2)}) copy-start(f32[40,40]{1,0:T(8,128)} %rr_out.1) | copy-start | bytes 19204
  17.9 54.1 %copy-start.17 = (f32[16,256]{1,0:T(8,128)S(1)}, f32[16,256]{1,0:T(8,128)}, u32[]{:S(2)}) copy-start(f32[16,256]{1,0:T(8,128)} %e_in.1) | copy-start | bytes 49156
  17.9 54.1 %copy-start.18 = (f32[8,40]{1,0:T(8,128)S(1)}, f32[8,40]{1,0:T(8,128)}, u32[]{:S(2)}) copy-start(f32[8,40]{1,0:T(8,128)} %w_out.1) | copy-start | bytes 3844
  17.9 54.1 %copy-start.19 = (f32[16,128]{1,0:T(8,128)S(1)}, f32[16,128]{1,0:T(8,128)}, u32[]{:S(2)}) copy-start(f32[16,128]{1,0:T(8,128)} %l_in.1) | copy-start | bytes 24580
  17.9 54.1 %copy-start.20 = (f32[16,128]{1,0:T(8,128)S(1)}, f32[16,128]{1,0:T(8,128)}, u32[]{:S(2)}) copy-start(f32[16,128]{1,0:T(8,128)} %rl_in.1) | copy-start | bytes 24580
  18.0 54.1 %copy-start.21 = (f32[1128]{0:T(1024)S(1)}, f32[1128]{0:T(1024)}, u32[]{:S(2)}) copy-start(f32[1128]{0:T(1024)} %first.1) | copy-start | bytes 13540
  18.0 54.1 %copy-start.22 = (f32[1128]{0:T(1024)S(1)}, f32[1128]{0:T(1024)}, u32[]{:S(2)}) copy-start(f32[1128]{0:T(1024)} %second.1) | copy-start | bytes 13540
  18.0 54.1 %copy-start.23 = (f32[1128]{0:T(1024)S(1)}, f32[1128]{0:T(1024)}, u32[]{:S(2)}) copy-start(f32[1128]{0:T(1024)} %e_small.1) | copy-start | bytes 13540
  18.0 54.1 %copy-start.25 = (f32[8,64]{1,0:T(8,128)S(1)}, f32[8,64]{1,0:T(8,128)}, u32[]{:S(2)}) copy-start(f32[8,64]{1,0:T(8,128)} %l_out.1) | copy-start | bytes 6148
  18.0 54.1 %copy-start.26 = (f32[8,64]{1,0:T(8,128)S(1)}, f32[8,64]{1,0:T(8,128)}, u32[]{:S(2)}) copy-start(f32[8,64]{1,0:T(8,128)} %rl_out.1) | copy-start | bytes 6148
  18.0 54.1 %copy-start.27 = (f32[8,40]{1,0:T(8,128)S(1)}, f32[8,40]{1,0:T(8,128)}, u32[]{:S(2)}) copy-start(f32[8,40]{1,0:T(8,128)} %e_out.1) | copy-start | bytes 3844
  43.8 1.7 %collective-permute-start.7 = (bf16[640,256]{1,0:T(8,128)(2,1)S(1)}, bf16[640,256]{1,0:T(8,128)(2,1)S(1)}, u32[]{:S(2)}, u32[]{:S(2)}) collective-permute-start(bf16[640,256]{1,0:T(8,128)(2,1)S(1)} %get-tuple-element.43), channel_id=1, source_target_pairs={{0,1},{1,0},{2,3},{3,2},{4,5},{5,4},{6,7},{7,6},{8,9},{9,8},{10,11... | collective-permute-start | bytes 983048 | tf_op jit(solution)/shard_map/ppermute | solution.py:158
  45.7 4.8 %collective-permute-start.8 = (bf16[160,256]{1,0:T(8,128)(2,1)S(1)}, bf16[160,256]{1,0:T(8,128)(2,1)S(1)}, u32[]{:S(2)}, u32[]{:S(2)}) collective-permute-start(bf16[160,256]{1,0:T(8,128)(2,1)S(1)} %get-tuple-element.45), channel_id=1, source_target_pairs={{0,8},{8,0},{16,24},{24,16},{1,9},{9,1},{17,25},{25,17},{2,10},{10... | collective-permute-start | bytes 245768 | tf_op jit(solution)/shard_map/ppermute | solution.py:158
  47.3 5.3 %collective-permute-start.9 = (bf16[160,256]{1,0:T(8,128)(2,1)S(1)}, bf16[160,256]{1,0:T(8,128)(2,1)S(1)}, u32[]{:S(2)}, u32[]{:S(2)}) collective-permute-start(bf16[160,256]{1,0:T(8,128)(2,1)S(1)} %get-tuple-element.46), channel_id=1, source_target_pairs={{0,16},{8,24},{16,0},{24,8},{1,17},{9,25},{17,1},{25,9},{2,18},{10... | collective-permute-start | bytes 245768 | tf_op jit(solution)/shard_map/ppermute | solution.py:158
  48.8 5.3 %collective-permute-start.10 = (bf16[160,256]{1,0:T(8,128)(2,1)S(1)}, bf16[160,256]{1,0:T(8,128)(2,1)S(1)}, u32[]{:S(2)}, u32[]{:S(2)}) collective-permute-start(bf16[160,256]{1,0:T(8,128)(2,1)S(1)} %get-tuple-element.47), channel_id=1, source_target_pairs={{0,24},{8,16},{16,8},{24,0},{1,25},{9,17},{17,9},{25,1},{2,26},{10... | collective-permute-start | bytes 245768 | tf_op jit(solution)/shard_map/ppermute | solution.py:158
  54.3 6.9 %collective-permute-start.13 = (bf16[160,256]{1,0:T(8,128)(2,1)S(1)}, bf16[160,256]{1,0:T(8,128)(2,1)S(1)}, u32[]{:S(2)}, u32[]{:S(2)}) collective-permute-start(bf16[160,256]{1,0:T(8,128)(2,1)S(1)} %join.2.own_ref), channel_id=1, source_target_pairs={{0,6},{1,7},{2,4},{3,5},{4,2},{5,3},{6,0},{7,1},{8,14},{9,15},{10,... | collective-permute-start | bytes 245768 | tf_op jit(solution)/shard_map/ppermute | solution.py:158
  56.9 6.7 %collective-permute-start.12 = (bf16[160,256]{1,0:T(8,128)(2,1)S(1)}, bf16[160,256]{1,0:T(8,128)(2,1)S(1)}, u32[]{:S(2)}, u32[]{:S(2)}) collective-permute-start(bf16[160,256]{1,0:T(8,128)(2,1)S(1)} %join.2.own_ref), channel_id=1, source_target_pairs={{0,4},{1,5},{2,6},{3,7},{4,0},{5,1},{6,2},{7,3},{8,12},{9,13},{10,... | collective-permute-start | bytes 245768 | tf_op jit(solution)/shard_map/ppermute | solution.py:158
  56.9 6.7 %collective-permute-start.11 = (bf16[160,256]{1,0:T(8,128)(2,1)S(1)}, bf16[160,256]{1,0:T(8,128)(2,1)S(1)}, u32[]{:S(2)}, u32[]{:S(2)}) collective-permute-start(bf16[160,256]{1,0:T(8,128)(2,1)S(1)} %join.2.own_ref), channel_id=1, source_target_pairs={{0,2},{1,3},{2,0},{3,1},{4,6},{5,7},{6,4},{7,5},{8,10},{9,11},{10,... | collective-permute-start | bytes 245768 | tf_op jit(solution)/shard_map/ppermute | solution.py:158
  63.7 5.8 %collective-permute-start.16 = (bf16[160,256]{1,0:T(8,128)(2,1)S(1)}, bf16[160,256]{1,0:T(8,128)(2,1)S(1)}, u32[]{:S(2)}, u32[]{:S(2)}) collective-permute-start(bf16[160,256]{1,0:T(8,128)(2,1)S(1)} %join.3.piece_0), channel_id=1, source_target_pairs={{0,24},{8,16},{16,8},{24,0},{1,25},{9,17},{17,9},{25,1},{2,26},{10... | collective-permute-start | bytes 245768 | tf_op jit(solution)/shard_map/ppermute | solution.py:158
  64.8 5.2 %collective-permute-start.15 = (bf16[160,256]{1,0:T(8,128)(2,1)S(1)}, bf16[160,256]{1,0:T(8,128)(2,1)S(1)}, u32[]{:S(2)}, u32[]{:S(2)}) collective-permute-start(bf16[160,256]{1,0:T(8,128)(2,1)S(1)} %join.3.piece_0), channel_id=1, source_target_pairs={{0,16},{8,24},{16,0},{24,8},{1,17},{9,25},{17,1},{25,9},{2,18},{10... | collective-permute-start | bytes 245768 | tf_op jit(solution)/shard_map/ppermute | solution.py:158
  66.2 4.4 %collective-permute-start.14 = (bf16[160,256]{1,0:T(8,128)(2,1)S(1)}, bf16[160,256]{1,0:T(8,128)(2,1)S(1)}, u32[]{:S(2)}, u32[]{:S(2)}) collective-permute-start(bf16[160,256]{1,0:T(8,128)(2,1)S(1)} %join.3.piece_0), channel_id=1, source_target_pairs={{0,8},{8,0},{16,24},{24,16},{1,9},{9,1},{17,25},{25,17},{2,10},{10... | collective-permute-start | bytes 245768 | tf_op jit(solution)/shard_map/ppermute | solution.py:158
  67.2 3.4 %collective-permute-start.17 = (bf16[160,256]{1,0:T(8,128)(2,1)S(1)}, bf16[160,256]{1,0:T(8,128)(2,1)S(1)}, u32[]{:S(2)}, u32[]{:S(2)}) collective-permute-start(bf16[160,256]{1,0:T(8,128)(2,1)S(1)} %join.3.piece_0), channel_id=1, source_target_pairs={{0,1},{1,0},{2,3},{3,2},{4,5},{5,4},{6,7},{7,6},{8,9},{9,8},{10,11... | collective-permute-start | bytes 245768 | tf_op jit(solution)/shard_map/ppermute | solution.py:158
  69.4 1.3 %collective-permute-start.20 = (bf16[160,256]{1,0:T(8,128)(2,1)S(1)}, bf16[160,256]{1,0:T(8,128)(2,1)S(1)}, u32[]{:S(2)}, u32[]{:S(2)}) collective-permute-start(bf16[160,256]{1,0:T(8,128)(2,1)S(1)} %collective-permute-done.16.piece_3), channel_id=1, source_target_pairs={{0,1},{1,0},{2,3},{3,2},{4,5},{5,4},{6,7},{7,6},{8,9},{9,8},{10,11... | collective-permute-start | bytes 245768 | tf_op jit(solution)/shard_map/ppermute | solution.py:158
  70.0 1.3 %collective-permute-start.19 = (bf16[160,256]{1,0:T(8,128)(2,1)S(1)}, bf16[160,256]{1,0:T(8,128)(2,1)S(1)}, u32[]{:S(2)}, u32[]{:S(2)}) collective-permute-start(bf16[160,256]{1,0:T(8,128)(2,1)S(1)} %collective-permute-done.15.piece_2), channel_id=1, source_target_pairs={{0,1},{1,0},{2,3},{3,2},{4,5},{5,4},{6,7},{7,6},{8,9},{9,8},{10,11... | collective-permute-start | bytes 245768 | tf_op jit(solution)/shard_map/ppermute | solution.py:158
  70.6 1.3 %collective-permute-start.18 = (bf16[160,256]{1,0:T(8,128)(2,1)S(1)}, bf16[160,256]{1,0:T(8,128)(2,1)S(1)}, u32[]{:S(2)}, u32[]{:S(2)}) collective-permute-start(bf16[160,256]{1,0:T(8,128)(2,1)S(1)} %collective-permute-done.14.piece_1), channel_id=1, source_target_pairs={{0,1},{1,0},{2,3},{3,2},{4,5},{5,4},{6,7},{7,6},{8,9},{9,8},{10,11... | collective-permute-start | bytes 245768 | tf_op jit(solution)/shard_map/ppermute | solution.py:158

commit v6 on v5

--- a/solution.py
+++ b/solution.py
@@ -191,6 +191,11 @@
     return [whole[g] for g in (0, 2, 4, 6, 1, 3, 5, 7)], dom_id * 0
 
 
+def parted(rows):
+    high = rows.astype(bf16).astype(f32)
+    return jnp.concatenate([high, rows - high], axis=0)
+
+
 def column_of(row):
     return jnp.broadcast_to(row.reshape(1, -1), (LANES, row.shape[0])).T
 
@@ -204,14 +209,8 @@
     lab_ref,
     msk_ref,
     send_ref,
-    piece_0,
-    piece_1,
-    piece_2,
-    piece_3,
-    piece_4,
-    piece_5,
-    piece_6,
-    piece_7,
+    piece_refs,
+    shard_refs,
     small_ref,
     keep_ref,
     send_out_ref,
@@ -254,8 +253,23 @@
     final = nodes - LANES
 
     digits = jnp.zeros((OUT_G, LANES), f32)
-    pieces = (piece_0, piece_1, piece_2, piece_3, piece_4, piece_5, piece_6, piece_7)
-    for j, piece in enumerate(pieces):
+    own_count = jnp.zeros((1, 1), f32)
+    first = GROUPS - len(piece_refs)
+    if first == 1:
+        (win_ref, wgat_ref, wout_ref) = shard_refs
+        group = spot_ref[0]
+        at_in = pl.ds(pl.multiple_of(group * IN_G, IN_G), IN_G)
+        at_gat = pl.ds(pl.multiple_of(group * GAT_G, GAT_G), GAT_G)
+        at_out = pl.ds(pl.multiple_of(group * OUT_G, OUT_G), OUT_G)
+        wi_ref[at_in, :] = win_ref[...].astype(bf16)
+        for layer in range(2):
+            for side in range(2):
+                wg_ref[layer, at_gat, side * HID : (side + 1) * HID] = wgat_ref[layer, side].astype(bf16)
+        wof_ref[at_out, :] = jnp.zeros((OUT_G, LANES), f32)
+        wof_ref[at_out, 0:CLASSES] = wout_ref[...]
+        marked = jnp.sum(msk_ref[...].astype(f32), axis=1, keepdims=True)
+        own_count = jnp.sum(marked, axis=0, keepdims=True)
+    for j, piece in enumerate(piece_refs, first):
         group = jnp.bitwise_xor(spot_ref[0], 2 * (j & 3) + (j >> 2))
 
         def rows_of(width):
@@ -320,7 +334,7 @@
     wo_ref[...] = wof_ref[:, 0:CLASSES].astype(bf16)
     wo_t = wof_ref[...].T[0:CLASSES].astype(bf16)
     digits = jnp.sum(digits, axis=0, keepdims=True)
-    inv_count = 1.0 / (digits[:, 0:1] * 256.0 + digits[:, 1:2])
+    inv_count = 1.0 / (digits[:, 0:1] * 256.0 + digits[:, 1:2] + own_count)
 
     row_id = lax.broadcasted_iota(jnp.int32, (LANES, LANES), 0)
     lane_id = lax.broadcasted_iota(jnp.int32, (LANES, LANES), 1)
@@ -547,13 +561,10 @@
         precision=highest, preferred_element_type=f32,
     )
     loss = jnp.broadcast_to(jnp.sum(loss_ref[...], axis=1, keepdims=True), (8, LANES))
-    loss_high = loss.astype(bf16).astype(f32)
-    rest = HID - HSIZE - CLASSES - 16
-    last = jnp.concatenate(
-        [g_bias_two, g_bias_out, loss_high, loss - loss_high, jnp.zeros((rest, LANES), f32)], axis=0
-    )
+    rest = HID - HSIZE - CLASSES - 8
+    last = jnp.concatenate([g_bias_two, g_bias_out, loss, jnp.zeros((rest, LANES), f32)], axis=0)
     columns = columns + jnp.where(lane_wide == 4, last, 0.0)
-    out_ref[ROW_MISC : ROW_MISC + 16, :] = columns.T[0:16].astype(bf16)
+    out_ref[ROW_MISC : ROW_MISC + 16, :] = parted(columns.T[0:8]).astype(bf16)
     out_ref[ROW_MISC + 16 :, :] = jnp.zeros((ROWS - ROW_MISC - 16, HID), bf16)
     core = jnp.bitwise_and(dom_ref[0], 1)
     width = ROWS // 2
@@ -561,7 +572,9 @@
     send_out_ref[...] = out_ref[pl.ds(pl.multiple_of((1 - core) * width, width), width), :]
 
 
-def run_model(section_id, dom_id, spot, features, src_all, labels, label_mask, send_index, pieces, small_params):
+def run_model(
+    section_id, dom_id, spot, features, src_all, labels, label_mask, send_index, pieces, shards, small_params
+):
     nodes = features.shape[1]
     blocks = nodes // LANES
     scratch = [
@@ -595,7 +608,10 @@
         pltpu.VMEM((GROUPS, 32, HID), bf16),
     ]
     def body(*refs):
-        pl.run_scoped(lambda *buffers: model_kernel(*refs, *buffers), *scratch)
+        ahead, cut = (8, 8 + len(pieces))
+        after = cut + len(shards)
+        head = refs[:ahead] + (refs[ahead:cut], refs[cut:after]) + refs[after:]
+        pl.run_scoped(lambda *buffers: model_kernel(*head, *buffers), *scratch)
 
     grid_spec = pltpu.PrefetchScalarGridSpec(
         num_scalar_prefetch=3,
@@ -604,7 +620,7 @@
             pl.BlockSpec((1, nodes, FEAT), lambda i, m, d, p: (m[0], 0, 0)),
             pl.BlockSpec((1, DEG, nodes), lambda i, m, d, p: (m[0], 0, 0)),
         ]
-        + vmem(12),
+        + vmem(4 + len(pieces) + len(shards)),
         out_specs=vmem(2),
     )
     return pl.pallas_call(
@@ -613,21 +629,14 @@
         out_shape=[jax.ShapeDtypeStruct((ROWS // 2, HID), bf16)] * 2,
         compiler_params=pltpu.CompilerParams(vmem_limit_bytes=50 * 1024 * 1024),
         name="model",
-    )(section_id, dom_id, spot, features, src_all, labels, label_mask, send_index, *pieces, small_params)
+    )(section_id, dom_id, spot, features, src_all, labels, label_mask, send_index, *pieces, *shards, small_params)
 
 
 def settled(total, is_last):
     base = ROW_MISC % PIECE
-    block = total[base : base + 8]
-    row = lax.broadcasted_iota(jnp.int32, (8, HID), 0)
-    lane = lax.broadcasted_iota(jnp.int32, (8, HID), 1)
-    spot = HSIZE + CLASSES
-    joined = block + pltpu.roll(block, HID - 8, 1)
-    high = joined.astype(bf16).astype(f32)
-    low = pltpu.roll(joined - high, 8, 1)
-    here = (row == 4) & (lane >= spot) & (lane < spot + 16) & (is_last == 1)
-    block = jnp.where(here, jnp.where(lane < spot + 8, high, low), block)
-    return jnp.concatenate([total[:base], block, total[base + 8 :]], axis=0).astype(bf16)
+    block = total[base : base + 16]
+    block = jnp.where(is_last == 1, parted(block[0:8] + block[8:16]), block)
+    return jnp.concatenate([total[:base], block, total[base + 16 :]], axis=0).astype(bf16)
 
 
 def last_piece(core, section):
@@ -796,11 +805,12 @@
         sum_ref[pl.ds(pl.multiple_of(spot * PIECE, PIECE), PIECE), :] = piece[...]
     grads = sum_ref[0:ROW_MISC, :].astype(f32)
     squares = jnp.sum(grads * grads)
-    misc = sum_ref[ROW_MISC : ROW_MISC + 8, :].astype(f32)
+    misc = sum_ref[ROW_MISC : ROW_MISC + 16, :].astype(f32)
+    misc = misc[0:8] + misc[8:16]
     row = lax.broadcasted_iota(jnp.int32, (8, HID), 0)
     lane = lax.broadcasted_iota(jnp.int32, (8, HID), 1)
     spot = HSIZE + CLASSES
-    loss_ref[0] = jnp.sum(jnp.where((row == 4) & ((lane == spot) | (lane == spot + 8)), misc, 0.0))
+    loss_ref[0] = jnp.sum(jnp.where((row == 4) & (lane == spot), misc, 0.0))
     small_part = jnp.where((row < 4) | ((row == 4) & (lane < spot)), misc, 0.0)
     squares = squares + jnp.sum(small_part * small_part)
     norm = jnp.sqrt(jnp.broadcast_to(squares, (1, 1)))
@@ -892,11 +902,25 @@
 ):
     dom_id = lax.axis_index("dom").astype(jnp.int32).reshape(1)
     section_id = lax.axis_index("section").astype(jnp.int32).reshape(1)
+    size = lax.axis_size("dom")
     src_all = jnp.swapaxes(sources, 1, 2)
     packed = pack_inputs(section_id, features, src_all, labels, label_mask, send_index, w_in, w_gat, w_out)
     pieces, spot = gather_weights(dom_id, packed, w_in, w_gat, w_out, label_mask)
+    shards = ()
+    if size == GROUPS:
+        (pieces, shards) = (pieces[1:], (w_in, w_gat, w_out))
     keep, send = run_model(
-        section_id, dom_id, spot, features, src_all, labels, label_mask, send_index, pieces, small_params
+        section_id,
+        dom_id,
+        spot,
+        features,
+        src_all,
+        labels,
+        label_mask,
+        send_index,
+        pieces,
+        shards,
+        small_params,
     )
     pieces, spots = sum_gradients((section_id, dom_id), keep, send)
     state = (

time: 74.9 us -> 73.6 us (0.983)
  local copies, waits for them, and re-layouts: 1.03 us -> 0.15 us
    unnamed x56 -> x54, local copies, waits for them, and re-layouts: 1.03 us -> 0.15 us
where the time goes in v6:
time: 73.6 us; the launch traced here: 73.4 us
  Pallas kernels  30.5 us (41%)
  waiting for transfers between devices  23.6 us (32%)
  starting transfers between devices  18.1 us (25%)
  between operations  1.08 us (1%)
    pallas_call x1, Pallas kernels, run_model(): pl.pallas_call(body, grid_spec=grid_spec, out_shape=[jax.ShapeDtypeStruct...  25.8 us
    ppermute x21, waiting for transfers between devices, crossed(): lax.ppermute(value, axis, [(i, i ^ mask) for i in range(lax.axis_size(axi...  23.6 us
    ppermute x21, starting transfers between devices, crossed(): lax.ppermute(value, axis, [(i, i ^ mask) for i in range(lax.axis_size(axi...  18.1 us
    pallas_call x1, Pallas kernels, per_device(): pl.pallas_call(update_kernel, out_shape=[jax.ShapeDtypeStruct(v.shape, f3...  2.63 us
    pallas_call x1, Pallas kernels, pack_inputs(): pl.pallas_call(pack_kernel, grid_spec=grid_spec, out_shape=jax.ShapeDtype...  1.87 us
  transfers between devices with their start and end apart: 21, of which 16 were waited for; matrix products, arithmetic and copies ran while one was open for 0% of the time, Pallas kernels for 0%

profile of v6, /device:TPU:0, one launch (start us, length us, event | category | flops | bytes accessed | tf_op | source)
XLA Modules:
  0.0 73.4 jit_solution(9291762230848886599)
XLA Ops:
  0.8 1.9 %pack.1 = bf16[176,256]{1,0:T(8,128)(2,1)} custom-call(s32[1]{0:T(128)} %bitcast.1.section_ref.refs_0_, bf16[4,2048,128]{2,1,0:T(8,128)(2,1)} %refs_3_.1, s32[4,8,2048]{2,1,0:T(8,128)} %bitcast.5, s32[4,2048]{1,0:T(4,128)} %refs_5_.1, s32[4,2048]{1,0:T(4,128)} %refs_6_.1, s32[4,64]{1,0:T(4,128)} %refs_7_.1, f32[16,256]{1,0:T(8,128)} %w_in.1, ...), custom_call_target="tpu_custom_call" | custom-call | tf_op jit(solution)/shard_map/pack/pallas_call | solution.py:148
  2.6 5.0 %collective-permute-start.2 = (bf16[176,256]{1,0:T(8,128)(2,1)}, bf16[176,256]{1,0:T(8,128)(2,1)S(1)}, u32[]{:S(2)}, u32[]{:S(2)}) collective-permute-start(bf16[176,256]{1,0:T(8,128)(2,1)} %pack.1), channel_id=1, source_target_pairs={{0,6},{1,7},{2,4},{3,5},{4,2},{5,3},{6,0},{7,1},{8,14},{9,15},{10,... | collective-permute-start | bytes 270344 | tf_op jit(solution)/shard_map/ppermute | solution.py:158
  7.7 0.0 collective-permute-start.1
  7.7 0.6 collective-permute-start
  8.2 0.0 collective-permute-start.3
  8.2 3.0 %collective-permute-done.2.refs_10_ = bf16[176,256]{1,0:T(8,128)(2,1)S(1)} collective-permute-done((bf16[176,256]{1,0:T(8,128)(2,1)}, bf16[176,256]{1,0:T(8,128)(2,1)S(1)}, u32[]{:S(2)}, u32[]{:S(2)}) %collective-permute-start.2) | collective-permute-done | bytes 90144 | tf_op jit(solution)/shard_map/ppermute | solution.py:158
  11.2 0.0 collective-permute-start.6
  11.2 4.2 %collective-permute-done.1.refs_9_ = bf16[176,256]{1,0:T(8,128)(2,1)S(1)} collective-permute-done((bf16[176,256]{1,0:T(8,128)(2,1)}, bf16[176,256]{1,0:T(8,128)(2,1)S(1)}, u32[]{:S(2)}, u32[]{:S(2)}) %collective-permute-start.1) | collective-permute-done | bytes 90144 | tf_op jit(solution)/shard_map/ppermute | solution.py:158
  15.4 0.0 collective-permute-start.5
  15.5 0.0 collective-permute-done.refs_8_
  15.5 0.5 collective-permute-start.4
  16.0 0.0 collective-permute-done.3.refs_11_
  16.0 0.0 collective-permute-done.6.refs_14_
  16.0 0.8 %collective-permute-done.5.refs_13_ = bf16[176,256]{1,0:T(8,128)(2,1)S(1)} collective-permute-done((bf16[176,256]{1,0:T(8,128)(2,1)S(1)}, bf16[176,256]{1,0:T(8,128)(2,1)S(1)}, u32[]{:S(2)}, u32[]{:S(2)}) %collective-permute-start.5) | collective-permute-done | bytes 90144 | tf_op jit(solution)/shard_map/ppermute | solution.py:158
  16.7 0.2 collective-permute-done.4.refs_12_
  17.0 0.0 copy-start.2
  17.0 0.0 copy-start.3
  17.0 0.0 copy-start.5
  17.0 0.0 copy-start.6
  17.0 0.0 copy-start.10
  17.0 0.0 copy-start.11
  17.0 0.0 copy-start.12
  17.0 0.0 copy-start.15
  17.1 0.0 copy-start.16
  17.1 0.0 copy-start.17
  17.1 0.0 copy-start.18
  17.1 0.0 copy-start.19
  17.1 0.0 copy-start.20
  17.1 0.0 copy-start.21
  17.1 0.0 copy-start.22
  17.1 0.0 copy-start.24
  17.2 0.0 copy-start.25
  17.2 0.0 copy-start.26
  17.2 25.8 %model.1 = (bf16[640,256]{1,0:T(8,128)(2,1)S(1)}, bf16[640,256]{1,0:T(8,128)(2,1)S(1)}) custom-call(s32[1]{0:T(128)} %bitcast.1.section_ref.refs_0_, s32[1]{0:T(128)} %bitcast.refs_1_.refs_2_.dom_ref.spot_ref, s32[1]{0:T(128)} %bitcast.refs_1_.refs_2_.dom_ref.spot_ref, bf16[4,2048,128]{2,1,0:T(8,128)(2,1)S(1)} %copy-done, s32[4,8,2048]{2,1,0:T(8,128)S(1)} %bitcast.6, ...), custom_call_target="tpu_custom_call" | custom-call | tf_op jit(solution)/shard_map/model/pallas_call | solution.py:626
  43.0 0.4 collective-permute-start.7
  43.4 1.3 %collective-permute-done.7.got_ref = bf16[640,256]{1,0:T(8,128)(2,1)S(1)} collective-permute-done((bf16[640,256]{1,0:T(8,128)(2,1)S(1)}, bf16[640,256]{1,0:T(8,128)(2,1)S(1)}, u32[]{:S(2)}, u32[]{:S(2)}) %collective-permute-start.7) | collective-permute-done | bytes 327712 | tf_op jit(solution)/shard_map/ppermute | solution.py:158
  44.7 0.1 split.1
  44.8 1.6 %collective-permute-start.8 = (bf16[160,256]{1,0:T(8,128)(2,1)S(1)}, bf16[160,256]{1,0:T(8,128)(2,1)S(1)}, u32[]{:S(2)}, u32[]{:S(2)}) collective-permute-start(bf16[160,256]{1,0:T(8,128)(2,1)S(1)} %get-tuple-element.45), channel_id=1, source_target_pairs={{0,8},{8,0},{16,24},{24,16},{1,9},{9,1},{17,25},{25,17},{2,10},{10... | collective-permute-start | bytes 245768 | tf_op jit(solution)/shard_map/ppermute | solution.py:158
  46.3 1.5 %collective-permute-start.9 = (bf16[160,256]{1,0:T(8,128)(2,1)S(1)}, bf16[160,256]{1,0:T(8,128)(2,1)S(1)}, u32[]{:S(2)}, u32[]{:S(2)}) collective-permute-start(bf16[160,256]{1,0:T(8,128)(2,1)S(1)} %get-tuple-element.46), channel_id=1, source_target_pairs={{0,16},{8,24},{16,0},{24,8},{1,17},{9,25},{17,1},{25,9},{2,18},{10... | collective-permute-start | bytes 245768 | tf_op jit(solution)/shard_map/ppermute | solution.py:158
  47.8 0.5 collective-permute-start.10
  48.3 1.2 %collective-permute-done.8.one_ref = bf16[160,256]{1,0:T(8,128)(2,1)S(1)} collective-permute-done((bf16[160,256]{1,0:T(8,128)(2,1)S(1)}, bf16[160,256]{1,0:T(8,128)(2,1)S(1)}, u32[]{:S(2)}, u32[]{:S(2)}) %collective-permute-start.8) | collective-permute-done | bytes 81952 | tf_op jit(solution)/shard_map/ppermute | solution.py:158
  49.5 2.0 %collective-permute-done.9.two_ref = bf16[160,256]{1,0:T(8,128)(2,1)S(1)} collective-permute-done((bf16[160,256]{1,0:T(8,128)(2,1)S(1)}, bf16[160,256]{1,0:T(8,128)(2,1)S(1)}, u32[]{:S(2)}, u32[]{:S(2)}) %collective-permute-start.9) | collective-permute-done | bytes 81952 | tf_op jit(solution)/shard_map/ppermute | solution.py:158
  51.6 1.6 %collective-permute-done.10.three_ref = bf16[160,256]{1,0:T(8,128)(2,1)S(1)} collective-permute-done((bf16[160,256]{1,0:T(8,128)(2,1)S(1)}, bf16[160,256]{1,0:T(8,128)(2,1)S(1)}, u32[]{:S(2)}, u32[]{:S(2)}) %collective-permute-start.10) | collective-permute-done | bytes 81952 | tf_op jit(solution)/shard_map/ppermute | solution.py:158
  53.2 2.6 %collective-permute-start.13 = (bf16[160,256]{1,0:T(8,128)(2,1)S(1)}, bf16[160,256]{1,0:T(8,128)(2,1)S(1)}, u32[]{:S(2)}, u32[]{:S(2)}) collective-permute-start(bf16[160,256]{1,0:T(8,128)(2,1)S(1)} %join.2.own_ref), channel_id=1, source_target_pairs={{0,6},{1,7},{2,4},{3,5},{4,2},{5,3},{6,0},{7,1},{8,14},{9,15},{10,... | collective-permute-start | bytes 245768 | tf_op jit(solution)/shard_map/ppermute | solution.py:158
  55.8 0.0 collective-permute-start.12
  55.8 1.8 %collective-permute-start.11 = (bf16[160,256]{1,0:T(8,128)(2,1)S(1)}, bf16[160,256]{1,0:T(8,128)(2,1)S(1)}, u32[]{:S(2)}, u32[]{:S(2)}) collective-permute-start(bf16[160,256]{1,0:T(8,128)(2,1)S(1)} %join.2.own_ref), channel_id=1, source_target_pairs={{0,2},{1,3},{2,0},{3,1},{4,6},{5,7},{6,4},{7,5},{8,10},{9,11},{10,... | collective-permute-start | bytes 245768 | tf_op jit(solution)/shard_map/ppermute | solution.py:158
  57.7 2.5 %collective-permute-done.13.three_ref = bf16[160,256]{1,0:T(8,128)(2,1)S(1)} collective-permute-done((bf16[160,256]{1,0:T(8,128)(2,1)S(1)}, bf16[160,256]{1,0:T(8,128)(2,1)S(1)}, u32[]{:S(2)}, u32[]{:S(2)}) %collective-permute-start.13) | collective-permute-done | bytes 81952 | tf_op jit(solution)/shard_map/ppermute | solution.py:158
  60.2 2.3 %collective-permute-done.12.two_ref = bf16[160,256]{1,0:T(8,128)(2,1)S(1)} collective-permute-done((bf16[160,256]{1,0:T(8,128)(2,1)S(1)}, bf16[160,256]{1,0:T(8,128)(2,1)S(1)}, u32[]{:S(2)}, u32[]{:S(2)}) %collective-permute-start.12) | collective-permute-done | bytes 81952 | tf_op jit(solution)/shard_map/ppermute | solution.py:158
  62.5 0.0 collective-permute-done.11.one_ref
  62.5 0.9 %collective-permute-start.16 = (bf16[160,256]{1,0:T(8,128)(2,1)S(1)}, bf16[160,256]{1,0:T(8,128)(2,1)S(1)}, u32[]{:S(2)}, u32[]{:S(2)}) collective-permute-start(bf16[160,256]{1,0:T(8,128)(2,1)S(1)} %join.3.piece_0), channel_id=1, source_target_pairs={{0,24},{8,16},{16,8},{24,0},{1,25},{9,17},{17,9},{25,1},{2,26},{10... | collective-permute-start | bytes 245768 | tf_op jit(solution)/shard_map/ppermute | solution.py:158
  63.5 1.5 %collective-permute-start.15 = (bf16[160,256]{1,0:T(8,128)(2,1)S(1)}, bf16[160,256]{1,0:T(8,128)(2,1)S(1)}, u32[]{:S(2)}, u32[]{:S(2)}) collective-permute-start(bf16[160,256]{1,0:T(8,128)(2,1)S(1)} %join.3.piece_0), channel_id=1, source_target_pairs={{0,16},{8,24},{16,0},{24,8},{1,17},{9,25},{17,1},{25,9},{2,18},{10... | collective-permute-start | bytes 245768 | tf_op jit(solution)/shard_map/ppermute | solution.py:158
  64.9 1.2 %collective-permute-start.14 = (bf16[160,256]{1,0:T(8,128)(2,1)S(1)}, bf16[160,256]{1,0:T(8,128)(2,1)S(1)}, u32[]{:S(2)}, u32[]{:S(2)}) collective-permute-start(bf16[160,256]{1,0:T(8,128)(2,1)S(1)} %join.3.piece_0), channel_id=1, source_target_pairs={{0,8},{8,0},{16,24},{24,16},{1,9},{9,1},{17,25},{25,17},{2,10},{10... | collective-permute-start | bytes 245768 | tf_op jit(solution)/shard_map/ppermute | solution.py:158
  66.1 0.0 collective-permute-start.17
  66.1 2.1 %collective-permute-done.16.piece_3 = bf16[160,256]{1,0:T(8,128)(2,1)S(1)} collective-permute-done((bf16[160,256]{1,0:T(8,128)(2,1)S(1)}, bf16[160,256]{1,0:T(8,128)(2,1)S(1)}, u32[]{:S(2)}, u32[]{:S(2)}) %collective-permute-start.16) | collective-permute-done | bytes 81952 | tf_op jit(solution)/shard_map/ppermute | solution.py:158
  68.2 0.0 collective-permute-start.20
  68.2 0.6 collective-permute-done.15.piece_2
  68.8 0.0 collective-permute-start.19
  68.8 0.6 collective-permute-done.14.piece_1
  69.4 0.0 collective-permute-start.18
  69.4 0.0 collective-permute-done.17.piece_4
  69.4 0.1 collective-permute-done.20.piece_7
  69.4 0.6 collective-permute-done.19.piece_6
  70.1 0.6 collective-permute-done.18.piece_5
  70.8 2.6 %update.1 = (f32[16,256]{1,0:T(8,128)}, f32[2,2,32,256]{3,2,1,0:T(8,128)}, f32[8,40]{1,0:T(8,128)}, f32[1128]{0:T(1024)}, f32[16,128]{1,0:T(8,128)}, /*index=5*/...) custom-call(s32[1]{0:T(128)} %bitcast.refs_1_.refs_2_.dom_ref.spot_r, ...), custom_call_target="tpu_custom_call" | custom-call | tf_op jit(solution)/shard_map/update/pallas_call | solution.py:951
  (38 shorter events, 0.2 us)
Async XLA Ops:
  0.7 16.2 %copy-start.13 = (f32[8,40]{1,0:T(8,128)S(1)}, f32[8,40]{1,0:T(8,128)}, u32[]{:S(2)}) copy-start(f32[8,40]{1,0:T(8,128)} %w_out.1) | copy-start | bytes 3844
  0.7 16.2 %copy-start.1 = (f32[2,2,32,256]{3,2,1,0:T(8,128)S(1)}, f32[2,2,32,256]{3,2,1,0:T(8,128)}, u32[]{:S(2)}) copy-start(f32[2,2,32,256]{3,2,1,0:T(8,128)} %w_gat.1) | copy-start | bytes 393220
  0.7 16.2 %copy-start.7 = (f32[16,256]{1,0:T(8,128)S(1)}, f32[16,256]{1,0:T(8,128)}, u32[]{:S(2)}) copy-start(f32[16,256]{1,0:T(8,128)} %w_in.1) | copy-start | bytes 49156
  0.7 16.2 %copy-start.9 = (s32[4,2048]{1,0:T(4,128)S(1)}, s32[4,2048]{1,0:T(4,128)}, u32[]{:S(2)}) copy-start(s32[4,2048]{1,0:T(4,128)} %refs_6_.1) | copy-start | bytes 98308
  0.7 16.2 %copy-start.8 = (s32[4,2048]{1,0:T(4,128)S(1)}, s32[4,2048]{1,0:T(4,128)}, u32[]{:S(2)}) copy-start(s32[4,2048]{1,0:T(4,128)} %refs_5_.1) | copy-start | bytes 98308
  0.7 16.2 %copy-start.23 = (s32[4,64]{1,0:T(4,128)S(1)}, s32[4,64]{1,0:T(4,128)}, u32[]{:S(2)}) copy-start(s32[4,64]{1,0:T(4,128)} %refs_7_.1) | copy-start | bytes 3076
  0.7 16.2 %copy-start = (bf16[4,2048,128]{2,1,0:T(8,128)(2,1)S(1)}, bf16[4,2048,128]{2,1,0:T(8,128)(2,1)}, u32[]{:S(2)}) copy-start(bf16[4,2048,128]{2,1,0:T(8,128)(2,1)} %refs_3_.1) | copy-start | bytes 6291460
  0.7 16.2 %copy-start.4 = (s32[4,2048,8]{1,2,0:T(8,128)S(1)}, s32[4,2048,8]{1,2,0:T(8,128)}, u32[]{:S(2)}) copy-start(s32[4,2048,8]{1,2,0:T(8,128)} %param.28) | copy-start | bytes 786436
  0.7 16.2 %copy-start.14 = (f32[1128]{0:T(1024)S(1)}, f32[1128]{0:T(1024)}, u32[]{:S(2)}) copy-start(f32[1128]{0:T(1024)} %small.1) | copy-start | bytes 13540
  2.6 8.6 %collective-permute-start.2 = (bf16[176,256]{1,0:T(8,128)(2,1)}, bf16[176,256]{1,0:T(8,128)(2,1)S(1)}, u32[]{:S(2)}, u32[]{:S(2)}) collective-permute-start(bf16[176,256]{1,0:T(8,128)(2,1)} %pack.1), channel_id=1, source_target_pairs={{0,6},{1,7},{2,4},{3,5},{4,2},{5,3},{6,0},{7,1},{8,14},{9,15},{10,... | collective-permute-start | bytes 270344 | tf_op jit(solution)/shard_map/ppermute | solution.py:158
  7.7 7.8 %collective-permute-start.1 = (bf16[176,256]{1,0:T(8,128)(2,1)}, bf16[176,256]{1,0:T(8,128)(2,1)S(1)}, u32[]{:S(2)}, u32[]{:S(2)}) collective-permute-start(bf16[176,256]{1,0:T(8,128)(2,1)} %pack.1), channel_id=1, source_target_pairs={{0,4},{1,5},{2,6},{3,7},{4,0},{5,1},{6,2},{7,3},{8,12},{9,13},{10,... | collective-permute-start | bytes 270344 | tf_op jit(solution)/shard_map/ppermute | solution.py:158
  7.7 7.8 %collective-permute-start = (bf16[176,256]{1,0:T(8,128)(2,1)}, bf16[176,256]{1,0:T(8,128)(2,1)S(1)}, u32[]{:S(2)}, u32[]{:S(2)}) collective-permute-start(bf16[176,256]{1,0:T(8,128)(2,1)} %pack.1), channel_id=1, source_target_pairs={{0,2},{1,3},{2,0},{3,1},{4,6},{5,7},{6,4},{7,5},{8,10},{9,11},{10,... | collective-permute-start | bytes 270344 | tf_op jit(solution)/shard_map/ppermute | solution.py:158
  8.2 7.7 %collective-permute-start.3 = (bf16[176,256]{1,0:T(8,128)(2,1)}, bf16[176,256]{1,0:T(8,128)(2,1)S(1)}, u32[]{:S(2)}, u32[]{:S(2)}) collective-permute-start(bf16[176,256]{1,0:T(8,128)(2,1)} %pack.1), channel_id=1, source_target_pairs={{0,1},{1,0},{2,3},{3,2},{4,5},{5,4},{6,7},{7,6},{8,9},{9,8},{10,11... | collective-permute-start | bytes 270344 | tf_op jit(solution)/shard_map/ppermute | solution.py:158
  11.2 4.7 %collective-permute-start.6 = (bf16[176,256]{1,0:T(8,128)(2,1)S(1)}, bf16[176,256]{1,0:T(8,128)(2,1)S(1)}, u32[]{:S(2)}, u32[]{:S(2)}) collective-permute-start(bf16[176,256]{1,0:T(8,128)(2,1)S(1)} %collective-permute-done.2.refs_10_), channel_id=1, source_target_pairs={{0,1},{1,0},{2,3},{3,2},{4,5},{5,4},{6,7},{7,6},{8,9},{9,8},{10,11... | collective-permute-start | bytes 270344 | tf_op jit(solution)/shard_map/ppermute | solution.py:158
  15.4 1.3 %collective-permute-start.5 = (bf16[176,256]{1,0:T(8,128)(2,1)S(1)}, bf16[176,256]{1,0:T(8,128)(2,1)S(1)}, u32[]{:S(2)}, u32[]{:S(2)}) collective-permute-start(bf16[176,256]{1,0:T(8,128)(2,1)S(1)} %collective-permute-done.1.refs_9_), channel_id=1, source_target_pairs={{0,1},{1,0},{2,3},{3,2},{4,5},{5,4},{6,7},{7,6},{8,9},{9,8},{10,11... | collective-permute-start | bytes 270344 | tf_op jit(solution)/shard_map/ppermute | solution.py:158
  15.5 1.4 %collective-permute-start.4 = (bf16[176,256]{1,0:T(8,128)(2,1)S(1)}, bf16[176,256]{1,0:T(8,128)(2,1)S(1)}, u32[]{:S(2)}, u32[]{:S(2)}) collective-permute-start(bf16[176,256]{1,0:T(8,128)(2,1)S(1)} %collective-permute-done.refs_8_), channel_id=1, source_target_pairs={{0,1},{1,0},{2,3},{3,2},{4,5},{5,4},{6,7},{7,6},{8,9},{9,8},{10,11... | collective-permute-start | bytes 270344 | tf_op jit(solution)/shard_map/ppermute | solution.py:158
  17.0 53.7 %copy-start.2 = (f32[2,2,256,256]{3,2,1,0:T(8,128)S(1)}, f32[2,2,256,256]{3,2,1,0:T(8,128)}, u32[]{:S(2)}) copy-start(f32[2,2,256,256]{3,2,1,0:T(8,128)} %r_gat.1) | copy-start | bytes 3145732
  17.0 53.7 %copy-start.3 = (f32[2,2,256,256]{3,2,1,0:T(8,128)S(1)}, f32[2,2,256,256]{3,2,1,0:T(8,128)}, u32[]{:S(2)}) copy-start(f32[2,2,256,256]{3,2,1,0:T(8,128)} %rr_gat.1) | copy-start | bytes 3145732
  17.0 53.7 %copy-start.5 = (f32[256,256]{1,0:T(8,128)S(1)}, f32[256,256]{1,0:T(8,128)}, u32[]{:S(2)}) copy-start(f32[256,256]{1,0:T(8,128)} %r_in.1) | copy-start | bytes 786436
  17.0 53.7 %copy-start.6 = (f32[256,256]{1,0:T(8,128)S(1)}, f32[256,256]{1,0:T(8,128)}, u32[]{:S(2)}) copy-start(f32[256,256]{1,0:T(8,128)} %rr_in.1) | copy-start | bytes 786436
  17.0 53.7 %copy-start.10 = (f32[2,2,32,256]{3,2,1,0:T(8,128)S(1)}, f32[2,2,32,256]{3,2,1,0:T(8,128)}, u32[]{:S(2)}) copy-start(f32[2,2,32,256]{3,2,1,0:T(8,128)} %l_gat.1) | copy-start | bytes 393220
  17.0 53.7 %copy-start.11 = (f32[2,2,32,256]{3,2,1,0:T(8,128)S(1)}, f32[2,2,32,256]{3,2,1,0:T(8,128)}, u32[]{:S(2)}) copy-start(f32[2,2,32,256]{3,2,1,0:T(8,128)} %rl_gat.1) | copy-start | bytes 393220
  17.0 53.7 %copy-start.12 = (f32[2,2,32,256]{3,2,1,0:T(8,128)S(1)}, f32[2,2,32,256]{3,2,1,0:T(8,128)}, u32[]{:S(2)}) copy-start(f32[2,2,32,256]{3,2,1,0:T(8,128)} %e_gat.1) | copy-start | bytes 393220
  17.0 53.7 %copy-start.15 = (f32[40,40]{1,0:T(8,128)S(1)}, f32[40,40]{1,0:T(8,128)}, u32[]{:S(2)}) copy-start(f32[40,40]{1,0:T(8,128)} %r_out.1) | copy-start | bytes 19204
  17.1 53.7 %copy-start.16 = (f32[40,40]{1,0:T(8,128)S(1)}, f32[40,40]{1,0:T(8,128)}, u32[]{:S(2)}) copy-start(f32[40,40]{1,0:T(8,128)} %rr_out.1) | copy-start | bytes 19204
  17.1 53.6 %copy-start.17 = (f32[16,256]{1,0:T(8,128)S(1)}, f32[16,256]{1,0:T(8,128)}, u32[]{:S(2)}) copy-start(f32[16,256]{1,0:T(8,128)} %e_in.1) | copy-start | bytes 49156
  17.1 53.6 %copy-start.18 = (f32[16,128]{1,0:T(8,128)S(1)}, f32[16,128]{1,0:T(8,128)}, u32[]{:S(2)}) copy-start(f32[16,128]{1,0:T(8,128)} %l_in.1) | copy-start | bytes 24580
  17.1 53.6 %copy-start.19 = (f32[16,128]{1,0:T(8,128)S(1)}, f32[16,128]{1,0:T(8,128)}, u32[]{:S(2)}) copy-start(f32[16,128]{1,0:T(8,128)} %rl_in.1) | copy-start | bytes 24580
  17.1 53.6 %copy-start.20 = (f32[1128]{0:T(1024)S(1)}, f32[1128]{0:T(1024)}, u32[]{:S(2)}) copy-start(f32[1128]{0:T(1024)} %first.1) | copy-start | bytes 13540
  17.1 53.6 %copy-start.21 = (f32[1128]{0:T(1024)S(1)}, f32[1128]{0:T(1024)}, u32[]{:S(2)}) copy-start(f32[1128]{0:T(1024)} %second.1) | copy-start | bytes 13540
  17.1 53.6 %copy-start.22 = (f32[1128]{0:T(1024)S(1)}, f32[1128]{0:T(1024)}, u32[]{:S(2)}) copy-start(f32[1128]{0:T(1024)} %e_small.1) | copy-start | bytes 13540
  17.1 53.6 %copy-start.24 = (f32[8,64]{1,0:T(8,128)S(1)}, f32[8,64]{1,0:T(8,128)}, u32[]{:S(2)}) copy-start(f32[8,64]{1,0:T(8,128)} %l_out.1) | copy-start | bytes 6148
  17.2 53.6 %copy-start.25 = (f32[8,64]{1,0:T(8,128)S(1)}, f32[8,64]{1,0:T(8,128)}, u32[]{:S(2)}) copy-start(f32[8,64]{1,0:T(8,128)} %rl_out.1) | copy-start | bytes 6148
  17.2 53.6 %copy-start.26 = (f32[8,40]{1,0:T(8,128)S(1)}, f32[8,40]{1,0:T(8,128)}, u32[]{:S(2)}) copy-start(f32[8,40]{1,0:T(8,128)} %e_out.1) | copy-start | bytes 3844
  43.0 1.7 %collective-permute-start.7 = (bf16[640,256]{1,0:T(8,128)(2,1)S(1)}, bf16[640,256]{1,0:T(8,128)(2,1)S(1)}, u32[]{:S(2)}, u32[]{:S(2)}) collective-permute-start(bf16[640,256]{1,0:T(8,128)(2,1)S(1)} %get-tuple-element.43), channel_id=1, source_target_pairs={{0,1},{1,0},{2,3},{3,2},{4,5},{5,4},{6,7},{7,6},{8,9},{9,8},{10,11... | collective-permute-start | bytes 983048 | tf_op jit(solution)/shard_map/ppermute | solution.py:158
  44.8 4.8 %collective-permute-start.8 = (bf16[160,256]{1,0:T(8,128)(2,1)S(1)}, bf16[160,256]{1,0:T(8,128)(2,1)S(1)}, u32[]{:S(2)}, u32[]{:S(2)}) collective-permute-start(bf16[160,256]{1,0:T(8,128)(2,1)S(1)} %get-tuple-element.45), channel_id=1, source_target_pairs={{0,8},{8,0},{16,24},{24,16},{1,9},{9,1},{17,25},{25,17},{2,10},{10... | collective-permute-start | bytes 245768 | tf_op jit(solution)/shard_map/ppermute | solution.py:158
  46.3 5.3 %collective-permute-start.9 = (bf16[160,256]{1,0:T(8,128)(2,1)S(1)}, bf16[160,256]{1,0:T(8,128)(2,1)S(1)}, u32[]{:S(2)}, u32[]{:S(2)}) collective-permute-start(bf16[160,256]{1,0:T(8,128)(2,1)S(1)} %get-tuple-element.46), channel_id=1, source_target_pairs={{0,16},{8,24},{16,0},{24,8},{1,17},{9,25},{17,1},{25,9},{2,18},{10... | collective-permute-start | bytes 245768 | tf_op jit(solution)/shard_map/ppermute | solution.py:158
  47.8 5.3 %collective-permute-start.10 = (bf16[160,256]{1,0:T(8,128)(2,1)S(1)}, bf16[160,256]{1,0:T(8,128)(2,1)S(1)}, u32[]{:S(2)}, u32[]{:S(2)}) collective-permute-start(bf16[160,256]{1,0:T(8,128)(2,1)S(1)} %get-tuple-element.47), channel_id=1, source_target_pairs={{0,24},{8,16},{16,8},{24,0},{1,25},{9,17},{17,9},{25,1},{2,26},{10... | collective-permute-start | bytes 245768 | tf_op jit(solution)/shard_map/ppermute | solution.py:158
  53.2 7.0 %collective-permute-start.13 = (bf16[160,256]{1,0:T(8,128)(2,1)S(1)}, bf16[160,256]{1,0:T(8,128)(2,1)S(1)}, u32[]{:S(2)}, u32[]{:S(2)}) collective-permute-start(bf16[160,256]{1,0:T(8,128)(2,1)S(1)} %join.2.own_ref), channel_id=1, source_target_pairs={{0,6},{1,7},{2,4},{3,5},{4,2},{5,3},{6,0},{7,1},{8,14},{9,15},{10,... | collective-permute-start | bytes 245768 | tf_op jit(solution)/shard_map/ppermute | solution.py:158
  55.8 6.7 %collective-permute-start.12 = (bf16[160,256]{1,0:T(8,128)(2,1)S(1)}, bf16[160,256]{1,0:T(8,128)(2,1)S(1)}, u32[]{:S(2)}, u32[]{:S(2)}) collective-permute-start(bf16[160,256]{1,0:T(8,128)(2,1)S(1)} %join.2.own_ref), channel_id=1, source_target_pairs={{0,4},{1,5},{2,6},{3,7},{4,0},{5,1},{6,2},{7,3},{8,12},{9,13},{10,... | collective-permute-start | bytes 245768 | tf_op jit(solution)/shard_map/ppermute | solution.py:158
  55.8 6.7 %collective-permute-start.11 = (bf16[160,256]{1,0:T(8,128)(2,1)S(1)}, bf16[160,256]{1,0:T(8,128)(2,1)S(1)}, u32[]{:S(2)}, u32[]{:S(2)}) collective-permute-start(bf16[160,256]{1,0:T(8,128)(2,1)S(1)} %join.2.own_ref), channel_id=1, source_target_pairs={{0,2},{1,3},{2,0},{3,1},{4,6},{5,7},{6,4},{7,5},{8,10},{9,11},{10,... | collective-permute-start | bytes 245768 | tf_op jit(solution)/shard_map/ppermute | solution.py:158
  62.5 5.6 %collective-permute-start.16 = (bf16[160,256]{1,0:T(8,128)(2,1)S(1)}, bf16[160,256]{1,0:T(8,128)(2,1)S(1)}, u32[]{:S(2)}, u32[]{:S(2)}) collective-permute-start(bf16[160,256]{1,0:T(8,128)(2,1)S(1)} %join.3.piece_0), channel_id=1, source_target_pairs={{0,24},{8,16},{16,8},{24,0},{1,25},{9,17},{17,9},{25,1},{2,26},{10... | collective-permute-start | bytes 245768 | tf_op jit(solution)/shard_map/ppermute | solution.py:158
  63.5 5.3 %collective-permute-start.15 = (bf16[160,256]{1,0:T(8,128)(2,1)S(1)}, bf16[160,256]{1,0:T(8,128)(2,1)S(1)}, u32[]{:S(2)}, u32[]{:S(2)}) collective-permute-start(bf16[160,256]{1,0:T(8,128)(2,1)S(1)} %join.3.piece_0), channel_id=1, source_target_pairs={{0,16},{8,24},{16,0},{24,8},{1,17},{9,25},{17,1},{25,9},{2,18},{10... | collective-permute-start | bytes 245768 | tf_op jit(solution)/shard_map/ppermute | solution.py:158
  64.9 4.4 %collective-permute-start.14 = (bf16[160,256]{1,0:T(8,128)(2,1)S(1)}, bf16[160,256]{1,0:T(8,128)(2,1)S(1)}, u32[]{:S(2)}, u32[]{:S(2)}) collective-permute-start(bf16[160,256]{1,0:T(8,128)(2,1)S(1)} %join.3.piece_0), channel_id=1, source_target_pairs={{0,8},{8,0},{16,24},{24,16},{1,9},{9,1},{17,25},{25,17},{2,10},{10... | collective-permute-start | bytes 245768 | tf_op jit(solution)/shard_map/ppermute | solution.py:158
  66.1 3.3 %collective-permute-start.17 = (bf16[160,256]{1,0:T(8,128)(2,1)S(1)}, bf16[160,256]{1,0:T(8,128)(2,1)S(1)}, u32[]{:S(2)}, u32[]{:S(2)}) collective-permute-start(bf16[160,256]{1,0:T(8,128)(2,1)S(1)} %join.3.piece_0), channel_id=1, source_target_pairs={{0,1},{1,0},{2,3},{3,2},{4,5},{5,4},{6,7},{7,6},{8,9},{9,8},{10,11... | collective-permute-start | bytes 245768 | tf_op jit(solution)/shard_map/ppermute | solution.py:158
  68.2 1.3 %collective-permute-start.20 = (bf16[160,256]{1,0:T(8,128)(2,1)S(1)}, bf16[160,256]{1,0:T(8,128)(2,1)S(1)}, u32[]{:S(2)}, u32[]{:S(2)}) collective-permute-start(bf16[160,256]{1,0:T(8,128)(2,1)S(1)} %collective-permute-done.16.piece_3), channel_id=1, source_target_pairs={{0,1},{1,0},{2,3},{3,2},{4,5},{5,4},{6,7},{7,6},{8,9},{9,8},{10,11... | collective-permute-start | bytes 245768 | tf_op jit(solution)/shard_map/ppermute | solution.py:158
  68.8 1.3 %collective-permute-start.19 = (bf16[160,256]{1,0:T(8,128)(2,1)S(1)}, bf16[160,256]{1,0:T(8,128)(2,1)S(1)}, u32[]{:S(2)}, u32[]{:S(2)}) collective-permute-start(bf16[160,256]{1,0:T(8,128)(2,1)S(1)} %collective-permute-done.15.piece_2), channel_id=1, source_target_pairs={{0,1},{1,0},{2,3},{3,2},{4,5},{5,4},{6,7},{7,6},{8,9},{9,8},{10,11... | collective-permute-start | bytes 245768 | tf_op jit(solution)/shard_map/ppermute | solution.py:158
  69.4 1.3 %collective-permute-start.18 = (bf16[160,256]{1,0:T(8,128)(2,1)S(1)}, bf16[160,256]{1,0:T(8,128)(2,1)S(1)}, u32[]{:S(2)}, u32[]{:S(2)}) collective-permute-start(bf16[160,256]{1,0:T(8,128)(2,1)S(1)} %collective-permute-done.14.piece_1), channel_id=1, source_target_pairs={{0,1},{1,0},{2,3},{3,2},{4,5},{5,4},{6,7},{7,6},{8,9},{9,8},{10,11... | collective-permute-start | bytes 245768 | tf_op jit(solution)/shard_map/ppermute | solution.py:158

commit v7 on v6

--- a/solution.py
+++ b/solution.py
@@ -382,14 +382,14 @@
     for k in range(DEG):
         eye_ref[:, tile_of(k)] = eye
 
-    @pl.loop(0, blocks)
-    def _(i):
-        at = lanes_of(i, LANES)
+    def one_hot(u_at):
+        parts = []
         for k in range(DEG):
-            spot = jnp.broadcast_to(edge_ref[k : k + 1, at].astype(f32), (16, LANES)).astype(bf16)
+            spot = jnp.broadcast_to(edge_ref[k : k + 1, u_at].astype(f32), (16, LANES)).astype(bf16)
             hit = wide_spots == spot[None]
             hit = jnp.where(hit, jnp.ones((8, 16, LANES), bf16), jnp.zeros((8, 16, LANES), bf16))
-            e_ref[i, :, tile_of(k)] = hit.reshape(LANES, LANES)
+            parts.append(hit.reshape(LANES, LANES))
+        return parts
 
     for layer in range(2):
 
@@ -408,7 +408,14 @@
             for u in ways:
                 right = both_ref[layer, HID : 2 * HID, ats[u]]
                 left_f = left[u].astype(f32)
-                mixed_rows = [dot_nn(left[u], e_ref[ids[u], :, 0 : 2 * LANES]).astype(bf16)]
+                if layer == 0:
+                    parts = one_hot(ats[u])
+                    for k in range(DEG):
+                        e_ref[ids[u], :, tile_of(k)] = parts[k]
+                    hot = jnp.concatenate(parts[0:2], axis=1)
+                else:
+                    hot = e_ref[ids[u], :, 0 : 2 * LANES]
+                mixed_rows = [dot_nn(left[u], hot).astype(bf16)]
                 for k in range(2, DEG):
                     index = jnp.broadcast_to(edge_ref[k : k + 1, ats[u]], (HID, LANES))
                     picked = jnp.take_along_axis(left_f, index, axis=1, mode="promise_in_bounds")

time: 73.6 us -> 73 us (level)
  no operation moved by 1% of the time
where the time goes in v7:
time: 73 us; the launch traced here: 72.8 us
  Pallas kernels  29.9 us (41%)
  waiting for transfers between devices  23.6 us (32%)
  starting transfers between devices  18.2 us (25%)
  between operations  1.08 us (1%)
    pallas_call x1, Pallas kernels, run_model(): pl.pallas_call(body, grid_spec=grid_spec, out_shape=[jax.ShapeDtypeStruct...  25.2 us
    ppermute x21, waiting for transfers between devices, crossed(): lax.ppermute(value, axis, [(i, i ^ mask) for i in range(lax.axis_size(axi...  23.6 us
    ppermute x21, starting transfers between devices, crossed(): lax.ppermute(value, axis, [(i, i ^ mask) for i in range(lax.axis_size(axi...  18.2 us
    pallas_call x1, Pallas kernels, per_device(): pl.pallas_call(update_kernel, out_shape=[jax.ShapeDtypeStruct(v.shape, f3...  2.63 us
    pallas_call x1, Pallas kernels, pack_inputs(): pl.pallas_call(pack_kernel, grid_spec=grid_spec, out_shape=jax.ShapeDtype...  1.87 us
  transfers between devices with their start and end apart: 21, of which 16 were waited for; matrix products, arithmetic and copies ran while one was open for 0% of the time, Pallas kernels for 0%

profile of v7, /device:TPU:0, one launch (start us, length us, event | category | flops | bytes accessed | tf_op | source)
XLA Modules:
  0.0 72.8 jit_solution(8076132355187083520)
XLA Ops:
  0.8 1.9 %pack.1 = bf16[176,256]{1,0:T(8,128)(2,1)} custom-call(s32[1]{0:T(128)} %bitcast.1.section_ref.refs_0_, bf16[4,2048,128]{2,1,0:T(8,128)(2,1)} %refs_3_.1, s32[4,8,2048]{2,1,0:T(8,128)} %bitcast.5, s32[4,2048]{1,0:T(4,128)} %refs_5_.1, s32[4,2048]{1,0:T(4,128)} %refs_6_.1, s32[4,64]{1,0:T(4,128)} %refs_7_.1, f32[16,256]{1,0:T(8,128)} %w_in.1, ...), custom_call_target="tpu_custom_call" | custom-call | tf_op jit(solution)/shard_map/pack/pallas_call | solution.py:148
  2.6 5.0 %collective-permute-start.2 = (bf16[176,256]{1,0:T(8,128)(2,1)}, bf16[176,256]{1,0:T(8,128)(2,1)S(1)}, u32[]{:S(2)}, u32[]{:S(2)}) collective-permute-start(bf16[176,256]{1,0:T(8,128)(2,1)} %pack.1), channel_id=1, source_target_pairs={{0,6},{1,7},{2,4},{3,5},{4,2},{5,3},{6,0},{7,1},{8,14},{9,15},{10,... | collective-permute-start | bytes 270344 | tf_op jit(solution)/shard_map/ppermute | solution.py:158
  7.7 0.0 collective-permute-start.1
  7.7 0.6 collective-permute-start
  8.2 0.0 collective-permute-start.3
  8.2 3.0 %collective-permute-done.2.refs_10_ = bf16[176,256]{1,0:T(8,128)(2,1)S(1)} collective-permute-done((bf16[176,256]{1,0:T(8,128)(2,1)}, bf16[176,256]{1,0:T(8,128)(2,1)S(1)}, u32[]{:S(2)}, u32[]{:S(2)}) %collective-permute-start.2) | collective-permute-done | bytes 90144 | tf_op jit(solution)/shard_map/ppermute | solution.py:158
  11.2 0.0 collective-permute-start.6
  11.2 4.2 %collective-permute-done.1.refs_9_ = bf16[176,256]{1,0:T(8,128)(2,1)S(1)} collective-permute-done((bf16[176,256]{1,0:T(8,128)(2,1)}, bf16[176,256]{1,0:T(8,128)(2,1)S(1)}, u32[]{:S(2)}, u32[]{:S(2)}) %collective-permute-start.1) | collective-permute-done | bytes 90144 | tf_op jit(solution)/shard_map/ppermute | solution.py:158
  15.4 0.0 collective-permute-start.5
  15.5 0.0 collective-permute-done.refs_8_
  15.5 0.5 collective-permute-start.4
  16.0 0.0 collective-permute-done.3.refs_11_
  16.0 0.0 collective-permute-done.6.refs_14_
  16.0 0.8 %collective-permute-done.5.refs_13_ = bf16[176,256]{1,0:T(8,128)(2,1)S(1)} collective-permute-done((bf16[176,256]{1,0:T(8,128)(2,1)S(1)}, bf16[176,256]{1,0:T(8,128)(2,1)S(1)}, u32[]{:S(2)}, u32[]{:S(2)}) %collective-permute-start.5) | collective-permute-done | bytes 90144 | tf_op jit(solution)/shard_map/ppermute | solution.py:158
  16.7 0.2 collective-permute-done.4.refs_12_
  17.0 0.0 copy-start.2
  17.0 0.0 copy-start.3
  17.0 0.0 copy-start.5
  17.0 0.0 copy-start.6
  17.0 0.0 copy-start.10
  17.0 0.0 copy-start.11
  17.0 0.0 copy-start.12
  17.0 0.0 copy-start.15
  17.1 0.0 copy-start.16
  17.1 0.0 copy-start.17
  17.1 0.0 copy-start.18
  17.1 0.0 copy-start.19
  17.1 0.0 copy-start.20
  17.1 0.0 copy-start.21
  17.1 0.0 copy-start.22
  17.1 0.0 copy-start.24
  17.2 0.0 copy-start.25
  17.2 0.0 copy-start.26
  17.2 25.2 %model.1 = (bf16[640,256]{1,0:T(8,128)(2,1)S(1)}, bf16[640,256]{1,0:T(8,128)(2,1)S(1)}) custom-call(s32[1]{0:T(128)} %bitcast.1.section_ref.refs_0_, s32[1]{0:T(128)} %bitcast.refs_1_.refs_2_.dom_ref.spot_ref, s32[1]{0:T(128)} %bitcast.refs_1_.refs_2_.dom_ref.spot_ref, bf16[4,2048,128]{2,1,0:T(8,128)(2,1)S(1)} %copy-done, s32[4,8,2048]{2,1,0:T(8,128)S(1)} %bitcast.6, ...), custom_call_target="tpu_custom_call" | custom-call | tf_op jit(solution)/shard_map/model/pallas_call | solution.py:633
  42.4 0.5 collective-permute-start.7
  42.8 1.3 %collective-permute-done.7.got_ref = bf16[640,256]{1,0:T(8,128)(2,1)S(1)} collective-permute-done((bf16[640,256]{1,0:T(8,128)(2,1)S(1)}, bf16[640,256]{1,0:T(8,128)(2,1)S(1)}, u32[]{:S(2)}, u32[]{:S(2)}) %collective-permute-start.7) | collective-permute-done | bytes 327712 | tf_op jit(solution)/shard_map/ppermute | solution.py:158
  44.1 0.1 split.1
  44.1 1.6 %collective-permute-start.8 = (bf16[160,256]{1,0:T(8,128)(2,1)S(1)}, bf16[160,256]{1,0:T(8,128)(2,1)S(1)}, u32[]{:S(2)}, u32[]{:S(2)}) collective-permute-start(bf16[160,256]{1,0:T(8,128)(2,1)S(1)} %get-tuple-element.45), channel_id=1, source_target_pairs={{0,8},{8,0},{16,24},{24,16},{1,9},{9,1},{17,25},{25,17},{2,10},{10... | collective-permute-start | bytes 245768 | tf_op jit(solution)/shard_map/ppermute | solution.py:158
  45.7 1.5 %collective-permute-start.9 = (bf16[160,256]{1,0:T(8,128)(2,1)S(1)}, bf16[160,256]{1,0:T(8,128)(2,1)S(1)}, u32[]{:S(2)}, u32[]{:S(2)}) collective-permute-start(bf16[160,256]{1,0:T(8,128)(2,1)S(1)} %get-tuple-element.46), channel_id=1, source_target_pairs={{0,16},{8,24},{16,0},{24,8},{1,17},{9,25},{17,1},{25,9},{2,18},{10... | collective-permute-start | bytes 245768 | tf_op jit(solution)/shard_map/ppermute | solution.py:158
  47.2 0.5 collective-permute-start.10
  47.7 1.2 %collective-permute-done.8.one_ref = bf16[160,256]{1,0:T(8,128)(2,1)S(1)} collective-permute-done((bf16[160,256]{1,0:T(8,128)(2,1)S(1)}, bf16[160,256]{1,0:T(8,128)(2,1)S(1)}, u32[]{:S(2)}, u32[]{:S(2)}) %collective-permute-start.8) | collective-permute-done | bytes 81952 | tf_op jit(solution)/shard_map/ppermute | solution.py:158
  48.9 2.0 %collective-permute-done.9.two_ref = bf16[160,256]{1,0:T(8,128)(2,1)S(1)} collective-permute-done((bf16[160,256]{1,0:T(8,128)(2,1)S(1)}, bf16[160,256]{1,0:T(8,128)(2,1)S(1)}, u32[]{:S(2)}, u32[]{:S(2)}) %collective-permute-start.9) | collective-permute-done | bytes 81952 | tf_op jit(solution)/shard_map/ppermute | solution.py:158
  51.0 1.6 %collective-permute-done.10.three_ref = bf16[160,256]{1,0:T(8,128)(2,1)S(1)} collective-permute-done((bf16[160,256]{1,0:T(8,128)(2,1)S(1)}, bf16[160,256]{1,0:T(8,128)(2,1)S(1)}, u32[]{:S(2)}, u32[]{:S(2)}) %collective-permute-start.10) | collective-permute-done | bytes 81952 | tf_op jit(solution)/shard_map/ppermute | solution.py:158
  52.6 2.6 %collective-permute-start.13 = (bf16[160,256]{1,0:T(8,128)(2,1)S(1)}, bf16[160,256]{1,0:T(8,128)(2,1)S(1)}, u32[]{:S(2)}, u32[]{:S(2)}) collective-permute-start(bf16[160,256]{1,0:T(8,128)(2,1)S(1)} %join.2.own_ref), channel_id=1, source_target_pairs={{0,6},{1,7},{2,4},{3,5},{4,2},{5,3},{6,0},{7,1},{8,14},{9,15},{10,... | collective-permute-start | bytes 245768 | tf_op jit(solution)/shard_map/ppermute | solution.py:158
  55.2 0.0 collective-permute-start.12
  55.2 1.9 %collective-permute-start.11 = (bf16[160,256]{1,0:T(8,128)(2,1)S(1)}, bf16[160,256]{1,0:T(8,128)(2,1)S(1)}, u32[]{:S(2)}, u32[]{:S(2)}) collective-permute-start(bf16[160,256]{1,0:T(8,128)(2,1)S(1)} %join.2.own_ref), channel_id=1, source_target_pairs={{0,2},{1,3},{2,0},{3,1},{4,6},{5,7},{6,4},{7,5},{8,10},{9,11},{10,... | collective-permute-start | bytes 245768 | tf_op jit(solution)/shard_map/ppermute | solution.py:158
  57.1 2.5 %collective-permute-done.13.three_ref = bf16[160,256]{1,0:T(8,128)(2,1)S(1)} collective-permute-done((bf16[160,256]{1,0:T(8,128)(2,1)S(1)}, bf16[160,256]{1,0:T(8,128)(2,1)S(1)}, u32[]{:S(2)}, u32[]{:S(2)}) %collective-permute-start.13) | collective-permute-done | bytes 81952 | tf_op jit(solution)/shard_map/ppermute | solution.py:158
  59.6 2.3 %collective-permute-done.12.two_ref = bf16[160,256]{1,0:T(8,128)(2,1)S(1)} collective-permute-done((bf16[160,256]{1,0:T(8,128)(2,1)S(1)}, bf16[160,256]{1,0:T(8,128)(2,1)S(1)}, u32[]{:S(2)}, u32[]{:S(2)}) %collective-permute-start.12) | collective-permute-done | bytes 81952 | tf_op jit(solution)/shard_map/ppermute | solution.py:158
  61.9 0.0 collective-permute-done.11.one_ref
  61.9 0.9 %collective-permute-start.16 = (bf16[160,256]{1,0:T(8,128)(2,1)S(1)}, bf16[160,256]{1,0:T(8,128)(2,1)S(1)}, u32[]{:S(2)}, u32[]{:S(2)}) collective-permute-start(bf16[160,256]{1,0:T(8,128)(2,1)S(1)} %join.3.piece_0), channel_id=1, source_target_pairs={{0,24},{8,16},{16,8},{24,0},{1,25},{9,17},{17,9},{25,1},{2,26},{10... | collective-permute-start | bytes 245768 | tf_op jit(solution)/shard_map/ppermute | solution.py:158
  62.9 1.5 %collective-permute-start.15 = (bf16[160,256]{1,0:T(8,128)(2,1)S(1)}, bf16[160,256]{1,0:T(8,128)(2,1)S(1)}, u32[]{:S(2)}, u32[]{:S(2)}) collective-permute-start(bf16[160,256]{1,0:T(8,128)(2,1)S(1)} %join.3.piece_0), channel_id=1, source_target_pairs={{0,16},{8,24},{16,0},{24,8},{1,17},{9,25},{17,1},{25,9},{2,18},{10... | collective-permute-start | bytes 245768 | tf_op jit(solution)/shard_map/ppermute | solution.py:158
  64.3 1.2 %collective-permute-start.14 = (bf16[160,256]{1,0:T(8,128)(2,1)S(1)}, bf16[160,256]{1,0:T(8,128)(2,1)S(1)}, u32[]{:S(2)}, u32[]{:S(2)}) collective-permute-start(bf16[160,256]{1,0:T(8,128)(2,1)S(1)} %join.3.piece_0), channel_id=1, source_target_pairs={{0,8},{8,0},{16,24},{24,16},{1,9},{9,1},{17,25},{25,17},{2,10},{10... | collective-permute-start | bytes 245768 | tf_op jit(solution)/shard_map/ppermute | solution.py:158
  65.5 0.0 collective-permute-start.17
  65.5 2.1 %collective-permute-done.16.piece_3 = bf16[160,256]{1,0:T(8,128)(2,1)S(1)} collective-permute-done((bf16[160,256]{1,0:T(8,128)(2,1)S(1)}, bf16[160,256]{1,0:T(8,128)(2,1)S(1)}, u32[]{:S(2)}, u32[]{:S(2)}) %collective-permute-start.16) | collective-permute-done | bytes 81952 | tf_op jit(solution)/shard_map/ppermute | solution.py:158
  67.5 0.0 collective-permute-start.20
  67.5 0.6 collective-permute-done.15.piece_2
  68.2 0.0 collective-permute-start.19
  68.2 0.6 collective-permute-done.14.piece_1
  68.8 0.0 collective-permute-start.18
  68.8 0.0 collective-permute-done.17.piece_4
  68.8 0.1 collective-permute-done.20.piece_7
  68.8 0.6 collective-permute-done.19.piece_6
  69.5 0.6 collective-permute-done.18.piece_5
  70.2 2.6 %update.1 = (f32[16,256]{1,0:T(8,128)}, f32[2,2,32,256]{3,2,1,0:T(8,128)}, f32[8,40]{1,0:T(8,128)}, f32[1128]{0:T(1024)}, f32[16,128]{1,0:T(8,128)}, /*index=5*/...) custom-call(s32[1]{0:T(128)} %bitcast.refs_1_.refs_2_.dom_ref.spot_r, ...), custom_call_target="tpu_custom_call" | custom-call | tf_op jit(solution)/shard_map/update/pallas_call | solution.py:958
  (38 shorter events, 0.2 us)
Async XLA Ops:
  0.7 16.2 %copy-start.13 = (f32[8,40]{1,0:T(8,128)S(1)}, f32[8,40]{1,0:T(8,128)}, u32[]{:S(2)}) copy-start(f32[8,40]{1,0:T(8,128)} %w_out.1) | copy-start | bytes 3844
  0.7 16.2 %copy-start.1 = (f32[2,2,32,256]{3,2,1,0:T(8,128)S(1)}, f32[2,2,32,256]{3,2,1,0:T(8,128)}, u32[]{:S(2)}) copy-start(f32[2,2,32,256]{3,2,1,0:T(8,128)} %w_gat.1) | copy-start | bytes 393220
  0.7 16.2 %copy-start.7 = (f32[16,256]{1,0:T(8,128)S(1)}, f32[16,256]{1,0:T(8,128)}, u32[]{:S(2)}) copy-start(f32[16,256]{1,0:T(8,128)} %w_in.1) | copy-start | bytes 49156
  0.7 16.2 %copy-start.9 = (s32[4,2048]{1,0:T(4,128)S(1)}, s32[4,2048]{1,0:T(4,128)}, u32[]{:S(2)}) copy-start(s32[4,2048]{1,0:T(4,128)} %refs_6_.1) | copy-start | bytes 98308
  0.7 16.2 %copy-start.8 = (s32[4,2048]{1,0:T(4,128)S(1)}, s32[4,2048]{1,0:T(4,128)}, u32[]{:S(2)}) copy-start(s32[4,2048]{1,0:T(4,128)} %refs_5_.1) | copy-start | bytes 98308
  0.7 16.2 %copy-start.23 = (s32[4,64]{1,0:T(4,128)S(1)}, s32[4,64]{1,0:T(4,128)}, u32[]{:S(2)}) copy-start(s32[4,64]{1,0:T(4,128)} %refs_7_.1) | copy-start | bytes 3076
  0.7 16.2 %copy-start = (bf16[4,2048,128]{2,1,0:T(8,128)(2,1)S(1)}, bf16[4,2048,128]{2,1,0:T(8,128)(2,1)}, u32[]{:S(2)}) copy-start(bf16[4,2048,128]{2,1,0:T(8,128)(2,1)} %refs_3_.1) | copy-start | bytes 6291460
  0.7 16.2 %copy-start.4 = (s32[4,2048,8]{1,2,0:T(8,128)S(1)}, s32[4,2048,8]{1,2,0:T(8,128)}, u32[]{:S(2)}) copy-start(s32[4,2048,8]{1,2,0:T(8,128)} %param.28) | copy-start | bytes 786436
  0.7 16.2 %copy-start.14 = (f32[1128]{0:T(1024)S(1)}, f32[1128]{0:T(1024)}, u32[]{:S(2)}) copy-start(f32[1128]{0:T(1024)} %small.1) | copy-start | bytes 13540
  2.6 8.6 %collective-permute-start.2 = (bf16[176,256]{1,0:T(8,128)(2,1)}, bf16[176,256]{1,0:T(8,128)(2,1)S(1)}, u32[]{:S(2)}, u32[]{:S(2)}) collective-permute-start(bf16[176,256]{1,0:T(8,128)(2,1)} %pack.1), channel_id=1, source_target_pairs={{0,6},{1,7},{2,4},{3,5},{4,2},{5,3},{6,0},{7,1},{8,14},{9,15},{10,... | collective-permute-start | bytes 270344 | tf_op jit(solution)/shard_map/ppermute | solution.py:158
  7.7 7.8 %collective-permute-start.1 = (bf16[176,256]{1,0:T(8,128)(2,1)}, bf16[176,256]{1,0:T(8,128)(2,1)S(1)}, u32[]{:S(2)}, u32[]{:S(2)}) collective-permute-start(bf16[176,256]{1,0:T(8,128)(2,1)} %pack.1), channel_id=1, source_target_pairs={{0,4},{1,5},{2,6},{3,7},{4,0},{5,1},{6,2},{7,3},{8,12},{9,13},{10,... | collective-permute-start | bytes 270344 | tf_op jit(solution)/shard_map/ppermute | solution.py:158
  7.7 7.8 %collective-permute-start = (bf16[176,256]{1,0:T(8,128)(2,1)}, bf16[176,256]{1,0:T(8,128)(2,1)S(1)}, u32[]{:S(2)}, u32[]{:S(2)}) collective-permute-start(bf16[176,256]{1,0:T(8,128)(2,1)} %pack.1), channel_id=1, source_target_pairs={{0,2},{1,3},{2,0},{3,1},{4,6},{5,7},{6,4},{7,5},{8,10},{9,11},{10,... | collective-permute-start | bytes 270344 | tf_op jit(solution)/shard_map/ppermute | solution.py:158
  8.2 7.7 %collective-permute-start.3 = (bf16[176,256]{1,0:T(8,128)(2,1)}, bf16[176,256]{1,0:T(8,128)(2,1)S(1)}, u32[]{:S(2)}, u32[]{:S(2)}) collective-permute-start(bf16[176,256]{1,0:T(8,128)(2,1)} %pack.1), channel_id=1, source_target_pairs={{0,1},{1,0},{2,3},{3,2},{4,5},{5,4},{6,7},{7,6},{8,9},{9,8},{10,11... | collective-permute-start | bytes 270344 | tf_op jit(solution)/shard_map/ppermute | solution.py:158
  11.2 4.7 %collective-permute-start.6 = (bf16[176,256]{1,0:T(8,128)(2,1)S(1)}, bf16[176,256]{1,0:T(8,128)(2,1)S(1)}, u32[]{:S(2)}, u32[]{:S(2)}) collective-permute-start(bf16[176,256]{1,0:T(8,128)(2,1)S(1)} %collective-permute-done.2.refs_10_), channel_id=1, source_target_pairs={{0,1},{1,0},{2,3},{3,2},{4,5},{5,4},{6,7},{7,6},{8,9},{9,8},{10,11... | collective-permute-start | bytes 270344 | tf_op jit(solution)/shard_map/ppermute | solution.py:158
  15.4 1.3 %collective-permute-start.5 = (bf16[176,256]{1,0:T(8,128)(2,1)S(1)}, bf16[176,256]{1,0:T(8,128)(2,1)S(1)}, u32[]{:S(2)}, u32[]{:S(2)}) collective-permute-start(bf16[176,256]{1,0:T(8,128)(2,1)S(1)} %collective-permute-done.1.refs_9_), channel_id=1, source_target_pairs={{0,1},{1,0},{2,3},{3,2},{4,5},{5,4},{6,7},{7,6},{8,9},{9,8},{10,11... | collective-permute-start | bytes 270344 | tf_op jit(solution)/shard_map/ppermute | solution.py:158
  15.5 1.4 %collective-permute-start.4 = (bf16[176,256]{1,0:T(8,128)(2,1)S(1)}, bf16[176,256]{1,0:T(8,128)(2,1)S(1)}, u32[]{:S(2)}, u32[]{:S(2)}) collective-permute-start(bf16[176,256]{1,0:T(8,128)(2,1)S(1)} %collective-permute-done.refs_8_), channel_id=1, source_target_pairs={{0,1},{1,0},{2,3},{3,2},{4,5},{5,4},{6,7},{7,6},{8,9},{9,8},{10,11... | collective-permute-start | bytes 270344 | tf_op jit(solution)/shard_map/ppermute | solution.py:158
  17.0 53.1 %copy-start.2 = (f32[2,2,256,256]{3,2,1,0:T(8,128)S(1)}, f32[2,2,256,256]{3,2,1,0:T(8,128)}, u32[]{:S(2)}) copy-start(f32[2,2,256,256]{3,2,1,0:T(8,128)} %r_gat.1) | copy-start | bytes 3145732
  17.0 53.1 %copy-start.3 = (f32[2,2,256,256]{3,2,1,0:T(8,128)S(1)}, f32[2,2,256,256]{3,2,1,0:T(8,128)}, u32[]{:S(2)}) copy-start(f32[2,2,256,256]{3,2,1,0:T(8,128)} %rr_gat.1) | copy-start | bytes 3145732
  17.0 53.1 %copy-start.5 = (f32[256,256]{1,0:T(8,128)S(1)}, f32[256,256]{1,0:T(8,128)}, u32[]{:S(2)}) copy-start(f32[256,256]{1,0:T(8,128)} %r_in.1) | copy-start | bytes 786436
  17.0 53.1 %copy-start.6 = (f32[256,256]{1,0:T(8,128)S(1)}, f32[256,256]{1,0:T(8,128)}, u32[]{:S(2)}) copy-start(f32[256,256]{1,0:T(8,128)} %rr_in.1) | copy-start | bytes 786436
  17.0 53.1 %copy-start.10 = (f32[2,2,32,256]{3,2,1,0:T(8,128)S(1)}, f32[2,2,32,256]{3,2,1,0:T(8,128)}, u32[]{:S(2)}) copy-start(f32[2,2,32,256]{3,2,1,0:T(8,128)} %l_gat.1) | copy-start | bytes 393220
  17.0 53.0 %copy-start.11 = (f32[2,2,32,256]{3,2,1,0:T(8,128)S(1)}, f32[2,2,32,256]{3,2,1,0:T(8,128)}, u32[]{:S(2)}) copy-start(f32[2,2,32,256]{3,2,1,0:T(8,128)} %rl_gat.1) | copy-start | bytes 393220
  17.0 53.0 %copy-start.12 = (f32[2,2,32,256]{3,2,1,0:T(8,128)S(1)}, f32[2,2,32,256]{3,2,1,0:T(8,128)}, u32[]{:S(2)}) copy-start(f32[2,2,32,256]{3,2,1,0:T(8,128)} %e_gat.1) | copy-start | bytes 393220
  17.0 53.0 %copy-start.15 = (f32[40,40]{1,0:T(8,128)S(1)}, f32[40,40]{1,0:T(8,128)}, u32[]{:S(2)}) copy-start(f32[40,40]{1,0:T(8,128)} %r_out.1) | copy-start | bytes 19204
  17.1 53.0 %copy-start.16 = (f32[40,40]{1,0:T(8,128)S(1)}, f32[40,40]{1,0:T(8,128)}, u32[]{:S(2)}) copy-start(f32[40,40]{1,0:T(8,128)} %rr_out.1) | copy-start | bytes 19204
  17.1 53.0 %copy-start.17 = (f32[16,256]{1,0:T(8,128)S(1)}, f32[16,256]{1,0:T(8,128)}, u32[]{:S(2)}) copy-start(f32[16,256]{1,0:T(8,128)} %e_in.1) | copy-start | bytes 49156
  17.1 53.0 %copy-start.18 = (f32[16,128]{1,0:T(8,128)S(1)}, f32[16,128]{1,0:T(8,128)}, u32[]{:S(2)}) copy-start(f32[16,128]{1,0:T(8,128)} %l_in.1) | copy-start | bytes 24580
  17.1 53.0 %copy-start.19 = (f32[16,128]{1,0:T(8,128)S(1)}, f32[16,128]{1,0:T(8,128)}, u32[]{:S(2)}) copy-start(f32[16,128]{1,0:T(8,128)} %rl_in.1) | copy-start | bytes 24580
  17.1 53.0 %copy-start.20 = (f32[1128]{0:T(1024)S(1)}, f32[1128]{0:T(1024)}, u32[]{:S(2)}) copy-start(f32[1128]{0:T(1024)} %first.1) | copy-start | bytes 13540
  17.1 53.0 %copy-start.21 = (f32[1128]{0:T(1024)S(1)}, f32[1128]{0:T(1024)}, u32[]{:S(2)}) copy-start(f32[1128]{0:T(1024)} %second.1) | copy-start | bytes 13540
  17.1 53.0 %copy-start.22 = (f32[1128]{0:T(1024)S(1)}, f32[1128]{0:T(1024)}, u32[]{:S(2)}) copy-start(f32[1128]{0:T(1024)} %e_small.1) | copy-start | bytes 13540
  17.1 53.0 %copy-start.24 = (f32[8,64]{1,0:T(8,128)S(1)}, f32[8,64]{1,0:T(8,128)}, u32[]{:S(2)}) copy-start(f32[8,64]{1,0:T(8,128)} %l_out.1) | copy-start | bytes 6148
  17.2 53.0 %copy-start.25 = (f32[8,64]{1,0:T(8,128)S(1)}, f32[8,64]{1,0:T(8,128)}, u32[]{:S(2)}) copy-start(f32[8,64]{1,0:T(8,128)} %rl_out.1) | copy-start | bytes 6148
  17.2 53.0 %copy-start.26 = (f32[8,40]{1,0:T(8,128)S(1)}, f32[8,40]{1,0:T(8,128)}, u32[]{:S(2)}) copy-start(f32[8,40]{1,0:T(8,128)} %e_out.1) | copy-start | bytes 3844
  42.4 1.7 %collective-permute-start.7 = (bf16[640,256]{1,0:T(8,128)(2,1)S(1)}, bf16[640,256]{1,0:T(8,128)(2,1)S(1)}, u32[]{:S(2)}, u32[]{:S(2)}) collective-permute-start(bf16[640,256]{1,0:T(8,128)(2,1)S(1)} %get-tuple-element.43), channel_id=1, source_target_pairs={{0,1},{1,0},{2,3},{3,2},{4,5},{5,4},{6,7},{7,6},{8,9},{9,8},{10,11... | collective-permute-start | bytes 983048 | tf_op jit(solution)/shard_map/ppermute | solution.py:158
  44.1 4.8 %collective-permute-start.8 = (bf16[160,256]{1,0:T(8,128)(2,1)S(1)}, bf16[160,256]{1,0:T(8,128)(2,1)S(1)}, u32[]{:S(2)}, u32[]{:S(2)}) collective-permute-start(bf16[160,256]{1,0:T(8,128)(2,1)S(1)} %get-tuple-element.45), channel_id=1, source_target_pairs={{0,8},{8,0},{16,24},{24,16},{1,9},{9,1},{17,25},{25,17},{2,10},{10... | collective-permute-start | bytes 245768 | tf_op jit(solution)/shard_map/ppermute | solution.py:158
  45.7 5.3 %collective-permute-start.9 = (bf16[160,256]{1,0:T(8,128)(2,1)S(1)}, bf16[160,256]{1,0:T(8,128)(2,1)S(1)}, u32[]{:S(2)}, u32[]{:S(2)}) collective-permute-start(bf16[160,256]{1,0:T(8,128)(2,1)S(1)} %get-tuple-element.46), channel_id=1, source_target_pairs={{0,16},{8,24},{16,0},{24,8},{1,17},{9,25},{17,1},{25,9},{2,18},{10... | collective-permute-start | bytes 245768 | tf_op jit(solution)/shard_map/ppermute | solution.py:158
  47.2 5.3 %collective-permute-start.10 = (bf16[160,256]{1,0:T(8,128)(2,1)S(1)}, bf16[160,256]{1,0:T(8,128)(2,1)S(1)}, u32[]{:S(2)}, u32[]{:S(2)}) collective-permute-start(bf16[160,256]{1,0:T(8,128)(2,1)S(1)} %get-tuple-element.47), channel_id=1, source_target_pairs={{0,24},{8,16},{16,8},{24,0},{1,25},{9,17},{17,9},{25,1},{2,26},{10... | collective-permute-start | bytes 245768 | tf_op jit(solution)/shard_map/ppermute | solution.py:158
  52.6 7.0 %collective-permute-start.13 = (bf16[160,256]{1,0:T(8,128)(2,1)S(1)}, bf16[160,256]{1,0:T(8,128)(2,1)S(1)}, u32[]{:S(2)}, u32[]{:S(2)}) collective-permute-start(bf16[160,256]{1,0:T(8,128)(2,1)S(1)} %join.2.own_ref), channel_id=1, source_target_pairs={{0,6},{1,7},{2,4},{3,5},{4,2},{5,3},{6,0},{7,1},{8,14},{9,15},{10,... | collective-permute-start | bytes 245768 | tf_op jit(solution)/shard_map/ppermute | solution.py:158
  55.2 6.7 %collective-permute-start.12 = (bf16[160,256]{1,0:T(8,128)(2,1)S(1)}, bf16[160,256]{1,0:T(8,128)(2,1)S(1)}, u32[]{:S(2)}, u32[]{:S(2)}) collective-permute-start(bf16[160,256]{1,0:T(8,128)(2,1)S(1)} %join.2.own_ref), channel_id=1, source_target_pairs={{0,4},{1,5},{2,6},{3,7},{4,0},{5,1},{6,2},{7,3},{8,12},{9,13},{10,... | collective-permute-start | bytes 245768 | tf_op jit(solution)/shard_map/ppermute | solution.py:158
  55.2 6.7 %collective-permute-start.11 = (bf16[160,256]{1,0:T(8,128)(2,1)S(1)}, bf16[160,256]{1,0:T(8,128)(2,1)S(1)}, u32[]{:S(2)}, u32[]{:S(2)}) collective-permute-start(bf16[160,256]{1,0:T(8,128)(2,1)S(1)} %join.2.own_ref), channel_id=1, source_target_pairs={{0,2},{1,3},{2,0},{3,1},{4,6},{5,7},{6,4},{7,5},{8,10},{9,11},{10,... | collective-permute-start | bytes 245768 | tf_op jit(solution)/shard_map/ppermute | solution.py:158
  61.9 5.6 %collective-permute-start.16 = (bf16[160,256]{1,0:T(8,128)(2,1)S(1)}, bf16[160,256]{1,0:T(8,128)(2,1)S(1)}, u32[]{:S(2)}, u32[]{:S(2)}) collective-permute-start(bf16[160,256]{1,0:T(8,128)(2,1)S(1)} %join.3.piece_0), channel_id=1, source_target_pairs={{0,24},{8,16},{16,8},{24,0},{1,25},{9,17},{17,9},{25,1},{2,26},{10... | collective-permute-start | bytes 245768 | tf_op jit(solution)/shard_map/ppermute | solution.py:158
  62.9 5.3 %collective-permute-start.15 = (bf16[160,256]{1,0:T(8,128)(2,1)S(1)}, bf16[160,256]{1,0:T(8,128)(2,1)S(1)}, u32[]{:S(2)}, u32[]{:S(2)}) collective-permute-start(bf16[160,256]{1,0:T(8,128)(2,1)S(1)} %join.3.piece_0), channel_id=1, source_target_pairs={{0,16},{8,24},{16,0},{24,8},{1,17},{9,25},{17,1},{25,9},{2,18},{10... | collective-permute-start | bytes 245768 | tf_op jit(solution)/shard_map/ppermute | solution.py:158
  64.3 4.4 %collective-permute-start.14 = (bf16[160,256]{1,0:T(8,128)(2,1)S(1)}, bf16[160,256]{1,0:T(8,128)(2,1)S(1)}, u32[]{:S(2)}, u32[]{:S(2)}) collective-permute-start(bf16[160,256]{1,0:T(8,128)(2,1)S(1)} %join.3.piece_0), channel_id=1, source_target_pairs={{0,8},{8,0},{16,24},{24,16},{1,9},{9,1},{17,25},{25,17},{2,10},{10... | collective-permute-start | bytes 245768 | tf_op jit(solution)/shard_map/ppermute | solution.py:158
  65.5 3.3 %collective-permute-start.17 = (bf16[160,256]{1,0:T(8,128)(2,1)S(1)}, bf16[160,256]{1,0:T(8,128)(2,1)S(1)}, u32[]{:S(2)}, u32[]{:S(2)}) collective-permute-start(bf16[160,256]{1,0:T(8,128)(2,1)S(1)} %join.3.piece_0), channel_id=1, source_target_pairs={{0,1},{1,0},{2,3},{3,2},{4,5},{5,4},{6,7},{7,6},{8,9},{9,8},{10,11... | collective-permute-start | bytes 245768 | tf_op jit(solution)/shard_map/ppermute | solution.py:158
  67.5 1.3 %collective-permute-start.20 = (bf16[160,256]{1,0:T(8,128)(2,1)S(1)}, bf16[160,256]{1,0:T(8,128)(2,1)S(1)}, u32[]{:S(2)}, u32[]{:S(2)}) collective-permute-start(bf16[160,256]{1,0:T(8,128)(2,1)S(1)} %collective-permute-done.16.piece_3), channel_id=1, source_target_pairs={{0,1},{1,0},{2,3},{3,2},{4,5},{5,4},{6,7},{7,6},{8,9},{9,8},{10,11... | collective-permute-start | bytes 245768 | tf_op jit(solution)/shard_map/ppermute | solution.py:158
  68.2 1.3 %collective-permute-start.19 = (bf16[160,256]{1,0:T(8,128)(2,1)S(1)}, bf16[160,256]{1,0:T(8,128)(2,1)S(1)}, u32[]{:S(2)}, u32[]{:S(2)}) collective-permute-start(bf16[160,256]{1,0:T(8,128)(2,1)S(1)} %collective-permute-done.15.piece_2), channel_id=1, source_target_pairs={{0,1},{1,0},{2,3},{3,2},{4,5},{5,4},{6,7},{7,6},{8,9},{9,8},{10,11... | collective-permute-start | bytes 245768 | tf_op jit(solution)/shard_map/ppermute | solution.py:158
  68.8 1.3 %collective-permute-start.18 = (bf16[160,256]{1,0:T(8,128)(2,1)S(1)}, bf16[160,256]{1,0:T(8,128)(2,1)S(1)}, u32[]{:S(2)}, u32[]{:S(2)}) collective-permute-start(bf16[160,256]{1,0:T(8,128)(2,1)S(1)} %collective-permute-done.14.piece_1), channel_id=1, source_target_pairs={{0,1},{1,0},{2,3},{3,2},{4,5},{5,4},{6,7},{7,6},{8,9},{9,8},{10,11... | collective-permute-start | bytes 245768 | tf_op jit(solution)/shard_map/ppermute | solution.py:158

commit v8 on v7

--- a/solution.py
+++ b/solution.py
@@ -435,7 +435,7 @@
                 for k in range(1, SLOTS):
                     total = total + grown[u][:, tile_of(k)]
                 inverse = 1.0 / total
-                grids = [zero] * HEADS
+                grids = [None] * HEADS
                 for k in range(SLOTS):
                     alpha = grown[u][:, tile_of(k)] * inverse
                     al_ref[layer, ids[u], :, tile_of(k)] = alpha
@@ -447,7 +447,8 @@
                     hit = spots == spot[None]
                     for h in range(HEADS):
                         part = jnp.broadcast_to(alpha[h : h + 1], (16, LANES)).astype(bf16)
-                        grids[h] = grids[h] + jnp.where(hit, part[None], zero)
+                        part = jnp.where(hit, part[None], zero)
+                        grids[h] = part if k == 0 else grids[h] + part
                 grids_all.append(grids)
             for u in ways:
                 pooled = None

time: 73 us -> 73 us (level)
  no operation moved by 1% of the time
where the time goes in v8:
time: 73 us; the launch traced here: 72.8 us
  Pallas kernels  29.9 us (41%)
  waiting for transfers between devices  23.6 us (32%)
  starting transfers between devices  18.2 us (25%)
  between operations  1.08 us (1%)
    pallas_call x1, Pallas kernels, run_model(): pl.pallas_call(body, grid_spec=grid_spec, out_shape=[jax.ShapeDtypeStruct...  25.2 us
    ppermute x21, waiting for transfers between devices, crossed(): lax.ppermute(value, axis, [(i, i ^ mask) for i in range(lax.axis_size(axi...  23.6 us
    ppermute x21, starting transfers between devices, crossed(): lax.ppermute(value, axis, [(i, i ^ mask) for i in range(lax.axis_size(axi...  18.2 us
    pallas_call x1, Pallas kernels, per_device(): pl.pallas_call(update_kernel, out_shape=[jax.ShapeDtypeStruct(v.shape, f3...  2.63 us
    pallas_call x1, Pallas kernels, pack_inputs(): pl.pallas_call(pack_kernel, grid_spec=grid_spec, out_shape=jax.ShapeDtype...  1.87 us
  transfers between devices with their start and end apart: 21, of which 16 were waited for; matrix products, arithmetic and copies ran while one was open for 0% of the time, Pallas kernels for 0%

profile of v8, /device:TPU:0, one launch (start us, length us, event | category | flops | bytes accessed | tf_op | source)
XLA Modules:
  0.0 72.8 jit_solution(420707053477023781)
XLA Ops:
  0.8 1.9 %pack.1 = bf16[176,256]{1,0:T(8,128)(2,1)} custom-call(s32[1]{0:T(128)} %bitcast.1.section_ref.refs_0_, bf16[4,2048,128]{2,1,0:T(8,128)(2,1)} %refs_3_.1, s32[4,8,2048]{2,1,0:T(8,128)} %bitcast.5, s32[4,2048]{1,0:T(4,128)} %refs_5_.1, s32[4,2048]{1,0:T(4,128)} %refs_6_.1, s32[4,64]{1,0:T(4,128)} %refs_7_.1, f32[16,256]{1,0:T(8,128)} %w_in.1, ...), custom_call_target="tpu_custom_call" | custom-call | tf_op jit(solution)/shard_map/pack/pallas_call | solution.py:148
  2.6 5.0 %collective-permute-start.2 = (bf16[176,256]{1,0:T(8,128)(2,1)}, bf16[176,256]{1,0:T(8,128)(2,1)S(1)}, u32[]{:S(2)}, u32[]{:S(2)}) collective-permute-start(bf16[176,256]{1,0:T(8,128)(2,1)} %pack.1), channel_id=1, source_target_pairs={{0,6},{1,7},{2,4},{3,5},{4,2},{5,3},{6,0},{7,1},{8,14},{9,15},{10,... | collective-permute-start | bytes 270344 | tf_op jit(solution)/shard_map/ppermute | solution.py:158
  7.7 0.0 collective-permute-start.1
  7.7 0.6 collective-permute-start
  8.2 0.0 collective-permute-start.3
  8.2 3.0 %collective-permute-done.2.refs_10_ = bf16[176,256]{1,0:T(8,128)(2,1)S(1)} collective-permute-done((bf16[176,256]{1,0:T(8,128)(2,1)}, bf16[176,256]{1,0:T(8,128)(2,1)S(1)}, u32[]{:S(2)}, u32[]{:S(2)}) %collective-permute-start.2) | collective-permute-done | bytes 90144 | tf_op jit(solution)/shard_map/ppermute | solution.py:158
  11.2 0.0 collective-permute-start.6
  11.2 4.2 %collective-permute-done.1.refs_9_ = bf16[176,256]{1,0:T(8,128)(2,1)S(1)} collective-permute-done((bf16[176,256]{1,0:T(8,128)(2,1)}, bf16[176,256]{1,0:T(8,128)(2,1)S(1)}, u32[]{:S(2)}, u32[]{:S(2)}) %collective-permute-start.1) | collective-permute-done | bytes 90144 | tf_op jit(solution)/shard_map/ppermute | solution.py:158
  15.4 0.0 collective-permute-start.5
  15.5 0.0 collective-permute-done.refs_8_
  15.5 0.5 collective-permute-start.4
  16.0 0.0 collective-permute-done.3.refs_11_
  16.0 0.0 collective-permute-done.6.refs_14_
  16.0 0.8 %collective-permute-done.5.refs_13_ = bf16[176,256]{1,0:T(8,128)(2,1)S(1)} collective-permute-done((bf16[176,256]{1,0:T(8,128)(2,1)S(1)}, bf16[176,256]{1,0:T(8,128)(2,1)S(1)}, u32[]{:S(2)}, u32[]{:S(2)}) %collective-permute-start.5) | collective-permute-done | bytes 90144 | tf_op jit(solution)/shard_map/ppermute | solution.py:158
  16.7 0.2 collective-permute-done.4.refs_12_
  17.0 0.0 copy-start.2
  17.0 0.0 copy-start.3
  17.0 0.0 copy-start.5
  17.0 0.0 copy-start.6
  17.0 0.0 copy-start.10
  17.0 0.0 copy-start.11
  17.0 0.0 copy-start.12
  17.0 0.0 copy-start.15
  17.1 0.0 copy-start.16
  17.1 0.0 copy-start.17
  17.1 0.0 copy-start.18
  17.1 0.0 copy-start.19
  17.1 0.0 copy-start.20
  17.1 0.0 copy-start.21
  17.1 0.0 copy-start.22
  17.1 0.0 copy-start.24
  17.2 0.0 copy-start.25
  17.2 0.0 copy-start.26
  17.2 25.2 %model.1 = (bf16[640,256]{1,0:T(8,128)(2,1)S(1)}, bf16[640,256]{1,0:T(8,128)(2,1)S(1)}) custom-call(s32[1]{0:T(128)} %bitcast.1.section_ref.refs_0_, s32[1]{0:T(128)} %bitcast.refs_1_.refs_2_.dom_ref.spot_ref, s32[1]{0:T(128)} %bitcast.refs_1_.refs_2_.dom_ref.spot_ref, bf16[4,2048,128]{2,1,0:T(8,128)(2,1)S(1)} %copy-done, s32[4,8,2048]{2,1,0:T(8,128)S(1)} %bitcast.6, ...), custom_call_target="tpu_custom_call" | custom-call | tf_op jit(solution)/shard_map/model/pallas_call | solution.py:634
  42.4 0.5 collective-permute-start.7
  42.8 1.3 %collective-permute-done.7.got_ref = bf16[640,256]{1,0:T(8,128)(2,1)S(1)} collective-permute-done((bf16[640,256]{1,0:T(8,128)(2,1)S(1)}, bf16[640,256]{1,0:T(8,128)(2,1)S(1)}, u32[]{:S(2)}, u32[]{:S(2)}) %collective-permute-start.7) | collective-permute-done | bytes 327712 | tf_op jit(solution)/shard_map/ppermute | solution.py:158
  44.1 0.1 split.1
  44.2 1.6 %collective-permute-start.8 = (bf16[160,256]{1,0:T(8,128)(2,1)S(1)}, bf16[160,256]{1,0:T(8,128)(2,1)S(1)}, u32[]{:S(2)}, u32[]{:S(2)}) collective-permute-start(bf16[160,256]{1,0:T(8,128)(2,1)S(1)} %get-tuple-element.45), channel_id=1, source_target_pairs={{0,8},{8,0},{16,24},{24,16},{1,9},{9,1},{17,25},{25,17},{2,10},{10... | collective-permute-start | bytes 245768 | tf_op jit(solution)/shard_map/ppermute | solution.py:158
  45.7 1.5 %collective-permute-start.9 = (bf16[160,256]{1,0:T(8,128)(2,1)S(1)}, bf16[160,256]{1,0:T(8,128)(2,1)S(1)}, u32[]{:S(2)}, u32[]{:S(2)}) collective-permute-start(bf16[160,256]{1,0:T(8,128)(2,1)S(1)} %get-tuple-element.46), channel_id=1, source_target_pairs={{0,16},{8,24},{16,0},{24,8},{1,17},{9,25},{17,1},{25,9},{2,18},{10... | collective-permute-start | bytes 245768 | tf_op jit(solution)/shard_map/ppermute | solution.py:158
  47.3 0.5 collective-permute-start.10
  47.7 1.2 %collective-permute-done.8.one_ref = bf16[160,256]{1,0:T(8,128)(2,1)S(1)} collective-permute-done((bf16[160,256]{1,0:T(8,128)(2,1)S(1)}, bf16[160,256]{1,0:T(8,128)(2,1)S(1)}, u32[]{:S(2)}, u32[]{:S(2)}) %collective-permute-start.8) | collective-permute-done | bytes 81952 | tf_op jit(solution)/shard_map/ppermute | solution.py:158
  49.0 2.0 %collective-permute-done.9.two_ref = bf16[160,256]{1,0:T(8,128)(2,1)S(1)} collective-permute-done((bf16[160,256]{1,0:T(8,128)(2,1)S(1)}, bf16[160,256]{1,0:T(8,128)(2,1)S(1)}, u32[]{:S(2)}, u32[]{:S(2)}) %collective-permute-start.9) | collective-permute-done | bytes 81952 | tf_op jit(solution)/shard_map/ppermute | solution.py:158
  51.0 1.6 %collective-permute-done.10.three_ref = bf16[160,256]{1,0:T(8,128)(2,1)S(1)} collective-permute-done((bf16[160,256]{1,0:T(8,128)(2,1)S(1)}, bf16[160,256]{1,0:T(8,128)(2,1)S(1)}, u32[]{:S(2)}, u32[]{:S(2)}) %collective-permute-start.10) | collective-permute-done | bytes 81952 | tf_op jit(solution)/shard_map/ppermute | solution.py:158
  52.6 2.6 %collective-permute-start.13 = (bf16[160,256]{1,0:T(8,128)(2,1)S(1)}, bf16[160,256]{1,0:T(8,128)(2,1)S(1)}, u32[]{:S(2)}, u32[]{:S(2)}) collective-permute-start(bf16[160,256]{1,0:T(8,128)(2,1)S(1)} %join.2.own_ref), channel_id=1, source_target_pairs={{0,6},{1,7},{2,4},{3,5},{4,2},{5,3},{6,0},{7,1},{8,14},{9,15},{10,... | collective-permute-start | bytes 245768 | tf_op jit(solution)/shard_map/ppermute | solution.py:158
  55.2 0.0 collective-permute-start.12
  55.2 1.9 %collective-permute-start.11 = (bf16[160,256]{1,0:T(8,128)(2,1)S(1)}, bf16[160,256]{1,0:T(8,128)(2,1)S(1)}, u32[]{:S(2)}, u32[]{:S(2)}) collective-permute-start(bf16[160,256]{1,0:T(8,128)(2,1)S(1)} %join.2.own_ref), channel_id=1, source_target_pairs={{0,2},{1,3},{2,0},{3,1},{4,6},{5,7},{6,4},{7,5},{8,10},{9,11},{10,... | collective-permute-start | bytes 245768 | tf_op jit(solution)/shard_map/ppermute | solution.py:158
  57.1 2.5 %collective-permute-done.13.three_ref = bf16[160,256]{1,0:T(8,128)(2,1)S(1)} collective-permute-done((bf16[160,256]{1,0:T(8,128)(2,1)S(1)}, bf16[160,256]{1,0:T(8,128)(2,1)S(1)}, u32[]{:S(2)}, u32[]{:S(2)}) %collective-permute-start.13) | collective-permute-done | bytes 81952 | tf_op jit(solution)/shard_map/ppermute | solution.py:158
  59.6 2.3 %collective-permute-done.12.two_ref = bf16[160,256]{1,0:T(8,128)(2,1)S(1)} collective-permute-done((bf16[160,256]{1,0:T(8,128)(2,1)S(1)}, bf16[160,256]{1,0:T(8,128)(2,1)S(1)}, u32[]{:S(2)}, u32[]{:S(2)}) %collective-permute-start.12) | collective-permute-done | bytes 81952 | tf_op jit(solution)/shard_map/ppermute | solution.py:158
  61.9 0.0 collective-permute-done.11.one_ref
  62.0 0.9 %collective-permute-start.16 = (bf16[160,256]{1,0:T(8,128)(2,1)S(1)}, bf16[160,256]{1,0:T(8,128)(2,1)S(1)}, u32[]{:S(2)}, u32[]{:S(2)}) collective-permute-start(bf16[160,256]{1,0:T(8,128)(2,1)S(1)} %join.3.piece_0), channel_id=1, source_target_pairs={{0,24},{8,16},{16,8},{24,0},{1,25},{9,17},{17,9},{25,1},{2,26},{10... | collective-permute-start | bytes 245768 | tf_op jit(solution)/shard_map/ppermute | solution.py:158
  62.9 1.5 %collective-permute-start.15 = (bf16[160,256]{1,0:T(8,128)(2,1)S(1)}, bf16[160,256]{1,0:T(8,128)(2,1)S(1)}, u32[]{:S(2)}, u32[]{:S(2)}) collective-permute-start(bf16[160,256]{1,0:T(8,128)(2,1)S(1)} %join.3.piece_0), channel_id=1, source_target_pairs={{0,16},{8,24},{16,0},{24,8},{1,17},{9,25},{17,1},{25,9},{2,18},{10... | collective-permute-start | bytes 245768 | tf_op jit(solution)/shard_map/ppermute | solution.py:158
  64.3 1.2 %collective-permute-start.14 = (bf16[160,256]{1,0:T(8,128)(2,1)S(1)}, bf16[160,256]{1,0:T(8,128)(2,1)S(1)}, u32[]{:S(2)}, u32[]{:S(2)}) collective-permute-start(bf16[160,256]{1,0:T(8,128)(2,1)S(1)} %join.3.piece_0), channel_id=1, source_target_pairs={{0,8},{8,0},{16,24},{24,16},{1,9},{9,1},{17,25},{25,17},{2,10},{10... | collective-permute-start | bytes 245768 | tf_op jit(solution)/shard_map/ppermute | solution.py:158
  65.5 0.0 collective-permute-start.17
  65.5 2.1 %collective-permute-done.16.piece_3 = bf16[160,256]{1,0:T(8,128)(2,1)S(1)} collective-permute-done((bf16[160,256]{1,0:T(8,128)(2,1)S(1)}, bf16[160,256]{1,0:T(8,128)(2,1)S(1)}, u32[]{:S(2)}, u32[]{:S(2)}) %collective-permute-start.16) | collective-permute-done | bytes 81952 | tf_op jit(solution)/shard_map/ppermute | solution.py:158
  67.6 0.0 collective-permute-start.20
  67.6 0.6 collective-permute-done.15.piece_2
  68.2 0.0 collective-permute-start.19
  68.2 0.6 collective-permute-done.14.piece_1
  68.8 0.0 collective-permute-start.18
  68.8 0.0 collective-permute-done.17.piece_4
  68.8 0.1 collective-permute-done.20.piece_7
  68.8 0.6 collective-permute-done.19.piece_6
  69.5 0.6 collective-permute-done.18.piece_5
  70.2 2.6 %update.1 = (f32[16,256]{1,0:T(8,128)}, f32[2,2,32,256]{3,2,1,0:T(8,128)}, f32[8,40]{1,0:T(8,128)}, f32[1128]{0:T(1024)}, f32[16,128]{1,0:T(8,128)}, /*index=5*/...) custom-call(s32[1]{0:T(128)} %bitcast.refs_1_.refs_2_.dom_ref.spot_r, ...), custom_call_target="tpu_custom_call" | custom-call | tf_op jit(solution)/shard_map/update/pallas_call | solution.py:959
  (38 shorter events, 0.2 us)
Async XLA Ops:
  0.7 16.2 %copy-start.13 = (f32[8,40]{1,0:T(8,128)S(1)}, f32[8,40]{1,0:T(8,128)}, u32[]{:S(2)}) copy-start(f32[8,40]{1,0:T(8,128)} %w_out.1) | copy-start | bytes 3844
  0.7 16.2 %copy-start.1 = (f32[2,2,32,256]{3,2,1,0:T(8,128)S(1)}, f32[2,2,32,256]{3,2,1,0:T(8,128)}, u32[]{:S(2)}) copy-start(f32[2,2,32,256]{3,2,1,0:T(8,128)} %w_gat.1) | copy-start | bytes 393220
  0.7 16.2 %copy-start.7 = (f32[16,256]{1,0:T(8,128)S(1)}, f32[16,256]{1,0:T(8,128)}, u32[]{:S(2)}) copy-start(f32[16,256]{1,0:T(8,128)} %w_in.1) | copy-start | bytes 49156
  0.7 16.2 %copy-start.9 = (s32[4,2048]{1,0:T(4,128)S(1)}, s32[4,2048]{1,0:T(4,128)}, u32[]{:S(2)}) copy-start(s32[4,2048]{1,0:T(4,128)} %refs_6_.1) | copy-start | bytes 98308
  0.7 16.2 %copy-start.8 = (s32[4,2048]{1,0:T(4,128)S(1)}, s32[4,2048]{1,0:T(4,128)}, u32[]{:S(2)}) copy-start(s32[4,2048]{1,0:T(4,128)} %refs_5_.1) | copy-start | bytes 98308
  0.7 16.2 %copy-start.23 = (s32[4,64]{1,0:T(4,128)S(1)}, s32[4,64]{1,0:T(4,128)}, u32[]{:S(2)}) copy-start(s32[4,64]{1,0:T(4,128)} %refs_7_.1) | copy-start | bytes 3076
  0.7 16.2 %copy-start = (bf16[4,2048,128]{2,1,0:T(8,128)(2,1)S(1)}, bf16[4,2048,128]{2,1,0:T(8,128)(2,1)}, u32[]{:S(2)}) copy-start(bf16[4,2048,128]{2,1,0:T(8,128)(2,1)} %refs_3_.1) | copy-start | bytes 6291460
  0.7 16.2 %copy-start.4 = (s32[4,2048,8]{1,2,0:T(8,128)S(1)}, s32[4,2048,8]{1,2,0:T(8,128)}, u32[]{:S(2)}) copy-start(s32[4,2048,8]{1,2,0:T(8,128)} %param.28) | copy-start | bytes 786436
  0.7 16.2 %copy-start.14 = (f32[1128]{0:T(1024)S(1)}, f32[1128]{0:T(1024)}, u32[]{:S(2)}) copy-start(f32[1128]{0:T(1024)} %small.1) | copy-start | bytes 13540
  2.6 8.6 %collective-permute-start.2 = (bf16[176,256]{1,0:T(8,128)(2,1)}, bf16[176,256]{1,0:T(8,128)(2,1)S(1)}, u32[]{:S(2)}, u32[]{:S(2)}) collective-permute-start(bf16[176,256]{1,0:T(8,128)(2,1)} %pack.1), channel_id=1, source_target_pairs={{0,6},{1,7},{2,4},{3,5},{4,2},{5,3},{6,0},{7,1},{8,14},{9,15},{10,... | collective-permute-start | bytes 270344 | tf_op jit(solution)/shard_map/ppermute | solution.py:158
  7.7 7.8 %collective-permute-start.1 = (bf16[176,256]{1,0:T(8,128)(2,1)}, bf16[176,256]{1,0:T(8,128)(2,1)S(1)}, u32[]{:S(2)}, u32[]{:S(2)}) collective-permute-start(bf16[176,256]{1,0:T(8,128)(2,1)} %pack.1), channel_id=1, source_target_pairs={{0,4},{1,5},{2,6},{3,7},{4,0},{5,1},{6,2},{7,3},{8,12},{9,13},{10,... | collective-permute-start | bytes 270344 | tf_op jit(solution)/shard_map/ppermute | solution.py:158
  7.7 7.8 %collective-permute-start = (bf16[176,256]{1,0:T(8,128)(2,1)}, bf16[176,256]{1,0:T(8,128)(2,1)S(1)}, u32[]{:S(2)}, u32[]{:S(2)}) collective-permute-start(bf16[176,256]{1,0:T(8,128)(2,1)} %pack.1), channel_id=1, source_target_pairs={{0,2},{1,3},{2,0},{3,1},{4,6},{5,7},{6,4},{7,5},{8,10},{9,11},{10,... | collective-permute-start | bytes 270344 | tf_op jit(solution)/shard_map/ppermute | solution.py:158
  8.2 7.7 %collective-permute-start.3 = (bf16[176,256]{1,0:T(8,128)(2,1)}, bf16[176,256]{1,0:T(8,128)(2,1)S(1)}, u32[]{:S(2)}, u32[]{:S(2)}) collective-permute-start(bf16[176,256]{1,0:T(8,128)(2,1)} %pack.1), channel_id=1, source_target_pairs={{0,1},{1,0},{2,3},{3,2},{4,5},{5,4},{6,7},{7,6},{8,9},{9,8},{10,11... | collective-permute-start | bytes 270344 | tf_op jit(solution)/shard_map/ppermute | solution.py:158
  11.2 4.7 %collective-permute-start.6 = (bf16[176,256]{1,0:T(8,128)(2,1)S(1)}, bf16[176,256]{1,0:T(8,128)(2,1)S(1)}, u32[]{:S(2)}, u32[]{:S(2)}) collective-permute-start(bf16[176,256]{1,0:T(8,128)(2,1)S(1)} %collective-permute-done.2.refs_10_), channel_id=1, source_target_pairs={{0,1},{1,0},{2,3},{3,2},{4,5},{5,4},{6,7},{7,6},{8,9},{9,8},{10,11... | collective-permute-start | bytes 270344 | tf_op jit(solution)/shard_map/ppermute | solution.py:158
  15.4 1.3 %collective-permute-start.5 = (bf16[176,256]{1,0:T(8,128)(2,1)S(1)}, bf16[176,256]{1,0:T(8,128)(2,1)S(1)}, u32[]{:S(2)}, u32[]{:S(2)}) collective-permute-start(bf16[176,256]{1,0:T(8,128)(2,1)S(1)} %collective-permute-done.1.refs_9_), channel_id=1, source_target_pairs={{0,1},{1,0},{2,3},{3,2},{4,5},{5,4},{6,7},{7,6},{8,9},{9,8},{10,11... | collective-permute-start | bytes 270344 | tf_op jit(solution)/shard_map/ppermute | solution.py:158
  15.5 1.4 %collective-permute-start.4 = (bf16[176,256]{1,0:T(8,128)(2,1)S(1)}, bf16[176,256]{1,0:T(8,128)(2,1)S(1)}, u32[]{:S(2)}, u32[]{:S(2)}) collective-permute-start(bf16[176,256]{1,0:T(8,128)(2,1)S(1)} %collective-permute-done.refs_8_), channel_id=1, source_target_pairs={{0,1},{1,0},{2,3},{3,2},{4,5},{5,4},{6,7},{7,6},{8,9},{9,8},{10,11... | collective-permute-start | bytes 270344 | tf_op jit(solution)/shard_map/ppermute | solution.py:158
  17.0 53.1 %copy-start.2 = (f32[2,2,256,256]{3,2,1,0:T(8,128)S(1)}, f32[2,2,256,256]{3,2,1,0:T(8,128)}, u32[]{:S(2)}) copy-start(f32[2,2,256,256]{3,2,1,0:T(8,128)} %r_gat.1) | copy-start | bytes 3145732
  17.0 53.1 %copy-start.3 = (f32[2,2,256,256]{3,2,1,0:T(8,128)S(1)}, f32[2,2,256,256]{3,2,1,0:T(8,128)}, u32[]{:S(2)}) copy-start(f32[2,2,256,256]{3,2,1,0:T(8,128)} %rr_gat.1) | copy-start | bytes 3145732
  17.0 53.1 %copy-start.5 = (f32[256,256]{1,0:T(8,128)S(1)}, f32[256,256]{1,0:T(8,128)}, u32[]{:S(2)}) copy-start(f32[256,256]{1,0:T(8,128)} %r_in.1) | copy-start | bytes 786436
  17.0 53.1 %copy-start.6 = (f32[256,256]{1,0:T(8,128)S(1)}, f32[256,256]{1,0:T(8,128)}, u32[]{:S(2)}) copy-start(f32[256,256]{1,0:T(8,128)} %rr_in.1) | copy-start | bytes 786436
  17.0 53.1 %copy-start.10 = (f32[2,2,32,256]{3,2,1,0:T(8,128)S(1)}, f32[2,2,32,256]{3,2,1,0:T(8,128)}, u32[]{:S(2)}) copy-start(f32[2,2,32,256]{3,2,1,0:T(8,128)} %l_gat.1) | copy-start | bytes 393220
  17.0 53.1 %copy-start.11 = (f32[2,2,32,256]{3,2,1,0:T(8,128)S(1)}, f32[2,2,32,256]{3,2,1,0:T(8,128)}, u32[]{:S(2)}) copy-start(f32[2,2,32,256]{3,2,1,0:T(8,128)} %rl_gat.1) | copy-start | bytes 393220
  17.0 53.1 %copy-start.12 = (f32[2,2,32,256]{3,2,1,0:T(8,128)S(1)}, f32[2,2,32,256]{3,2,1,0:T(8,128)}, u32[]{:S(2)}) copy-start(f32[2,2,32,256]{3,2,1,0:T(8,128)} %e_gat.1) | copy-start | bytes 393220
  17.0 53.1 %copy-start.15 = (f32[40,40]{1,0:T(8,128)S(1)}, f32[40,40]{1,0:T(8,128)}, u32[]{:S(2)}) copy-start(f32[40,40]{1,0:T(8,128)} %r_out.1) | copy-start | bytes 19204
  17.1 53.1 %copy-start.16 = (f32[40,40]{1,0:T(8,128)S(1)}, f32[40,40]{1,0:T(8,128)}, u32[]{:S(2)}) copy-start(f32[40,40]{1,0:T(8,128)} %rr_out.1) | copy-start | bytes 19204
  17.1 53.1 %copy-start.17 = (f32[16,256]{1,0:T(8,128)S(1)}, f32[16,256]{1,0:T(8,128)}, u32[]{:S(2)}) copy-start(f32[16,256]{1,0:T(8,128)} %e_in.1) | copy-start | bytes 49156
  17.1 53.1 %copy-start.18 = (f32[16,128]{1,0:T(8,128)S(1)}, f32[16,128]{1,0:T(8,128)}, u32[]{:S(2)}) copy-start(f32[16,128]{1,0:T(8,128)} %l_in.1) | copy-start | bytes 24580
  17.1 53.1 %copy-start.19 = (f32[16,128]{1,0:T(8,128)S(1)}, f32[16,128]{1,0:T(8,128)}, u32[]{:S(2)}) copy-start(f32[16,128]{1,0:T(8,128)} %rl_in.1) | copy-start | bytes 24580
  17.1 53.1 %copy-start.20 = (f32[1128]{0:T(1024)S(1)}, f32[1128]{0:T(1024)}, u32[]{:S(2)}) copy-start(f32[1128]{0:T(1024)} %first.1) | copy-start | bytes 13540
  17.1 53.0 %copy-start.21 = (f32[1128]{0:T(1024)S(1)}, f32[1128]{0:T(1024)}, u32[]{:S(2)}) copy-start(f32[1128]{0:T(1024)} %second.1) | copy-start | bytes 13540
  17.1 53.0 %copy-start.22 = (f32[1128]{0:T(1024)S(1)}, f32[1128]{0:T(1024)}, u32[]{:S(2)}) copy-start(f32[1128]{0:T(1024)} %e_small.1) | copy-start | bytes 13540
  17.1 53.0 %copy-start.24 = (f32[8,64]{1,0:T(8,128)S(1)}, f32[8,64]{1,0:T(8,128)}, u32[]{:S(2)}) copy-start(f32[8,64]{1,0:T(8,128)} %l_out.1) | copy-start | bytes 6148
  17.2 53.0 %copy-start.25 = (f32[8,64]{1,0:T(8,128)S(1)}, f32[8,64]{1,0:T(8,128)}, u32[]{:S(2)}) copy-start(f32[8,64]{1,0:T(8,128)} %rl_out.1) | copy-start | bytes 6148
  17.2 53.0 %copy-start.26 = (f32[8,40]{1,0:T(8,128)S(1)}, f32[8,40]{1,0:T(8,128)}, u32[]{:S(2)}) copy-start(f32[8,40]{1,0:T(8,128)} %e_out.1) | copy-start | bytes 3844
  42.4 1.7 %collective-permute-start.7 = (bf16[640,256]{1,0:T(8,128)(2,1)S(1)}, bf16[640,256]{1,0:T(8,128)(2,1)S(1)}, u32[]{:S(2)}, u32[]{:S(2)}) collective-permute-start(bf16[640,256]{1,0:T(8,128)(2,1)S(1)} %get-tuple-element.43), channel_id=1, source_target_pairs={{0,1},{1,0},{2,3},{3,2},{4,5},{5,4},{6,7},{7,6},{8,9},{9,8},{10,11... | collective-permute-start | bytes 983048 | tf_op jit(solution)/shard_map/ppermute | solution.py:158
  44.2 4.8 %collective-permute-start.8 = (bf16[160,256]{1,0:T(8,128)(2,1)S(1)}, bf16[160,256]{1,0:T(8,128)(2,1)S(1)}, u32[]{:S(2)}, u32[]{:S(2)}) collective-permute-start(bf16[160,256]{1,0:T(8,128)(2,1)S(1)} %get-tuple-element.45), channel_id=1, source_target_pairs={{0,8},{8,0},{16,24},{24,16},{1,9},{9,1},{17,25},{25,17},{2,10},{10... | collective-permute-start | bytes 245768 | tf_op jit(solution)/shard_map/ppermute | solution.py:158
  45.7 5.3 %collective-permute-start.9 = (bf16[160,256]{1,0:T(8,128)(2,1)S(1)}, bf16[160,256]{1,0:T(8,128)(2,1)S(1)}, u32[]{:S(2)}, u32[]{:S(2)}) collective-permute-start(bf16[160,256]{1,0:T(8,128)(2,1)S(1)} %get-tuple-element.46), channel_id=1, source_target_pairs={{0,16},{8,24},{16,0},{24,8},{1,17},{9,25},{17,1},{25,9},{2,18},{10... | collective-permute-start | bytes 245768 | tf_op jit(solution)/shard_map/ppermute | solution.py:158
  47.3 5.3 %collective-permute-start.10 = (bf16[160,256]{1,0:T(8,128)(2,1)S(1)}, bf16[160,256]{1,0:T(8,128)(2,1)S(1)}, u32[]{:S(2)}, u32[]{:S(2)}) collective-permute-start(bf16[160,256]{1,0:T(8,128)(2,1)S(1)} %get-tuple-element.47), channel_id=1, source_target_pairs={{0,24},{8,16},{16,8},{24,0},{1,25},{9,17},{17,9},{25,1},{2,26},{10... | collective-permute-start | bytes 245768 | tf_op jit(solution)/shard_map/ppermute | solution.py:158
  52.6 7.0 %collective-permute-start.13 = (bf16[160,256]{1,0:T(8,128)(2,1)S(1)}, bf16[160,256]{1,0:T(8,128)(2,1)S(1)}, u32[]{:S(2)}, u32[]{:S(2)}) collective-permute-start(bf16[160,256]{1,0:T(8,128)(2,1)S(1)} %join.2.own_ref), channel_id=1, source_target_pairs={{0,6},{1,7},{2,4},{3,5},{4,2},{5,3},{6,0},{7,1},{8,14},{9,15},{10,... | collective-permute-start | bytes 245768 | tf_op jit(solution)/shard_map/ppermute | solution.py:158
  55.2 6.7 %collective-permute-start.12 = (bf16[160,256]{1,0:T(8,128)(2,1)S(1)}, bf16[160,256]{1,0:T(8,128)(2,1)S(1)}, u32[]{:S(2)}, u32[]{:S(2)}) collective-permute-start(bf16[160,256]{1,0:T(8,128)(2,1)S(1)} %join.2.own_ref), channel_id=1, source_target_pairs={{0,4},{1,5},{2,6},{3,7},{4,0},{5,1},{6,2},{7,3},{8,12},{9,13},{10,... | collective-permute-start | bytes 245768 | tf_op jit(solution)/shard_map/ppermute | solution.py:158
  55.2 6.7 %collective-permute-start.11 = (bf16[160,256]{1,0:T(8,128)(2,1)S(1)}, bf16[160,256]{1,0:T(8,128)(2,1)S(1)}, u32[]{:S(2)}, u32[]{:S(2)}) collective-permute-start(bf16[160,256]{1,0:T(8,128)(2,1)S(1)} %join.2.own_ref), channel_id=1, source_target_pairs={{0,2},{1,3},{2,0},{3,1},{4,6},{5,7},{6,4},{7,5},{8,10},{9,11},{10,... | collective-permute-start | bytes 245768 | tf_op jit(solution)/shard_map/ppermute | solution.py:158
  62.0 5.6 %collective-permute-start.16 = (bf16[160,256]{1,0:T(8,128)(2,1)S(1)}, bf16[160,256]{1,0:T(8,128)(2,1)S(1)}, u32[]{:S(2)}, u32[]{:S(2)}) collective-permute-start(bf16[160,256]{1,0:T(8,128)(2,1)S(1)} %join.3.piece_0), channel_id=1, source_target_pairs={{0,24},{8,16},{16,8},{24,0},{1,25},{9,17},{17,9},{25,1},{2,26},{10... | collective-permute-start | bytes 245768 | tf_op jit(solution)/shard_map/ppermute | solution.py:158
  62.9 5.3 %collective-permute-start.15 = (bf16[160,256]{1,0:T(8,128)(2,1)S(1)}, bf16[160,256]{1,0:T(8,128)(2,1)S(1)}, u32[]{:S(2)}, u32[]{:S(2)}) collective-permute-start(bf16[160,256]{1,0:T(8,128)(2,1)S(1)} %join.3.piece_0), channel_id=1, source_target_pairs={{0,16},{8,24},{16,0},{24,8},{1,17},{9,25},{17,1},{25,9},{2,18},{10... | collective-permute-start | bytes 245768 | tf_op jit(solution)/shard_map/ppermute | solution.py:158
  64.3 4.4 %collective-permute-start.14 = (bf16[160,256]{1,0:T(8,128)(2,1)S(1)}, bf16[160,256]{1,0:T(8,128)(2,1)S(1)}, u32[]{:S(2)}, u32[]{:S(2)}) collective-permute-start(bf16[160,256]{1,0:T(8,128)(2,1)S(1)} %join.3.piece_0), channel_id=1, source_target_pairs={{0,8},{8,0},{16,24},{24,16},{1,9},{9,1},{17,25},{25,17},{2,10},{10... | collective-permute-start | bytes 245768 | tf_op jit(solution)/shard_map/ppermute | solution.py:158
  65.5 3.3 %collective-permute-start.17 = (bf16[160,256]{1,0:T(8,128)(2,1)S(1)}, bf16[160,256]{1,0:T(8,128)(2,1)S(1)}, u32[]{:S(2)}, u32[]{:S(2)}) collective-permute-start(bf16[160,256]{1,0:T(8,128)(2,1)S(1)} %join.3.piece_0), channel_id=1, source_target_pairs={{0,1},{1,0},{2,3},{3,2},{4,5},{5,4},{6,7},{7,6},{8,9},{9,8},{10,11... | collective-permute-start | bytes 245768 | tf_op jit(solution)/shard_map/ppermute | solution.py:158
  67.6 1.3 %collective-permute-start.20 = (bf16[160,256]{1,0:T(8,128)(2,1)S(1)}, bf16[160,256]{1,0:T(8,128)(2,1)S(1)}, u32[]{:S(2)}, u32[]{:S(2)}) collective-permute-start(bf16[160,256]{1,0:T(8,128)(2,1)S(1)} %collective-permute-done.16.piece_3), channel_id=1, source_target_pairs={{0,1},{1,0},{2,3},{3,2},{4,5},{5,4},{6,7},{7,6},{8,9},{9,8},{10,11... | collective-permute-start | bytes 245768 | tf_op jit(solution)/shard_map/ppermute | solution.py:158
  68.2 1.3 %collective-permute-start.19 = (bf16[160,256]{1,0:T(8,128)(2,1)S(1)}, bf16[160,256]{1,0:T(8,128)(2,1)S(1)}, u32[]{:S(2)}, u32[]{:S(2)}) collective-permute-start(bf16[160,256]{1,0:T(8,128)(2,1)S(1)} %collective-permute-done.15.piece_2), channel_id=1, source_target_pairs={{0,1},{1,0},{2,3},{3,2},{4,5},{5,4},{6,7},{7,6},{8,9},{9,8},{10,11... | collective-permute-start | bytes 245768 | tf_op jit(solution)/shard_map/ppermute | solution.py:158
  68.8 1.3 %collective-permute-start.18 = (bf16[160,256]{1,0:T(8,128)(2,1)S(1)}, bf16[160,256]{1,0:T(8,128)(2,1)S(1)}, u32[]{:S(2)}, u32[]{:S(2)}) collective-permute-start(bf16[160,256]{1,0:T(8,128)(2,1)S(1)} %collective-permute-done.14.piece_1), channel_id=1, source_target_pairs={{0,1},{1,0},{2,3},{3,2},{4,5},{5,4},{6,7},{7,6},{8,9},{9,8},{10,11... | collective-permute-start | bytes 245768 | tf_op jit(solution)/shard_map/ppermute | solution.py:158
